TPU v7x, 32 devices: a whole 2x2x4 slice. The times are simulated.
32 devices in a mesh: rep: 8 (over y, x, core), exp: 4 (over z).
Axes of the slice: x: 2, y: 2, z: 4, core: 2. Of those that a mesh axis runs over, the one named last changes fastest.
Arguments:
- tokens: bfloat16 [4096, 2048], P(('rep', 'exp')), may hold values from -6 to 6
- expert_ids: int32 [4096, 1], P(('rep', 'exp')), may hold values from 0 to 3
- norm_gain: float32 [2048], replicated, may hold values from 0.1 to 1.9
- up_weight: bfloat16 [4, 2048, 4096], P('exp', None, 'rep'), may hold values from -0.125 to 0.125
- down_weight: bfloat16 [4, 4096, 2048], P('exp', 'rep'), may hold values from -0.09375 to 0.09375
- cotangent: bfloat16 [4096, 2048], P(('rep', 'exp')), may hold values from -6 to 6
Outputs:
- mixed: bfloat16 [4096, 2048], P(('rep', 'exp'))
- grad_tokens: bfloat16 [4096, 2048], P(('rep', 'exp'))
- grad_up: bfloat16 [4, 2048, 4096], P('exp', None, 'rep')
- grad_down: bfloat16 [4, 4096, 2048], P('exp', 'rep')
- grad_gain: float32 [2048], replicated
All inputs are finite; a program needn't handle non-finite values.
Results may differ from a plain program's by a relative error of at most 0.014.
Values may be sent and summed in bfloat16 or wider, within the bound.
No kernel may reach another device: no remote copies, remote signals or barrier semaphores. Data moves between devices by JAX's collectives and lax.ppermute only.
A program may use at most 128 MiB of HBM per device.

v0:
```python
import jax
import jax.numpy as jnp
from jax import lax
from jax.sharding import PartitionSpec as P

gelu_coef = 0.7978845608028654
cubic_coef = 0.044715


def gelu_parts(inputs):
    inner = gelu_coef * (inputs + cubic_coef * inputs * inputs * inputs)
    tangent = jnp.tanh(inner)
    values = 0.5 * inputs * (1.0 + tangent)
    slopes = 0.5 * (1.0 + tangent) + 0.5 * inputs * (1.0 - tangent * tangent) * gelu_coef * (
        1.0 + 3.0 * cubic_coef * inputs * inputs
    )
    return (values, slopes)


def local(tokens, expert_ids, norm_gain, up_weight, down_weight, cotangent):
    groups = lax.axis_size("exp")
    copies = lax.axis_size("rep")
    tok_rows = tokens.shape[0]
    width = tokens.shape[1]
    capacity = 3 * tok_rows // (4 * groups)
    slot_total = groups * capacity
    wide_tokens = tokens.astype(jnp.float32)
    scales = lax.rsqrt(jnp.mean(wide_tokens * wide_tokens, axis=1, keepdims=True) + 1e-06)
    normed = (wide_tokens * scales * norm_gain).astype(jnp.bfloat16)
    expert_row = expert_ids[:, 0]
    one_hot = (expert_row[:, None] == jnp.arange(groups, dtype=jnp.int32)[None, :]).astype(
        jnp.int32
    )
    ranks = jnp.sum((jnp.cumsum(one_hot, axis=0) - one_hot) * one_hot, axis=1)
    slot_of = jnp.where(ranks < capacity, expert_row * capacity + ranks, -1)
    placing = (jnp.arange(slot_total, dtype=jnp.int32)[:, None] == slot_of[None, :]).astype(
        jnp.bfloat16
    )
    send_in = (
        jnp.dot(placing, normed, preferred_element_type=jnp.float32)
        .astype(jnp.bfloat16)
        .reshape(groups, capacity, width)
    )
    send_cot = (
        jnp.dot(placing, cotangent, preferred_element_type=jnp.float32)
        .astype(jnp.bfloat16)
        .reshape(groups, capacity, width)
    )
    recv_in, recv_cot = (
        lax.all_to_all(send_in, "exp", split_axis=0, concat_axis=0, tiled=True),
        lax.all_to_all(send_cot, "exp", split_axis=0, concat_axis=0, tiled=True),
    )
    rows_in, rows_cot = (
        lax.all_gather(recv_in, "rep", axis=0, tiled=True),
        lax.all_gather(recv_cot, "rep", axis=0, tiled=True),
    )
    row_total = copies * slot_total
    flat_in = rows_in.reshape(row_total, width)
    flat_cot = rows_cot.reshape(row_total, width)
    up_mat = up_weight[0]
    down_mat = down_weight[0]
    pre_act = jnp.dot(flat_in, up_mat, preferred_element_type=jnp.float32)
    values, slopes = gelu_parts(pre_act)
    hidden = values.astype(jnp.bfloat16)
    d_act = lax.dot_general(
        flat_cot, down_mat, (((1,), (1,)), ((), ())), preferred_element_type=jnp.float32
    )
    d_pre = (d_act * slopes).astype(jnp.bfloat16)
    grad_down = lax.dot_general(
        hidden, flat_cot, (((0,), (0,)), ((), ())), preferred_element_type=jnp.float32
    ).astype(jnp.bfloat16)
    grad_up = lax.dot_general(
        flat_in, d_pre, (((0,), (0,)), ((), ())), preferred_element_type=jnp.float32
    ).astype(jnp.bfloat16)
    out_terms = jnp.dot(hidden, down_mat, preferred_element_type=jnp.float32).reshape(
        copies * groups, capacity, width
    )
    back_terms = lax.dot_general(
        d_pre, up_mat, (((1,), (1,)), ((), ())), preferred_element_type=jnp.float32
    ).reshape(copies * groups, capacity, width)
    out_sum, back_sum = (
        lax.psum_scatter(
            out_terms.astype(jnp.bfloat16), "rep", scatter_dimension=0, tiled=True
        ).astype(jnp.float32),
        lax.psum_scatter(
            back_terms.astype(jnp.bfloat16), "rep", scatter_dimension=0, tiled=True
        ).astype(jnp.float32),
    )
    home_out, home_back = (
        lax.all_to_all(
            out_sum.astype(jnp.bfloat16), "exp", split_axis=0, concat_axis=0, tiled=True
        ),
        lax.all_to_all(
            back_sum.astype(jnp.bfloat16), "exp", split_axis=0, concat_axis=0, tiled=True
        ),
    )
    mixed = lax.dot_general(
        placing,
        home_out.reshape(slot_total, width),
        (((0,), (0,)), ((), ())),
        preferred_element_type=jnp.float32,
    ).astype(jnp.bfloat16)
    d_normed = lax.dot_general(
        placing,
        home_back.reshape(slot_total, width),
        (((0,), (0,)), ((), ())),
        preferred_element_type=jnp.float32,
    )
    gained = d_normed * norm_gain
    cubed = scales * scales * scales
    grad_tokens = (
        scales * gained
        - wide_tokens * cubed * jnp.mean(gained * wide_tokens, axis=1, keepdims=True)
    ).astype(jnp.bfloat16)
    grad_gain = lax.psum(jnp.sum(d_normed * wide_tokens * scales, axis=0), ("rep", "exp"))
    return (mixed, grad_tokens, grad_up[None], grad_down[None], grad_gain)


def solution(mesh):
    return jax.shard_map(
        local,
        mesh=mesh,
        in_specs=(
            P(("rep", "exp"), None),
            P(("rep", "exp"), None),
            P(),
            P("exp", None, "rep"),
            P("exp", "rep", None),
            P(("rep", "exp"), None),
        ),
        out_specs=(
            P(("rep", "exp"), None),
            P(("rep", "exp"), None),
            P("exp", None, "rep"),
            P("exp", "rep", None),
            P(),
        ),
        check_vma=False,
    )
```

profile of v0, /device:TPU:0, one launch (start us, length us, event | category | flops | bytes accessed | tf_op | source)
XLA Modules:
  0.0 259.7 jit_solution(7180434090292597934)
XLA Ops:
  7.2 0.0 all-gather.3.cloned.1.call-start
  7.2 1.4 fusion.17
  8.7 0.7 fusion.29
  9.4 0.2 reduce_window_sum.11
  9.6 0.8 select_reduce_fusion
  10.4 0.7 compare_select_fusion
  11.1 1.4 convolution_convert_fusion.6
  12.5 17.9 %all_to_all.20 = bf16[4,24,2048]{2,1,0:T(8,128)(2,1)} all-to-all(bf16[4,24,2048]{2,1,0:T(8,128)(2,1)S(1)} %bitcast.47), channel_id=1, replica_groups=mesh['rep'=8,'exp'=4] {'exp'}, dimensions={0} | all-to-all | bytes 786432 | tf_op jit(solution)/shard_map/all_to_all | solution.py:50
  30.4 0.0 all-gather.5.cloned.1.call-start
  30.5 0.3 convolution_convert_fusion.5
  30.7 13.9 %all_to_all.21 = bf16[4,24,2048]{2,1,0:T(8,128)(2,1)} all-to-all(bf16[4,24,2048]{2,1,0:T(8,128)(2,1)S(1)} %bitcast.44), channel_id=1, replica_groups=mesh['rep'=8,'exp'=4] {'exp'}, dimensions={0} | all-to-all | bytes 786432 | tf_op jit(solution)/shard_map/all_to_all | solution.py:51
  44.7 0.0 reduce-scatter.3.cloned.1.call-start
  44.7 17.3 %all-gather.3.cloned.1.call-done = bf16[32,24,2048]{2,1,0:T(8,128)(2,1)} async-done(((bf16[4,24,2048]{2,1,0:T(8,128)(2,1)}), bf16[32,24,2048]{2,1,0:T(8,128)(2,1)}) %all-gather.3.cloned.1.call-update) | async-done | bytes 3145744 | tf_op jit(solution)/shard_map/all_gather | solution.py:54
  62.0 5.2 %multiply_convert_fusion = (bf16[768,512]{1,0:T(8,128)(2,1)S(1)}, f32[768,512]{1,0:T(8,128)}) fusion(bf16[768,2048]{1,0:T(8,128)(2,1)} %bitcast.50, bf16[1,2048,512]{2,1,0:T(8,128)(2,1)S(1)} %copy-done), kind=kOutput, calls=%fused_computation.29 | convolution fusion | flops 1614151680 | bytes 7602176 | tf_op jit(solution)/shard_map/dot_general | solution.py:62
  67.2 0.9 copy-done.2
  68.0 3.5 %convolution_convert_fusion.1 = bf16[32,24,2048]{2,1,0:T(8,128)(2,1)} fusion(bf16[32,24,512]{2,1,0:T(8,128)(2,1)S(1)} %bitcast.45, bf16[1,512,2048]{2,1,0:T(8,128)(2,1)S(1)} %copy-done.5), kind=kOutput, calls=%fused_computation.1 | convolution fusion | flops 1612185600 | bytes 6029312 | tf_op jit(solution)/shard_map/dot_general | solution.py:75
  71.6 0.0 reduce-scatter.5.cloned.1.call-start
  71.6 24.6 %all-gather.5.cloned.1.call-done = bf16[32,24,2048]{2,1,0:T(8,128)(2,1)} async-done(((bf16[4,24,2048]{2,1,0:T(8,128)(2,1)}), bf16[32,24,2048]{2,1,0:T(8,128)(2,1)}) %all-gather.5.cloned.1.call-update) | async-done | bytes 3145744 | tf_op jit(solution)/shard_map/all_gather | solution.py:55
  96.2 5.5 %fusion.14 = bf16[768,512]{1,0:T(8,128)(2,1)S(1)} fusion(f32[768,512]{1,0:T(8,128)} %get-tuple-element.10, bf16[768,2048]{1,0:T(8,128)(2,1)} %bitcast.41, bf16[1,512,2048]{2,1,0:T(8,128)(2,1)} %param.10), kind=kOutput, calls=%fused_computation.28 | convolution fusion | flops 1618083840 | bytes 7602176 | tf_op jit(solution)/shard_map/dot_general | solution.py:65
  101.7 0.9 copy-done.6
  102.7 3.5 %convolution_convert_fusion = bf16[32,24,2048]{2,1,0:T(8,128)(2,1)} fusion(bf16[32,24,512]{2,1,0:T(8,128)(2,1)S(1)} %bitcast.52, bf16[1,2048,512]{2,1,0:T(8,128)(2,1)S(1)} %copy-done), kind=kOutput, calls=%fused_computation | convolution fusion | flops 1612185600 | bytes 6029312 | tf_op jit(solution)/shard_map/dot_general | solution.py:78
  106.2 39.7 %reduce-scatter.3.cloned.1.call-done = bf16[4,24,2048]{2,1,0:T(8,128)(2,1)} async-done(((bf16[32,24,2048]{2,1,0:T(8,128)(2,1)}), bf16[4,24,2048]{2,1,0:T(8,128)(2,1)}) %reduce-scatter.3.cloned.1.call-update) | async-done | bytes 393232 | tf_op jit(solution)/shard_map/reduce_scatter | solution.py:82
  145.9 4.6 %all-to-all-start.1 = ((bf16[4,24,2048]{2,1,0:T(8,128)(2,1)}), bf16[4,24,2048]{2,1,0:T(8,128)(2,1)S(1)}, u32[]{:S(2)}, u32[]{:S(2)}) async-start(bf16[4,24,2048]{2,1,0:T(8,128)(2,1)} %reduce-scatter.3.cloned.1.call-done), calls=%async_computation.2 | async-start | bytes 786432 | tf_op jit(solution)/shard_map/all_to_all | solution.py:90
  150.5 5.3 %fusion.1 = bf16[1,512,2048]{2,1,0:T(8,128)(2,1)} fusion(bf16[768,512]{1,0:T(8,128)(2,1)} %copy-done.2, bf16[768,2048]{1,0:T(8,128)(2,1)} %bitcast.42), kind=kOutput, calls=%fused_computation.5 | convolution fusion | flops 1611661312 | bytes 6029312 | tf_op jit(solution)/shard_map/dot_general | solution.py:69
  155.7 40.0 %reduce-scatter.5.cloned.1.call-done = bf16[4,24,2048]{2,1,0:T(8,128)(2,1)} async-done(((bf16[32,24,2048]{2,1,0:T(8,128)(2,1)}), bf16[4,24,2048]{2,1,0:T(8,128)(2,1)}) %reduce-scatter.5.cloned.1.call-update) | async-done | bytes 393232 | tf_op jit(solution)/shard_map/reduce_scatter | solution.py:85
  195.8 4.6 %all-to-all-start.3 = ((bf16[4,24,2048]{2,1,0:T(8,128)(2,1)}), bf16[4,24,2048]{2,1,0:T(8,128)(2,1)S(1)}, u32[]{:S(2)}, u32[]{:S(2)}) async-start(bf16[4,24,2048]{2,1,0:T(8,128)(2,1)} %reduce-scatter.5.cloned.1.call-done), calls=%async_computation.5 | async-start | bytes 786432 | tf_op jit(solution)/shard_map/all_to_all | solution.py:93
  200.4 5.3 %fusion = bf16[1,2048,512]{2,1,0:T(8,128)(2,1)} fusion(bf16[768,2048]{1,0:T(8,128)(2,1)} %bitcast.51, bf16[768,512]{1,0:T(8,128)(2,1)} %copy-done.6), kind=kOutput, calls=%fused_computation.4 | convolution fusion | flops 1611661312 | bytes 6029312 | tf_op jit(solution)/shard_map/dot_general | solution.py:72
  205.6 1.1 convolution_convert_fusion.4
  206.8 5.3 %all-to-all-done.3 = bf16[4,24,2048]{2,1,0:T(8,128)(2,1)S(1)} async-done(((bf16[4,24,2048]{2,1,0:T(8,128)(2,1)}), bf16[4,24,2048]{2,1,0:T(8,128)(2,1)S(1)}, u32[]{:S(2)}, u32[]{:S(2)}) %all-to-all-start.3) | async-done | bytes 393248 | tf_op jit(solution)/shard_map/all_to_all | solution.py:93
  212.0 1.4 fusion.25
  213.4 37.3 %psum.7 = f32[2048]{0:T(1024)} all-reduce(f32[2048]{0:T(1024)S(1)} %get-tuple-element.5), channel_id=1, replica_groups=mesh['rep'=8,'exp'=4] {'rep','exp'}, use_global_device_ids=true, to_apply=%region_7.8 | all-reduce | flops 2048 | bytes 16384 | tf_op jit(solution)/shard_map/psum | solution.py:115
  250.7 2.4 fusion.22
  (19 shorter events, 0.1 us)
Async XLA Ops:
  7.2 54.8 %copy-start = (bf16[1,2048,512]{2,1,0:T(8,128)(2,1)S(1)}, bf16[1,2048,512]{2,1,0:T(8,128)(2,1)}, u32[]{:S(2)}) copy-start(bf16[1,2048,512]{2,1,0:T(8,128)(2,1)} %param.9) | copy-start | bytes 6291460
  7.2 23.3 %copy-start.3 = (bf16[128,2048]{1,0:T(8,128)(2,1)S(1)}, bf16[128,2048]{1,0:T(8,128)(2,1)}, u32[]{:S(2)}) copy-start(bf16[128,2048]{1,0:T(8,128)(2,1)} %param.11) | copy-start | bytes 1572868
  7.2 54.8 %all-gather.3.cloned.1.call-start = ((), (), s32[]{:S(2)}) async-start(), calls=%async_computation.6 | async-start | bytes 3538944 | tf_op jit(solution)/shard_map/all_gather | solution.py:54
  30.4 65.8 %all-gather.5.cloned.1.call-start = ((), (), s32[]{:S(2)}) async-start(), calls=%async_computation.8 | async-start | bytes 3538944 | tf_op jit(solution)/shard_map/all_gather | solution.py:55
  44.7 101.2 %reduce-scatter.3.cloned.1.call-start = ((), (), s32[]{:S(2)}) async-start(), calls=%async_computation.7 | async-start | bytes 3538944 | tf_op jit(solution)/shard_map/reduce_scatter | solution.py:82
  62.0 6.1 %copy-start.5 = (bf16[1,512,2048]{2,1,0:T(8,128)(2,1)S(1)}, bf16[1,512,2048]{2,1,0:T(8,128)(2,1)}, u32[]{:S(2)}) copy-start(bf16[1,512,2048]{2,1,0:T(8,128)(2,1)} %param.10) | copy-start | bytes 6291460
  67.2 0.9 copy-start.2
  71.6 124.1 %reduce-scatter.5.cloned.1.call-start = ((), (), s32[]{:S(2)}) async-start(), calls=%async_computation.9 | async-start | bytes 3538944 | tf_op jit(solution)/shard_map/reduce_scatter | solution.py:85
  101.7 0.9 copy-start.6
  145.9 49.9 %all-to-all-start.1 = ((bf16[4,24,2048]{2,1,0:T(8,128)(2,1)}), bf16[4,24,2048]{2,1,0:T(8,128)(2,1)S(1)}, u32[]{:S(2)}, u32[]{:S(2)}) async-start(bf16[4,24,2048]{2,1,0:T(8,128)(2,1)} %reduce-scatter.3.cloned.1.call-done), calls=%async_computation.2 | async-start | bytes 786432 | tf_op jit(solution)/shard_map/all_to_all | solution.py:90
  195.8 16.3 %all-to-all-start.3 = ((bf16[4,24,2048]{2,1,0:T(8,128)(2,1)}), bf16[4,24,2048]{2,1,0:T(8,128)(2,1)S(1)}, u32[]{:S(2)}, u32[]{:S(2)}) async-start(bf16[4,24,2048]{2,1,0:T(8,128)(2,1)} %reduce-scatter.5.cloned.1.call-done), calls=%async_computation.5 | async-start | bytes 786432 | tf_op jit(solution)/shard_map/all_to_all | solution.py:93
  200.4 11.7 %copy-start.1 = (bf16[128,2048]{1,0:T(8,128)(2,1)S(1)}, bf16[128,2048]{1,0:T(8,128)(2,1)}, u32[]{:S(2)}) copy-start(bf16[128,2048]{1,0:T(8,128)(2,1)} %param.6) | copy-start | bytes 1572868
  200.4 11.7 %copy-start.4 = (f32[2048]{0:T(1024)S(1)}, f32[2048]{0:T(1024)}, u32[]{:S(2)}) copy-start(f32[2048]{0:T(1024)} %param.8) | copy-start | bytes 24580
Sparse Core Ops, SparseCore 0:
  30.5 31.4 all-gather.2
  63.9 32.3 all-gather.4
  99.6 46.2 reduce-scatter.2
  149.5 46.2 reduce-scatter.4
where the time goes:
time: 261 us; the launch traced here: 260 us
  waiting for transfers between devices  127 us (49%)
  blocking collectives  69.1 us (26%)
  matrix products  32.4 us (12%)
  between operations  13.8 us (5%)
  starting transfers between devices  9.36 us (4%)
  other arithmetic  6.27 us (2%)
    reduce_scatter x1, waiting for transfers between devices, local(): lax.psum_scatter(back_terms.astype(jnp.bfloat16), 'rep', scatter_dimensio...  40 us
    reduce_scatter x1, waiting for transfers between devices, local(): lax.psum_scatter(out_terms.astype(jnp.bfloat16), 'rep', scatter_dimension...  39.7 us
    psum x1, blocking collectives, local(): lax.psum(jnp.sum(d_normed * wide_tokens * scales, axis=0), ('rep', 'exp'))  37.3 us
    all_gather x1, waiting for transfers between devices, local(): lax.all_gather(recv_cot, 'rep', axis=0, tiled=True)  24.6 us
    all_to_all x1, blocking collectives, local(): lax.all_to_all(send_in, 'exp', split_axis=0, concat_axis=0, tiled=True)  17.9 us
    all_gather x1, waiting for transfers between devices, local(): lax.all_gather(recv_in, 'rep', axis=0, tiled=True)  17.3 us
    all_to_all x1, blocking collectives, local(): lax.all_to_all(send_cot, 'exp', split_axis=0, concat_axis=0, tiled=True)  13.9 us
    dot_general x1, matrix products, local(): lax.dot_general(flat_cot, down_mat, (((1,), (1,)), ((), ())), preferred_e...  5.51 us
  transfers between devices with their start and end apart: 6, of which 5 were waited for; matrix products, arithmetic and copies ran while one was open for 11% of the time, Pallas kernels for 0%

commit v1 on v0

v1 whole, which is shorter than its diff:
```python
import functools

import jax
import jax.numpy as jnp
from jax import lax
from jax.experimental import pallas as pl
from jax.experimental.pallas import tpu as pltpu
from jax.sharding import PartitionSpec as P

gelu_coef = 0.7978845608028654
cubic_coef = 0.044715
bf16 = jnp.bfloat16
f32 = jnp.float32
NN = (((1,), (0,)), ((), ()))
NT = (((1,), (1,)), ((), ()))
TN = (((0,), (0,)), ((), ()))


def mm(a, b, dims=NN):
    return lax.dot_general(a, b, dims, preferred_element_type=f32)


def gelu_parts(inputs):
    inner = gelu_coef * (inputs + cubic_coef * inputs * inputs * inputs)
    tangent = jnp.tanh(inner)
    values = 0.5 * inputs * (1.0 + tangent)
    slopes = 0.5 * (1.0 + tangent) + 0.5 * inputs * (1.0 - tangent * tangent) * gelu_coef * (
        1.0 + 3.0 * cubic_coef * inputs * inputs
    )
    return (values, slopes)


def call(kernel, out_shape, args, flops=0, moved=0):
    vmem = pl.BlockSpec(memory_space=pltpu.VMEM)
    return pl.pallas_call(
        kernel,
        out_shape=out_shape,
        in_specs=[vmem] * len(args),
        out_specs=jax.tree.map(lambda _: vmem, out_shape),
        compiler_params=pltpu.CompilerParams(vmem_limit_bytes=48 * 1024 * 1024),
        cost_estimate=pl.CostEstimate(flops=flops, bytes_accessed=moved, transcendentals=0),
    )(*args)


def shaped(shape, dtype=bf16):
    return jax.ShapeDtypeStruct(shape, dtype)


def place_kernel(groups, capacity, tok_ref, id_ref, me_ref, gain_ref, cot_ref, slot_ref, *sends):
    count = tok_ref.shape[0]
    id_row = jnp.broadcast_to(id_ref[...], (count, count))
    id_col = jnp.transpose(id_row)
    at_row = lax.broadcasted_iota(jnp.int32, (count, count), 0)
    at_col = lax.broadcasted_iota(jnp.int32, (count, count), 1)
    earlier = jnp.where((id_row == id_col) & (at_row < at_col), 1, 0)
    ranks = jnp.sum(earlier, axis=0, keepdims=True)
    ahead = id_ref[...] - me_ref[...]
    ahead = jnp.where(ahead < 0, ahead + groups, ahead)
    slots = jnp.where(ranks < capacity, ahead * capacity + ranks, -1)
    slot_ref[...] = slots
    wide = tok_ref[...].astype(f32)
    scales = lax.rsqrt(jnp.mean(wide * wide, axis=1, keepdims=True) + 1e-06)
    normed = (wide * scales * gain_ref[...]).astype(bf16)
    cots = cot_ref[...]
    for k in range(groups):
        rows = lax.broadcasted_iota(jnp.int32, (capacity, count), 0) + k * capacity
        placing = jnp.where(rows == slots, 1.0, 0.0).astype(bf16)
        sends[k][...] = mm(placing, normed).astype(bf16)
        sends[groups + k][...] = mm(placing, cots).astype(bf16)


def forward_kernel(in_ref, up_a, up_b, down_a, down_b, hid_a, hid_b, slope_ref, keep_a, send_a, keep_b, send_b):
    units = up_a.shape[1]
    width = in_ref.shape[1]
    for j, (up, hid) in enumerate(((up_a, hid_a), (up_b, hid_b))):
        step = min(units, 256)

        @pl.loop(0, units // step)
        def _(i):
            at = pl.ds(pl.multiple_of(i * step, step), step)
            values, slopes = gelu_parts(mm(in_ref[...], up[:, at]))
            hid[:, at] = values.astype(bf16)
            slope_ref[j, :, at] = slopes

    quarter = in_ref.shape[0] // 4

    @pl.loop(0, width // 256)
    def _(i):
        at = pl.ds(pl.multiple_of(i * 256, 256), 256)
        total = mm(hid_a[...], down_a[:, at]) + mm(hid_b[...], down_b[:, at])
        keep_a[:, at] = total[:quarter]
        send_a[:, at] = total[quarter : 2 * quarter].astype(bf16)
        keep_b[:, at] = total[2 * quarter : 3 * quarter]
        send_b[:, at] = total[3 * quarter :].astype(bf16)


def backward_kernel(
    cot_ref, in_ref, slope_ref, up_a, up_b, down_a, down_b, pre_a, pre_b, gain_ref, keep_a, send_a, keep_b, send_b
):
    units = up_a.shape[1]
    width = in_ref.shape[1]
    for j, (down, pre) in enumerate(((down_a, pre_a), (down_b, pre_b))):
        step = min(units, 256)

        @pl.loop(0, units // step)
        def _(i):
            at = pl.ds(pl.multiple_of(i * step, step), step)
            pre[:, at] = (mm(cot_ref[...], down[at, :], NT) * slope_ref[j, :, at]).astype(bf16)

    quarter = in_ref.shape[0] // 4

    @pl.loop(0, width // 256)
    def _(i):
        at = pl.ds(pl.multiple_of(i * 256, 256), 256)
        total = mm(pre_a[...], up_a[at, :], NT) + mm(pre_b[...], up_b[at, :], NT)
        gain_ref[:, at] = jnp.sum(total * in_ref[:, at].astype(f32), axis=0, keepdims=True)
        keep_a[:, at] = total[:quarter]
        send_a[:, at] = total[quarter : 2 * quarter].astype(bf16)
        keep_b[:, at] = total[2 * quarter : 3 * quarter]
        send_b[:, at] = total[3 * quarter :].astype(bf16)


def grad_kernel(left_a, left_b, right_a, right_b, out_ref):
    rows = out_ref.shape[0]

    @pl.loop(0, rows // 256)
    def _(i):
        at = pl.ds(pl.multiple_of(i * 256, 256), 256)
        out_ref[at, :] = (mm(left_a[:, at], right_a[...], TN) + mm(left_b[:, at], right_b[...], TN)).astype(bf16)


def mixed_kernel(capacity, slot_ref, *refs):
    out_ref = refs[-1]
    count = slot_ref.shape[1]
    total = None
    for k, ref in enumerate(refs[:-1]):
        rows = lax.broadcasted_iota(jnp.int32, (capacity, count), 0) + k * capacity
        placing = jnp.where(rows == slot_ref[...], 1.0, 0.0).astype(bf16)
        part = mm(placing, ref[...], TN)
        total = part if total is None else total + part
    out_ref[...] = total.astype(bf16)


def token_kernel(capacity, slot_ref, tok_ref, gain_ref, *refs):
    out_ref = refs[-1]
    count = slot_ref.shape[1]
    total = None
    for k, ref in enumerate(refs[:-1]):
        rows = lax.broadcasted_iota(jnp.int32, (capacity, count), 0) + k * capacity
        placing = jnp.where(rows == slot_ref[...], 1.0, 0.0).astype(bf16)
        part = mm(placing, ref[...], TN)
        total = part if total is None else total + part
    wide = tok_ref[...].astype(f32)
    scales = lax.rsqrt(jnp.mean(wide * wide, axis=1, keepdims=True) + 1e-06)
    gained = total * gain_ref[...]
    cubed = scales * scales * scales
    out_ref[...] = (
        scales * gained - wide * (cubed * jnp.mean(gained * wide, axis=1, keepdims=True))
    ).astype(bf16)


def local(tokens, expert_ids, norm_gain, up_weight, down_weight, cotangent):
    groups = lax.axis_size("exp")
    copies = lax.axis_size("rep")
    count, width = tokens.shape
    capacity = 3 * count // (4 * groups)
    slots = groups * capacity
    half = slots // 2
    units = up_weight.shape[2]
    rows = slots * copies // 2
    bits = []
    while (2 << len(bits)) < copies:
        bits.append(2 << len(bits))
    orders = (tuple(bits), tuple(reversed(bits)))

    def swap(x, bit):
        return lax.ppermute(x, "rep", [(i, i ^ bit) for i in range(copies)])

    def shift(x, k):
        return lax.ppermute(x, "exp", [(i, (i + k) % groups) for i in range(groups)])

    up_a, down_a = up_weight[0], down_weight[0]
    up_b, down_b = swap(up_a, 1), swap(down_a, 1)

    me = lax.axis_index("exp").astype(jnp.int32).reshape(1, 1)
    gain_row = norm_gain.reshape(1, width)
    slot_row, *sends = call(
        functools.partial(place_kernel, groups, capacity),
        [shaped((1, count), jnp.int32)] + [shaped((capacity, width))] * (2 * groups),
        (tokens, expert_ids.reshape(1, count), me, gain_row, cotangent),
    )

    def gather(blocks):
        arrived = [blocks[0]] + [shift(blocks[k], k) for k in range(1, groups)]
        halves = [
            jnp.concatenate(arrived[: groups // 2], axis=0),
            jnp.concatenate(arrived[groups // 2 :], axis=0),
        ]
        for i in range(len(bits)):
            for h in range(2):
                halves[h] = jnp.concatenate([halves[h], swap(halves[h], orders[h][i])], axis=0)
        return jnp.concatenate(halves, axis=0)

    def scatter(keeps, sends):
        keeps, sends = list(keeps), list(sends)
        for i in range(len(bits)):
            for h in range(2):
                got = keeps[h] + swap(sends[h], orders[h][len(bits) - 1 - i]).astype(f32)
                cut = got.shape[0] // 2
                if i < len(bits) - 1:
                    keeps[h], sends[h] = got[:cut], got[cut:].astype(bf16)
                else:
                    keeps[h] = got.astype(bf16)
        blocks = []
        for k in range(groups):
            h, at = divmod(k, groups // 2)
            block = keeps[h][at * capacity : (at + 1) * capacity]
            blocks.append(shift(block, groups - k) if k else block)
        return blocks

    in_rows = gather(sends[:groups])
    cot_rows = gather(sends[groups:])
    work = 4 * rows * width * 2 * units
    quarter = rows // 4
    parts = [shaped((quarter, width), f32), shaped((quarter, width))] * 2
    hid_a, hid_b, slopes, *out_parts = call(
        forward_kernel,
        [shaped((rows, units))] * 2 + [shaped((2, rows, units), f32)] + parts,
        (in_rows, up_a, up_b, down_a, down_b),
        work,
        8 << 20,
    )
    pre_a, pre_b, gain_part, *back_parts = call(
        backward_kernel,
        [shaped((rows, units))] * 2 + [shaped((1, width), f32)] + parts,
        (cot_rows, in_rows, slopes, up_a, up_b, down_a, down_b),
        work,
        8 << 20,
    )
    home_out = scatter(out_parts[0::2], out_parts[1::2])
    home_back = scatter(back_parts[0::2], back_parts[1::2])
    grad_down = call(
        grad_kernel,
        shaped((units, width)),
        (hid_a, swap(hid_b, 1), cot_rows, swap(cot_rows, 1)),
        work // 2,
        8 << 20,
    )
    grad_up = call(
        grad_kernel,
        shaped((width, units)),
        (in_rows, swap(in_rows, 1), pre_a, swap(pre_b, 1)),
        work // 2,
        8 << 20,
    )
    total = gain_part
    for bit in [1] + bits:
        total = total + swap(total, bit)
    step = 1
    while step < groups:
        total = total + lax.ppermute(total, "exp", [(i, i ^ step) for i in range(groups)])
        step *= 2
    grad_gain = (total / gain_row).reshape(width)
    mixed = call(functools.partial(mixed_kernel, capacity), shaped((count, width)), (slot_row, *home_out))
    grad_tokens = call(
        functools.partial(token_kernel, capacity), shaped((count, width)), (slot_row, tokens, gain_row, *home_back)
    )
    return (mixed, grad_tokens, grad_up[None], grad_down[None], grad_gain)


def solution(mesh):
    return jax.shard_map(
        local,
        mesh=mesh,
        in_specs=(
            P(("rep", "exp"), None),
            P(("rep", "exp"), None),
            P(),
            P("exp", None, "rep"),
            P("exp", "rep", None),
            P(("rep", "exp"), None),
        ),
        out_specs=(
            P(("rep", "exp"), None),
            P(("rep", "exp"), None),
            P("exp", None, "rep"),
            P("exp", "rep", None),
            P(),
        ),
        check_vma=False,
    )
```

time: 261 us -> 144 us (0.55)
  waiting for transfers between devices: 127 us -> 53.9 us
  blocking collectives: 69.1 us -> 0 us
  starting transfers between devices: 9.36 us -> 48 us
  Pallas kernels: 0 us -> 33.4 us
  matrix products: 32.4 us -> 0 us
  between operations: 13.8 us -> 1.07 us
  other arithmetic: 6.27 us -> 1.38 us
  local copies, waits for them, and re-layouts: 1.83 us -> 6.27 us
    reduce_scatter x2 -> x0, waiting for transfers between devices: 79.7 us -> none  [the longest x1 40 us: local(): lax.psum_scatter(back_terms.astype(jnp.bfloat16), 'rep', scatter_dimensio...]
    ppermute x0 -> x39, waiting for transfers between devices: none -> 53.9 us  [the longest x25 41.3 us: swap(): return lax.ppermute(x, 'rep', [(i, i ^ bit) for i in range(copies)])]
    ppermute x0 -> x39, starting transfers between devices: none -> 48 us  [the longest x25 24.3 us: swap(): return lax.ppermute(x, 'rep', [(i, i ^ bit) for i in range(copies)])]
    all_gather x2 -> x0, waiting for transfers between devices: 41.8 us -> none  [the longest x1 24.6 us: local(): lax.all_gather(recv_cot, 'rep', axis=0, tiled=True)]
    psum x1 -> x0, blocking collectives: 37.3 us -> none  [local(): lax.psum(jnp.sum(d_normed * wide_tokens * scales, axis=0), ('rep', 'exp'))]
    pallas_call x0 -> x7, Pallas kernels: none -> 33.4 us  [call(): pl.pallas_call(kernel, out_shape=out_shape, in_specs=[vmem] * len(args),...]
    dot_general x10 -> x0, matrix products: 32.4 us -> none  [the longest x1 5.51 us: local(): lax.dot_general(flat_cot, down_mat, (((1,), (1,)), ((), ())), preferred_e...]
    all_to_all x2 -> x0, blocking collectives: 31.8 us -> none  [the longest x1 17.9 us: local(): lax.all_to_all(send_in, 'exp', split_axis=0, concat_axis=0, tiled=True)]
  transfers between devices with their start and end apart: 6 -> 39, of which waited for: 5 -> 19; matrix products, arithmetic and copies ran while one was open for 11% -> 1% of each run, Pallas kernels for 0% -> 7%
where the time goes in v1:
time: 144 us
  waiting for transfers between devices  53.9 us (37%)
  starting transfers between devices  48 us (33%)
  Pallas kernels  33.4 us (23%)
  local copies, waits for them, and re-layouts  6.27 us (4%)
    ppermute x25, waiting for transfers between devices, swap(): return lax.ppermute(x, 'rep', [(i, i ^ bit) for i in range(copies)])  41.3 us
    pallas_call x7, Pallas kernels, call(): pl.pallas_call(kernel, out_shape=out_shape, in_specs=[vmem] * len(args),...  33.4 us
    ppermute x25, starting transfers between devices, swap(): return lax.ppermute(x, 'rep', [(i, i ^ bit) for i in range(copies)])  24.3 us
    ppermute x12, starting transfers between devices, shift(): lax.ppermute(x, 'exp', [(i, (i + k) % groups) for i in range(groups)])  21 us
    ppermute x12, waiting for transfers between devices, shift(): lax.ppermute(x, 'exp', [(i, (i + k) % groups) for i in range(groups)])  9.84 us
    unnamed x33, local copies, waits for them, and re-layouts  6.07 us
  transfers between devices with their start and end apart: 39, of which 19 were waited for; matrix products, arithmetic and copies ran while one was open for 1% of the time, Pallas kernels for 7%

profile of v1, /device:TPU:0, one launch (start us, length us, event | category | flops | bytes accessed | tf_op | source)
XLA Modules:
  0.0 144.0 jit_solution(8040375809411330519)
XLA Ops:
  5.0 3.1 %collective-permute-start = (bf16[24,2048]{1,0:T(8,128)(2,1)S(1)}, bf16[24,2048]{1,0:T(8,128)(2,1)S(1)}, u32[]{:S(2)}, u32[]{:S(2)}) collective-permute-start(bf16[24,2048]{1,0:T(8,128)(2,1)S(1)} %get-tuple-element.30), channel_id=1, source_target_pairs={{0,1},{1,2},{2,3},{3,0},{4,5},{5,6},{6,7},{7,4},{8,9},{9,10},{10,1... | collective-permute-start | bytes 294920 | tf_op jit(solution)/shard_map/ppermute | solution.py:180
  8.1 2.6 %collective-permute-start.3 = (bf16[24,2048]{1,0:T(8,128)(2,1)S(1)}, bf16[24,2048]{1,0:T(8,128)(2,1)S(1)}, u32[]{:S(2)}, u32[]{:S(2)}) collective-permute-start(bf16[24,2048]{1,0:T(8,128)(2,1)S(1)} %get-tuple-element.31), channel_id=1, source_target_pairs={{0,2},{1,3},{2,0},{3,1},{4,6},{5,7},{6,4},{7,5},{8,10},{9,11},{10,... | collective-permute-start | bytes 294920 | tf_op jit(solution)/shard_map/ppermute | solution.py:180
  13.8 2.9 %collective-permute-start.16 = (bf16[24,2048]{1,0:T(8,128)(2,1)S(1)}, bf16[24,2048]{1,0:T(8,128)(2,1)S(1)}, u32[]{:S(2)}, u32[]{:S(2)}) collective-permute-start(bf16[24,2048]{1,0:T(8,128)(2,1)S(1)} %get-tuple-element.38), channel_id=1, source_target_pairs={{0,1},{1,2},{2,3},{3,0},{4,5},{5,6},{6,7},{7,4},{8,9},{9,10},{10,1... | collective-permute-start | bytes 294920 | tf_op jit(solution)/shard_map/ppermute | solution.py:180
  16.7 3.6 %collective-permute-done.16 = bf16[24,2048]{1,0:T(8,128)(2,1)S(1)} collective-permute-done((bf16[24,2048]{1,0:T(8,128)(2,1)S(1)}, bf16[24,2048]{1,0:T(8,128)(2,1)S(1)}, u32[]{:S(2)}, u32[]{:S(2)}) %collective-permute-start.16) | collective-permute-done | bytes 98336 | tf_op jit(solution)/shard_map/ppermute | solution.py:180
  20.3 3.3 %collective-permute-start.19 = (bf16[24,2048]{1,0:T(8,128)(2,1)S(1)}, bf16[24,2048]{1,0:T(8,128)(2,1)S(1)}, u32[]{:S(2)}, u32[]{:S(2)}) collective-permute-start(bf16[24,2048]{1,0:T(8,128)(2,1)S(1)} %get-tuple-element.39), channel_id=1, source_target_pairs={{0,2},{1,3},{2,0},{3,1},{4,6},{5,7},{6,4},{7,5},{8,10},{9,11},{10,... | collective-permute-start | bytes 294920 | tf_op jit(solution)/shard_map/ppermute | solution.py:180
  25.7 1.6 %collective-permute-done.19 = bf16[24,2048]{1,0:T(8,128)(2,1)S(1)} collective-permute-done((bf16[24,2048]{1,0:T(8,128)(2,1)S(1)}, bf16[24,2048]{1,0:T(8,128)(2,1)S(1)}, u32[]{:S(2)}, u32[]{:S(2)}) %collective-permute-start.19) | collective-permute-done | bytes 98336 | tf_op jit(solution)/shard_map/ppermute | solution.py:180
  27.3 1.5 %collective-permute-start.5 = (bf16[48,2048]{1,0:T(8,128)(2,1)S(1)}, bf16[48,2048]{1,0:T(8,128)(2,1)S(1)}, u32[]{:S(2)}, u32[]{:S(2)}) collective-permute-start(bf16[48,2048]{1,0:T(8,128)(2,1)S(1)} %pad_maximum_fusion.5), channel_id=1, source_target_pairs={{0,16},{4,20},{8,24},{12,28},{16,0},{20,4},{24,8},{28,12},{1,17},{... | collective-permute-start | bytes 589832 | tf_op jit(solution)/shard_map/ppermute | solution.py:177
  32.9 2.1 %collective-permute-done.5 = bf16[48,2048]{1,0:T(8,128)(2,1)S(1)} collective-permute-done((bf16[48,2048]{1,0:T(8,128)(2,1)S(1)}, bf16[48,2048]{1,0:T(8,128)(2,1)S(1)}, u32[]{:S(2)}, u32[]{:S(2)}) %collective-permute-start.5) | collective-permute-done | bytes 196640 | tf_op jit(solution)/shard_map/ppermute | solution.py:177
  36.3 1.5 %collective-permute-start.6 = (bf16[96,2048]{1,0:T(8,128)(2,1)S(1)}, bf16[96,2048]{1,0:T(8,128)(2,1)S(1)}, u32[]{:S(2)}, u32[]{:S(2)}) collective-permute-start(bf16[96,2048]{1,0:T(8,128)(2,1)S(1)} %pad_maximum_fusion.1), channel_id=1, source_target_pairs={{0,8},{4,12},{8,0},{12,4},{16,24},{20,28},{24,16},{28,20},{1,9},{5... | collective-permute-start | bytes 1179656 | tf_op jit(solution)/shard_map/ppermute | solution.py:177
  37.9 1.7 %collective-permute-done.21 = bf16[48,2048]{1,0:T(8,128)(2,1)S(1)} collective-permute-done((bf16[48,2048]{1,0:T(8,128)(2,1)S(1)}, bf16[48,2048]{1,0:T(8,128)(2,1)S(1)}, u32[]{:S(2)}, u32[]{:S(2)}) %collective-permute-start.21) | collective-permute-done | bytes 196640 | tf_op jit(solution)/shard_map/ppermute | solution.py:177
  40.8 7.0 %collective-permute-done.2 = bf16[96,2048]{1,0:T(8,128)(2,1)S(1)} collective-permute-done((bf16[96,2048]{1,0:T(8,128)(2,1)S(1)}, bf16[96,2048]{1,0:T(8,128)(2,1)S(1)}, u32[]{:S(2)}, u32[]{:S(2)}) %collective-permute-start.2) | collective-permute-done | bytes 393248 | tf_op jit(solution)/shard_map/ppermute | solution.py:177
  49.2 2.8 %collective-permute-done.18 = bf16[96,2048]{1,0:T(8,128)(2,1)S(1)} collective-permute-done((bf16[96,2048]{1,0:T(8,128)(2,1)S(1)}, bf16[96,2048]{1,0:T(8,128)(2,1)S(1)}, u32[]{:S(2)}, u32[]{:S(2)}) %collective-permute-start.18) | collective-permute-done | bytes 393248 | tf_op jit(solution)/shard_map/ppermute | solution.py:177
  52.2 3.4 %collective-permute-done.22 = bf16[96,2048]{1,0:T(8,128)(2,1)S(1)} collective-permute-done((bf16[96,2048]{1,0:T(8,128)(2,1)S(1)}, bf16[96,2048]{1,0:T(8,128)(2,1)S(1)}, u32[]{:S(2)}, u32[]{:S(2)}) %collective-permute-start.22) | collective-permute-done | bytes 393248 | tf_op jit(solution)/shard_map/ppermute | solution.py:177
  56.9 10.0 %shard_map.102 = (bf16[384,512]{1,0:T(8,128)(2,1)S(1)}, bf16[384,512]{1,0:T(8,128)(2,1)S(1)}, f32[2,384,512]{2,1,0:T(8,128)S(1)}, f32[96,2048]{1,0:T(8,128)S(1)}...) custom-call(bf16[384,2048]{1,0:T(8,128)(2,1)} %copy-done, ...), custom_call_target="tpu_custom_call" | custom-call | flops 3221225472 | bytes 8388608 | tf_op jit(solution)/shard_map/pallas_call | solution.py:35
  68.2 10.2 %shard_map.104 = (bf16[384,512]{1,0:T(8,128)(2,1)S(1)}, bf16[384,512]{1,0:T(8,128)(2,1)S(1)}, f32[1,2048]{1,0:T(1,128)S(1)}, f32[96,2048]{1,0:T(8,128)S(1)}, bf1...) custom-call(bf16[384,2048]{1,0:T(8,128)(2,1)S(1)} %constant_dynamic-update-slice_fusion.8.cot_ref.rig, ...), custom_call_target="tpu_custom_call" | custom-call | flops 3221225472 | bytes 8388608 | tf_op jit(solution)/shard_map/pallas_call | solution.py:35
  81.1 2.3 %collective-permute-done.35 = f32[1,2048]{1,0:T(1,128)S(1)} collective-permute-done((f32[1,2048]{1,0:T(1,128)S(1)}, f32[1,2048]{1,0:T(1,128)S(1)}, u32[]{:S(2)}, u32[]{:S(2)}) %collective-permute-start.35) | collective-permute-done | bytes 8224 | tf_op jit(solution)/shard_map/ppermute | solution.py:177
  84.8 2.3 %collective-permute-done.36 = f32[1,2048]{1,0:T(1,128)S(1)} collective-permute-done((f32[1,2048]{1,0:T(1,128)S(1)}, f32[1,2048]{1,0:T(1,128)S(1)}, u32[]{:S(2)}, u32[]{:S(2)}) %collective-permute-start.36) | collective-permute-done | bytes 8224 | tf_op jit(solution)/shard_map/ppermute | solution.py:177
  88.1 2.7 %collective-permute-done.37 = f32[1,2048]{1,0:T(1,128)S(1)} collective-permute-done((f32[1,2048]{1,0:T(1,128)S(1)}, f32[1,2048]{1,0:T(1,128)S(1)}, u32[]{:S(2)}, u32[]{:S(2)}) %collective-permute-start.37) | collective-permute-done | bytes 8224 | tf_op jit(solution)/shard_map/ppermute | solution.py:261
  90.8 1.7 %collective-permute-start.38 = (f32[1,2048]{1,0:T(1,128)S(1)}, f32[1,2048]{1,0:T(1,128)S(1)}, u32[]{:S(2)}, u32[]{:S(2)}) collective-permute-start(f32[1,2048]{1,0:T(1,128)S(1)} %add.50), channel_id=1, source_target_pairs={{0,2},{1,3},{2,0},{3,1},{4,6},{5,7},{6,4},{7,5},{8,10},{9,11},{10,... | collective-permute-start | bytes 24584 | tf_op jit(solution)/shard_map/ppermute | solution.py:261
  93.0 1.5 %collective-permute-start.9 = (bf16[96,2048]{1,0:T(8,128)(2,1)S(1)}, bf16[96,2048]{1,0:T(8,128)(2,1)S(1)}, u32[]{:S(2)}, u32[]{:S(2)}) collective-permute-start(bf16[96,2048]{1,0:T(8,128)(2,1)S(1)} %get-tuple-element.34), channel_id=1, source_target_pairs={{0,16},{4,20},{8,24},{12,28},{16,0},{20,4},{24,8},{28,12},{1,17},{... | collective-permute-start | bytes 1179656 | tf_op jit(solution)/shard_map/ppermute | solution.py:177
  97.4 7.6 %collective-permute-done.9 = bf16[96,2048]{1,0:T(8,128)(2,1)S(1)} collective-permute-done((bf16[96,2048]{1,0:T(8,128)(2,1)S(1)}, bf16[96,2048]{1,0:T(8,128)(2,1)S(1)}, u32[]{:S(2)}, u32[]{:S(2)}) %collective-permute-start.9) | collective-permute-done | bytes 393248 | tf_op jit(solution)/shard_map/ppermute | solution.py:177
  106.8 5.7 %collective-permute-done.23 = bf16[96,2048]{1,0:T(8,128)(2,1)S(1)} collective-permute-done((bf16[96,2048]{1,0:T(8,128)(2,1)S(1)}, bf16[96,2048]{1,0:T(8,128)(2,1)S(1)}, u32[]{:S(2)}, u32[]{:S(2)}) %collective-permute-start.23) | collective-permute-done | bytes 393248 | tf_op jit(solution)/shard_map/ppermute | solution.py:177
  112.6 1.6 %collective-permute-done.26 = bf16[96,2048]{1,0:T(8,128)(2,1)S(1)} collective-permute-done((bf16[96,2048]{1,0:T(8,128)(2,1)S(1)}, bf16[96,2048]{1,0:T(8,128)(2,1)S(1)}, u32[]{:S(2)}, u32[]{:S(2)}) %collective-permute-start.26) | collective-permute-done | bytes 393248 | tf_op jit(solution)/shard_map/ppermute | solution.py:177
  115.9 1.6 %collective-permute-start.13 = (bf16[48,2048]{1,0:T(8,128)(2,1)S(1)}, bf16[48,2048]{1,0:T(8,128)(2,1)S(1)}, u32[]{:S(2)}, u32[]{:S(2)}) collective-permute-start(bf16[48,2048]{1,0:T(8,128)(2,1)S(1)} %slice.102), channel_id=1, source_target_pairs={{0,16},{4,20},{8,24},{12,28},{16,0},{20,4},{24,8},{28,12},{1,17},{... | collective-permute-start | bytes 589832 | tf_op jit(solution)/shard_map/ppermute | solution.py:177
  118.0 5.1 %shard_map.106 = bf16[2048,512]{1,0:T(8,128)(2,1)} custom-call(bf16[384,2048]{1,0:T(8,128)(2,1)S(1)} %copy-done.1, bf16[384,2048]{1,0:T(8,128)(2,1)S(1)} %collective-permute-done.30.left_b, bf16[384,512]{1,0:T(8,128)(2,1)S(1)} %get-tuple-element.46.right_a, bf16[384,512]{1,0:T(8,128)(2,1)S(1)} %collective-permute-done.31.right_b), custom_call_target="tpu_custom_call" | custom-call | flops 1610612736 | bytes 8388608 | tf_op jit(solution)/shard_map/pallas_call | solution.py:35
  123.7 1.7 %collective-permute-start.11 = (bf16[24,2048]{1,0:T(8,128)(2,1)S(1)}, bf16[24,2048]{1,0:T(8,128)(2,1)S(1)}, u32[]{:S(2)}, u32[]{:S(2)}) collective-permute-start(bf16[24,2048]{1,0:T(8,128)(2,1)S(1)} %get-tuple-element.57), channel_id=1, source_target_pairs={{0,3},{1,0},{2,1},{3,2},{4,7},{5,4},{6,5},{7,6},{8,11},{9,8},{10,9... | collective-permute-start | bytes 294920 | tf_op jit(solution)/shard_map/ppermute | solution.py:180
  126.6 2.2 %collective-permute-done.27 = bf16[48,2048]{1,0:T(8,128)(2,1)S(1)} collective-permute-done((bf16[48,2048]{1,0:T(8,128)(2,1)S(1)}, bf16[48,2048]{1,0:T(8,128)(2,1)S(1)}, u32[]{:S(2)}, u32[]{:S(2)}) %collective-permute-start.27) | collective-permute-done | bytes 196640 | tf_op jit(solution)/shard_map/ppermute | solution.py:177
  130.0 2.8 %collective-permute-start.25 = (bf16[24,2048]{1,0:T(8,128)(2,1)S(1)}, bf16[24,2048]{1,0:T(8,128)(2,1)S(1)}, u32[]{:S(2)}, u32[]{:S(2)}) collective-permute-start(bf16[24,2048]{1,0:T(8,128)(2,1)S(1)} %get-tuple-element.53), channel_id=1, source_target_pairs={{0,3},{1,0},{2,1},{3,2},{4,7},{5,4},{6,5},{7,6},{8,11},{9,8},{10,9... | collective-permute-start | bytes 294920 | tf_op jit(solution)/shard_map/ppermute | solution.py:180
  133.4 3.9 %shard_map.107 = bf16[512,2048]{1,0:T(8,128)(2,1)} custom-call(bf16[384,512]{1,0:T(8,128)(2,1)S(1)} %get-tuple-element.48.left_a, bf16[384,512]{1,0:T(8,128)(2,1)S(1)} %collective-permute-done.32.left_b, bf16[384,2048]{1,0:T(8,128)(2,1)S(1)} %constant_dynamic-update-slice_fusion.8.cot_ref.right_a, bf16[384,2048]{1,0:T(8,128)(2,1)S(1)} %collective-permute-done.33.right_b), custom_call_target="tpu_custom_call" | custom-call | flops 1610612736 | bytes 8388608 | tf_op jit(solution)/shard_map/pallas_call | solution.py:35
  137.4 1.5 %shard_map.103 = bf16[128,2048]{1,0:T(8,128)(2,1)} custom-call(s32[1,128]{1,0:T(1,128)S(1)} %get-tuple-element.28.slot_ref, bf16[24,2048]{1,0:T(8,128)(2,1)S(1)} %get-tuple-element.58.refs_0_, bf16[24,2048]{1,0:T(8,128)(2,1)S(1)} %collective-permute-done.11.refs_1_, bf16[24,2048]{1,0:T(8,128)(2,1)S(1)} %collective-permute-done.14.refs_2_, ...), custom_call_target="tpu_custom_call" | custom-call | tf_op jit(solution)/shard_map/pallas_call | solution.py:35
  138.9 3.4 %collective-permute-done.28.refs_2_ = bf16[24,2048]{1,0:T(8,128)(2,1)S(1)} collective-permute-done((bf16[24,2048]{1,0:T(8,128)(2,1)S(1)}, bf16[24,2048]{1,0:T(8,128)(2,1)S(1)}, u32[]{:S(2)}, u32[]{:S(2)}) %collective-permute-start.28) | collective-permute-done | bytes 98336 | tf_op jit(solution)/shard_map/ppermute | solution.py:180
  142.3 1.7 %shard_map.105 = bf16[128,2048]{1,0:T(8,128)(2,1)} custom-call(s32[1,128]{1,0:T(1,128)S(1)} %get-tuple-element.28.slot_ref, bf16[128,2048]{1,0:T(8,128)(2,1)S(1)} %copy-done.3, f32[1,2048]{1,0:T(1,128)S(1)} %bitcast.10, bf16[24,2048]{1,0:T(8,128)(2,1)S(1)} %get-tuple-element.54.refs_0_, bf16[24,2048]{1,0:T(8,128)(2,1)S(1)} %collective-permute-done.25.refs_1_, ...), custom_call_target="tpu_custom_call" | custom-call | tf_op jit(solution)/shard_map/pallas_call | solution.py:35
  (117 shorter events, 36.3 us)
Async XLA Ops:
  5.0 8.8 %collective-permute-start = (bf16[24,2048]{1,0:T(8,128)(2,1)S(1)}, bf16[24,2048]{1,0:T(8,128)(2,1)S(1)}, u32[]{:S(2)}, u32[]{:S(2)}) collective-permute-start(bf16[24,2048]{1,0:T(8,128)(2,1)S(1)} %get-tuple-element.30), channel_id=1, source_target_pairs={{0,1},{1,2},{2,3},{3,0},{4,5},{5,6},{6,7},{7,4},{8,9},{9,10},{10,1... | collective-permute-start | bytes 294920 | tf_op jit(solution)/shard_map/ppermute | solution.py:180
  8.1 15.6 %collective-permute-start.3 = (bf16[24,2048]{1,0:T(8,128)(2,1)S(1)}, bf16[24,2048]{1,0:T(8,128)(2,1)S(1)}, u32[]{:S(2)}, u32[]{:S(2)}) collective-permute-start(bf16[24,2048]{1,0:T(8,128)(2,1)S(1)} %get-tuple-element.31), channel_id=1, source_target_pairs={{0,2},{1,3},{2,0},{3,1},{4,6},{5,7},{6,4},{7,5},{8,10},{9,11},{10,... | collective-permute-start | bytes 294920 | tf_op jit(solution)/shard_map/ppermute | solution.py:180
  10.7 13.5 %collective-permute-start.4 = (bf16[24,2048]{1,0:T(8,128)(2,1)S(1)}, bf16[24,2048]{1,0:T(8,128)(2,1)S(1)}, u32[]{:S(2)}, u32[]{:S(2)}) collective-permute-start(bf16[24,2048]{1,0:T(8,128)(2,1)S(1)} %get-tuple-element.32), channel_id=1, source_target_pairs={{0,3},{1,0},{2,1},{3,2},{4,7},{5,4},{6,5},{7,6},{8,11},{9,8},{10,9... | collective-permute-start | bytes 294920 | tf_op jit(solution)/shard_map/ppermute | solution.py:180
  12.0 43.6 %collective-permute-start.7 = (bf16[2048,512]{1,0:T(8,128)(2,1)}, bf16[2048,512]{1,0:T(8,128)(2,1)S(1)}, u32[]{:S(2)}, u32[]{:S(2)}) collective-permute-start(bf16[2048,512]{1,0:T(8,128)(2,1)} %bitcast.12), channel_id=1, source_target_pairs={{0,4},{4,0},{8,12},{12,8},{16,20},{20,16},{24,28},{28,24},{1,5},{5... | collective-permute-start | bytes 6291464 | tf_op jit(solution)/shard_map/ppermute | solution.py:177
  12.0 43.6 %collective-permute-start.8 = (bf16[512,2048]{1,0:T(8,128)(2,1)}, bf16[512,2048]{1,0:T(8,128)(2,1)}, u32[]{:S(2)}, u32[]{:S(2)}) collective-permute-start(bf16[512,2048]{1,0:T(8,128)(2,1)} %bitcast.15), channel_id=1, source_target_pairs={{0,4},{4,0},{8,12},{12,8},{16,20},{20,16},{24,28},{28,24},{1,5},{5... | collective-permute-start | bytes 6291464 | tf_op jit(solution)/shard_map/ppermute | solution.py:177
  13.8 6.5 %collective-permute-start.16 = (bf16[24,2048]{1,0:T(8,128)(2,1)S(1)}, bf16[24,2048]{1,0:T(8,128)(2,1)S(1)}, u32[]{:S(2)}, u32[]{:S(2)}) collective-permute-start(bf16[24,2048]{1,0:T(8,128)(2,1)S(1)} %get-tuple-element.38), channel_id=1, source_target_pairs={{0,1},{1,2},{2,3},{3,0},{4,5},{5,6},{6,7},{7,4},{8,9},{9,10},{10,1... | collective-permute-start | bytes 294920 | tf_op jit(solution)/shard_map/ppermute | solution.py:180
  20.3 7.0 %collective-permute-start.19 = (bf16[24,2048]{1,0:T(8,128)(2,1)S(1)}, bf16[24,2048]{1,0:T(8,128)(2,1)S(1)}, u32[]{:S(2)}, u32[]{:S(2)}) collective-permute-start(bf16[24,2048]{1,0:T(8,128)(2,1)S(1)} %get-tuple-element.39), channel_id=1, source_target_pairs={{0,2},{1,3},{2,0},{3,1},{4,6},{5,7},{6,4},{7,5},{8,10},{9,11},{10,... | collective-permute-start | bytes 294920 | tf_op jit(solution)/shard_map/ppermute | solution.py:180
  24.1 7.6 %collective-permute-start.1 = (bf16[48,2048]{1,0:T(8,128)(2,1)S(1)}, bf16[48,2048]{1,0:T(8,128)(2,1)S(1)}, u32[]{:S(2)}, u32[]{:S(2)}) collective-permute-start(bf16[48,2048]{1,0:T(8,128)(2,1)S(1)} %pad_maximum_fusion.4), channel_id=1, source_target_pairs={{0,8},{4,12},{8,0},{12,4},{16,24},{20,28},{24,16},{28,20},{1,9},{5... | collective-permute-start | bytes 589832 | tf_op jit(solution)/shard_map/ppermute | solution.py:177
  27.3 7.8 %collective-permute-start.5 = (bf16[48,2048]{1,0:T(8,128)(2,1)S(1)}, bf16[48,2048]{1,0:T(8,128)(2,1)S(1)}, u32[]{:S(2)}, u32[]{:S(2)}) collective-permute-start(bf16[48,2048]{1,0:T(8,128)(2,1)S(1)} %pad_maximum_fusion.5), channel_id=1, source_target_pairs={{0,16},{4,20},{8,24},{12,28},{16,0},{20,4},{24,8},{28,12},{1,17},{... | collective-permute-start | bytes 589832 | tf_op jit(solution)/shard_map/ppermute | solution.py:177
  28.8 7.5 %collective-permute-start.17 = (bf16[48,2048]{1,0:T(8,128)(2,1)S(1)}, bf16[48,2048]{1,0:T(8,128)(2,1)S(1)}, u32[]{:S(2)}, u32[]{:S(2)}) collective-permute-start(bf16[48,2048]{1,0:T(8,128)(2,1)S(1)} %pad_maximum_fusion.6), channel_id=1, source_target_pairs={{0,8},{4,12},{8,0},{12,4},{16,24},{20,28},{24,16},{28,20},{1,9},{5... | collective-permute-start | bytes 589832 | tf_op jit(solution)/shard_map/ppermute | solution.py:177
  31.7 7.8 %collective-permute-start.21 = (bf16[48,2048]{1,0:T(8,128)(2,1)S(1)}, bf16[48,2048]{1,0:T(8,128)(2,1)S(1)}, u32[]{:S(2)}, u32[]{:S(2)}) collective-permute-start(bf16[48,2048]{1,0:T(8,128)(2,1)S(1)} %pad_maximum_fusion.7), channel_id=1, source_target_pairs={{0,16},{4,20},{8,24},{12,28},{16,0},{20,4},{24,8},{28,12},{1,17},{... | collective-permute-start | bytes 589832 | tf_op jit(solution)/shard_map/ppermute | solution.py:177
  35.0 12.8 %collective-permute-start.2 = (bf16[96,2048]{1,0:T(8,128)(2,1)S(1)}, bf16[96,2048]{1,0:T(8,128)(2,1)S(1)}, u32[]{:S(2)}, u32[]{:S(2)}) collective-permute-start(bf16[96,2048]{1,0:T(8,128)(2,1)S(1)} %pad_maximum_fusion), channel_id=1, source_target_pairs={{0,16},{4,20},{8,24},{12,28},{16,0},{20,4},{24,8},{28,12},{1,17},{... | collective-permute-start | bytes 1179656 | tf_op jit(solution)/shard_map/ppermute | solution.py:177
  36.3 15.8 %collective-permute-start.6 = (bf16[96,2048]{1,0:T(8,128)(2,1)S(1)}, bf16[96,2048]{1,0:T(8,128)(2,1)S(1)}, u32[]{:S(2)}, u32[]{:S(2)}) collective-permute-start(bf16[96,2048]{1,0:T(8,128)(2,1)S(1)} %pad_maximum_fusion.1), channel_id=1, source_target_pairs={{0,8},{4,12},{8,0},{12,4},{16,24},{20,28},{24,16},{28,20},{1,9},{5... | collective-permute-start | bytes 1179656 | tf_op jit(solution)/shard_map/ppermute | solution.py:177
  39.6 12.4 %collective-permute-start.18 = (bf16[96,2048]{1,0:T(8,128)(2,1)S(1)}, bf16[96,2048]{1,0:T(8,128)(2,1)S(1)}, u32[]{:S(2)}, u32[]{:S(2)}) collective-permute-start(bf16[96,2048]{1,0:T(8,128)(2,1)S(1)} %pad_maximum_fusion.2), channel_id=1, source_target_pairs={{0,16},{4,20},{8,24},{12,28},{16,0},{20,4},{24,8},{28,12},{1,17},{... | collective-permute-start | bytes 1179656 | tf_op jit(solution)/shard_map/ppermute | solution.py:177
  47.8 7.8 %collective-permute-start.22 = (bf16[96,2048]{1,0:T(8,128)(2,1)S(1)}, bf16[96,2048]{1,0:T(8,128)(2,1)S(1)}, u32[]{:S(2)}, u32[]{:S(2)}) collective-permute-start(bf16[96,2048]{1,0:T(8,128)(2,1)S(1)} %pad_maximum_fusion.3), channel_id=1, source_target_pairs={{0,8},{4,12},{8,0},{12,4},{16,24},{20,28},{24,16},{28,20},{1,9},{5... | collective-permute-start | bytes 1179656 | tf_op jit(solution)/shard_map/ppermute | solution.py:177
  92.5 23.4 %collective-permute-start.30 = (bf16[384,2048]{1,0:T(8,128)(2,1)S(1)}, bf16[384,2048]{1,0:T(8,128)(2,1)S(1)}, u32[]{:S(2)}, u32[]{:S(2)}) collective-permute-start(bf16[384,2048]{1,0:T(8,128)(2,1)S(1)} %copy-done.1), channel_id=1, source_target_pairs={{0,4},{4,0},{8,12},{12,8},{16,20},{20,16},{24,28},{28,24},{1,5},{5... | collective-permute-start | bytes 4718600 | tf_op jit(solution)/shard_map/ppermute | solution.py:177
  92.5 37.5 %collective-permute-start.33 = (bf16[384,2048]{1,0:T(8,128)(2,1)S(1)}, bf16[384,2048]{1,0:T(8,128)(2,1)S(1)}, u32[]{:S(2)}, u32[]{:S(2)}) collective-permute-start(bf16[384,2048]{1,0:T(8,128)(2,1)S(1)} %constant_dynamic-update-slice_fusion.8.cot_ref.right_a), channel_id=1, source_target_pairs={{0,4},{4,0},{8,12},{12,8},{16,20},{20,16},{24,28},{28,24},{1,5},{5... | collective-permute-start | bytes 4718600 | tf_op jit(solution)/shard_map/ppermute | solution.py:177
  93.0 12.0 %collective-permute-start.9 = (bf16[96,2048]{1,0:T(8,128)(2,1)S(1)}, bf16[96,2048]{1,0:T(8,128)(2,1)S(1)}, u32[]{:S(2)}, u32[]{:S(2)}) collective-permute-start(bf16[96,2048]{1,0:T(8,128)(2,1)S(1)} %get-tuple-element.34), channel_id=1, source_target_pairs={{0,16},{4,20},{8,24},{12,28},{16,0},{20,4},{24,8},{28,12},{1,17},{... | collective-permute-start | bytes 1179656 | tf_op jit(solution)/shard_map/ppermute | solution.py:177
  94.6 12.1 %collective-permute-start.12 = (bf16[96,2048]{1,0:T(8,128)(2,1)S(1)}, bf16[96,2048]{1,0:T(8,128)(2,1)S(1)}, u32[]{:S(2)}, u32[]{:S(2)}) collective-permute-start(bf16[96,2048]{1,0:T(8,128)(2,1)S(1)} %get-tuple-element.36), channel_id=1, source_target_pairs={{0,8},{4,12},{8,0},{12,4},{16,24},{20,28},{24,16},{28,20},{1,9},{5... | collective-permute-start | bytes 1179656 | tf_op jit(solution)/shard_map/ppermute | solution.py:177
  96.0 16.4 %collective-permute-start.23 = (bf16[96,2048]{1,0:T(8,128)(2,1)S(1)}, bf16[96,2048]{1,0:T(8,128)(2,1)S(1)}, u32[]{:S(2)}, u32[]{:S(2)}) collective-permute-start(bf16[96,2048]{1,0:T(8,128)(2,1)S(1)} %get-tuple-element.43), channel_id=1, source_target_pairs={{0,16},{4,20},{8,24},{12,28},{16,0},{20,4},{24,8},{28,12},{1,17},{... | collective-permute-start | bytes 1179656 | tf_op jit(solution)/shard_map/ppermute | solution.py:177
  105.0 9.2 %collective-permute-start.26 = (bf16[96,2048]{1,0:T(8,128)(2,1)S(1)}, bf16[96,2048]{1,0:T(8,128)(2,1)S(1)}, u32[]{:S(2)}, u32[]{:S(2)}) collective-permute-start(bf16[96,2048]{1,0:T(8,128)(2,1)S(1)} %get-tuple-element.45), channel_id=1, source_target_pairs={{0,8},{4,12},{8,0},{12,4},{16,24},{20,28},{24,16},{28,20},{1,9},{5... | collective-permute-start | bytes 1179656 | tf_op jit(solution)/shard_map/ppermute | solution.py:177
  106.6 10.9 %collective-permute-start.31 = (bf16[384,512]{1,0:T(8,128)(2,1)S(1)}, bf16[384,512]{1,0:T(8,128)(2,1)S(1)}, u32[]{:S(2)}, u32[]{:S(2)}) collective-permute-start(bf16[384,512]{1,0:T(8,128)(2,1)S(1)} %get-tuple-element.47), channel_id=1, source_target_pairs={{0,4},{4,0},{8,12},{12,8},{16,20},{20,16},{24,28},{28,24},{1,5},{5... | collective-permute-start | bytes 1179656 | tf_op jit(solution)/shard_map/ppermute | solution.py:177
  112.5 20.3 %collective-permute-start.32 = (bf16[384,512]{1,0:T(8,128)(2,1)S(1)}, bf16[384,512]{1,0:T(8,128)(2,1)S(1)}, u32[]{:S(2)}, u32[]{:S(2)}) collective-permute-start(bf16[384,512]{1,0:T(8,128)(2,1)S(1)} %get-tuple-element.49), channel_id=1, source_target_pairs={{0,4},{4,0},{8,12},{12,8},{16,20},{20,16},{24,28},{28,24},{1,5},{5... | collective-permute-start | bytes 1179656 | tf_op jit(solution)/shard_map/ppermute | solution.py:177
  114.2 8.9 %collective-permute-start.10 = (bf16[48,2048]{1,0:T(8,128)(2,1)S(1)}, bf16[48,2048]{1,0:T(8,128)(2,1)S(1)}, u32[]{:S(2)}, u32[]{:S(2)}) collective-permute-start(bf16[48,2048]{1,0:T(8,128)(2,1)S(1)} %slice.103), channel_id=1, source_target_pairs={{0,8},{4,12},{8,0},{12,4},{16,24},{20,28},{24,16},{28,20},{1,9},{5... | collective-permute-start | bytes 589832 | tf_op jit(solution)/shard_map/ppermute | solution.py:177
  115.9 7.8 %collective-permute-start.13 = (bf16[48,2048]{1,0:T(8,128)(2,1)S(1)}, bf16[48,2048]{1,0:T(8,128)(2,1)S(1)}, u32[]{:S(2)}, u32[]{:S(2)}) collective-permute-start(bf16[48,2048]{1,0:T(8,128)(2,1)S(1)} %slice.102), channel_id=1, source_target_pairs={{0,16},{4,20},{8,24},{12,28},{16,0},{20,4},{24,8},{28,12},{1,17},{... | collective-permute-start | bytes 589832 | tf_op jit(solution)/shard_map/ppermute | solution.py:177
  117.5 8.0 %collective-permute-start.24 = (bf16[48,2048]{1,0:T(8,128)(2,1)S(1)}, bf16[48,2048]{1,0:T(8,128)(2,1)S(1)}, u32[]{:S(2)}, u32[]{:S(2)}) collective-permute-start(bf16[48,2048]{1,0:T(8,128)(2,1)S(1)} %slice.101), channel_id=1, source_target_pairs={{0,8},{4,12},{8,0},{12,4},{16,24},{20,28},{24,16},{28,20},{1,9},{5... | collective-permute-start | bytes 589832 | tf_op jit(solution)/shard_map/ppermute | solution.py:177
  123.7 9.0 %collective-permute-start.11 = (bf16[24,2048]{1,0:T(8,128)(2,1)S(1)}, bf16[24,2048]{1,0:T(8,128)(2,1)S(1)}, u32[]{:S(2)}, u32[]{:S(2)}) collective-permute-start(bf16[24,2048]{1,0:T(8,128)(2,1)S(1)} %get-tuple-element.57), channel_id=1, source_target_pairs={{0,3},{1,0},{2,1},{3,2},{4,7},{5,4},{6,5},{7,6},{8,11},{9,8},{10,9... | collective-permute-start | bytes 294920 | tf_op jit(solution)/shard_map/ppermute | solution.py:180
  125.5 11.9 %collective-permute-start.14 = (bf16[24,2048]{1,0:T(8,128)(2,1)S(1)}, bf16[24,2048]{1,0:T(8,128)(2,1)S(1)}, u32[]{:S(2)}, u32[]{:S(2)}) collective-permute-start(bf16[24,2048]{1,0:T(8,128)(2,1)S(1)} %get-tuple-element.56), channel_id=1, source_target_pairs={{0,2},{1,3},{2,0},{3,1},{4,6},{5,7},{6,4},{7,5},{8,10},{9,11},{10,... | collective-permute-start | bytes 294920 | tf_op jit(solution)/shard_map/ppermute | solution.py:180
  128.8 8.6 %collective-permute-start.15 = (bf16[24,2048]{1,0:T(8,128)(2,1)S(1)}, bf16[24,2048]{1,0:T(8,128)(2,1)S(1)}, u32[]{:S(2)}, u32[]{:S(2)}) collective-permute-start(bf16[24,2048]{1,0:T(8,128)(2,1)S(1)} %get-tuple-element.55), channel_id=1, source_target_pairs={{0,1},{1,2},{2,3},{3,0},{4,5},{5,6},{6,7},{7,4},{8,9},{9,10},{10,1... | collective-permute-start | bytes 294920 | tf_op jit(solution)/shard_map/ppermute | solution.py:180
  130.0 8.9 %collective-permute-start.25 = (bf16[24,2048]{1,0:T(8,128)(2,1)S(1)}, bf16[24,2048]{1,0:T(8,128)(2,1)S(1)}, u32[]{:S(2)}, u32[]{:S(2)}) collective-permute-start(bf16[24,2048]{1,0:T(8,128)(2,1)S(1)} %get-tuple-element.53), channel_id=1, source_target_pairs={{0,3},{1,0},{2,1},{3,2},{4,7},{5,4},{6,5},{7,6},{8,11},{9,8},{10,9... | collective-permute-start | bytes 294920 | tf_op jit(solution)/shard_map/ppermute | solution.py:180
  132.8 9.5 %collective-permute-start.28 = (bf16[24,2048]{1,0:T(8,128)(2,1)S(1)}, bf16[24,2048]{1,0:T(8,128)(2,1)S(1)}, u32[]{:S(2)}, u32[]{:S(2)}) collective-permute-start(bf16[24,2048]{1,0:T(8,128)(2,1)S(1)} %get-tuple-element.52), channel_id=1, source_target_pairs={{0,2},{1,3},{2,0},{3,1},{4,6},{5,7},{6,4},{7,5},{8,10},{9,11},{10,... | collective-permute-start | bytes 294920 | tf_op jit(solution)/shard_map/ppermute | solution.py:180
  132.8 9.5 %collective-permute-start.29 = (bf16[24,2048]{1,0:T(8,128)(2,1)S(1)}, bf16[24,2048]{1,0:T(8,128)(2,1)S(1)}, u32[]{:S(2)}, u32[]{:S(2)}) collective-permute-start(bf16[24,2048]{1,0:T(8,128)(2,1)S(1)} %get-tuple-element.51), channel_id=1, source_target_pairs={{0,1},{1,2},{2,3},{3,0},{4,5},{5,6},{6,7},{7,4},{8,9},{9,10},{10,1... | collective-permute-start | bytes 294920 | tf_op jit(solution)/shard_map/ppermute | solution.py:180
  (17 other events, 99.7 us)

commit v2 on v1

v2 whole, which is shorter than its diff:
```python
import functools

import jax
import jax.numpy as jnp
from jax import lax
from jax.experimental import pallas as pl
from jax.experimental.pallas import tpu as pltpu
from jax.sharding import PartitionSpec as P

gelu_coef = 0.7978845608028654
cubic_coef = 0.044715
bf16 = jnp.bfloat16
f32 = jnp.float32
NN = (((1,), (0,)), ((), ()))
NT = (((1,), (1,)), ((), ()))
TN = (((0,), (0,)), ((), ()))


ROOM = 20 * 1024 * 1024


def mm(a, b, dims=NN):
    return lax.dot_general(a, b, dims, preferred_element_type=f32)


def gelu_parts(inputs):
    inner = gelu_coef * (inputs + cubic_coef * inputs * inputs * inputs)
    tangent = jnp.tanh(inner)
    values = 0.5 * inputs * (1.0 + tangent)
    slopes = 0.5 * (1.0 + tangent) + 0.5 * inputs * (1.0 - tangent * tangent) * gelu_coef * (
        1.0 + 3.0 * cubic_coef * inputs * inputs
    )
    return (values, slopes)


def call(name, kernel, out_shape, args, flops=0, moved=0, scratch=()):
    vmem = pl.BlockSpec(memory_space=pltpu.VMEM)
    return pl.pallas_call(
        kernel,
        name=name,
        out_shape=out_shape,
        in_specs=[vmem] * len(args),
        out_specs=jax.tree.map(lambda _: vmem, out_shape),
        scratch_shapes=scratch,
        compiler_params=pltpu.CompilerParams(vmem_limit_bytes=ROOM),
        cost_estimate=pl.CostEstimate(flops=flops, bytes_accessed=moved, transcendentals=0),
    )(*args)


def after(values, *events):
    return lax.optimization_barrier((values, events))[0]


def shaped(shape, dtype=bf16):
    return jax.ShapeDtypeStruct(shape, dtype)


def block_places(slot_row, k, capacity):
    at = slot_row - k * capacity
    return jnp.where((at >= 0) & (at < capacity), at, -2 * capacity)


def place_kernel(groups, capacity, tok_ref, id_ref, me_ref, gain_ref, cot_ref, slot_ref, *refs):
    sends, both = refs[:groups], refs[groups]
    count = tok_ref.shape[0]
    id_row = jnp.broadcast_to(id_ref[...], (count, count))
    id_col = jnp.transpose(id_row)
    at_row = lax.broadcasted_iota(jnp.int32, (count, count), 0)
    at_col = lax.broadcasted_iota(jnp.int32, (count, count), 1)
    earlier = jnp.where((id_row == id_col) & (at_row < at_col), 1, 0)
    ranks = jnp.sum(earlier, axis=0, keepdims=True)
    ahead = id_ref[...] - me_ref[...]
    ahead = jnp.where(ahead < 0, ahead + groups, ahead)
    slots = jnp.where(ranks < capacity, ahead * capacity + ranks, -1)
    slot_ref[...] = slots
    wide = tok_ref[...].astype(f32)
    scales = lax.rsqrt(jnp.mean(wide * wide, axis=1, keepdims=True) + 1e-06)
    both[:count] = (wide * scales * gain_ref[...]).astype(bf16)
    both[count:] = cot_ref[...]
    rows = lax.broadcasted_iota(jnp.int32, (2 * capacity, 2 * count), 0)
    for k in range(groups):
        places = block_places(slots, k, capacity)
        wanted = jnp.concatenate([places, places + capacity], axis=1)
        placing = jnp.where(rows == wanted, 1.0, 0.0).astype(bf16)
        sends[k][...] = mm(placing, both[...]).astype(bf16)


def hidden_kernel(in_ref, cot_ref, up_a, up_b, down_a, down_b, hid_a, hid_b, pre_a, pre_b):
    units = up_a.shape[1]
    step = min(units, 256)
    for up, down, hid, pre in ((up_a, down_a, hid_a, pre_a), (up_b, down_b, hid_b, pre_b)):
        for i in range(units // step):
            at = pl.ds(i * step, step)
            values, slopes = gelu_parts(mm(in_ref[...], up[:, at]))
            hid[:, at] = values.astype(bf16)
            pre[:, at] = (mm(cot_ref[...], down[at, :], NT) * slopes).astype(bf16)


def row_kernel(
    piece, in_ref, hid_a, hid_b, pre_a, pre_b, up_a, up_b, down_a, down_b,
    gain_ref, keep_out, send_out, keep_back, send_back,
):
    rows, width = in_ref.shape
    pieces = rows // piece
    for i in range(width // 256):
        at = pl.ds(i * 256, 256)
        total = mm(hid_a[...], down_a[:, at]) + mm(hid_b[...], down_b[:, at])
        keep_out[:, at] = total[: rows // 2]
        send_out[:, at] = total[rows // 2 :].astype(bf16)
        total = mm(pre_a[...], up_a[at, :], NT) + mm(pre_b[...], up_b[at, :], NT)
        gain_ref[:, at] = jnp.sum(total * in_ref[:, at].astype(f32), axis=0, keepdims=True)
        for p in range(pieces):
            part = total[p * piece : (p + 1) * piece]
            to = pl.ds((p // 2) * piece, piece)
            if p % 2:
                send_back[to, at] = part.astype(bf16)
            else:
                keep_back[to, at] = part


def grad_kernel(left_a, left_b, right_a, right_b, out_ref, left, right):
    rows = left_a.shape[0]
    left[:rows], left[rows:] = left_a[...], left_b[...]
    right[:rows], right[rows:] = right_a[...], right_b[...]
    for i in range(out_ref.shape[0] // 256):
        at = pl.ds(i * 256, 256)
        out_ref[at, :] = mm(left[:, at], right[...], TN).astype(bf16)


def token_kernel(capacity, slot_ref, tok_ref, gain_ref, *refs):
    blocks, mixed_ref, grad_ref = refs[:-2], refs[-2], refs[-1]
    count = slot_ref.shape[1]
    rows = lax.broadcasted_iota(jnp.int32, (2 * capacity, count), 0)
    mixed, d_normed = 0.0, 0.0
    for k, ref in enumerate(blocks):
        places = block_places(slot_ref[...], k, capacity)
        block = ref[...]
        mixed += mm(jnp.where(rows == places, 1.0, 0.0).astype(bf16), block, TN)
        d_normed += mm(jnp.where(rows == places + capacity, 1.0, 0.0).astype(bf16), block, TN)
    mixed_ref[...] = mixed.astype(bf16)
    wide = tok_ref[...].astype(f32)
    scales = lax.rsqrt(jnp.mean(wide * wide, axis=1, keepdims=True) + 1e-06)
    gained = d_normed * gain_ref[...]
    cubed = scales * scales * scales
    grad_ref[...] = (
        scales * gained - wide * (cubed * jnp.mean(gained * wide, axis=1, keepdims=True))
    ).astype(bf16)


def local(tokens, expert_ids, norm_gain, up_weight, down_weight, cotangent):
    groups = lax.axis_size("exp")
    copies = lax.axis_size("rep")
    count, width = tokens.shape
    capacity = 3 * count // (4 * groups)
    piece = groups * capacity // 2
    units = up_weight.shape[2]
    rows = piece * copies // 2
    bits = []
    while (2 << len(bits)) < copies:
        bits.append(2 << len(bits))

    def swap(x, bit):
        return lax.ppermute(x, "rep", [(i, i ^ bit) for i in range(copies)])

    def shift(x, k):
        return lax.ppermute(x, "exp", [(i, (i + k) % groups) for i in range(groups)])

    def join(*arrays):
        return jnp.concatenate(arrays, axis=0)

    up_a, down_a = up_weight[0], down_weight[0]
    up_b, down_b = swap(up_a, 1), swap(down_a, 1)

    me = lax.axis_index("exp").astype(jnp.int32).reshape(1, 1)
    gain_row = norm_gain.reshape(1, width)
    slot_row, *blocks = call(
        "place",
        functools.partial(place_kernel, groups, capacity),
        [shaped((1, count), jnp.int32)] + [shaped((2 * capacity, width))] * groups,
        (tokens, expert_ids.reshape(1, count), me, gain_row, cotangent),
        scratch=[pltpu.VMEM((2 * count, width), bf16)],
    )
    arrived = [blocks[0]] + [shift(blocks[k], k) for k in range(1, groups)]

    def start(n, cap_cut):
        mine = range(n * groups // 2, (n + 1) * groups // 2)
        return {0: join(*[arrived[k][cap_cut] for k in mine])}

    def grow(held, bit):
        known = sorted(held)
        got = swap(join(*[held[at] for at in known]), bit)
        return {**held, **{at ^ bit: got[n * piece : (n + 1) * piece] for n, at in enumerate(known)}}

    def ordered(held):
        return join(*[held[at] for at in sorted(held)])

    def halved(x, first):
        cut = x.shape[0] // 2
        if first:
            x = x.reshape(-1, 2, piece, width)
            return x[:, 0].reshape(cut, width), x[:, 1].reshape(cut, width)
        return x[:cut], x[cut:]

    down_bits = list(reversed(bits))
    work = 8 * rows * width * 2 * units
    weights = (up_a, up_b, down_a, down_b)

    def gather(n):
        pair = [start(n, slice(0, capacity)), start(n, slice(capacity, None))]
        for bit, back_bit in zip(bits, down_bits):
            pair = [grow(pair[0], bit), grow(pair[1], back_bit)]
            yield pair

    def compute(in_rows, cot_rows):
        acts = call(
            "hidden",
            hidden_kernel,
            [shaped((rows, units))] * 4,
            (in_rows, cot_rows, *weights),
            work // 2,
            8 << 20,
        )
        kept = [shaped((rows // 2, width), f32), shaped((rows // 2, width))] * 2
        parts = call(
            "rows",
            functools.partial(row_kernel, piece),
            [shaped((1, width), f32)] + kept,
            (in_rows, *acts, *weights),
            work // 2,
            8 << 20,
        )
        return acts, parts

    def scatter(parts, events):
        out, back = parts[1:3], parts[3:5]
        for n, (bit, back_bit) in enumerate(zip(down_bits, bits)):
            got = swap(out[1], bit), swap(back[1], back_bit)
            got = after(got, *events[n])
            out, back = out[0] + got[0].astype(f32), back[0] + got[1].astype(f32)
            if n < len(bits) - 1:
                out, back = halved(out, False), halved(back, True)
                out, back = (out[0], out[1].astype(bf16)), (back[0], back[1].astype(bf16))
                yield (out, back)
            else:
                yield out.astype(bf16), back.astype(bf16)

    def homeward(n, out_rows, back_rows):
        for i in range(groups // 2):
            k = n * groups // 2 + i
            cut = slice(i * capacity, (i + 1) * capacity)
            block = join(out_rows[cut], back_rows[cut])
            home[k] = shift(block, groups - k) if k else block

    *_, first = gather(0)
    steps = list(gather(1))
    in_1, cot_1 = after((ordered(first[0]), ordered(first[1])), steps[-2][0], steps[-2][1])
    acts_1, parts_1 = compute(in_1, cot_1)
    second = after(steps[-1], parts_1[0])
    in_2, cot_2 = ordered(second[0]), ordered(second[1])
    acts_2, parts_2 = compute(in_2, cot_2)
    in_all, cot_all = join(in_1, in_2), join(cot_1, cot_2)
    hid_a, hid_b, pre_a, pre_b = [join(a, b) for a, b in zip(acts_1, acts_2)]
    wide_rows = pltpu.VMEM((4 * rows, width), bf16)
    unit_rows = pltpu.VMEM((4 * rows, units), bf16)
    grad_down = call(
        "grad_down",
        grad_kernel,
        shaped((units, width)),
        (hid_a, swap(hid_b, 1), cot_all, swap(cot_all, 1)),
        work // 4,
        8 << 20,
        [unit_rows, wide_rows],
    )
    grad_up = call(
        "grad_up",
        grad_kernel,
        shaped((width, units)),
        (in_all, swap(in_all, 1), pre_a, swap(pre_b, 1)),
        work // 4,
        8 << 20,
        [wide_rows, unit_rows],
    )
    home = [None] * groups
    *_, sums_1 = scatter(parts_1, [(parts_2[0],)] + [(grad_down,)] * len(bits))
    *_, sums_2 = scatter(parts_2, [(grad_up,)] + [()] * len(bits))
    homeward(0, *sums_1)
    homeward(1, *sums_2)

    total = parts_1[0] + parts_2[0]
    total = after(total, grad_up)
    for bit in [1] + bits:
        total = total + swap(total, bit)
    step = 1
    while step < groups:
        total = total + lax.ppermute(total, "exp", [(i, i ^ step) for i in range(groups)])
        step *= 2
    grad_gain = (total / gain_row).reshape(width)
    mixed, grad_tokens = call(
        "tokens",
        functools.partial(token_kernel, capacity),
        [shaped((count, width))] * 2,
        (slot_row, tokens, gain_row, *home),
    )
    return (mixed, grad_tokens, grad_up[None], grad_down[None], grad_gain)


def solution(mesh):
    return jax.shard_map(
        local,
        mesh=mesh,
        in_specs=(
            P(("rep", "exp"), None),
            P(("rep", "exp"), None),
            P(),
            P("exp", None, "rep"),
            P("exp", "rep", None),
            P(("rep", "exp"), None),
        ),
        out_specs=(
            P(("rep", "exp"), None),
            P(("rep", "exp"), None),
            P("exp", None, "rep"),
            P("exp", "rep", None),
            P(),
        ),
        check_vma=False,
    )
```

time: 144 us -> 126 us (0.88)
  Pallas kernels: 33.4 us -> 18.6 us
  starting transfers between devices: 48 us -> 40.9 us
  waiting for transfers between devices: 53.9 us -> 57.1 us
    pallas_call x7 -> x8, Pallas kernels: 33.4 us -> 18.6 us  [call(): pl.pallas_call(kernel, name=name, out_shape=out_shape, in_specs=[vmem] *...]
    ppermute x12 -> x6, waiting for transfers between devices: 9.84 us -> 18.3 us  [shift(): lax.ppermute(x, 'exp', [(i, (i + k) % groups) for i in range(groups)])]
    ppermute x12 -> x6, starting transfers between devices: 21 us -> 15.1 us  [shift(): lax.ppermute(x, 'exp', [(i, (i + k) % groups) for i in range(groups)])]
    ppermute x25, waiting for transfers between devices: 41.3 us -> 36.8 us  [swap(): return lax.ppermute(x, 'rep', [(i, i ^ bit) for i in range(copies)])]
    ppermute x25, starting transfers between devices: 24.3 us -> 20.9 us  [swap(): return lax.ppermute(x, 'rep', [(i, i ^ bit) for i in range(copies)])]
    ppermute x2, starting transfers between devices: 2.69 us -> 4.92 us  [local(): lax.ppermute(total, 'exp', [(i, i ^ step) for i in range(groups)])]
    unnamed x33 -> x25, local copies, waits for them, and re-layouts: 6.07 us -> 5.69 us
  transfers between devices with their start and end apart: 39 -> 33, of which waited for: 19 -> 12; matrix products, arithmetic and copies ran while one was open for 1% -> 2% of each run, Pallas kernels for 7% -> 9%
where the time goes in v2:
time: 126 us; the launch traced here: 125 us
  waiting for transfers between devices  57.1 us (45%)
  starting transfers between devices  40.9 us (32%)
  Pallas kernels  18.6 us (15%)
  local copies, waits for them, and re-layouts  6.02 us (5%)
  other arithmetic  1.65 us (1%)
    ppermute x25, waiting for transfers between devices, swap(): return lax.ppermute(x, 'rep', [(i, i ^ bit) for i in range(copies)])  36.8 us
    ppermute x25, starting transfers between devices, swap(): return lax.ppermute(x, 'rep', [(i, i ^ bit) for i in range(copies)])  20.9 us
    pallas_call x8, Pallas kernels, call(): pl.pallas_call(kernel, name=name, out_shape=out_shape, in_specs=[vmem] *...  18.6 us
    ppermute x6, waiting for transfers between devices, shift(): lax.ppermute(x, 'exp', [(i, (i + k) % groups) for i in range(groups)])  18.3 us
    ppermute x6, starting transfers between devices, shift(): lax.ppermute(x, 'exp', [(i, (i + k) % groups) for i in range(groups)])  15.1 us
    unnamed x25, local copies, waits for them, and re-layouts  5.69 us
    ppermute x2, starting transfers between devices, local(): lax.ppermute(total, 'exp', [(i, i ^ step) for i in range(groups)])  4.92 us
  transfers between devices with their start and end apart: 33, of which 12 were waited for; matrix products, arithmetic and copies ran while one was open for 2% of the time, Pallas kernels for 9%

profile of v2, /device:TPU:0, one launch (start us, length us, event | category | flops | bytes accessed | tf_op | source)
XLA Modules:
  0.0 125.4 jit_solution(11556457994752731666)
XLA Ops:
  5.1 3.1 %collective-permute-start = (bf16[48,2048]{1,0:T(8,128)(2,1)S(1)}, bf16[48,2048]{1,0:T(8,128)(2,1)S(1)}, u32[]{:S(2)}, u32[]{:S(2)}) collective-permute-start(bf16[48,2048]{1,0:T(8,128)(2,1)S(1)} %get-tuple-element.51), channel_id=1, source_target_pairs={{0,1},{1,2},{2,3},{3,0},{4,5},{5,6},{6,7},{7,4},{8,9},{9,10},{10,1... | collective-permute-start | bytes 589832 | tf_op jit(solution)/shard_map/ppermute | solution.py:166
  8.2 2.6 %collective-permute-start.5 = (bf16[48,2048]{1,0:T(8,128)(2,1)S(1)}, bf16[48,2048]{1,0:T(8,128)(2,1)S(1)}, u32[]{:S(2)}, u32[]{:S(2)}) collective-permute-start(bf16[48,2048]{1,0:T(8,128)(2,1)S(1)} %get-tuple-element.52), channel_id=1, source_target_pairs={{0,2},{1,3},{2,0},{3,1},{4,6},{5,7},{6,4},{7,5},{8,10},{9,11},{10,... | collective-permute-start | bytes 589832 | tf_op jit(solution)/shard_map/ppermute | solution.py:166
  10.8 1.3 %collective-permute-start.6 = (bf16[48,2048]{1,0:T(8,128)(2,1)S(1)}, bf16[48,2048]{1,0:T(8,128)(2,1)S(1)}, u32[]{:S(2)}, u32[]{:S(2)}) collective-permute-start(bf16[48,2048]{1,0:T(8,128)(2,1)S(1)} %get-tuple-element.53), channel_id=1, source_target_pairs={{0,3},{1,0},{2,1},{3,2},{4,7},{5,4},{6,5},{7,6},{8,11},{9,8},{10,9... | collective-permute-start | bytes 589832 | tf_op jit(solution)/shard_map/ppermute | solution.py:166
  12.7 11.0 %collective-permute-done.5 = bf16[48,2048]{1,0:T(8,128)(2,1)S(1)} collective-permute-done((bf16[48,2048]{1,0:T(8,128)(2,1)S(1)}, bf16[48,2048]{1,0:T(8,128)(2,1)S(1)}, u32[]{:S(2)}, u32[]{:S(2)}) %collective-permute-start.5) | collective-permute-done | bytes 196640 | tf_op jit(solution)/shard_map/ppermute | solution.py:166
  23.8 1.5 %collective-permute-start.7 = (bf16[48,2048]{1,0:T(8,128)(2,1)S(1)}, bf16[48,2048]{1,0:T(8,128)(2,1)S(1)}, u32[]{:S(2)}, u32[]{:S(2)}) collective-permute-start(bf16[48,2048]{1,0:T(8,128)(2,1)S(1)} %pad_maximum_fusion.12), channel_id=1, source_target_pairs={{0,8},{4,12},{8,0},{12,4},{16,24},{20,28},{24,16},{28,20},{1,9},{5... | collective-permute-start | bytes 589832 | tf_op jit(solution)/shard_map/ppermute | solution.py:163
  25.3 1.6 %collective-permute-start.8 = (bf16[48,2048]{1,0:T(8,128)(2,1)S(1)}, bf16[48,2048]{1,0:T(8,128)(2,1)S(1)}, u32[]{:S(2)}, u32[]{:S(2)}) collective-permute-start(bf16[48,2048]{1,0:T(8,128)(2,1)S(1)} %pad_maximum_fusion.13), channel_id=1, source_target_pairs={{0,16},{4,20},{8,24},{12,28},{16,0},{20,4},{24,8},{28,12},{1,17},{... | collective-permute-start | bytes 589832 | tf_op jit(solution)/shard_map/ppermute | solution.py:163
  27.6 4.3 %collective-permute-done.8 = bf16[48,2048]{1,0:T(8,128)(2,1)S(1)} collective-permute-done((bf16[48,2048]{1,0:T(8,128)(2,1)S(1)}, bf16[48,2048]{1,0:T(8,128)(2,1)S(1)}, u32[]{:S(2)}, u32[]{:S(2)}) %collective-permute-start.8) | collective-permute-done | bytes 196640 | tf_op jit(solution)/shard_map/ppermute | solution.py:163
  31.8 1.5 %collective-permute-start.3 = (bf16[48,2048]{1,0:T(8,128)(2,1)S(1)}, bf16[48,2048]{1,0:T(8,128)(2,1)S(1)}, u32[]{:S(2)}, u32[]{:S(2)}) collective-permute-start(bf16[48,2048]{1,0:T(8,128)(2,1)S(1)} %pad_maximum_fusion.11), channel_id=1, source_target_pairs={{0,16},{4,20},{8,24},{12,28},{16,0},{20,4},{24,8},{28,12},{1,17},{... | collective-permute-start | bytes 589832 | tf_op jit(solution)/shard_map/ppermute | solution.py:163
  33.4 4.1 %collective-permute-done.3 = bf16[48,2048]{1,0:T(8,128)(2,1)S(1)} collective-permute-done((bf16[48,2048]{1,0:T(8,128)(2,1)S(1)}, bf16[48,2048]{1,0:T(8,128)(2,1)S(1)}, u32[]{:S(2)}, u32[]{:S(2)}) %collective-permute-start.3) | collective-permute-done | bytes 196640 | tf_op jit(solution)/shard_map/ppermute | solution.py:163
  38.1 1.5 %collective-permute-start.4 = (bf16[96,2048]{1,0:T(8,128)(2,1)S(1)}, bf16[96,2048]{1,0:T(8,128)(2,1)S(1)}, u32[]{:S(2)}, u32[]{:S(2)}) collective-permute-start(bf16[96,2048]{1,0:T(8,128)(2,1)S(1)} %pad_maximum_fusion.3), channel_id=1, source_target_pairs={{0,8},{4,12},{8,0},{12,4},{16,24},{20,28},{24,16},{28,20},{1,9},{5... | collective-permute-start | bytes 1179656 | tf_op jit(solution)/shard_map/ppermute | solution.py:163
  39.7 1.6 %collective-permute-start.13 = (bf16[96,2048]{1,0:T(8,128)(2,1)S(1)}, bf16[96,2048]{1,0:T(8,128)(2,1)S(1)}, u32[]{:S(2)}, u32[]{:S(2)}) collective-permute-start(bf16[96,2048]{1,0:T(8,128)(2,1)S(1)} %pad_maximum_fusion.4), channel_id=1, source_target_pairs={{0,16},{4,20},{8,24},{12,28},{16,0},{20,4},{24,8},{28,12},{1,17},{... | collective-permute-start | bytes 1179656 | tf_op jit(solution)/shard_map/ppermute | solution.py:163
  41.3 13.2 %collective-permute-done.4 = bf16[96,2048]{1,0:T(8,128)(2,1)S(1)} collective-permute-done((bf16[96,2048]{1,0:T(8,128)(2,1)S(1)}, bf16[96,2048]{1,0:T(8,128)(2,1)S(1)}, u32[]{:S(2)}, u32[]{:S(2)}) %collective-permute-start.4) | collective-permute-done | bytes 393248 | tf_op jit(solution)/shard_map/ppermute | solution.py:163
  54.5 1.5 %collective-permute-start.2 = (bf16[96,2048]{1,0:T(8,128)(2,1)S(1)}, bf16[96,2048]{1,0:T(8,128)(2,1)S(1)}, u32[]{:S(2)}, u32[]{:S(2)}) collective-permute-start(bf16[96,2048]{1,0:T(8,128)(2,1)S(1)} %pad_maximum_fusion.2), channel_id=1, source_target_pairs={{0,16},{4,20},{8,24},{12,28},{16,0},{20,4},{24,8},{28,12},{1,17},{... | collective-permute-start | bytes 1179656 | tf_op jit(solution)/shard_map/ppermute | solution.py:163
  56.1 6.2 %collective-permute-done.2 = bf16[96,2048]{1,0:T(8,128)(2,1)S(1)} collective-permute-done((bf16[96,2048]{1,0:T(8,128)(2,1)S(1)}, bf16[96,2048]{1,0:T(8,128)(2,1)S(1)}, u32[]{:S(2)}, u32[]{:S(2)}) %collective-permute-start.2) | collective-permute-done | bytes 393248 | tf_op jit(solution)/shard_map/ppermute | solution.py:163
  64.6 2.3 %hidden.2 = (bf16[192,512]{1,0:T(8,128)(2,1)S(1)}, bf16[192,512]{1,0:T(8,128)(2,1)S(1)}, bf16[192,512]{1,0:T(8,128)(2,1)S(1)}, bf16[192,512]{1,0:T(8,128)(2,1)S(1)}) custom-call(bf16[192,2048]{1,0:T(8,128)(2,1)S(1)} %pad_maximum_fusion.in_ref, bf16[192,2048]{1,0:T(8,128)(2,1)S(1)} %slice_dynamic-update-slice_fusion.cot_ref, bf16[2048,512]{1,0:T(8,128)(2,1)S(1)} %bitcast.27, ...), custom_call_target="tpu_custom_call" | custom-call | flops 1610612736 | bytes 8388608 | tf_op jit(solution)/shard_map/hidden/pallas_call | solution.py:38
  66.9 2.2 %rows.2 = (f32[1,2048]{1,0:T(1,128)S(1)}, f32[96,2048]{1,0:T(8,128)S(1)}, bf16[96,2048]{1,0:T(8,128)(2,1)S(1)}, f32[96,2048]{1,0:T(8,128)S(1)}, bf16[96,2048]{1,0:T(8,128)(2,1)S(1)}) custom-call(bf16[192,2048]{1,0:T(8,128)(2,1)S(1)} %pad_maximum_fusion.in_ref, bf16[192,512]{1,0:T(8,128)(2,1)S(1)} %get-tuple-element.56.hid_a, ...), custom_call_target="tpu_custom_call" | custom-call | flops 1610612736 | bytes 8388608 | tf_op jit(solution)/shard_map/rows/pallas_call | solution.py:38
  69.1 1.6 %collective-permute-start.11 = (bf16[96,2048]{1,0:T(8,128)(2,1)S(1)}, bf16[96,2048]{1,0:T(8,128)(2,1)S(1)}, u32[]{:S(2)}, u32[]{:S(2)}) collective-permute-start(bf16[96,2048]{1,0:T(8,128)(2,1)S(1)} %get-tuple-element.61), channel_id=1, source_target_pairs={{0,16},{4,20},{8,24},{12,28},{16,0},{20,4},{24,8},{28,12},{1,17},{... | collective-permute-start | bytes 1179656 | tf_op jit(solution)/shard_map/ppermute | solution.py:163
  72.0 2.3 %hidden.3 = (bf16[192,512]{1,0:T(8,128)(2,1)S(1)}, bf16[192,512]{1,0:T(8,128)(2,1)S(1)}, bf16[192,512]{1,0:T(8,128)(2,1)S(1)}, bf16[192,512]{1,0:T(8,128)(2,1)S(1)}) custom-call(bf16[192,2048]{1,0:T(8,128)(2,1)S(1)} %get-tuple-element.102.in_ref, bf16[192,2048]{1,0:T(8,128)(2,1)S(1)} %pad_maximum_fusion.1.cot_ref, bf16[2048,512]{1,0:T(8,128)(2,1)S(1)} %bitcast.29, ...), custom_call_target="tpu_custom_call" | custom-call | flops 1610612736 | bytes 8388608 | tf_op jit(solution)/shard_map/hidden/pallas_call | solution.py:38
  74.4 2.2 %rows.3 = (f32[1,2048]{1,0:T(1,128)S(1)}, f32[96,2048]{1,0:T(8,128)S(1)}, bf16[96,2048]{1,0:T(8,128)(2,1)S(1)}, f32[96,2048]{1,0:T(8,128)S(1)}, bf16[96,2048]{1,0:T(8,128)(2,1)S(1)}) custom-call(bf16[192,2048]{1,0:T(8,128)(2,1)S(1)} %get-tuple-element.102.in_ref, bf16[192,512]{1,0:T(8,128)(2,1)S(1)} %get-tuple-element.72.hid_a, ...), custom_call_target="tpu_custom_call" | custom-call | flops 1610612736 | bytes 8388608 | tf_op jit(solution)/shard_map/rows/pallas_call | solution.py:38
  79.1 2.8 %collective-permute-done.12 = bf16[96,2048]{1,0:T(8,128)(2,1)S(1)} collective-permute-done((bf16[96,2048]{1,0:T(8,128)(2,1)S(1)}, bf16[96,2048]{1,0:T(8,128)(2,1)S(1)}, u32[]{:S(2)}, u32[]{:S(2)}) %collective-permute-start.12) | collective-permute-done | bytes 393248 | tf_op jit(solution)/shard_map/ppermute | solution.py:163
  82.8 1.6 %collective-permute-start.15 = (bf16[48,2048]{1,0:T(8,128)(2,1)S(1)}, bf16[48,2048]{1,0:T(8,128)(2,1)S(1)}, u32[]{:S(2)}, u32[]{:S(2)}) collective-permute-start(bf16[48,2048]{1,0:T(8,128)(2,1)S(1)} %slice.184), channel_id=1, source_target_pairs={{0,8},{4,12},{8,0},{12,4},{16,24},{20,28},{24,16},{28,20},{1,9},{5... | collective-permute-start | bytes 589832 | tf_op jit(solution)/shard_map/ppermute | solution.py:163
  84.4 3.2 %grad_up.1 = bf16[2048,512]{1,0:T(8,128)(2,1)} custom-call(bf16[384,2048]{1,0:T(8,128)(2,1)S(1)} %get-tuple-element.101.left_a, bf16[384,2048]{1,0:T(8,128)(2,1)S(1)} %collective-permute-done.22.left_b, bf16[384,512]{1,0:T(8,128)(2,1)S(1)} %pad_maximum_fusion.8.right_a, bf16[384,512]{1,0:T(8,128)(2,1)S(1)} %collective-permute-done.23.right_b), custom_call_target="tpu_custom_call" | custom-call | flops 805306368 | bytes 8388608 | tf_op jit(solution)/shard_map/grad_up/pallas_call | solution.py:38
  90.5 3.2 %grad_down.1 = bf16[512,2048]{1,0:T(8,128)(2,1)} custom-call(bf16[384,512]{1,0:T(8,128)(2,1)S(1)} %pad_maximum_fusion.6.left_a, bf16[384,512]{1,0:T(8,128)(2,1)S(1)} %collective-permute-done.17.left_b, bf16[384,2048]{1,0:T(8,128)(2,1)S(1)} %constant_dynamic-update-slice_fusion.7.right_a, bf16[384,2048]{1,0:T(8,128)(2,1)S(1)} %collective-permute-done.18.right_b), custom_call_target="tpu_custom_call" | custom-call | flops 805306368 | bytes 8388608 | tf_op jit(solution)/shard_map/grad_down/pallas_call | solution.py:38
  93.6 1.7 %collective-permute-done.16 = bf16[48,2048]{1,0:T(8,128)(2,1)S(1)} collective-permute-done((bf16[48,2048]{1,0:T(8,128)(2,1)S(1)}, bf16[48,2048]{1,0:T(8,128)(2,1)S(1)}, u32[]{:S(2)}, u32[]{:S(2)}) %collective-permute-start.16) | collective-permute-done | bytes 196640 | tf_op jit(solution)/shard_map/ppermute | solution.py:163
  95.6 3.6 %collective-permute-done.29 = f32[1,2048]{1,0:T(1,128)S(1)} collective-permute-done((f32[1,2048]{1,0:T(1,128)S(1)}, f32[1,2048]{1,0:T(1,128)S(1)}, u32[]{:S(2)}, u32[]{:S(2)}) %collective-permute-start.29) | collective-permute-done | bytes 8224 | tf_op jit(solution)/shard_map/ppermute | solution.py:163
  100.1 4.0 %collective-permute-start.19 = (bf16[48,2048]{1,0:T(8,128)(2,1)S(1)}, bf16[48,2048]{1,0:T(8,128)(2,1)S(1)}, u32[]{:S(2)}, u32[]{:S(2)}) collective-permute-start(bf16[48,2048]{1,0:T(8,128)(2,1)S(1)} %pad_maximum_fusion.15), channel_id=1, source_target_pairs={{0,3},{1,0},{2,1},{3,2},{4,7},{5,4},{6,5},{7,6},{8,11},{9,8},{10,9... | collective-permute-start | bytes 589832 | tf_op jit(solution)/shard_map/ppermute | solution.py:166
  104.1 3.8 %collective-permute-start.31 = (f32[1,2048]{1,0:T(1,128)S(1)}, f32[1,2048]{1,0:T(1,128)S(1)}, u32[]{:S(2)}, u32[]{:S(2)}) collective-permute-start(f32[1,2048]{1,0:T(1,128)S(1)} %add.53), channel_id=1, source_target_pairs={{0,1},{1,0},{2,3},{3,2},{4,5},{5,4},{6,7},{7,6},{8,9},{9,8},{10,11... | collective-permute-start | bytes 24584 | tf_op jit(solution)/shard_map/ppermute | solution.py:295
  108.0 1.6 %collective-permute-done.31 = f32[1,2048]{1,0:T(1,128)S(1)} collective-permute-done((f32[1,2048]{1,0:T(1,128)S(1)}, f32[1,2048]{1,0:T(1,128)S(1)}, u32[]{:S(2)}, u32[]{:S(2)}) %collective-permute-start.31) | collective-permute-done | bytes 8224 | tf_op jit(solution)/shard_map/ppermute | solution.py:295
  110.9 2.0 %collective-permute-start.26 = (bf16[48,2048]{1,0:T(8,128)(2,1)S(1)}, bf16[48,2048]{1,0:T(8,128)(2,1)S(1)}, u32[]{:S(2)}, u32[]{:S(2)}) collective-permute-start(bf16[48,2048]{1,0:T(8,128)(2,1)S(1)} %pad_maximum_fusion.16), channel_id=1, source_target_pairs={{0,2},{1,3},{2,0},{3,1},{4,6},{5,7},{6,4},{7,5},{8,10},{9,11},{10,... | collective-permute-start | bytes 589832 | tf_op jit(solution)/shard_map/ppermute | solution.py:166
  112.9 2.1 %collective-permute-start.27 = (bf16[48,2048]{1,0:T(8,128)(2,1)S(1)}, bf16[48,2048]{1,0:T(8,128)(2,1)S(1)}, u32[]{:S(2)}, u32[]{:S(2)}) collective-permute-start(bf16[48,2048]{1,0:T(8,128)(2,1)S(1)} %pad_maximum_fusion.17), channel_id=1, source_target_pairs={{0,1},{1,2},{2,3},{3,0},{4,5},{5,6},{6,7},{7,4},{8,9},{9,10},{10,1... | collective-permute-start | bytes 589832 | tf_op jit(solution)/shard_map/ppermute | solution.py:166
  115.9 7.3 %collective-permute-done.26.refs_2_ = bf16[48,2048]{1,0:T(8,128)(2,1)S(1)} collective-permute-done((bf16[48,2048]{1,0:T(8,128)(2,1)S(1)}, bf16[48,2048]{1,0:T(8,128)(2,1)S(1)}, u32[]{:S(2)}, u32[]{:S(2)}) %collective-permute-start.26) | collective-permute-done | bytes 196640 | tf_op jit(solution)/shard_map/ppermute | solution.py:166
  123.2 2.2 %tokens.1 = (bf16[128,2048]{1,0:T(8,128)(2,1)}, bf16[128,2048]{1,0:T(8,128)(2,1)}) custom-call(s32[1,128]{1,0:T(1,128)S(1)} %get-tuple-element.49.slot_ref, bf16[128,2048]{1,0:T(8,128)(2,1)S(1)} %copy-done.3, f32[1,2048]{1,0:T(1,128)S(1)} %bitcast.38, bf16[48,2048]{1,0:T(8,128)(2,1)S(1)} %pad_maximum_fusion.14.refs_0_, ...), custom_call_target="tpu_custom_call" | custom-call | tf_op jit(solution)/shard_map/tokens/pallas_call | solution.py:38
  (116 shorter events, 19.5 us)
Async XLA Ops:
  5.1 21.8 %collective-permute-start = (bf16[48,2048]{1,0:T(8,128)(2,1)S(1)}, bf16[48,2048]{1,0:T(8,128)(2,1)S(1)}, u32[]{:S(2)}, u32[]{:S(2)}) collective-permute-start(bf16[48,2048]{1,0:T(8,128)(2,1)S(1)} %get-tuple-element.51), channel_id=1, source_target_pairs={{0,1},{1,2},{2,3},{3,0},{4,5},{5,6},{6,7},{7,4},{8,9},{9,10},{10,1... | collective-permute-start | bytes 589832 | tf_op jit(solution)/shard_map/ppermute | solution.py:166
  8.2 15.5 %collective-permute-start.5 = (bf16[48,2048]{1,0:T(8,128)(2,1)S(1)}, bf16[48,2048]{1,0:T(8,128)(2,1)S(1)}, u32[]{:S(2)}, u32[]{:S(2)}) collective-permute-start(bf16[48,2048]{1,0:T(8,128)(2,1)S(1)} %get-tuple-element.52), channel_id=1, source_target_pairs={{0,2},{1,3},{2,0},{3,1},{4,6},{5,7},{6,4},{7,5},{8,10},{9,11},{10,... | collective-permute-start | bytes 589832 | tf_op jit(solution)/shard_map/ppermute | solution.py:166
  10.8 12.9 %collective-permute-start.6 = (bf16[48,2048]{1,0:T(8,128)(2,1)S(1)}, bf16[48,2048]{1,0:T(8,128)(2,1)S(1)}, u32[]{:S(2)}, u32[]{:S(2)}) collective-permute-start(bf16[48,2048]{1,0:T(8,128)(2,1)S(1)} %get-tuple-element.53), channel_id=1, source_target_pairs={{0,3},{1,0},{2,1},{3,2},{4,7},{5,4},{6,5},{7,6},{8,11},{9,8},{10,9... | collective-permute-start | bytes 589832 | tf_op jit(solution)/shard_map/ppermute | solution.py:166
  12.2 50.5 %collective-permute-start.9 = (bf16[2048,512]{1,0:T(8,128)(2,1)}, bf16[2048,512]{1,0:T(8,128)(2,1)S(1)}, u32[]{:S(2)}, u32[]{:S(2)}) collective-permute-start(bf16[2048,512]{1,0:T(8,128)(2,1)} %bitcast.26), channel_id=1, source_target_pairs={{0,4},{4,0},{8,12},{12,8},{16,20},{20,16},{24,28},{28,24},{1,5},{5... | collective-permute-start | bytes 6291464 | tf_op jit(solution)/shard_map/ppermute | solution.py:163
  12.2 50.5 %collective-permute-start.10 = (bf16[512,2048]{1,0:T(8,128)(2,1)}, bf16[512,2048]{1,0:T(8,128)(2,1)S(1)}, u32[]{:S(2)}, u32[]{:S(2)}) collective-permute-start(bf16[512,2048]{1,0:T(8,128)(2,1)} %bitcast.31), channel_id=1, source_target_pairs={{0,4},{4,0},{8,12},{12,8},{16,20},{20,16},{24,28},{28,24},{1,5},{5... | collective-permute-start | bytes 6291464 | tf_op jit(solution)/shard_map/ppermute | solution.py:163
  23.8 14.3 %collective-permute-start.7 = (bf16[48,2048]{1,0:T(8,128)(2,1)S(1)}, bf16[48,2048]{1,0:T(8,128)(2,1)S(1)}, u32[]{:S(2)}, u32[]{:S(2)}) collective-permute-start(bf16[48,2048]{1,0:T(8,128)(2,1)S(1)} %pad_maximum_fusion.12), channel_id=1, source_target_pairs={{0,8},{4,12},{8,0},{12,4},{16,24},{20,28},{24,16},{28,20},{1,9},{5... | collective-permute-start | bytes 589832 | tf_op jit(solution)/shard_map/ppermute | solution.py:163
  25.3 6.5 %collective-permute-start.8 = (bf16[48,2048]{1,0:T(8,128)(2,1)S(1)}, bf16[48,2048]{1,0:T(8,128)(2,1)S(1)}, u32[]{:S(2)}, u32[]{:S(2)}) collective-permute-start(bf16[48,2048]{1,0:T(8,128)(2,1)S(1)} %pad_maximum_fusion.13), channel_id=1, source_target_pairs={{0,16},{4,20},{8,24},{12,28},{16,0},{20,4},{24,8},{28,12},{1,17},{... | collective-permute-start | bytes 589832 | tf_op jit(solution)/shard_map/ppermute | solution.py:163
  27.0 12.7 %collective-permute-start.1 = (bf16[48,2048]{1,0:T(8,128)(2,1)S(1)}, bf16[48,2048]{1,0:T(8,128)(2,1)S(1)}, u32[]{:S(2)}, u32[]{:S(2)}) collective-permute-start(bf16[48,2048]{1,0:T(8,128)(2,1)S(1)} %pad_maximum_fusion.10), channel_id=1, source_target_pairs={{0,8},{4,12},{8,0},{12,4},{16,24},{20,28},{24,16},{28,20},{1,9},{5... | collective-permute-start | bytes 589832 | tf_op jit(solution)/shard_map/ppermute | solution.py:163
  31.8 5.7 %collective-permute-start.3 = (bf16[48,2048]{1,0:T(8,128)(2,1)S(1)}, bf16[48,2048]{1,0:T(8,128)(2,1)S(1)}, u32[]{:S(2)}, u32[]{:S(2)}) collective-permute-start(bf16[48,2048]{1,0:T(8,128)(2,1)S(1)} %pad_maximum_fusion.11), channel_id=1, source_target_pairs={{0,16},{4,20},{8,24},{12,28},{16,0},{20,4},{24,8},{28,12},{1,17},{... | collective-permute-start | bytes 589832 | tf_op jit(solution)/shard_map/ppermute | solution.py:163
  37.5 25.1 %collective-permute-start.14 = (bf16[96,2048]{1,0:T(8,128)(2,1)S(1)}, bf16[96,2048]{1,0:T(8,128)(2,1)S(1)}, u32[]{:S(2)}, u32[]{:S(2)}) collective-permute-start(bf16[96,2048]{1,0:T(8,128)(2,1)S(1)} %pad_maximum_fusion.5), channel_id=1, source_target_pairs={{0,8},{4,12},{8,0},{12,4},{16,24},{20,28},{24,16},{28,20},{1,9},{5... | collective-permute-start | bytes 1179656 | tf_op jit(solution)/shard_map/ppermute | solution.py:163
  38.1 16.4 %collective-permute-start.4 = (bf16[96,2048]{1,0:T(8,128)(2,1)S(1)}, bf16[96,2048]{1,0:T(8,128)(2,1)S(1)}, u32[]{:S(2)}, u32[]{:S(2)}) collective-permute-start(bf16[96,2048]{1,0:T(8,128)(2,1)S(1)} %pad_maximum_fusion.3), channel_id=1, source_target_pairs={{0,8},{4,12},{8,0},{12,4},{16,24},{20,28},{24,16},{28,20},{1,9},{5... | collective-permute-start | bytes 1179656 | tf_op jit(solution)/shard_map/ppermute | solution.py:163
  39.7 22.9 %collective-permute-start.13 = (bf16[96,2048]{1,0:T(8,128)(2,1)S(1)}, bf16[96,2048]{1,0:T(8,128)(2,1)S(1)}, u32[]{:S(2)}, u32[]{:S(2)}) collective-permute-start(bf16[96,2048]{1,0:T(8,128)(2,1)S(1)} %pad_maximum_fusion.4), channel_id=1, source_target_pairs={{0,16},{4,20},{8,24},{12,28},{16,0},{20,4},{24,8},{28,12},{1,17},{... | collective-permute-start | bytes 1179656 | tf_op jit(solution)/shard_map/ppermute | solution.py:163
  54.5 7.8 %collective-permute-start.2 = (bf16[96,2048]{1,0:T(8,128)(2,1)S(1)}, bf16[96,2048]{1,0:T(8,128)(2,1)S(1)}, u32[]{:S(2)}, u32[]{:S(2)}) collective-permute-start(bf16[96,2048]{1,0:T(8,128)(2,1)S(1)} %pad_maximum_fusion.2), channel_id=1, source_target_pairs={{0,16},{4,20},{8,24},{12,28},{16,0},{20,4},{24,8},{28,12},{1,17},{... | collective-permute-start | bytes 1179656 | tf_op jit(solution)/shard_map/ppermute | solution.py:163
  69.1 10.0 %collective-permute-start.11 = (bf16[96,2048]{1,0:T(8,128)(2,1)S(1)}, bf16[96,2048]{1,0:T(8,128)(2,1)S(1)}, u32[]{:S(2)}, u32[]{:S(2)}) collective-permute-start(bf16[96,2048]{1,0:T(8,128)(2,1)S(1)} %get-tuple-element.61), channel_id=1, source_target_pairs={{0,16},{4,20},{8,24},{12,28},{16,0},{20,4},{24,8},{28,12},{1,17},{... | collective-permute-start | bytes 1179656 | tf_op jit(solution)/shard_map/ppermute | solution.py:163
  70.7 11.2 %collective-permute-start.12 = (bf16[96,2048]{1,0:T(8,128)(2,1)S(1)}, bf16[96,2048]{1,0:T(8,128)(2,1)S(1)}, u32[]{:S(2)}, u32[]{:S(2)}) collective-permute-start(bf16[96,2048]{1,0:T(8,128)(2,1)S(1)} %get-tuple-element.62), channel_id=1, source_target_pairs={{0,8},{4,12},{8,0},{12,4},{16,24},{20,28},{24,16},{28,20},{1,9},{5... | collective-permute-start | bytes 1179656 | tf_op jit(solution)/shard_map/ppermute | solution.py:163
  76.7 10.9 %collective-permute-start.20 = (bf16[96,2048]{1,0:T(8,128)(2,1)S(1)}, bf16[96,2048]{1,0:T(8,128)(2,1)S(1)}, u32[]{:S(2)}, u32[]{:S(2)}) collective-permute-start(bf16[96,2048]{1,0:T(8,128)(2,1)S(1)} %get-tuple-element.83), channel_id=1, source_target_pairs={{0,16},{4,20},{8,24},{12,28},{16,0},{20,4},{24,8},{28,12},{1,17},{... | collective-permute-start | bytes 1179656 | tf_op jit(solution)/shard_map/ppermute | solution.py:163
  77.2 11.1 %collective-permute-start.21 = (bf16[96,2048]{1,0:T(8,128)(2,1)S(1)}, bf16[96,2048]{1,0:T(8,128)(2,1)S(1)}, u32[]{:S(2)}, u32[]{:S(2)}) collective-permute-start(bf16[96,2048]{1,0:T(8,128)(2,1)S(1)} %get-tuple-element.84), channel_id=1, source_target_pairs={{0,8},{4,12},{8,0},{12,4},{16,24},{20,28},{24,16},{28,20},{1,9},{5... | collective-permute-start | bytes 1179656 | tf_op jit(solution)/shard_map/ppermute | solution.py:163
  78.2 4.6 %collective-permute-start.22 = (bf16[384,2048]{1,0:T(8,128)(2,1)S(1)}, bf16[384,2048]{1,0:T(8,128)(2,1)S(1)}, u32[]{:S(2)}, u32[]{:S(2)}) collective-permute-start(bf16[384,2048]{1,0:T(8,128)(2,1)S(1)} %get-tuple-element.101.left_a), channel_id=1, source_target_pairs={{0,4},{4,0},{8,12},{12,8},{16,20},{20,16},{24,28},{28,24},{1,5},{5... | collective-permute-start | bytes 4718600 | tf_op jit(solution)/shard_map/ppermute | solution.py:163
  81.9 7.6 %collective-permute-start.18 = (bf16[384,2048]{1,0:T(8,128)(2,1)S(1)}, bf16[384,2048]{1,0:T(8,128)(2,1)S(1)}, u32[]{:S(2)}, u32[]{:S(2)}) collective-permute-start(bf16[384,2048]{1,0:T(8,128)(2,1)S(1)} %constant_dynamic-update-slice_fusion.7.right_a), channel_id=1, source_target_pairs={{0,4},{4,0},{8,12},{12,8},{16,20},{20,16},{24,28},{28,24},{1,5},{5... | collective-permute-start | bytes 4718600 | tf_op jit(solution)/shard_map/ppermute | solution.py:163
  82.2 6.4 %collective-permute-start.17 = (bf16[384,512]{1,0:T(8,128)(2,1)S(1)}, bf16[384,512]{1,0:T(8,128)(2,1)S(1)}, u32[]{:S(2)}, u32[]{:S(2)}) collective-permute-start(bf16[384,512]{1,0:T(8,128)(2,1)S(1)} %pad_maximum_fusion.7), channel_id=1, source_target_pairs={{0,4},{4,0},{8,12},{12,8},{16,20},{20,16},{24,28},{28,24},{1,5},{5... | collective-permute-start | bytes 1179656 | tf_op jit(solution)/shard_map/ppermute | solution.py:163
  82.8 10.9 %collective-permute-start.15 = (bf16[48,2048]{1,0:T(8,128)(2,1)S(1)}, bf16[48,2048]{1,0:T(8,128)(2,1)S(1)}, u32[]{:S(2)}, u32[]{:S(2)}) collective-permute-start(bf16[48,2048]{1,0:T(8,128)(2,1)S(1)} %slice.184), channel_id=1, source_target_pairs={{0,8},{4,12},{8,0},{12,4},{16,24},{20,28},{24,16},{28,20},{1,9},{5... | collective-permute-start | bytes 589832 | tf_op jit(solution)/shard_map/ppermute | solution.py:163
  87.5 7.8 %collective-permute-start.16 = (bf16[48,2048]{1,0:T(8,128)(2,1)S(1)}, bf16[48,2048]{1,0:T(8,128)(2,1)S(1)}, u32[]{:S(2)}, u32[]{:S(2)}) collective-permute-start(bf16[48,2048]{1,0:T(8,128)(2,1)S(1)} %fusion.6), channel_id=1, source_target_pairs={{0,16},{4,20},{8,24},{12,28},{16,0},{20,4},{24,8},{28,12},{1,17},{... | collective-permute-start | bytes 589832 | tf_op jit(solution)/shard_map/ppermute | solution.py:163
  88.4 7.1 %collective-permute-start.28 = (f32[1,2048]{1,0:T(1,128)S(1)}, f32[1,2048]{1,0:T(1,128)S(1)}, u32[]{:S(2)}, u32[]{:S(2)}) collective-permute-start(f32[1,2048]{1,0:T(1,128)S(1)} %add.50), channel_id=1, source_target_pairs={{0,4},{4,0},{8,12},{12,8},{16,20},{20,16},{24,28},{28,24},{1,5},{5... | collective-permute-start | bytes 24584 | tf_op jit(solution)/shard_map/ppermute | solution.py:163
  88.6 22.1 %collective-permute-start.24 = (bf16[48,2048]{1,0:T(8,128)(2,1)S(1)}, bf16[48,2048]{1,0:T(8,128)(2,1)S(1)}, u32[]{:S(2)}, u32[]{:S(2)}) collective-permute-start(bf16[48,2048]{1,0:T(8,128)(2,1)S(1)} %slice.183), channel_id=1, source_target_pairs={{0,8},{4,12},{8,0},{12,4},{16,24},{20,28},{24,16},{28,20},{1,9},{5... | collective-permute-start | bytes 589832 | tf_op jit(solution)/shard_map/ppermute | solution.py:163
  89.5 21.2 %collective-permute-start.25 = (bf16[48,2048]{1,0:T(8,128)(2,1)S(1)}, bf16[48,2048]{1,0:T(8,128)(2,1)S(1)}, u32[]{:S(2)}, u32[]{:S(2)}) collective-permute-start(bf16[48,2048]{1,0:T(8,128)(2,1)S(1)} %fusion.7), channel_id=1, source_target_pairs={{0,16},{4,20},{8,24},{12,28},{16,0},{20,4},{24,8},{28,12},{1,17},{... | collective-permute-start | bytes 589832 | tf_op jit(solution)/shard_map/ppermute | solution.py:163
  95.5 3.7 %collective-permute-start.29 = (f32[1,2048]{1,0:T(1,128)S(1)}, f32[1,2048]{1,0:T(1,128)S(1)}, u32[]{:S(2)}, u32[]{:S(2)}) collective-permute-start(f32[1,2048]{1,0:T(1,128)S(1)} %add.51), channel_id=1, source_target_pairs={{0,8},{4,12},{8,0},{12,4},{16,24},{20,28},{24,16},{28,20},{1,9},{5... | collective-permute-start | bytes 24584 | tf_op jit(solution)/shard_map/ppermute | solution.py:163
  99.2 4.9 %collective-permute-start.30 = (f32[1,2048]{1,0:T(1,128)S(1)}, f32[1,2048]{1,0:T(1,128)S(1)}, u32[]{:S(2)}, u32[]{:S(2)}) collective-permute-start(f32[1,2048]{1,0:T(1,128)S(1)} %add.52), channel_id=1, source_target_pairs={{0,16},{4,20},{8,24},{12,28},{16,0},{20,4},{24,8},{28,12},{1,17},{... | collective-permute-start | bytes 24584 | tf_op jit(solution)/shard_map/ppermute | solution.py:163
  100.1 15.7 %collective-permute-start.19 = (bf16[48,2048]{1,0:T(8,128)(2,1)S(1)}, bf16[48,2048]{1,0:T(8,128)(2,1)S(1)}, u32[]{:S(2)}, u32[]{:S(2)}) collective-permute-start(bf16[48,2048]{1,0:T(8,128)(2,1)S(1)} %pad_maximum_fusion.15), channel_id=1, source_target_pairs={{0,3},{1,0},{2,1},{3,2},{4,7},{5,4},{6,5},{7,6},{8,11},{9,8},{10,9... | collective-permute-start | bytes 589832 | tf_op jit(solution)/shard_map/ppermute | solution.py:166
  104.1 5.5 %collective-permute-start.31 = (f32[1,2048]{1,0:T(1,128)S(1)}, f32[1,2048]{1,0:T(1,128)S(1)}, u32[]{:S(2)}, u32[]{:S(2)}) collective-permute-start(f32[1,2048]{1,0:T(1,128)S(1)} %add.53), channel_id=1, source_target_pairs={{0,1},{1,0},{2,3},{3,2},{4,5},{5,4},{6,7},{7,6},{8,9},{9,8},{10,11... | collective-permute-start | bytes 24584 | tf_op jit(solution)/shard_map/ppermute | solution.py:295
  109.6 5.6 %collective-permute-start.32 = (f32[1,2048]{1,0:T(1,128)S(1)}, f32[1,2048]{1,0:T(1,128)S(1)}, u32[]{:S(2)}, u32[]{:S(2)}) collective-permute-start(f32[1,2048]{1,0:T(1,128)S(1)} %add.54), channel_id=1, source_target_pairs={{0,2},{1,3},{2,0},{3,1},{4,6},{5,7},{6,4},{7,5},{8,10},{9,11},{10,... | collective-permute-start | bytes 24584 | tf_op jit(solution)/shard_map/ppermute | solution.py:295
  110.9 12.3 %collective-permute-start.26 = (bf16[48,2048]{1,0:T(8,128)(2,1)S(1)}, bf16[48,2048]{1,0:T(8,128)(2,1)S(1)}, u32[]{:S(2)}, u32[]{:S(2)}) collective-permute-start(bf16[48,2048]{1,0:T(8,128)(2,1)S(1)} %pad_maximum_fusion.16), channel_id=1, source_target_pairs={{0,2},{1,3},{2,0},{3,1},{4,6},{5,7},{6,4},{7,5},{8,10},{9,11},{10,... | collective-permute-start | bytes 589832 | tf_op jit(solution)/shard_map/ppermute | solution.py:166
  112.9 10.3 %collective-permute-start.27 = (bf16[48,2048]{1,0:T(8,128)(2,1)S(1)}, bf16[48,2048]{1,0:T(8,128)(2,1)S(1)}, u32[]{:S(2)}, u32[]{:S(2)}) collective-permute-start(bf16[48,2048]{1,0:T(8,128)(2,1)S(1)} %pad_maximum_fusion.17), channel_id=1, source_target_pairs={{0,1},{1,2},{2,3},{3,0},{4,5},{5,6},{6,7},{7,4},{8,9},{9,10},{10,1... | collective-permute-start | bytes 589832 | tf_op jit(solution)/shard_map/ppermute | solution.py:166
  (9 other events, 29.5 us)

commit v3 on v2

--- a/solution.py
+++ b/solution.py
@@ -17,6 +17,7 @@
 
 
 ROOM = 20 * 1024 * 1024
+PLACE_ROOM = 60 * 1024 * 1024
 
 
 def mm(a, b, dims=NN):
@@ -33,16 +34,16 @@
     return (values, slopes)
 
 
-def call(name, kernel, out_shape, args, flops=0, moved=0, scratch=()):
+def call(name, kernel, out_shape, args, flops=0, moved=0, scratch=(), place=pltpu.VMEM, room=ROOM):
     vmem = pl.BlockSpec(memory_space=pltpu.VMEM)
     return pl.pallas_call(
         kernel,
         name=name,
         out_shape=out_shape,
-        in_specs=[vmem] * len(args),
+        in_specs=[pl.BlockSpec(memory_space=place)] * len(args),
         out_specs=jax.tree.map(lambda _: vmem, out_shape),
         scratch_shapes=scratch,
-        compiler_params=pltpu.CompilerParams(vmem_limit_bytes=ROOM),
+        compiler_params=pltpu.CompilerParams(vmem_limit_bytes=room),
         cost_estimate=pl.CostEstimate(flops=flops, bytes_accessed=moved, transcendentals=0),
     )(*args)
 
@@ -60,23 +61,31 @@
     return jnp.where((at >= 0) & (at < capacity), at, -2 * capacity)
 
 
-def place_kernel(groups, capacity, tok_ref, id_ref, me_ref, gain_ref, cot_ref, slot_ref, *refs):
-    sends, both = refs[:groups], refs[groups]
+def place_kernel(groups, capacity, tok_in, id_in, gain_in, cot_in, slot_ref, *refs):
+    sends, both, tok_ref, id_ref, gain_ref, sems = refs[:groups], *refs[groups:]
     count = tok_ref.shape[0]
+    sources = (id_in, tok_in, gain_in, cot_in)
+    targets = (id_ref, tok_ref, gain_ref, both.at[pl.ds(count, count)])
+    copies = [pltpu.make_async_copy(a, b, sems.at[i]) for i, (a, b) in enumerate(zip(sources, targets))]
+    for copy in copies:
+        copy.start()
+    copies[0].wait()
     id_row = jnp.broadcast_to(id_ref[...], (count, count))
     id_col = jnp.transpose(id_row)
     at_row = lax.broadcasted_iota(jnp.int32, (count, count), 0)
     at_col = lax.broadcasted_iota(jnp.int32, (count, count), 1)
     earlier = jnp.where((id_row == id_col) & (at_row < at_col), 1, 0)
     ranks = jnp.sum(earlier, axis=0, keepdims=True)
-    ahead = id_ref[...] - me_ref[...]
+    ahead = id_ref[...] - lax.axis_index("exp").astype(jnp.int32)
     ahead = jnp.where(ahead < 0, ahead + groups, ahead)
     slots = jnp.where(ranks < capacity, ahead * capacity + ranks, -1)
     slot_ref[...] = slots
+    copies[1].wait()
+    copies[2].wait()
     wide = tok_ref[...].astype(f32)
     scales = lax.rsqrt(jnp.mean(wide * wide, axis=1, keepdims=True) + 1e-06)
     both[:count] = (wide * scales * gain_ref[...]).astype(bf16)
-    both[count:] = cot_ref[...]
+    copies[3].wait()
     rows = lax.broadcasted_iota(jnp.int32, (2 * capacity, 2 * count), 0)
     for k in range(groups):
         places = block_places(slots, k, capacity)
@@ -171,28 +180,38 @@
     up_a, down_a = up_weight[0], down_weight[0]
     up_b, down_b = swap(up_a, 1), swap(down_a, 1)
 
-    me = lax.axis_index("exp").astype(jnp.int32).reshape(1, 1)
     gain_row = norm_gain.reshape(1, width)
     slot_row, *blocks = call(
         "place",
         functools.partial(place_kernel, groups, capacity),
         [shaped((1, count), jnp.int32)] + [shaped((2 * capacity, width))] * groups,
-        (tokens, expert_ids.reshape(1, count), me, gain_row, cotangent),
-        scratch=[pltpu.VMEM((2 * count, width), bf16)],
-    )
-    arrived = [blocks[0]] + [shift(blocks[k], k) for k in range(1, groups)]
-
-    def start(n, cap_cut):
-        mine = range(n * groups // 2, (n + 1) * groups // 2)
-        return {0: join(*[arrived[k][cap_cut] for k in mine])}
+        (tokens, expert_ids.reshape(1, count), gain_row, cotangent),
+        scratch=[
+            pltpu.VMEM((2 * count, width), bf16),
+            pltpu.VMEM((count, width), bf16),
+            pltpu.VMEM((1, count), jnp.int32),
+            pltpu.VMEM((1, width), f32),
+            pltpu.SemaphoreType.DMA((4,)),
+        ],
+        place=pltpu.HBM,
+        room=PLACE_ROOM,
+    )
+    early = groups // 2
+    arrived = [blocks[0]] + [shift(blocks[k], k) for k in range(1, early)]
+    blocks = after(blocks, arrived[1:])
+    arrived += [shift(blocks[k], k) for k in range(early, groups)]
+
+    def start(n):
+        mine = [arrived[k] for k in range(n * groups // 2, (n + 1) * groups // 2)]
+        return [{0: join(*[block[:capacity] for block in mine])}, {0: join(*[block[capacity:] for block in mine])}]
+
+    def ordered(held):
+        return join(*[held[at] for at in sorted(held)])
 
     def grow(held, bit):
         known = sorted(held)
-        got = swap(join(*[held[at] for at in known]), bit)
+        got = swap(ordered(held), bit)
         return {**held, **{at ^ bit: got[n * piece : (n + 1) * piece] for n, at in enumerate(known)}}
-
-    def ordered(held):
-        return join(*[held[at] for at in sorted(held)])
 
     def halved(x, first):
         cut = x.shape[0] // 2
@@ -205,14 +224,14 @@
     work = 8 * rows * width * 2 * units
     weights = (up_a, up_b, down_a, down_b)
 
-    def gather(n):
-        pair = [start(n, slice(0, capacity)), start(n, slice(capacity, None))]
-        for bit, back_bit in zip(bits, down_bits):
+    def gather(pair, events):
+        for n, (bit, back_bit) in enumerate(zip(bits, down_bits)):
+            pair = after(pair, *events[n]) if n in events else pair
             pair = [grow(pair[0], bit), grow(pair[1], back_bit)]
             yield pair
 
-    def compute(in_rows, cot_rows):
-        acts = call(
+    def hidden(in_rows, cot_rows):
+        return call(
             "hidden",
             hidden_kernel,
             [shaped((rows, units))] * 4,
@@ -220,8 +239,10 @@
             work // 2,
             8 << 20,
         )
+
+    def products(in_rows, acts):
         kept = [shaped((rows // 2, width), f32), shaped((rows // 2, width))] * 2
-        parts = call(
+        return call(
             "rows",
             functools.partial(row_kernel, piece),
             [shaped((1, width), f32)] + kept,
@@ -229,35 +250,50 @@
             work // 2,
             8 << 20,
         )
-        return acts, parts
-
-    def scatter(parts, events):
+
+    def packed(sums):
+        lead = lax.reduce_precision(sums, 8, 7)
+        return jnp.pad(join(lead, sums - lead), ((0, 6), (0, 0))).astype(bf16)
+
+    def unpacked(pair):
+        return pair[0:1].astype(f32) + pair[1:2].astype(f32)
+
+    def scatter(parts, events, sums=None):
         out, back = parts[1:3], parts[3:5]
         for n, (bit, back_bit) in enumerate(zip(down_bits, bits)):
-            got = swap(out[1], bit), swap(back[1], back_bit)
-            got = after(got, *events[n])
-            out, back = out[0] + got[0].astype(f32), back[0] + got[1].astype(f32)
+            sent = back[1] if sums is None else join(back[1], packed(sums))
+            got_out, got_back = after((swap(out[1], bit), swap(sent, back_bit)), *events[n])
+            if sums is not None:
+                sums = sums + unpacked(got_back[-8:])
+                got_back = got_back[:-8]
+            out, back = out[0] + got_out.astype(f32), back[0] + got_back.astype(f32)
             if n < len(bits) - 1:
                 out, back = halved(out, False), halved(back, True)
                 out, back = (out[0], out[1].astype(bf16)), (back[0], back[1].astype(bf16))
-                yield (out, back)
-            else:
-                yield out.astype(bf16), back.astype(bf16)
-
-    def homeward(n, out_rows, back_rows):
+        return out.astype(bf16), back.astype(bf16), sums
+
+    def homeward(n, out_rows, back_rows, sums):
+        other = []
         for i in range(groups // 2):
             k = n * groups // 2 + i
             cut = slice(i * capacity, (i + 1) * capacity)
             block = join(out_rows[cut], back_rows[cut])
-            home[k] = shift(block, groups - k) if k else block
-
-    *_, first = gather(0)
-    steps = list(gather(1))
-    in_1, cot_1 = after((ordered(first[0]), ordered(first[1])), steps[-2][0], steps[-2][1])
-    acts_1, parts_1 = compute(in_1, cot_1)
-    second = after(steps[-1], parts_1[0])
-    in_2, cot_2 = ordered(second[0]), ordered(second[1])
-    acts_2, parts_2 = compute(in_2, cot_2)
+            if k and sums is not None:
+                got = shift(join(block, packed(sums)), groups - k)
+                other.append(unpacked(got[-8:]))
+                home[k] = got[:-8]
+            else:
+                home[k] = shift(block, groups - k) if k else block
+        return other
+
+    steps = list(gather(start(0), {}))
+    in_1, cot_1 = [ordered(held) for held in steps[-1]]
+    acts_1 = hidden(in_1, cot_1)
+    steps = list(gather(start(1), {0: [ordered(held) for held in steps[0]], len(bits) - 1: (acts_1,)}))
+    parts_1 = products(after(in_1, steps[-2]), acts_1)
+    in_2, cot_2 = [ordered(held) for held in after(steps[-1], parts_1)]
+    acts_2 = hidden(in_2, cot_2)
+    parts_2 = products(in_2, acts_2)
     in_all, cot_all = join(in_1, in_2), join(cot_1, cot_2)
     hid_a, hid_b, pre_a, pre_b = [join(a, b) for a, b in zip(acts_1, acts_2)]
     wide_rows = pltpu.VMEM((4 * rows, width), bf16)
@@ -281,19 +317,14 @@
         [wide_rows, unit_rows],
     )
     home = [None] * groups
-    *_, sums_1 = scatter(parts_1, [(parts_2[0],)] + [(grad_down,)] * len(bits))
-    *_, sums_2 = scatter(parts_2, [(grad_up,)] + [()] * len(bits))
-    homeward(0, *sums_1)
-    homeward(1, *sums_2)
-
-    total = parts_1[0] + parts_2[0]
-    total = after(total, grad_up)
-    for bit in [1] + bits:
-        total = total + swap(total, bit)
-    step = 1
-    while step < groups:
-        total = total + lax.ppermute(total, "exp", [(i, i ^ step) for i in range(groups)])
-        step *= 2
+    sums = parts_1[0] + parts_2[0]
+    sums = sums + swap(sums, 1)
+    out_1, back_1, _ = scatter(parts_1, [(parts_2[0],)] + [(grad_down,)] * len(bits))
+    out_2, back_2, sums = scatter(parts_2, [(grad_up,)] + [()] * len(bits), sums)
+    homeward(0, out_1, back_1, None)
+    other = homeward(1, out_2, back_2, sums)
+    other += [unpacked(shift(packed(sums), groups - k)) for k in range(1, groups // 2)]
+    total = sum(other, sums)
     grad_gain = (total / gain_row).reshape(width)
     mixed, grad_tokens = call(
         "tokens",

time: 126 us -> 113 us (0.90)
  the two profiles are of different devices: /device:TPU:0 before, /device:TPU:9 now
where the time goes in v3:
time: 113 us
  waiting for transfers between devices  49 us (43%)
  starting transfers between devices  37.4 us (33%)
  Pallas kernels  20.3 us (18%)
  local copies, waits for them, and re-layouts  2.96 us (3%)
  other arithmetic  1.98 us (2%)
  between operations  1.26 us (1%)
    ppermute x23, starting transfers between devices, swap(): return lax.ppermute(x, 'rep', [(i, i ^ bit) for i in range(copies)])  28.9 us
    ppermute x23, waiting for transfers between devices, swap(): return lax.ppermute(x, 'rep', [(i, i ^ bit) for i in range(copies)])  24.8 us
    ppermute x7, waiting for transfers between devices, shift(): lax.ppermute(x, 'exp', [(i, (i + k) % groups) for i in range(groups)])  24.3 us
    pallas_call x8, Pallas kernels, call(): pl.pallas_call(kernel, name=name, out_shape=out_shape, in_specs=[pl.Block...  20.3 us
    ppermute x7, starting transfers between devices, shift(): lax.ppermute(x, 'exp', [(i, (i + k) % groups) for i in range(groups)])  8.44 us
    unnamed x23, local copies, waits for them, and re-layouts  2.66 us
  transfers between devices with their start and end apart: 30, of which 14 were waited for; matrix products, arithmetic and copies ran while one was open for 3% of the time, Pallas kernels for 14%

profile of v3, /device:TPU:9, one launch (start us, length us, event | category | flops | bytes accessed | tf_op | source)
XLA Modules:
  0.0 112.9 jit_solution(12808864621848038314)
XLA Ops:
  0.6 2.8 %place.1 = (s32[1,128]{1,0:T(1,128)}, bf16[48,2048]{1,0:T(8,128)(2,1)}, bf16[48,2048]{1,0:T(8,128)(2,1)}, bf16[48,2048]{1,0:T(8,128)(2,1)}, bf16[48,2048]{1,0:T(8,128)(2,1)}) custom-call(bf16[128,2048]{1,0:T(8,128)(2,1)} %tok_ref.1, s32[1,128]{1,0:T(1,128)} %bitcast.45, f32[1,2048]{1,0:T(1,128)} %bitcast.35, bf16[128,2048]{1,0:T(8,128)(2,1)} %cot_in.1), custom_call_target="tpu_custom_call" | custom-call | tf_op jit(solution)/shard_map/place/pallas_call | solution.py:39
  3.5 1.3 %collective-permute-start = (bf16[48,2048]{1,0:T(8,128)(2,1)}, bf16[48,2048]{1,0:T(8,128)(2,1)S(1)}, u32[]{:S(2)}, u32[]{:S(2)}) collective-permute-start(bf16[48,2048]{1,0:T(8,128)(2,1)} %get-tuple-element.57), channel_id=1, source_target_pairs={{0,1},{1,2},{2,3},{3,0},{4,5},{5,6},{6,7},{7,4},{8,9},{9,10},{10,1... | collective-permute-start | bytes 589832 | tf_op jit(solution)/shard_map/ppermute | solution.py:175
  6.8 2.7 %collective-permute-done = bf16[48,2048]{1,0:T(8,128)(2,1)S(1)} collective-permute-done((bf16[48,2048]{1,0:T(8,128)(2,1)}, bf16[48,2048]{1,0:T(8,128)(2,1)S(1)}, u32[]{:S(2)}, u32[]{:S(2)}) %collective-permute-start) | collective-permute-done | bytes 196640 | tf_op jit(solution)/shard_map/ppermute | solution.py:175
  9.5 2.3 %collective-permute-start.3 = (bf16[48,2048]{1,0:T(8,128)(2,1)}, bf16[48,2048]{1,0:T(8,128)(2,1)S(1)}, u32[]{:S(2)}, u32[]{:S(2)}) collective-permute-start(bf16[48,2048]{1,0:T(8,128)(2,1)} %get-tuple-element.60), channel_id=1, source_target_pairs={{0,2},{1,3},{2,0},{3,1},{4,6},{5,7},{6,4},{7,5},{8,10},{9,11},{10,... | collective-permute-start | bytes 589832 | tf_op jit(solution)/shard_map/ppermute | solution.py:175
  12.1 1.3 %collective-permute-start.1 = (bf16[48,2048]{1,0:T(8,128)(2,1)S(1)}, bf16[48,2048]{1,0:T(8,128)(2,1)S(1)}, u32[]{:S(2)}, u32[]{:S(2)}) collective-permute-start(bf16[48,2048]{1,0:T(8,128)(2,1)S(1)} %pad_maximum_fusion.14), channel_id=1, source_target_pairs={{0,8},{4,12},{8,0},{12,4},{16,24},{20,28},{24,16},{28,20},{1,9},{5... | collective-permute-start | bytes 589832 | tf_op jit(solution)/shard_map/ppermute | solution.py:172
  13.3 3.6 %collective-permute-done.1 = bf16[48,2048]{1,0:T(8,128)(2,1)S(1)} collective-permute-done((bf16[48,2048]{1,0:T(8,128)(2,1)S(1)}, bf16[48,2048]{1,0:T(8,128)(2,1)S(1)}, u32[]{:S(2)}, u32[]{:S(2)}) %collective-permute-start.1) | collective-permute-done | bytes 196640 | tf_op jit(solution)/shard_map/ppermute | solution.py:172
  18.2 3.2 %collective-permute-done.5 = bf16[48,2048]{1,0:T(8,128)(2,1)S(1)} collective-permute-done((bf16[48,2048]{1,0:T(8,128)(2,1)S(1)}, bf16[48,2048]{1,0:T(8,128)(2,1)S(1)}, u32[]{:S(2)}, u32[]{:S(2)}) %collective-permute-start.5) | collective-permute-done | bytes 196640 | tf_op jit(solution)/shard_map/ppermute | solution.py:172
  22.7 2.3 %collective-permute-done.3 = bf16[48,2048]{1,0:T(8,128)(2,1)S(1)} collective-permute-done((bf16[48,2048]{1,0:T(8,128)(2,1)}, bf16[48,2048]{1,0:T(8,128)(2,1)S(1)}, u32[]{:S(2)}, u32[]{:S(2)}) %collective-permute-start.3) | collective-permute-done | bytes 196640 | tf_op jit(solution)/shard_map/ppermute | solution.py:175
  27.0 5.6 %collective-permute-done.8 = bf16[96,2048]{1,0:T(8,128)(2,1)S(1)} collective-permute-done((bf16[96,2048]{1,0:T(8,128)(2,1)S(1)}, bf16[96,2048]{1,0:T(8,128)(2,1)S(1)}, u32[]{:S(2)}, u32[]{:S(2)}) %collective-permute-start.8) | collective-permute-done | bytes 393248 | tf_op jit(solution)/shard_map/ppermute | solution.py:172
  32.5 2.3 %collective-permute-start.7 = (bf16[48,2048]{1,0:T(8,128)(2,1)S(1)}, bf16[48,2048]{1,0:T(8,128)(2,1)S(1)}, u32[]{:S(2)}, u32[]{:S(2)}) collective-permute-start(bf16[48,2048]{1,0:T(8,128)(2,1)S(1)} %get-tuple-element.82), channel_id=1, source_target_pairs={{0,16},{4,20},{8,24},{12,28},{16,0},{20,4},{24,8},{28,12},{1,17},{... | collective-permute-start | bytes 589832 | tf_op jit(solution)/shard_map/ppermute | solution.py:172
  35.0 1.4 %copy-done = bf16[1,2048,512]{2,1,0:T(8,128)(2,1)S(1)} copy-done((bf16[1,2048,512]{2,1,0:T(8,128)(2,1)S(1)}, bf16[1,2048,512]{2,1,0:T(8,128)(2,1)}, u32[]{:S(2)}) %copy-start) | copy-done | bytes 2097176
  36.4 2.3 %hidden.2 = (bf16[192,512]{1,0:T(8,128)(2,1)S(1)}, bf16[192,512]{1,0:T(8,128)(2,1)S(1)}, bf16[192,512]{1,0:T(8,128)(2,1)S(1)}, bf16[192,512]{1,0:T(8,128)(2,1)S(1)}) custom-call(bf16[192,2048]{1,0:T(8,128)(2,1)S(1)} %pad_maximum_fusion.in_ref, bf16[192,2048]{1,0:T(8,128)(2,1)S(1)} %get-tuple-element.112.cot_ref, bf16[2048,512]{1,0:T(8,128)(2,1)S(1)} %bitcast.26, ...), custom_call_target="tpu_custom_call" | custom-call | flops 1610612736 | bytes 8388608 | tf_op jit(solution)/shard_map/hidden/pallas_call | solution.py:39
  38.7 1.3 %collective-permute-start.14 = (bf16[96,2048]{1,0:T(8,128)(2,1)S(1)}, bf16[96,2048]{1,0:T(8,128)(2,1)S(1)}, u32[]{:S(2)}, u32[]{:S(2)}) collective-permute-start(bf16[96,2048]{1,0:T(8,128)(2,1)S(1)} %pad_maximum_fusion.6), channel_id=1, source_target_pairs={{0,8},{4,12},{8,0},{12,4},{16,24},{20,28},{24,16},{28,20},{1,9},{5... | collective-permute-start | bytes 1179656 | tf_op jit(solution)/shard_map/ppermute | solution.py:172
  41.1 2.2 %rows.2 = (f32[1,2048]{1,0:T(1,128)S(1)}, f32[96,2048]{1,0:T(8,128)S(1)}, bf16[96,2048]{1,0:T(8,128)(2,1)S(1)}, f32[96,2048]{1,0:T(8,128)S(1)}, bf16[96,2048]{1,0:T(8,128)(2,1)S(1)}) custom-call(bf16[192,2048]{1,0:T(8,128)(2,1)S(1)} %pad_maximum_fusion.in_ref, bf16[192,512]{1,0:T(8,128)(2,1)S(1)} %get-tuple-element.65.hid_a, ...), custom_call_target="tpu_custom_call" | custom-call | flops 1610612736 | bytes 8388608 | tf_op jit(solution)/shard_map/rows/pallas_call | solution.py:39
  44.1 1.3 %collective-permute-done.14 = bf16[96,2048]{1,0:T(8,128)(2,1)S(1)} collective-permute-done((bf16[96,2048]{1,0:T(8,128)(2,1)S(1)}, bf16[96,2048]{1,0:T(8,128)(2,1)S(1)}, u32[]{:S(2)}, u32[]{:S(2)}) %collective-permute-start.14) | collective-permute-done | bytes 393248 | tf_op jit(solution)/shard_map/ppermute | solution.py:172
  45.4 2.5 %collective-permute-done.13 = bf16[96,2048]{1,0:T(8,128)(2,1)S(1)} collective-permute-done((bf16[96,2048]{1,0:T(8,128)(2,1)S(1)}, bf16[96,2048]{1,0:T(8,128)(2,1)S(1)}, u32[]{:S(2)}, u32[]{:S(2)}) %collective-permute-start.13) | collective-permute-done | bytes 393248 | tf_op jit(solution)/shard_map/ppermute | solution.py:172
  48.2 2.3 %hidden.3 = (bf16[192,512]{1,0:T(8,128)(2,1)S(1)}, bf16[192,512]{1,0:T(8,128)(2,1)S(1)}, bf16[192,512]{1,0:T(8,128)(2,1)S(1)}, bf16[192,512]{1,0:T(8,128)(2,1)S(1)}) custom-call(bf16[192,2048]{1,0:T(8,128)(2,1)S(1)} %get-tuple-element.124.in_ref, bf16[192,2048]{1,0:T(8,128)(2,1)S(1)} %pad_maximum_fusion.1.cot_ref, bf16[2048,512]{1,0:T(8,128)(2,1)S(1)} %bitcast.28, ...), custom_call_target="tpu_custom_call" | custom-call | flops 1610612736 | bytes 8388608 | tf_op jit(solution)/shard_map/hidden/pallas_call | solution.py:39
  50.5 2.2 %rows.3 = (f32[1,2048]{1,0:T(1,128)S(1)}, f32[96,2048]{1,0:T(8,128)S(1)}, bf16[96,2048]{1,0:T(8,128)(2,1)S(1)}, f32[96,2048]{1,0:T(8,128)S(1)}, bf16[96,2048]{1,0:T(8,128)(2,1)S(1)}) custom-call(bf16[192,2048]{1,0:T(8,128)(2,1)S(1)} %get-tuple-element.124.in_ref, bf16[192,512]{1,0:T(8,128)(2,1)S(1)} %get-tuple-element.86.hid_a, ...), custom_call_target="tpu_custom_call" | custom-call | flops 1610612736 | bytes 8388608 | tf_op jit(solution)/shard_map/rows/pallas_call | solution.py:39
  53.6 8.6 %collective-permute-start.21 = (f32[1,2048]{1,0:T(1,128)S(1)}, f32[1,2048]{1,0:T(1,128)S(1)}, u32[]{:S(2)}, u32[]{:S(2)}) collective-permute-start(f32[1,2048]{1,0:T(1,128)S(1)} %add.70), channel_id=1, source_target_pairs={{0,4},{4,0},{8,12},{12,8},{16,20},{20,16},{24,28},{28,24},{1,5},{5... | collective-permute-start | bytes 24584 | tf_op jit(solution)/shard_map/ppermute | solution.py:172
  62.3 1.3 %collective-permute-start.15 = (bf16[48,2048]{1,0:T(8,128)(2,1)S(1)}, bf16[48,2048]{1,0:T(8,128)(2,1)S(1)}, u32[]{:S(2)}, u32[]{:S(2)}) collective-permute-start(bf16[48,2048]{1,0:T(8,128)(2,1)S(1)} %slice.303), channel_id=1, source_target_pairs={{0,8},{4,12},{8,0},{12,4},{16,24},{20,28},{24,16},{28,20},{1,9},{5... | collective-permute-start | bytes 589832 | tf_op jit(solution)/shard_map/ppermute | solution.py:172
  66.9 1.7 %collective-permute-done.23.left_b = bf16[384,2048]{1,0:T(8,128)(2,1)S(1)} collective-permute-done((bf16[384,2048]{1,0:T(8,128)(2,1)S(1)}, bf16[384,2048]{1,0:T(8,128)(2,1)S(1)}, u32[]{:S(2)}, u32[]{:S(2)}) %collective-permute-start.23) | collective-permute-done | bytes 1572896 | tf_op jit(solution)/shard_map/ppermute | solution.py:172
  69.0 3.2 %grad_up.1 = bf16[2048,512]{1,0:T(8,128)(2,1)} custom-call(bf16[384,2048]{1,0:T(8,128)(2,1)S(1)} %get-tuple-element.123.left_a, bf16[384,2048]{1,0:T(8,128)(2,1)S(1)} %collective-permute-done.23.left_b, bf16[384,512]{1,0:T(8,128)(2,1)S(1)} %pad_maximum_fusion.9.right_a, bf16[384,512]{1,0:T(8,128)(2,1)S(1)} %collective-permute-done.24.right_b), custom_call_target="tpu_custom_call" | custom-call | flops 805306368 | bytes 8388608 | tf_op jit(solution)/shard_map/grad_up/pallas_call | solution.py:39
  72.2 1.8 %collective-permute-done.20 = bf16[96,2048]{1,0:T(8,128)(2,1)S(1)} collective-permute-done((bf16[96,2048]{1,0:T(8,128)(2,1)S(1)}, bf16[96,2048]{1,0:T(8,128)(2,1)S(1)}, u32[]{:S(2)}, u32[]{:S(2)}) %collective-permute-start.20) | collective-permute-done | bytes 393248 | tf_op jit(solution)/shard_map/ppermute | solution.py:172
  74.0 1.8 %collective-permute-start.18 = (bf16[384,2048]{1,0:T(8,128)(2,1)S(1)}, bf16[384,2048]{1,0:T(8,128)(2,1)S(1)}, u32[]{:S(2)}, u32[]{:S(2)}) collective-permute-start(bf16[384,2048]{1,0:T(8,128)(2,1)S(1)} %constant_dynamic-update-slice_fusion.7.right_a), channel_id=1, source_target_pairs={{0,4},{4,0},{8,12},{12,8},{16,20},{20,16},{24,28},{28,24},{1,5},{5... | collective-permute-start | bytes 4718600 | tf_op jit(solution)/shard_map/ppermute | solution.py:172
  75.8 2.2 %collective-permute-done.22 = bf16[104,2048]{1,0:T(8,128)(2,1)S(1)} collective-permute-done((bf16[104,2048]{1,0:T(8,128)(2,1)S(1)}, bf16[104,2048]{1,0:T(8,128)(2,1)S(1)}, u32[]{:S(2)}, u32[]{:S(2)}) %collective-permute-start.22) | collective-permute-done | bytes 426016 | tf_op jit(solution)/shard_map/ppermute | solution.py:172
  78.1 1.3 %collective-permute-start.25 = (bf16[48,2048]{1,0:T(8,128)(2,1)S(1)}, bf16[48,2048]{1,0:T(8,128)(2,1)S(1)}, u32[]{:S(2)}, u32[]{:S(2)}) collective-permute-start(bf16[48,2048]{1,0:T(8,128)(2,1)S(1)} %slice.302), channel_id=1, source_target_pairs={{0,8},{4,12},{8,0},{12,4},{16,24},{20,28},{24,16},{28,20},{1,9},{5... | collective-permute-start | bytes 589832 | tf_op jit(solution)/shard_map/ppermute | solution.py:172
  80.8 3.2 %grad_down.1 = bf16[512,2048]{1,0:T(8,128)(2,1)} custom-call(bf16[384,512]{1,0:T(8,128)(2,1)S(1)} %pad_maximum_fusion.7.left_a, bf16[384,512]{1,0:T(8,128)(2,1)S(1)} %collective-permute-done.17.left_b, bf16[384,2048]{1,0:T(8,128)(2,1)S(1)} %constant_dynamic-update-slice_fusion.7.right_a, bf16[384,2048]{1,0:T(8,128)(2,1)S(1)} %collective-permute-done.18.right_b), custom_call_target="tpu_custom_call" | custom-call | flops 805306368 | bytes 8388608 | tf_op jit(solution)/shard_map/grad_down/pallas_call | solution.py:39
  84.1 1.8 %collective-permute-done.26 = bf16[56,2048]{1,0:T(8,128)(2,1)S(1)} collective-permute-done((bf16[56,2048]{1,0:T(8,128)(2,1)S(1)}, bf16[56,2048]{1,0:T(8,128)(2,1)S(1)}, u32[]{:S(2)}, u32[]{:S(2)}) %collective-permute-start.26) | collective-permute-done | bytes 229408 | tf_op jit(solution)/shard_map/ppermute | solution.py:172
  86.2 3.1 %collective-permute-start.27 = (bf16[56,2048]{1,0:T(8,128)(2,1)S(1)}, bf16[56,2048]{1,0:T(8,128)(2,1)S(1)}, u32[]{:S(2)}, u32[]{:S(2)}) collective-permute-start(bf16[56,2048]{1,0:T(8,128)(2,1)S(1)} %get-tuple-element.152), channel_id=1, source_target_pairs={{0,2},{1,3},{2,0},{3,1},{4,6},{5,7},{6,4},{7,5},{8,10},{9,11},{10,... | collective-permute-start | bytes 688136 | tf_op jit(solution)/shard_map/ppermute | solution.py:175
  89.3 1.4 %collective-permute-start.19 = (bf16[48,2048]{1,0:T(8,128)(2,1)S(1)}, bf16[48,2048]{1,0:T(8,128)(2,1)S(1)}, u32[]{:S(2)}, u32[]{:S(2)}) collective-permute-start(bf16[48,2048]{1,0:T(8,128)(2,1)S(1)} %pad_maximum_fusion.19), channel_id=1, source_target_pairs={{0,3},{1,0},{2,1},{3,2},{4,7},{5,4},{6,5},{7,6},{8,11},{9,8},{10,9... | collective-permute-start | bytes 589832 | tf_op jit(solution)/shard_map/ppermute | solution.py:175
  90.8 19.2 %collective-permute-done.29 = bf16[8,2048]{1,0:T(8,128)(2,1)S(1)} collective-permute-done((bf16[8,2048]{1,0:T(8,128)(2,1)S(1)}, bf16[8,2048]{1,0:T(8,128)(2,1)S(1)}, u32[]{:S(2)}, u32[]{:S(2)}) %collective-permute-start.29) | collective-permute-done | bytes 32800 | tf_op jit(solution)/shard_map/ppermute | solution.py:175
  110.7 2.2 %tokens.1 = (bf16[128,2048]{1,0:T(8,128)(2,1)}, bf16[128,2048]{1,0:T(8,128)(2,1)}) custom-call(s32[1,128]{1,0:T(1,128)S(1)} %copy-done.4, bf16[128,2048]{1,0:T(8,128)(2,1)S(1)} %copy-done.2, f32[1,2048]{1,0:T(1,128)S(1)} %bitcast.37, bf16[48,2048]{1,0:T(8,128)(2,1)S(1)} %pad_maximum_fusion.18.refs_0_, bf16[48,2048]{1,0:T(8,128)(2,1)S(1)} %collective-permute-done.19.refs_1_, ...), custom_call_target="tpu_custom_call" | custom-call | tf_op jit(solution)/shard_map/tokens/pallas_call | solution.py:39
  (112 shorter events, 16.2 us)
Async XLA Ops:
  3.5 6.0 %collective-permute-start = (bf16[48,2048]{1,0:T(8,128)(2,1)}, bf16[48,2048]{1,0:T(8,128)(2,1)S(1)}, u32[]{:S(2)}, u32[]{:S(2)}) collective-permute-start(bf16[48,2048]{1,0:T(8,128)(2,1)} %get-tuple-element.57), channel_id=1, source_target_pairs={{0,1},{1,2},{2,3},{3,0},{4,5},{5,6},{6,7},{7,4},{8,9},{9,10},{10,1... | collective-permute-start | bytes 589832 | tf_op jit(solution)/shard_map/ppermute | solution.py:175
  4.8 30.2 %collective-permute-start.9 = (bf16[2048,512]{1,0:T(8,128)(2,1)}, bf16[2048,512]{1,0:T(8,128)(2,1)S(1)}, u32[]{:S(2)}, u32[]{:S(2)}) collective-permute-start(bf16[2048,512]{1,0:T(8,128)(2,1)} %bitcast.25), channel_id=1, source_target_pairs={{0,4},{4,0},{8,12},{12,8},{16,20},{20,16},{24,28},{28,24},{1,5},{5... | collective-permute-start | bytes 6291464 | tf_op jit(solution)/shard_map/ppermute | solution.py:172
  5.8 29.2 %collective-permute-start.10 = (bf16[512,2048]{1,0:T(8,128)(2,1)}, bf16[512,2048]{1,0:T(8,128)(2,1)S(1)}, u32[]{:S(2)}, u32[]{:S(2)}) collective-permute-start(bf16[512,2048]{1,0:T(8,128)(2,1)} %bitcast.30), channel_id=1, source_target_pairs={{0,4},{4,0},{8,12},{12,8},{16,20},{20,16},{24,28},{28,24},{1,5},{5... | collective-permute-start | bytes 6291464 | tf_op jit(solution)/shard_map/ppermute | solution.py:172
  9.5 15.6 %collective-permute-start.3 = (bf16[48,2048]{1,0:T(8,128)(2,1)}, bf16[48,2048]{1,0:T(8,128)(2,1)S(1)}, u32[]{:S(2)}, u32[]{:S(2)}) collective-permute-start(bf16[48,2048]{1,0:T(8,128)(2,1)} %get-tuple-element.60), channel_id=1, source_target_pairs={{0,2},{1,3},{2,0},{3,1},{4,6},{5,7},{6,4},{7,5},{8,10},{9,11},{10,... | collective-permute-start | bytes 589832 | tf_op jit(solution)/shard_map/ppermute | solution.py:175
  11.8 14.5 %collective-permute-start.4 = (bf16[48,2048]{1,0:T(8,128)(2,1)}, bf16[48,2048]{1,0:T(8,128)(2,1)S(1)}, u32[]{:S(2)}, u32[]{:S(2)}) collective-permute-start(bf16[48,2048]{1,0:T(8,128)(2,1)} %get-tuple-element.61), channel_id=1, source_target_pairs={{0,3},{1,0},{2,1},{3,2},{4,7},{5,4},{6,5},{7,6},{8,11},{9,8},{10,9... | collective-permute-start | bytes 589832 | tf_op jit(solution)/shard_map/ppermute | solution.py:175
  12.1 4.9 %collective-permute-start.1 = (bf16[48,2048]{1,0:T(8,128)(2,1)S(1)}, bf16[48,2048]{1,0:T(8,128)(2,1)S(1)}, u32[]{:S(2)}, u32[]{:S(2)}) collective-permute-start(bf16[48,2048]{1,0:T(8,128)(2,1)S(1)} %pad_maximum_fusion.14), channel_id=1, source_target_pairs={{0,8},{4,12},{8,0},{12,4},{16,24},{20,28},{24,16},{28,20},{1,9},{5... | collective-permute-start | bytes 589832 | tf_op jit(solution)/shard_map/ppermute | solution.py:172
  16.9 4.5 %collective-permute-start.5 = (bf16[48,2048]{1,0:T(8,128)(2,1)S(1)}, bf16[48,2048]{1,0:T(8,128)(2,1)S(1)}, u32[]{:S(2)}, u32[]{:S(2)}) collective-permute-start(bf16[48,2048]{1,0:T(8,128)(2,1)S(1)} %pad_maximum_fusion.17), channel_id=1, source_target_pairs={{0,16},{4,20},{8,24},{12,28},{16,0},{20,4},{24,8},{28,12},{1,17},{... | collective-permute-start | bytes 589832 | tf_op jit(solution)/shard_map/ppermute | solution.py:172
  21.5 13.5 %collective-permute-start.2 = (bf16[96,2048]{1,0:T(8,128)(2,1)S(1)}, bf16[96,2048]{1,0:T(8,128)(2,1)S(1)}, u32[]{:S(2)}, u32[]{:S(2)}) collective-permute-start(bf16[96,2048]{1,0:T(8,128)(2,1)S(1)} %pad_maximum_fusion.3), channel_id=1, source_target_pairs={{0,16},{4,20},{8,24},{12,28},{16,0},{20,4},{24,8},{28,12},{1,17},{... | collective-permute-start | bytes 1179656 | tf_op jit(solution)/shard_map/ppermute | solution.py:172
  25.1 7.5 %collective-permute-start.8 = (bf16[96,2048]{1,0:T(8,128)(2,1)S(1)}, bf16[96,2048]{1,0:T(8,128)(2,1)S(1)}, u32[]{:S(2)}, u32[]{:S(2)}) collective-permute-start(bf16[96,2048]{1,0:T(8,128)(2,1)S(1)} %pad_maximum_fusion.4), channel_id=1, source_target_pairs={{0,8},{4,12},{8,0},{12,4},{16,24},{20,28},{24,16},{28,20},{1,9},{5... | collective-permute-start | bytes 1179656 | tf_op jit(solution)/shard_map/ppermute | solution.py:172
  26.4 12.3 %collective-permute-start.6 = (bf16[48,2048]{1,0:T(8,128)(2,1)S(1)}, bf16[48,2048]{1,0:T(8,128)(2,1)S(1)}, u32[]{:S(2)}, u32[]{:S(2)}) collective-permute-start(bf16[48,2048]{1,0:T(8,128)(2,1)S(1)} %get-tuple-element.78), channel_id=1, source_target_pairs={{0,8},{4,12},{8,0},{12,4},{16,24},{20,28},{24,16},{28,20},{1,9},{5... | collective-permute-start | bytes 589832 | tf_op jit(solution)/shard_map/ppermute | solution.py:172
  32.5 6.1 %collective-permute-start.7 = (bf16[48,2048]{1,0:T(8,128)(2,1)S(1)}, bf16[48,2048]{1,0:T(8,128)(2,1)S(1)}, u32[]{:S(2)}, u32[]{:S(2)}) collective-permute-start(bf16[48,2048]{1,0:T(8,128)(2,1)S(1)} %get-tuple-element.82), channel_id=1, source_target_pairs={{0,16},{4,20},{8,24},{12,28},{16,0},{20,4},{24,8},{28,12},{1,17},{... | collective-permute-start | bytes 589832 | tf_op jit(solution)/shard_map/ppermute | solution.py:172
  38.7 6.7 %collective-permute-start.14 = (bf16[96,2048]{1,0:T(8,128)(2,1)S(1)}, bf16[96,2048]{1,0:T(8,128)(2,1)S(1)}, u32[]{:S(2)}, u32[]{:S(2)}) collective-permute-start(bf16[96,2048]{1,0:T(8,128)(2,1)S(1)} %pad_maximum_fusion.6), channel_id=1, source_target_pairs={{0,8},{4,12},{8,0},{12,4},{16,24},{20,28},{24,16},{28,20},{1,9},{5... | collective-permute-start | bytes 1179656 | tf_op jit(solution)/shard_map/ppermute | solution.py:172
  40.1 7.8 %collective-permute-start.13 = (bf16[96,2048]{1,0:T(8,128)(2,1)S(1)}, bf16[96,2048]{1,0:T(8,128)(2,1)S(1)}, u32[]{:S(2)}, u32[]{:S(2)}) collective-permute-start(bf16[96,2048]{1,0:T(8,128)(2,1)S(1)} %pad_maximum_fusion.5), channel_id=1, source_target_pairs={{0,16},{4,20},{8,24},{12,28},{16,0},{20,4},{24,8},{28,12},{1,17},{... | collective-permute-start | bytes 1179656 | tf_op jit(solution)/shard_map/ppermute | solution.py:172
  43.3 10.1 %collective-permute-start.11 = (bf16[96,2048]{1,0:T(8,128)(2,1)S(1)}, bf16[96,2048]{1,0:T(8,128)(2,1)S(1)}, u32[]{:S(2)}, u32[]{:S(2)}) collective-permute-start(bf16[96,2048]{1,0:T(8,128)(2,1)S(1)} %get-tuple-element.70), channel_id=1, source_target_pairs={{0,16},{4,20},{8,24},{12,28},{16,0},{20,4},{24,8},{28,12},{1,17},{... | collective-permute-start | bytes 1179656 | tf_op jit(solution)/shard_map/ppermute | solution.py:172
  43.9 9.5 %collective-permute-start.12 = (bf16[96,2048]{1,0:T(8,128)(2,1)S(1)}, bf16[96,2048]{1,0:T(8,128)(2,1)S(1)}, u32[]{:S(2)}, u32[]{:S(2)}) collective-permute-start(bf16[96,2048]{1,0:T(8,128)(2,1)S(1)} %get-tuple-element.71), channel_id=1, source_target_pairs={{0,8},{4,12},{8,0},{12,4},{16,24},{20,28},{24,16},{28,20},{1,9},{5... | collective-permute-start | bytes 1179656 | tf_op jit(solution)/shard_map/ppermute | solution.py:172
  53.6 11.5 %collective-permute-start.21 = (f32[1,2048]{1,0:T(1,128)S(1)}, f32[1,2048]{1,0:T(1,128)S(1)}, u32[]{:S(2)}, u32[]{:S(2)}) collective-permute-start(f32[1,2048]{1,0:T(1,128)S(1)} %add.70), channel_id=1, source_target_pairs={{0,4},{4,0},{8,12},{12,8},{16,20},{20,16},{24,28},{28,24},{1,5},{5... | collective-permute-start | bytes 24584 | tf_op jit(solution)/shard_map/ppermute | solution.py:172
  62.3 21.7 %collective-permute-start.15 = (bf16[48,2048]{1,0:T(8,128)(2,1)S(1)}, bf16[48,2048]{1,0:T(8,128)(2,1)S(1)}, u32[]{:S(2)}, u32[]{:S(2)}) collective-permute-start(bf16[48,2048]{1,0:T(8,128)(2,1)S(1)} %slice.303), channel_id=1, source_target_pairs={{0,8},{4,12},{8,0},{12,4},{16,24},{20,28},{24,16},{28,20},{1,9},{5... | collective-permute-start | bytes 589832 | tf_op jit(solution)/shard_map/ppermute | solution.py:172
  63.5 10.4 %collective-permute-start.20 = (bf16[96,2048]{1,0:T(8,128)(2,1)S(1)}, bf16[96,2048]{1,0:T(8,128)(2,1)S(1)}, u32[]{:S(2)}, u32[]{:S(2)}) collective-permute-start(bf16[96,2048]{1,0:T(8,128)(2,1)S(1)} %get-tuple-element.96), channel_id=1, source_target_pairs={{0,16},{4,20},{8,24},{12,28},{16,0},{20,4},{24,8},{28,12},{1,17},{... | collective-permute-start | bytes 1179656 | tf_op jit(solution)/shard_map/ppermute | solution.py:172
  64.5 1.9 %collective-permute-start.24 = (bf16[384,512]{1,0:T(8,128)(2,1)S(1)}, bf16[384,512]{1,0:T(8,128)(2,1)S(1)}, u32[]{:S(2)}, u32[]{:S(2)}) collective-permute-start(bf16[384,512]{1,0:T(8,128)(2,1)S(1)} %pad_maximum_fusion.10), channel_id=1, source_target_pairs={{0,4},{4,0},{8,12},{12,8},{16,20},{20,16},{24,28},{28,24},{1,5},{5... | collective-permute-start | bytes 1179656 | tf_op jit(solution)/shard_map/ppermute | solution.py:172
  65.1 3.6 %collective-permute-start.23 = (bf16[384,2048]{1,0:T(8,128)(2,1)S(1)}, bf16[384,2048]{1,0:T(8,128)(2,1)S(1)}, u32[]{:S(2)}, u32[]{:S(2)}) collective-permute-start(bf16[384,2048]{1,0:T(8,128)(2,1)S(1)} %get-tuple-element.123.left_a), channel_id=1, source_target_pairs={{0,4},{4,0},{8,12},{12,8},{16,20},{20,16},{24,28},{28,24},{1,5},{5... | collective-permute-start | bytes 4718600 | tf_op jit(solution)/shard_map/ppermute | solution.py:172
  65.2 12.8 %collective-permute-start.22 = (bf16[104,2048]{1,0:T(8,128)(2,1)S(1)}, bf16[104,2048]{1,0:T(8,128)(2,1)S(1)}, u32[]{:S(2)}, u32[]{:S(2)}) collective-permute-start(bf16[104,2048]{1,0:T(8,128)(2,1)S(1)} %pad_maximum_fusion.2), channel_id=1, source_target_pairs={{0,8},{4,12},{8,0},{12,4},{16,24},{20,28},{24,16},{28,20},{1,9},{5... | collective-permute-start | bytes 1277960 | tf_op jit(solution)/shard_map/ppermute | solution.py:172
  66.4 17.5 %collective-permute-start.16 = (bf16[48,2048]{1,0:T(8,128)(2,1)S(1)}, bf16[48,2048]{1,0:T(8,128)(2,1)S(1)}, u32[]{:S(2)}, u32[]{:S(2)}) collective-permute-start(bf16[48,2048]{1,0:T(8,128)(2,1)S(1)} %fusion.6), channel_id=1, source_target_pairs={{0,16},{4,20},{8,24},{12,28},{16,0},{20,4},{24,8},{28,12},{1,17},{... | collective-permute-start | bytes 589832 | tf_op jit(solution)/shard_map/ppermute | solution.py:172
  68.7 11.1 %collective-permute-start.17 = (bf16[384,512]{1,0:T(8,128)(2,1)S(1)}, bf16[384,512]{1,0:T(8,128)(2,1)S(1)}, u32[]{:S(2)}, u32[]{:S(2)}) collective-permute-start(bf16[384,512]{1,0:T(8,128)(2,1)S(1)} %pad_maximum_fusion.8), channel_id=1, source_target_pairs={{0,4},{4,0},{8,12},{12,8},{16,20},{20,16},{24,28},{28,24},{1,5},{5... | collective-permute-start | bytes 1179656 | tf_op jit(solution)/shard_map/ppermute | solution.py:172
  74.0 6.8 %collective-permute-start.18 = (bf16[384,2048]{1,0:T(8,128)(2,1)S(1)}, bf16[384,2048]{1,0:T(8,128)(2,1)S(1)}, u32[]{:S(2)}, u32[]{:S(2)}) collective-permute-start(bf16[384,2048]{1,0:T(8,128)(2,1)S(1)} %constant_dynamic-update-slice_fusion.7.right_a), channel_id=1, source_target_pairs={{0,4},{4,0},{8,12},{12,8},{16,20},{20,16},{24,28},{28,24},{1,5},{5... | collective-permute-start | bytes 4718600 | tf_op jit(solution)/shard_map/ppermute | solution.py:172
  78.1 6.0 %collective-permute-start.25 = (bf16[48,2048]{1,0:T(8,128)(2,1)S(1)}, bf16[48,2048]{1,0:T(8,128)(2,1)S(1)}, u32[]{:S(2)}, u32[]{:S(2)}) collective-permute-start(bf16[48,2048]{1,0:T(8,128)(2,1)S(1)} %slice.302), channel_id=1, source_target_pairs={{0,8},{4,12},{8,0},{12,4},{16,24},{20,28},{24,16},{28,20},{1,9},{5... | collective-permute-start | bytes 589832 | tf_op jit(solution)/shard_map/ppermute | solution.py:172
  79.8 6.1 %collective-permute-start.26 = (bf16[56,2048]{1,0:T(8,128)(2,1)S(1)}, bf16[56,2048]{1,0:T(8,128)(2,1)S(1)}, u32[]{:S(2)}, u32[]{:S(2)}) collective-permute-start(bf16[56,2048]{1,0:T(8,128)(2,1)S(1)} %pad_maximum_fusion.13), channel_id=1, source_target_pairs={{0,16},{4,20},{8,24},{12,28},{16,0},{20,4},{24,8},{28,12},{1,17},{... | collective-permute-start | bytes 688136 | tf_op jit(solution)/shard_map/ppermute | solution.py:172
  86.0 24.7 %copy-start.2 = (bf16[128,2048]{1,0:T(8,128)(2,1)S(1)}, bf16[128,2048]{1,0:T(8,128)(2,1)}, u32[]{:S(2)}) copy-start(bf16[128,2048]{1,0:T(8,128)(2,1)} %tok_ref.1) | copy-start | bytes 1572868
  86.0 24.7 %copy-start.4 = (s32[1,128]{1,0:T(1,128)S(1)}, s32[1,128]{1,0:T(1,128)}, u32[]{:S(2)}) copy-start(s32[1,128]{1,0:T(1,128)} %get-tuple-element.55.slot_ref) | copy-start | bytes 1540
  86.1 23.9 %collective-permute-start.28 = (bf16[56,2048]{1,0:T(8,128)(2,1)S(1)}, bf16[56,2048]{1,0:T(8,128)(2,1)S(1)}, u32[]{:S(2)}, u32[]{:S(2)}) collective-permute-start(bf16[56,2048]{1,0:T(8,128)(2,1)S(1)} %get-tuple-element.151), channel_id=1, source_target_pairs={{0,1},{1,2},{2,3},{3,0},{4,5},{5,6},{6,7},{7,4},{8,9},{9,10},{10,1... | collective-permute-start | bytes 688136 | tf_op jit(solution)/shard_map/ppermute | solution.py:175
  86.2 23.8 %collective-permute-start.27 = (bf16[56,2048]{1,0:T(8,128)(2,1)S(1)}, bf16[56,2048]{1,0:T(8,128)(2,1)S(1)}, u32[]{:S(2)}, u32[]{:S(2)}) collective-permute-start(bf16[56,2048]{1,0:T(8,128)(2,1)S(1)} %get-tuple-element.152), channel_id=1, source_target_pairs={{0,2},{1,3},{2,0},{3,1},{4,6},{5,7},{6,4},{7,5},{8,10},{9,11},{10,... | collective-permute-start | bytes 688136 | tf_op jit(solution)/shard_map/ppermute | solution.py:175
  89.3 21.4 %collective-permute-start.19 = (bf16[48,2048]{1,0:T(8,128)(2,1)S(1)}, bf16[48,2048]{1,0:T(8,128)(2,1)S(1)}, u32[]{:S(2)}, u32[]{:S(2)}) collective-permute-start(bf16[48,2048]{1,0:T(8,128)(2,1)S(1)} %pad_maximum_fusion.19), channel_id=1, source_target_pairs={{0,3},{1,0},{2,1},{3,2},{4,7},{5,4},{6,5},{7,6},{8,11},{9,8},{10,9... | collective-permute-start | bytes 589832 | tf_op jit(solution)/shard_map/ppermute | solution.py:175
  90.7 19.3 %collective-permute-start.29 = (bf16[8,2048]{1,0:T(8,128)(2,1)S(1)}, bf16[8,2048]{1,0:T(8,128)(2,1)S(1)}, u32[]{:S(2)}, u32[]{:S(2)}) collective-permute-start(bf16[8,2048]{1,0:T(8,128)(2,1)S(1)} %fusion.16), channel_id=1, source_target_pairs={{0,3},{1,0},{2,1},{3,2},{4,7},{5,4},{6,5},{7,6},{8,11},{9,8},{10,9... | collective-permute-start | bytes 98312 | tf_op jit(solution)/shard_map/ppermute | solution.py:175
  (3 other events, 34.4 us)

commit v4 on v3

--- a/solution.py
+++ b/solution.py
@@ -199,7 +199,7 @@
     early = groups // 2
     arrived = [blocks[0]] + [shift(blocks[k], k) for k in range(1, early)]
     blocks = after(blocks, arrived[1:])
-    arrived += [shift(blocks[k], k) for k in range(early, groups)]
+    arrived.append(shift(blocks[early], early))
 
     def start(n):
         mine = [arrived[k] for k in range(n * groups // 2, (n + 1) * groups // 2)]
@@ -289,6 +289,8 @@
     steps = list(gather(start(0), {}))
     in_1, cot_1 = [ordered(held) for held in steps[-1]]
     acts_1 = hidden(in_1, cot_1)
+    events = [ordered(held) for held in steps[0]]
+    arrived += [shift(after(blocks[k], events), k) for k in range(early + 1, groups)]
     steps = list(gather(start(1), {0: [ordered(held) for held in steps[0]], len(bits) - 1: (acts_1,)}))
     parts_1 = products(after(in_1, steps[-2]), acts_1)
     in_2, cot_2 = [ordered(held) for held in after(steps[-1], parts_1)]

time: 113 us -> 107 us (0.947)
  waiting for transfers between devices: 49 us -> 44.3 us
  starting transfers between devices: 37.4 us -> 35.6 us
    ppermute x23, waiting for transfers between devices: 24.8 us -> 17.2 us  [swap(): return lax.ppermute(x, 'rep', [(i, i ^ bit) for i in range(copies)])]
    ppermute x23, starting transfers between devices: 28.9 us -> 23.3 us  [swap(): return lax.ppermute(x, 'rep', [(i, i ^ bit) for i in range(copies)])]
    ppermute x7, starting transfers between devices: 8.44 us -> 12.3 us  [shift(): lax.ppermute(x, 'exp', [(i, (i + k) % groups) for i in range(groups)])]
    ppermute x7, waiting for transfers between devices: 24.3 us -> 27.1 us  [shift(): lax.ppermute(x, 'exp', [(i, (i + k) % groups) for i in range(groups)])]
    unnamed x23 -> x25, local copies, waits for them, and re-layouts: 2.66 us -> 2.66 us
  transfers between devices with their start and end apart: 30 -> 30, of which waited for: 14 -> 14; matrix products, arithmetic and copies ran while one was open for 3% -> 3% of each run, Pallas kernels for 14% -> 15%
where the time goes in v4:
time: 107 us; the launch traced here: 106 us
  waiting for transfers between devices  44.3 us (41%)
  starting transfers between devices  35.6 us (33%)
  Pallas kernels  20.5 us (19%)
  local copies, waits for them, and re-layouts  2.97 us (3%)
  other arithmetic  1.79 us (2%)
  between operations  1.25 us (1%)
    ppermute x7, waiting for transfers between devices, shift(): lax.ppermute(x, 'exp', [(i, (i + k) % groups) for i in range(groups)])  27.1 us
    ppermute x23, starting transfers between devices, swap(): return lax.ppermute(x, 'rep', [(i, i ^ bit) for i in range(copies)])  23.3 us
    pallas_call x8, Pallas kernels, call(): pl.pallas_call(kernel, name=name, out_shape=out_shape, in_specs=[pl.Block...  20.5 us
    ppermute x23, waiting for transfers between devices, swap(): return lax.ppermute(x, 'rep', [(i, i ^ bit) for i in range(copies)])  17.2 us
    ppermute x7, starting transfers between devices, shift(): lax.ppermute(x, 'exp', [(i, (i + k) % groups) for i in range(groups)])  12.3 us
    unnamed x25, local copies, waits for them, and re-layouts  2.66 us
  transfers between devices with their start and end apart: 30, of which 14 were waited for; matrix products, arithmetic and copies ran while one was open for 3% of the time, Pallas kernels for 15%

profile of v4, /device:TPU:9, one launch (start us, length us, event | category | flops | bytes accessed | tf_op | source)
XLA Modules:
  0.0 106.4 jit_solution(17054551103714039384)
XLA Ops:
  0.6 2.8 %place.1 = (s32[1,128]{1,0:T(1,128)}, bf16[48,2048]{1,0:T(8,128)(2,1)}, bf16[48,2048]{1,0:T(8,128)(2,1)}, bf16[48,2048]{1,0:T(8,128)(2,1)}, bf16[48,2048]{1,0:T(8,128)(2,1)}) custom-call(bf16[128,2048]{1,0:T(8,128)(2,1)} %tok_ref.1, s32[1,128]{1,0:T(1,128)} %bitcast.45, f32[1,2048]{1,0:T(1,128)} %bitcast.35, bf16[128,2048]{1,0:T(8,128)(2,1)} %cot_in.1), custom_call_target="tpu_custom_call" | custom-call | tf_op jit(solution)/shard_map/place/pallas_call | solution.py:39
  3.5 1.3 %collective-permute-start = (bf16[48,2048]{1,0:T(8,128)(2,1)}, bf16[48,2048]{1,0:T(8,128)(2,1)S(1)}, u32[]{:S(2)}, u32[]{:S(2)}) collective-permute-start(bf16[48,2048]{1,0:T(8,128)(2,1)} %get-tuple-element.58), channel_id=1, source_target_pairs={{0,1},{1,2},{2,3},{3,0},{4,5},{5,6},{6,7},{7,4},{8,9},{9,10},{10,1... | collective-permute-start | bytes 589832 | tf_op jit(solution)/shard_map/ppermute | solution.py:175
  6.8 2.7 %collective-permute-done = bf16[48,2048]{1,0:T(8,128)(2,1)S(1)} collective-permute-done((bf16[48,2048]{1,0:T(8,128)(2,1)}, bf16[48,2048]{1,0:T(8,128)(2,1)S(1)}, u32[]{:S(2)}, u32[]{:S(2)}) %collective-permute-start) | collective-permute-done | bytes 196640 | tf_op jit(solution)/shard_map/ppermute | solution.py:175
  9.5 2.3 %collective-permute-start.3 = (bf16[48,2048]{1,0:T(8,128)(2,1)}, bf16[48,2048]{1,0:T(8,128)(2,1)S(1)}, u32[]{:S(2)}, u32[]{:S(2)}) collective-permute-start(bf16[48,2048]{1,0:T(8,128)(2,1)} %get-tuple-element.61), channel_id=1, source_target_pairs={{0,2},{1,3},{2,0},{3,1},{4,6},{5,7},{6,4},{7,5},{8,10},{9,11},{10,... | collective-permute-start | bytes 589832 | tf_op jit(solution)/shard_map/ppermute | solution.py:175
  11.9 1.3 %collective-permute-start.1 = (bf16[48,2048]{1,0:T(8,128)(2,1)S(1)}, bf16[48,2048]{1,0:T(8,128)(2,1)S(1)}, u32[]{:S(2)}, u32[]{:S(2)}) collective-permute-start(bf16[48,2048]{1,0:T(8,128)(2,1)S(1)} %pad_maximum_fusion.14), channel_id=1, source_target_pairs={{0,8},{4,12},{8,0},{12,4},{16,24},{20,28},{24,16},{28,20},{1,9},{5... | collective-permute-start | bytes 589832 | tf_op jit(solution)/shard_map/ppermute | solution.py:172
  13.2 1.3 %collective-permute-start.4 = (bf16[48,2048]{1,0:T(8,128)(2,1)S(1)}, bf16[48,2048]{1,0:T(8,128)(2,1)S(1)}, u32[]{:S(2)}, u32[]{:S(2)}) collective-permute-start(bf16[48,2048]{1,0:T(8,128)(2,1)S(1)} %pad_maximum_fusion.15), channel_id=1, source_target_pairs={{0,16},{4,20},{8,24},{12,28},{16,0},{20,4},{24,8},{28,12},{1,17},{... | collective-permute-start | bytes 589832 | tf_op jit(solution)/shard_map/ppermute | solution.py:172
  14.5 2.3 %collective-permute-done.1 = bf16[48,2048]{1,0:T(8,128)(2,1)S(1)} collective-permute-done((bf16[48,2048]{1,0:T(8,128)(2,1)S(1)}, bf16[48,2048]{1,0:T(8,128)(2,1)S(1)}, u32[]{:S(2)}, u32[]{:S(2)}) %collective-permute-start.1) | collective-permute-done | bytes 196640 | tf_op jit(solution)/shard_map/ppermute | solution.py:172
  16.8 1.3 %collective-permute-start.2 = (bf16[96,2048]{1,0:T(8,128)(2,1)S(1)}, bf16[96,2048]{1,0:T(8,128)(2,1)S(1)}, u32[]{:S(2)}, u32[]{:S(2)}) collective-permute-start(bf16[96,2048]{1,0:T(8,128)(2,1)S(1)} %pad_maximum_fusion.3), channel_id=1, source_target_pairs={{0,16},{4,20},{8,24},{12,28},{16,0},{20,4},{24,8},{28,12},{1,17},{... | collective-permute-start | bytes 1179656 | tf_op jit(solution)/shard_map/ppermute | solution.py:172
  18.1 1.3 %collective-permute-start.8 = (bf16[96,2048]{1,0:T(8,128)(2,1)S(1)}, bf16[96,2048]{1,0:T(8,128)(2,1)S(1)}, u32[]{:S(2)}, u32[]{:S(2)}) collective-permute-start(bf16[96,2048]{1,0:T(8,128)(2,1)S(1)} %pad_maximum_fusion.4), channel_id=1, source_target_pairs={{0,8},{4,12},{8,0},{12,4},{16,24},{20,28},{24,16},{28,20},{1,9},{5... | collective-permute-start | bytes 1179656 | tf_op jit(solution)/shard_map/ppermute | solution.py:172
  19.4 1.4 %collective-permute-done.3 = bf16[48,2048]{1,0:T(8,128)(2,1)S(1)} collective-permute-done((bf16[48,2048]{1,0:T(8,128)(2,1)}, bf16[48,2048]{1,0:T(8,128)(2,1)S(1)}, u32[]{:S(2)}, u32[]{:S(2)}) %collective-permute-start.3) | collective-permute-done | bytes 196640 | tf_op jit(solution)/shard_map/ppermute | solution.py:175
  20.9 2.0 %collective-permute-start.5 = (bf16[48,2048]{1,0:T(8,128)(2,1)S(1)}, bf16[48,2048]{1,0:T(8,128)(2,1)S(1)}, u32[]{:S(2)}, u32[]{:S(2)}) collective-permute-start(bf16[48,2048]{1,0:T(8,128)(2,1)S(1)} %copy-done.5), channel_id=1, source_target_pairs={{0,3},{1,0},{2,1},{3,2},{4,7},{5,4},{6,5},{7,6},{8,11},{9,8},{10,9... | collective-permute-start | bytes 589832 | tf_op jit(solution)/shard_map/ppermute | solution.py:175
  22.9 3.7 %collective-permute-done.5 = bf16[48,2048]{1,0:T(8,128)(2,1)S(1)} collective-permute-done((bf16[48,2048]{1,0:T(8,128)(2,1)S(1)}, bf16[48,2048]{1,0:T(8,128)(2,1)S(1)}, u32[]{:S(2)}, u32[]{:S(2)}) %collective-permute-start.5) | collective-permute-done | bytes 196640 | tf_op jit(solution)/shard_map/ppermute | solution.py:175
  26.7 1.3 %collective-permute-start.6 = (bf16[48,2048]{1,0:T(8,128)(2,1)S(1)}, bf16[48,2048]{1,0:T(8,128)(2,1)S(1)}, u32[]{:S(2)}, u32[]{:S(2)}) collective-permute-start(bf16[48,2048]{1,0:T(8,128)(2,1)S(1)} %get-tuple-element.80), channel_id=1, source_target_pairs={{0,8},{4,12},{8,0},{12,4},{16,24},{20,28},{24,16},{28,20},{1,9},{5... | collective-permute-start | bytes 589832 | tf_op jit(solution)/shard_map/ppermute | solution.py:172
  29.4 1.4 %copy-done = bf16[1,2048,512]{2,1,0:T(8,128)(2,1)S(1)} copy-done((bf16[1,2048,512]{2,1,0:T(8,128)(2,1)S(1)}, bf16[1,2048,512]{2,1,0:T(8,128)(2,1)}, u32[]{:S(2)}) %copy-start) | copy-done | bytes 2097176
  30.8 2.3 %hidden.2 = (bf16[192,512]{1,0:T(8,128)(2,1)S(1)}, bf16[192,512]{1,0:T(8,128)(2,1)S(1)}, bf16[192,512]{1,0:T(8,128)(2,1)S(1)}, bf16[192,512]{1,0:T(8,128)(2,1)S(1)}) custom-call(bf16[192,2048]{1,0:T(8,128)(2,1)S(1)} %pad_maximum_fusion.in_ref, bf16[192,2048]{1,0:T(8,128)(2,1)S(1)} %get-tuple-element.114.cot_ref, bf16[2048,512]{1,0:T(8,128)(2,1)S(1)} %bitcast.26, ...), custom_call_target="tpu_custom_call" | custom-call | flops 1610612736 | bytes 8388608 | tf_op jit(solution)/shard_map/hidden/pallas_call | solution.py:39
  34.5 2.2 %rows.2 = (f32[1,2048]{1,0:T(1,128)S(1)}, f32[96,2048]{1,0:T(8,128)S(1)}, bf16[96,2048]{1,0:T(8,128)(2,1)S(1)}, f32[96,2048]{1,0:T(8,128)S(1)}, bf16[96,2048]{1,0:T(8,128)(2,1)S(1)}) custom-call(bf16[192,2048]{1,0:T(8,128)(2,1)S(1)} %pad_maximum_fusion.in_ref, bf16[192,512]{1,0:T(8,128)(2,1)S(1)} %get-tuple-element.67.hid_a, ...), custom_call_target="tpu_custom_call" | custom-call | flops 1610612736 | bytes 8388608 | tf_op jit(solution)/shard_map/rows/pallas_call | solution.py:39
  38.5 2.7 %collective-permute-done.14 = bf16[96,2048]{1,0:T(8,128)(2,1)S(1)} collective-permute-done((bf16[96,2048]{1,0:T(8,128)(2,1)S(1)}, bf16[96,2048]{1,0:T(8,128)(2,1)S(1)}, u32[]{:S(2)}, u32[]{:S(2)}) %collective-permute-start.14) | collective-permute-done | bytes 393248 | tf_op jit(solution)/shard_map/ppermute | solution.py:172
  41.5 2.3 %hidden.3 = (bf16[192,512]{1,0:T(8,128)(2,1)S(1)}, bf16[192,512]{1,0:T(8,128)(2,1)S(1)}, bf16[192,512]{1,0:T(8,128)(2,1)S(1)}, bf16[192,512]{1,0:T(8,128)(2,1)S(1)}) custom-call(bf16[192,2048]{1,0:T(8,128)(2,1)S(1)} %get-tuple-element.126.in_ref, bf16[192,2048]{1,0:T(8,128)(2,1)S(1)} %pad_maximum_fusion.1.cot_ref, bf16[2048,512]{1,0:T(8,128)(2,1)S(1)} %bitcast.28, ...), custom_call_target="tpu_custom_call" | custom-call | flops 1610612736 | bytes 8388608 | tf_op jit(solution)/shard_map/hidden/pallas_call | solution.py:39
  43.8 2.2 %rows.3 = (f32[1,2048]{1,0:T(1,128)S(1)}, f32[96,2048]{1,0:T(8,128)S(1)}, bf16[96,2048]{1,0:T(8,128)(2,1)S(1)}, f32[96,2048]{1,0:T(8,128)S(1)}, bf16[96,2048]{1,0:T(8,128)(2,1)S(1)}) custom-call(bf16[192,2048]{1,0:T(8,128)(2,1)S(1)} %get-tuple-element.126.in_ref, bf16[192,512]{1,0:T(8,128)(2,1)S(1)} %get-tuple-element.88.hid_a, ...), custom_call_target="tpu_custom_call" | custom-call | flops 1610612736 | bytes 8388608 | tf_op jit(solution)/shard_map/rows/pallas_call | solution.py:39
  46.1 2.9 %collective-permute-done.11 = bf16[96,2048]{1,0:T(8,128)(2,1)S(1)} collective-permute-done((bf16[96,2048]{1,0:T(8,128)(2,1)S(1)}, bf16[96,2048]{1,0:T(8,128)(2,1)S(1)}, u32[]{:S(2)}, u32[]{:S(2)}) %collective-permute-start.11) | collective-permute-done | bytes 393248 | tf_op jit(solution)/shard_map/ppermute | solution.py:172
  49.8 4.6 %collective-permute-start.21 = (f32[1,2048]{1,0:T(1,128)S(1)}, f32[1,2048]{1,0:T(1,128)S(1)}, u32[]{:S(2)}, u32[]{:S(2)}) collective-permute-start(f32[1,2048]{1,0:T(1,128)S(1)} %add.70), channel_id=1, source_target_pairs={{0,4},{4,0},{8,12},{12,8},{16,20},{20,16},{24,28},{28,24},{1,5},{5... | collective-permute-start | bytes 24584 | tf_op jit(solution)/shard_map/ppermute | solution.py:172
  58.5 1.9 %collective-permute-done.23.left_b = bf16[384,2048]{1,0:T(8,128)(2,1)S(1)} collective-permute-done((bf16[384,2048]{1,0:T(8,128)(2,1)S(1)}, bf16[384,2048]{1,0:T(8,128)(2,1)S(1)}, u32[]{:S(2)}, u32[]{:S(2)}) %collective-permute-start.23) | collective-permute-done | bytes 1572896 | tf_op jit(solution)/shard_map/ppermute | solution.py:172
  60.8 3.2 %grad_up.1 = bf16[2048,512]{1,0:T(8,128)(2,1)} custom-call(bf16[384,2048]{1,0:T(8,128)(2,1)S(1)} %get-tuple-element.125.left_a, bf16[384,2048]{1,0:T(8,128)(2,1)S(1)} %collective-permute-done.23.left_b, bf16[384,512]{1,0:T(8,128)(2,1)S(1)} %pad_maximum_fusion.9.right_a, bf16[384,512]{1,0:T(8,128)(2,1)S(1)} %collective-permute-done.24.right_b), custom_call_target="tpu_custom_call" | custom-call | flops 805306368 | bytes 8388608 | tf_op jit(solution)/shard_map/grad_up/pallas_call | solution.py:39
  64.0 1.6 %collective-permute-done.20 = bf16[96,2048]{1,0:T(8,128)(2,1)S(1)} collective-permute-done((bf16[96,2048]{1,0:T(8,128)(2,1)S(1)}, bf16[96,2048]{1,0:T(8,128)(2,1)S(1)}, u32[]{:S(2)}, u32[]{:S(2)}) %collective-permute-start.20) | collective-permute-done | bytes 393248 | tf_op jit(solution)/shard_map/ppermute | solution.py:172
  65.5 1.8 %collective-permute-start.18 = (bf16[384,2048]{1,0:T(8,128)(2,1)S(1)}, bf16[384,2048]{1,0:T(8,128)(2,1)S(1)}, u32[]{:S(2)}, u32[]{:S(2)}) collective-permute-start(bf16[384,2048]{1,0:T(8,128)(2,1)S(1)} %constant_dynamic-update-slice_fusion.7.right_a), channel_id=1, source_target_pairs={{0,4},{4,0},{8,12},{12,8},{16,20},{20,16},{24,28},{28,24},{1,5},{5... | collective-permute-start | bytes 4718600 | tf_op jit(solution)/shard_map/ppermute | solution.py:172
  67.4 2.8 %collective-permute-done.22 = bf16[104,2048]{1,0:T(8,128)(2,1)S(1)} collective-permute-done((bf16[104,2048]{1,0:T(8,128)(2,1)S(1)}, bf16[104,2048]{1,0:T(8,128)(2,1)S(1)}, u32[]{:S(2)}, u32[]{:S(2)}) %collective-permute-start.22) | collective-permute-done | bytes 426016 | tf_op jit(solution)/shard_map/ppermute | solution.py:172
  72.4 3.3 %grad_down.1 = bf16[512,2048]{1,0:T(8,128)(2,1)} custom-call(bf16[384,512]{1,0:T(8,128)(2,1)S(1)} %pad_maximum_fusion.7.left_a, bf16[384,512]{1,0:T(8,128)(2,1)S(1)} %collective-permute-done.17.left_b, bf16[384,2048]{1,0:T(8,128)(2,1)S(1)} %constant_dynamic-update-slice_fusion.7.right_a, bf16[384,2048]{1,0:T(8,128)(2,1)S(1)} %collective-permute-done.18.right_b), custom_call_target="tpu_custom_call" | custom-call | flops 805306368 | bytes 8388608 | tf_op jit(solution)/shard_map/grad_down/pallas_call | solution.py:39
  77.5 1.8 %collective-permute-start.28 = (bf16[56,2048]{1,0:T(8,128)(2,1)S(1)}, bf16[56,2048]{1,0:T(8,128)(2,1)S(1)}, u32[]{:S(2)}, u32[]{:S(2)}) collective-permute-start(bf16[56,2048]{1,0:T(8,128)(2,1)S(1)} %get-tuple-element.153), channel_id=1, source_target_pairs={{0,1},{1,2},{2,3},{3,0},{4,5},{5,6},{6,7},{7,4},{8,9},{9,10},{10,1... | collective-permute-start | bytes 688136 | tf_op jit(solution)/shard_map/ppermute | solution.py:175
  79.3 3.4 %collective-permute-start.27 = (bf16[56,2048]{1,0:T(8,128)(2,1)S(1)}, bf16[56,2048]{1,0:T(8,128)(2,1)S(1)}, u32[]{:S(2)}, u32[]{:S(2)}) collective-permute-start(bf16[56,2048]{1,0:T(8,128)(2,1)S(1)} %get-tuple-element.154), channel_id=1, source_target_pairs={{0,2},{1,3},{2,0},{3,1},{4,6},{5,7},{6,4},{7,5},{8,10},{9,11},{10,... | collective-permute-start | bytes 688136 | tf_op jit(solution)/shard_map/ppermute | solution.py:175
  82.7 1.4 %collective-permute-start.19 = (bf16[48,2048]{1,0:T(8,128)(2,1)S(1)}, bf16[48,2048]{1,0:T(8,128)(2,1)S(1)}, u32[]{:S(2)}, u32[]{:S(2)}) collective-permute-start(bf16[48,2048]{1,0:T(8,128)(2,1)S(1)} %pad_maximum_fusion.19), channel_id=1, source_target_pairs={{0,3},{1,0},{2,1},{3,2},{4,7},{5,4},{6,5},{7,6},{8,11},{9,8},{10,9... | collective-permute-start | bytes 589832 | tf_op jit(solution)/shard_map/ppermute | solution.py:175
  84.2 19.2 %collective-permute-done.29 = bf16[8,2048]{1,0:T(8,128)(2,1)S(1)} collective-permute-done((bf16[8,2048]{1,0:T(8,128)(2,1)S(1)}, bf16[8,2048]{1,0:T(8,128)(2,1)S(1)}, u32[]{:S(2)}, u32[]{:S(2)}) %collective-permute-start.29) | collective-permute-done | bytes 32800 | tf_op jit(solution)/shard_map/ppermute | solution.py:175
  104.1 2.2 %tokens.1 = (bf16[128,2048]{1,0:T(8,128)(2,1)}, bf16[128,2048]{1,0:T(8,128)(2,1)}) custom-call(s32[1,128]{1,0:T(1,128)S(1)} %copy-done.4, bf16[128,2048]{1,0:T(8,128)(2,1)S(1)} %copy-done.2, f32[1,2048]{1,0:T(1,128)S(1)} %bitcast.37, bf16[48,2048]{1,0:T(8,128)(2,1)S(1)} %pad_maximum_fusion.18.refs_0_, bf16[48,2048]{1,0:T(8,128)(2,1)S(1)} %collective-permute-done.19.refs_1_, ...), custom_call_target="tpu_custom_call" | custom-call | tf_op jit(solution)/shard_map/tokens/pallas_call | solution.py:39
  (114 shorter events, 17.0 us)
Async XLA Ops:
  3.5 6.0 %collective-permute-start = (bf16[48,2048]{1,0:T(8,128)(2,1)}, bf16[48,2048]{1,0:T(8,128)(2,1)S(1)}, u32[]{:S(2)}, u32[]{:S(2)}) collective-permute-start(bf16[48,2048]{1,0:T(8,128)(2,1)} %get-tuple-element.58), channel_id=1, source_target_pairs={{0,1},{1,2},{2,3},{3,0},{4,5},{5,6},{6,7},{7,4},{8,9},{9,10},{10,1... | collective-permute-start | bytes 589832 | tf_op jit(solution)/shard_map/ppermute | solution.py:175
  4.8 24.6 %collective-permute-start.9 = (bf16[2048,512]{1,0:T(8,128)(2,1)}, bf16[2048,512]{1,0:T(8,128)(2,1)S(1)}, u32[]{:S(2)}, u32[]{:S(2)}) collective-permute-start(bf16[2048,512]{1,0:T(8,128)(2,1)} %bitcast.25), channel_id=1, source_target_pairs={{0,4},{4,0},{8,12},{12,8},{16,20},{20,16},{24,28},{28,24},{1,5},{5... | collective-permute-start | bytes 6291464 | tf_op jit(solution)/shard_map/ppermute | solution.py:172
  5.8 23.6 %collective-permute-start.10 = (bf16[512,2048]{1,0:T(8,128)(2,1)}, bf16[512,2048]{1,0:T(8,128)(2,1)S(1)}, u32[]{:S(2)}, u32[]{:S(2)}) collective-permute-start(bf16[512,2048]{1,0:T(8,128)(2,1)} %bitcast.30), channel_id=1, source_target_pairs={{0,4},{4,0},{8,12},{12,8},{16,20},{20,16},{24,28},{28,24},{1,5},{5... | collective-permute-start | bytes 6291464 | tf_op jit(solution)/shard_map/ppermute | solution.py:172
  9.5 11.3 %collective-permute-start.3 = (bf16[48,2048]{1,0:T(8,128)(2,1)}, bf16[48,2048]{1,0:T(8,128)(2,1)S(1)}, u32[]{:S(2)}, u32[]{:S(2)}) collective-permute-start(bf16[48,2048]{1,0:T(8,128)(2,1)} %get-tuple-element.61), channel_id=1, source_target_pairs={{0,2},{1,3},{2,0},{3,1},{4,6},{5,7},{6,4},{7,5},{8,10},{9,11},{10,... | collective-permute-start | bytes 589832 | tf_op jit(solution)/shard_map/ppermute | solution.py:175
  11.9 4.9 %collective-permute-start.1 = (bf16[48,2048]{1,0:T(8,128)(2,1)S(1)}, bf16[48,2048]{1,0:T(8,128)(2,1)S(1)}, u32[]{:S(2)}, u32[]{:S(2)}) collective-permute-start(bf16[48,2048]{1,0:T(8,128)(2,1)S(1)} %pad_maximum_fusion.14), channel_id=1, source_target_pairs={{0,8},{4,12},{8,0},{12,4},{16,24},{20,28},{24,16},{28,20},{1,9},{5... | collective-permute-start | bytes 589832 | tf_op jit(solution)/shard_map/ppermute | solution.py:172
  13.2 4.9 %collective-permute-start.4 = (bf16[48,2048]{1,0:T(8,128)(2,1)S(1)}, bf16[48,2048]{1,0:T(8,128)(2,1)S(1)}, u32[]{:S(2)}, u32[]{:S(2)}) collective-permute-start(bf16[48,2048]{1,0:T(8,128)(2,1)S(1)} %pad_maximum_fusion.15), channel_id=1, source_target_pairs={{0,16},{4,20},{8,24},{12,28},{16,0},{20,4},{24,8},{28,12},{1,17},{... | collective-permute-start | bytes 589832 | tf_op jit(solution)/shard_map/ppermute | solution.py:172
  16.8 12.5 %collective-permute-start.2 = (bf16[96,2048]{1,0:T(8,128)(2,1)S(1)}, bf16[96,2048]{1,0:T(8,128)(2,1)S(1)}, u32[]{:S(2)}, u32[]{:S(2)}) collective-permute-start(bf16[96,2048]{1,0:T(8,128)(2,1)S(1)} %pad_maximum_fusion.3), channel_id=1, source_target_pairs={{0,16},{4,20},{8,24},{12,28},{16,0},{20,4},{24,8},{28,12},{1,17},{... | collective-permute-start | bytes 1179656 | tf_op jit(solution)/shard_map/ppermute | solution.py:172
  18.1 9.8 %collective-permute-start.8 = (bf16[96,2048]{1,0:T(8,128)(2,1)S(1)}, bf16[96,2048]{1,0:T(8,128)(2,1)S(1)}, u32[]{:S(2)}, u32[]{:S(2)}) collective-permute-start(bf16[96,2048]{1,0:T(8,128)(2,1)S(1)} %pad_maximum_fusion.4), channel_id=1, source_target_pairs={{0,8},{4,12},{8,0},{12,4},{16,24},{20,28},{24,16},{28,20},{1,9},{5... | collective-permute-start | bytes 1179656 | tf_op jit(solution)/shard_map/ppermute | solution.py:172
  20.9 5.8 %collective-permute-start.5 = (bf16[48,2048]{1,0:T(8,128)(2,1)S(1)}, bf16[48,2048]{1,0:T(8,128)(2,1)S(1)}, u32[]{:S(2)}, u32[]{:S(2)}) collective-permute-start(bf16[48,2048]{1,0:T(8,128)(2,1)S(1)} %copy-done.5), channel_id=1, source_target_pairs={{0,3},{1,0},{2,1},{3,2},{4,7},{5,4},{6,5},{7,6},{8,11},{9,8},{10,9... | collective-permute-start | bytes 589832 | tf_op jit(solution)/shard_map/ppermute | solution.py:175
  26.7 6.4 %collective-permute-start.6 = (bf16[48,2048]{1,0:T(8,128)(2,1)S(1)}, bf16[48,2048]{1,0:T(8,128)(2,1)S(1)}, u32[]{:S(2)}, u32[]{:S(2)}) collective-permute-start(bf16[48,2048]{1,0:T(8,128)(2,1)S(1)} %get-tuple-element.80), channel_id=1, source_target_pairs={{0,8},{4,12},{8,0},{12,4},{16,24},{20,28},{24,16},{28,20},{1,9},{5... | collective-permute-start | bytes 589832 | tf_op jit(solution)/shard_map/ppermute | solution.py:172
  28.0 5.1 %collective-permute-start.7 = (bf16[48,2048]{1,0:T(8,128)(2,1)S(1)}, bf16[48,2048]{1,0:T(8,128)(2,1)S(1)}, u32[]{:S(2)}, u32[]{:S(2)}) collective-permute-start(bf16[48,2048]{1,0:T(8,128)(2,1)S(1)} %get-tuple-element.84), channel_id=1, source_target_pairs={{0,16},{4,20},{8,24},{12,28},{16,0},{20,4},{24,8},{28,12},{1,17},{... | collective-permute-start | bytes 589832 | tf_op jit(solution)/shard_map/ppermute | solution.py:172
  33.1 8.1 %collective-permute-start.14 = (bf16[96,2048]{1,0:T(8,128)(2,1)S(1)}, bf16[96,2048]{1,0:T(8,128)(2,1)S(1)}, u32[]{:S(2)}, u32[]{:S(2)}) collective-permute-start(bf16[96,2048]{1,0:T(8,128)(2,1)S(1)} %pad_maximum_fusion.6), channel_id=1, source_target_pairs={{0,8},{4,12},{8,0},{12,4},{16,24},{20,28},{24,16},{28,20},{1,9},{5... | collective-permute-start | bytes 1179656 | tf_op jit(solution)/shard_map/ppermute | solution.py:172
  33.5 7.7 %collective-permute-start.13 = (bf16[96,2048]{1,0:T(8,128)(2,1)S(1)}, bf16[96,2048]{1,0:T(8,128)(2,1)S(1)}, u32[]{:S(2)}, u32[]{:S(2)}) collective-permute-start(bf16[96,2048]{1,0:T(8,128)(2,1)S(1)} %pad_maximum_fusion.5), channel_id=1, source_target_pairs={{0,16},{4,20},{8,24},{12,28},{16,0},{20,4},{24,8},{28,12},{1,17},{... | collective-permute-start | bytes 1179656 | tf_op jit(solution)/shard_map/ppermute | solution.py:172
  36.7 12.3 %collective-permute-start.11 = (bf16[96,2048]{1,0:T(8,128)(2,1)S(1)}, bf16[96,2048]{1,0:T(8,128)(2,1)S(1)}, u32[]{:S(2)}, u32[]{:S(2)}) collective-permute-start(bf16[96,2048]{1,0:T(8,128)(2,1)S(1)} %get-tuple-element.72), channel_id=1, source_target_pairs={{0,16},{4,20},{8,24},{12,28},{16,0},{20,4},{24,8},{28,12},{1,17},{... | collective-permute-start | bytes 1179656 | tf_op jit(solution)/shard_map/ppermute | solution.py:172
  37.3 12.3 %collective-permute-start.12 = (bf16[96,2048]{1,0:T(8,128)(2,1)S(1)}, bf16[96,2048]{1,0:T(8,128)(2,1)S(1)}, u32[]{:S(2)}, u32[]{:S(2)}) collective-permute-start(bf16[96,2048]{1,0:T(8,128)(2,1)S(1)} %get-tuple-element.73), channel_id=1, source_target_pairs={{0,8},{4,12},{8,0},{12,4},{16,24},{20,28},{24,16},{28,20},{1,9},{5... | collective-permute-start | bytes 1179656 | tf_op jit(solution)/shard_map/ppermute | solution.py:172
  49.8 7.1 %collective-permute-start.21 = (f32[1,2048]{1,0:T(1,128)S(1)}, f32[1,2048]{1,0:T(1,128)S(1)}, u32[]{:S(2)}, u32[]{:S(2)}) collective-permute-start(f32[1,2048]{1,0:T(1,128)S(1)} %add.70), channel_id=1, source_target_pairs={{0,4},{4,0},{8,12},{12,8},{16,20},{20,16},{24,28},{28,24},{1,5},{5... | collective-permute-start | bytes 24584 | tf_op jit(solution)/shard_map/ppermute | solution.py:172
  54.4 21.3 %collective-permute-start.15 = (bf16[48,2048]{1,0:T(8,128)(2,1)S(1)}, bf16[48,2048]{1,0:T(8,128)(2,1)S(1)}, u32[]{:S(2)}, u32[]{:S(2)}) collective-permute-start(bf16[48,2048]{1,0:T(8,128)(2,1)S(1)} %slice.303), channel_id=1, source_target_pairs={{0,8},{4,12},{8,0},{12,4},{16,24},{20,28},{24,16},{28,20},{1,9},{5... | collective-permute-start | bytes 589832 | tf_op jit(solution)/shard_map/ppermute | solution.py:172
  55.1 10.4 %collective-permute-start.20 = (bf16[96,2048]{1,0:T(8,128)(2,1)S(1)}, bf16[96,2048]{1,0:T(8,128)(2,1)S(1)}, u32[]{:S(2)}, u32[]{:S(2)}) collective-permute-start(bf16[96,2048]{1,0:T(8,128)(2,1)S(1)} %get-tuple-element.98), channel_id=1, source_target_pairs={{0,16},{4,20},{8,24},{12,28},{16,0},{20,4},{24,8},{28,12},{1,17},{... | collective-permute-start | bytes 1179656 | tf_op jit(solution)/shard_map/ppermute | solution.py:172
  56.3 1.9 %collective-permute-start.24 = (bf16[384,512]{1,0:T(8,128)(2,1)S(1)}, bf16[384,512]{1,0:T(8,128)(2,1)S(1)}, u32[]{:S(2)}, u32[]{:S(2)}) collective-permute-start(bf16[384,512]{1,0:T(8,128)(2,1)S(1)} %pad_maximum_fusion.10), channel_id=1, source_target_pairs={{0,4},{4,0},{8,12},{12,8},{16,20},{20,16},{24,28},{28,24},{1,5},{5... | collective-permute-start | bytes 1179656 | tf_op jit(solution)/shard_map/ppermute | solution.py:172
  56.8 3.6 %collective-permute-start.23 = (bf16[384,2048]{1,0:T(8,128)(2,1)S(1)}, bf16[384,2048]{1,0:T(8,128)(2,1)S(1)}, u32[]{:S(2)}, u32[]{:S(2)}) collective-permute-start(bf16[384,2048]{1,0:T(8,128)(2,1)S(1)} %get-tuple-element.125.left_a), channel_id=1, source_target_pairs={{0,4},{4,0},{8,12},{12,8},{16,20},{20,16},{24,28},{28,24},{1,5},{5... | collective-permute-start | bytes 4718600 | tf_op jit(solution)/shard_map/ppermute | solution.py:172
  57.0 13.2 %collective-permute-start.22 = (bf16[104,2048]{1,0:T(8,128)(2,1)S(1)}, bf16[104,2048]{1,0:T(8,128)(2,1)S(1)}, u32[]{:S(2)}, u32[]{:S(2)}) collective-permute-start(bf16[104,2048]{1,0:T(8,128)(2,1)S(1)} %pad_maximum_fusion.2), channel_id=1, source_target_pairs={{0,8},{4,12},{8,0},{12,4},{16,24},{20,28},{24,16},{28,20},{1,9},{5... | collective-permute-start | bytes 1277960 | tf_op jit(solution)/shard_map/ppermute | solution.py:172
  58.2 17.5 %collective-permute-start.16 = (bf16[48,2048]{1,0:T(8,128)(2,1)S(1)}, bf16[48,2048]{1,0:T(8,128)(2,1)S(1)}, u32[]{:S(2)}, u32[]{:S(2)}) collective-permute-start(bf16[48,2048]{1,0:T(8,128)(2,1)S(1)} %fusion.6), channel_id=1, source_target_pairs={{0,16},{4,20},{8,24},{12,28},{16,0},{20,4},{24,8},{28,12},{1,17},{... | collective-permute-start | bytes 589832 | tf_op jit(solution)/shard_map/ppermute | solution.py:172
  60.4 10.7 %collective-permute-start.17 = (bf16[384,512]{1,0:T(8,128)(2,1)S(1)}, bf16[384,512]{1,0:T(8,128)(2,1)S(1)}, u32[]{:S(2)}, u32[]{:S(2)}) collective-permute-start(bf16[384,512]{1,0:T(8,128)(2,1)S(1)} %pad_maximum_fusion.8), channel_id=1, source_target_pairs={{0,4},{4,0},{8,12},{12,8},{16,20},{20,16},{24,28},{28,24},{1,5},{5... | collective-permute-start | bytes 1179656 | tf_op jit(solution)/shard_map/ppermute | solution.py:172
  65.5 6.8 %collective-permute-start.18 = (bf16[384,2048]{1,0:T(8,128)(2,1)S(1)}, bf16[384,2048]{1,0:T(8,128)(2,1)S(1)}, u32[]{:S(2)}, u32[]{:S(2)}) collective-permute-start(bf16[384,2048]{1,0:T(8,128)(2,1)S(1)} %constant_dynamic-update-slice_fusion.7.right_a), channel_id=1, source_target_pairs={{0,4},{4,0},{8,12},{12,8},{16,20},{20,16},{24,28},{28,24},{1,5},{5... | collective-permute-start | bytes 4718600 | tf_op jit(solution)/shard_map/ppermute | solution.py:172
  70.3 5.7 %collective-permute-start.25 = (bf16[48,2048]{1,0:T(8,128)(2,1)S(1)}, bf16[48,2048]{1,0:T(8,128)(2,1)S(1)}, u32[]{:S(2)}, u32[]{:S(2)}) collective-permute-start(bf16[48,2048]{1,0:T(8,128)(2,1)S(1)} %slice.302), channel_id=1, source_target_pairs={{0,8},{4,12},{8,0},{12,4},{16,24},{20,28},{24,16},{28,20},{1,9},{5... | collective-permute-start | bytes 589832 | tf_op jit(solution)/shard_map/ppermute | solution.py:172
  71.2 6.1 %collective-permute-start.26 = (bf16[56,2048]{1,0:T(8,128)(2,1)S(1)}, bf16[56,2048]{1,0:T(8,128)(2,1)S(1)}, u32[]{:S(2)}, u32[]{:S(2)}) collective-permute-start(bf16[56,2048]{1,0:T(8,128)(2,1)S(1)} %pad_maximum_fusion.13), channel_id=1, source_target_pairs={{0,16},{4,20},{8,24},{12,28},{16,0},{20,4},{24,8},{28,12},{1,17},{... | collective-permute-start | bytes 688136 | tf_op jit(solution)/shard_map/ppermute | solution.py:172
  77.4 26.7 %copy-start.2 = (bf16[128,2048]{1,0:T(8,128)(2,1)S(1)}, bf16[128,2048]{1,0:T(8,128)(2,1)}, u32[]{:S(2)}) copy-start(bf16[128,2048]{1,0:T(8,128)(2,1)} %tok_ref.1) | copy-start | bytes 1572868
  77.4 26.7 %copy-start.4 = (s32[1,128]{1,0:T(1,128)S(1)}, s32[1,128]{1,0:T(1,128)}, u32[]{:S(2)}) copy-start(s32[1,128]{1,0:T(1,128)} %get-tuple-element.56.slot_ref) | copy-start | bytes 1540
  77.5 25.9 %collective-permute-start.28 = (bf16[56,2048]{1,0:T(8,128)(2,1)S(1)}, bf16[56,2048]{1,0:T(8,128)(2,1)S(1)}, u32[]{:S(2)}, u32[]{:S(2)}) collective-permute-start(bf16[56,2048]{1,0:T(8,128)(2,1)S(1)} %get-tuple-element.153), channel_id=1, source_target_pairs={{0,1},{1,2},{2,3},{3,0},{4,5},{5,6},{6,7},{7,4},{8,9},{9,10},{10,1... | collective-permute-start | bytes 688136 | tf_op jit(solution)/shard_map/ppermute | solution.py:175
  79.3 24.1 %collective-permute-start.27 = (bf16[56,2048]{1,0:T(8,128)(2,1)S(1)}, bf16[56,2048]{1,0:T(8,128)(2,1)S(1)}, u32[]{:S(2)}, u32[]{:S(2)}) collective-permute-start(bf16[56,2048]{1,0:T(8,128)(2,1)S(1)} %get-tuple-element.154), channel_id=1, source_target_pairs={{0,2},{1,3},{2,0},{3,1},{4,6},{5,7},{6,4},{7,5},{8,10},{9,11},{10,... | collective-permute-start | bytes 688136 | tf_op jit(solution)/shard_map/ppermute | solution.py:175
  82.7 21.4 %collective-permute-start.19 = (bf16[48,2048]{1,0:T(8,128)(2,1)S(1)}, bf16[48,2048]{1,0:T(8,128)(2,1)S(1)}, u32[]{:S(2)}, u32[]{:S(2)}) collective-permute-start(bf16[48,2048]{1,0:T(8,128)(2,1)S(1)} %pad_maximum_fusion.19), channel_id=1, source_target_pairs={{0,3},{1,0},{2,1},{3,2},{4,7},{5,4},{6,5},{7,6},{8,11},{9,8},{10,9... | collective-permute-start | bytes 589832 | tf_op jit(solution)/shard_map/ppermute | solution.py:175
  84.1 19.3 %collective-permute-start.29 = (bf16[8,2048]{1,0:T(8,128)(2,1)S(1)}, bf16[8,2048]{1,0:T(8,128)(2,1)S(1)}, u32[]{:S(2)}, u32[]{:S(2)}) collective-permute-start(bf16[8,2048]{1,0:T(8,128)(2,1)S(1)} %fusion.16), channel_id=1, source_target_pairs={{0,3},{1,0},{2,1},{3,2},{4,7},{5,4},{6,5},{7,6},{8,11},{9,8},{10,9... | collective-permute-start | bytes 98312 | tf_op jit(solution)/shard_map/ppermute | solution.py:175
  (4 other events, 44.6 us)

commit v5 on v4

--- a/solution.py
+++ b/solution.py
@@ -94,29 +94,49 @@
         sends[k][...] = mm(placing, both[...]).astype(bf16)
 
 
-def hidden_kernel(in_ref, cot_ref, up_a, up_b, down_a, down_b, hid_a, hid_b, pre_a, pre_b):
-    units = up_a.shape[1]
+def pack_kernel(up_ref, down_ref, pack_ref):
+    units = up_ref.shape[1]
+    pack_ref[:, :units] = up_ref[...]
+    for j in range(up_ref.shape[0] // units):
+        at = pl.ds(j * units, units)
+        pack_ref[at, units:] = down_ref[:, at]
+
+
+def hidden_kernel(in_ref, cot_ref, up_a, down_a, pack_b, hid_a, hid_b, pre_a, pre_b):
+    width, units = up_a.shape
     step = min(units, 256)
-    for up, down, hid, pre in ((up_a, down_a, hid_a, pre_a), (up_b, down_b, hid_b, pre_b)):
-        for i in range(units // step):
-            at = pl.ds(i * step, step)
-            values, slopes = gelu_parts(mm(in_ref[...], up[:, at]))
-            hid[:, at] = values.astype(bf16)
-            pre[:, at] = (mm(cot_ref[...], down[at, :], NT) * slopes).astype(bf16)
+    for i in range(units // step):
+        at = pl.ds(i * step, step)
+        values, slopes = gelu_parts(mm(in_ref[...], up_a[:, at]))
+        hid_a[:, at] = values.astype(bf16)
+        pre_a[:, at] = (mm(cot_ref[...], down_a[at, :], NT) * slopes).astype(bf16)
+    for i in range(units // step):
+        at = pl.ds(i * step, step)
+        values, slopes = gelu_parts(mm(in_ref[...], pack_b[:, at]))
+        hid_b[:, at] = values.astype(bf16)
+        total = None
+        for j in range(width // units):
+            block = pack_b[pl.ds(j * units + i * step, step), pl.ds(units, units)]
+            part = mm(cot_ref[:, pl.ds(j * units, units)], block, NT)
+            total = part if total is None else total + part
+        pre_b[:, at] = (total * slopes).astype(bf16)
 
 
 def row_kernel(
-    piece, in_ref, hid_a, hid_b, pre_a, pre_b, up_a, up_b, down_a, down_b,
+    piece, in_ref, hid_a, hid_b, pre_a, pre_b, up_a, down_a, pack_b,
     gain_ref, keep_out, send_out, keep_back, send_back,
 ):
     rows, width = in_ref.shape
     pieces = rows // piece
+    units = up_a.shape[1]
     for i in range(width // 256):
         at = pl.ds(i * 256, 256)
-        total = mm(hid_a[...], down_a[:, at]) + mm(hid_b[...], down_b[:, at])
+        j, off = divmod(i * 256, units)
+        down_b = pack_b[pl.ds(j * units, units), pl.ds(units + off, 256)]
+        total = mm(hid_a[...], down_a[:, at]) + mm(hid_b[...], down_b)
         keep_out[:, at] = total[: rows // 2]
         send_out[:, at] = total[rows // 2 :].astype(bf16)
-        total = mm(pre_a[...], up_a[at, :], NT) + mm(pre_b[...], up_b[at, :], NT)
+        total = mm(pre_a[...], up_a[at, :], NT) + mm(pre_b[...], pack_b[at, pl.ds(0, units)], NT)
         gain_ref[:, at] = jnp.sum(total * in_ref[:, at].astype(f32), axis=0, keepdims=True)
         for p in range(pieces):
             part = total[p * piece : (p + 1) * piece]
@@ -178,7 +198,6 @@
         return jnp.concatenate(arrays, axis=0)
 
     up_a, down_a = up_weight[0], down_weight[0]
-    up_b, down_b = swap(up_a, 1), swap(down_a, 1)
 
     gain_row = norm_gain.reshape(1, width)
     slot_row, *blocks = call(
@@ -196,6 +215,15 @@
         place=pltpu.HBM,
         room=PLACE_ROOM,
     )
+    pack_a = call(
+        "pack",
+        pack_kernel,
+        shaped((width, 2 * units)),
+        after((up_a, down_a), blocks[0]),
+        2,
+        8 << 20,
+    )
+    pack_b = swap(pack_a, 1)
     early = groups // 2
     arrived = [blocks[0]] + [shift(blocks[k], k) for k in range(1, early)]
     blocks = after(blocks, arrived[1:])
@@ -222,7 +250,7 @@
 
     down_bits = list(reversed(bits))
     work = 8 * rows * width * 2 * units
-    weights = (up_a, up_b, down_a, down_b)
+    weights = (up_a, down_a, pack_b)
 
     def gather(pair, events):
         for n, (bit, back_bit) in enumerate(zip(bits, down_bits)):
@@ -279,9 +307,7 @@
             cut = slice(i * capacity, (i + 1) * capacity)
             block = join(out_rows[cut], back_rows[cut])
             if k and sums is not None:
-                got = shift(join(block, packed(sums)), groups - k)
-                other.append(unpacked(got[-8:]))
-                home[k] = got[:-8]
+                home[k] = shift(block, groups - k)
             else:
                 home[k] = shift(block, groups - k) if k else block
         return other
@@ -321,12 +347,16 @@
     home = [None] * groups
     sums = parts_1[0] + parts_2[0]
     sums = sums + swap(sums, 1)
-    out_1, back_1, _ = scatter(parts_1, [(parts_2[0],)] + [(grad_down,)] * len(bits))
+    out_1, back_1, _ = scatter(parts_1, [(sums,)] + [(grad_down,)] * len(bits))
     out_2, back_2, sums = scatter(parts_2, [(grad_up,)] + [()] * len(bits), sums)
     homeward(0, out_1, back_1, None)
     other = homeward(1, out_2, back_2, sums)
-    other += [unpacked(shift(packed(sums), groups - k)) for k in range(1, groups // 2)]
-    total = sum(other, sums)
+    total = sums.reshape(16, width // 16)
+    step = 1
+    while step < groups:
+        total = total + lax.ppermute(total, "exp", [(i, i ^ step) for i in range(groups)])
+        step *= 2
+    total = total.reshape(1, width)
     grad_gain = (total / gain_row).reshape(width)
     mixed, grad_tokens = call(
         "tokens",

time: 107 us -> 98 us (0.916)
  the two profiles are of different devices: /device:TPU:9 before, /device:TPU:0 now
where the time goes in v5:
time: 98 us; the launch traced here: 97.8 us
  waiting for transfers between devices  34.9 us (36%)
  starting transfers between devices  34.6 us (35%)
  Pallas kernels  20.9 us (21%)
  local copies, waits for them, and re-layouts  4.31 us (4%)
  other arithmetic  1.79 us (2%)
  between operations  1.24 us (1%)
    pallas_call x9, Pallas kernels, call(): pl.pallas_call(kernel, name=name, out_shape=out_shape, in_specs=[pl.Block...  20.9 us
    ppermute x22, starting transfers between devices, swap(): return lax.ppermute(x, 'rep', [(i, i ^ bit) for i in range(copies)])  20.5 us
    ppermute x22, waiting for transfers between devices, swap(): return lax.ppermute(x, 'rep', [(i, i ^ bit) for i in range(copies)])  17.6 us
    ppermute x6, starting transfers between devices, shift(): lax.ppermute(x, 'exp', [(i, (i + k) % groups) for i in range(groups)])  11.9 us
    ppermute x2, waiting for transfers between devices, local(): lax.ppermute(total, 'exp', [(i, i ^ step) for i in range(groups)])  10.1 us
    ppermute x6, waiting for transfers between devices, shift(): lax.ppermute(x, 'exp', [(i, (i + k) % groups) for i in range(groups)])  7.26 us
    unnamed x29, local copies, waits for them, and re-layouts  4.04 us
    ppermute x2, starting transfers between devices, local(): lax.ppermute(total, 'exp', [(i, i ^ step) for i in range(groups)])  2.15 us
  transfers between devices with their start and end apart: 30, of which 14 were waited for; matrix products, arithmetic and copies ran while one was open for 2% of the time, Pallas kernels for 16%

profile of v5, /device:TPU:0, one launch (start us, length us, event | category | flops | bytes accessed | tf_op | source)
XLA Modules:
  0.0 97.8 jit_solution(6953635844257917199)
XLA Ops:
  0.6 2.8 %place.1 = (s32[1,128]{1,0:T(1,128)}, bf16[48,2048]{1,0:T(8,128)(2,1)}, bf16[48,2048]{1,0:T(8,128)(2,1)}, bf16[48,2048]{1,0:T(8,128)(2,1)}, bf16[48,2048]{1,0:T(8,128)(2,1)}) custom-call(bf16[128,2048]{1,0:T(8,128)(2,1)} %tok_ref.1, s32[1,128]{1,0:T(1,128)} %bitcast.47, f32[1,2048]{1,0:T(1,128)} %bitcast.37, bf16[128,2048]{1,0:T(8,128)(2,1)} %cot_in.1), custom_call_target="tpu_custom_call" | custom-call | tf_op jit(solution)/shard_map/place/pallas_call | solution.py:39
  3.5 3.1 %collective-permute-start = (bf16[48,2048]{1,0:T(8,128)(2,1)}, bf16[48,2048]{1,0:T(8,128)(2,1)S(1)}, u32[]{:S(2)}, u32[]{:S(2)}) collective-permute-start(bf16[48,2048]{1,0:T(8,128)(2,1)} %get-tuple-element.60), channel_id=1, source_target_pairs={{0,1},{1,2},{2,3},{3,0},{4,5},{5,6},{6,7},{7,4},{8,9},{9,10},{10,1... | collective-permute-start | bytes 589832 | tf_op jit(solution)/shard_map/ppermute | solution.py:195
  6.6 1.6 %copy-done = bf16[1,2048,512]{2,1,0:T(8,128)(2,1)S(1)} copy-done((bf16[1,2048,512]{2,1,0:T(8,128)(2,1)S(1)}, bf16[1,2048,512]{2,1,0:T(8,128)(2,1)}, u32[]{:S(2)}) %copy-start) | copy-done | bytes 2097176
  8.1 1.6 %copy-done.1 = bf16[1,512,2048]{2,1,0:T(8,128)(2,1)S(1)} copy-done((bf16[1,512,2048]{2,1,0:T(8,128)(2,1)S(1)}, bf16[1,512,2048]{2,1,0:T(8,128)(2,1)}, u32[]{:S(2)}) %copy-start.1) | copy-done | bytes 2097176
  10.7 3.0 %collective-permute-done = bf16[48,2048]{1,0:T(8,128)(2,1)S(1)} collective-permute-done((bf16[48,2048]{1,0:T(8,128)(2,1)}, bf16[48,2048]{1,0:T(8,128)(2,1)S(1)}, u32[]{:S(2)}, u32[]{:S(2)}) %collective-permute-start) | collective-permute-done | bytes 196640 | tf_op jit(solution)/shard_map/ppermute | solution.py:195
  14.5 1.6 %collective-permute-start.1 = (bf16[48,2048]{1,0:T(8,128)(2,1)S(1)}, bf16[48,2048]{1,0:T(8,128)(2,1)S(1)}, u32[]{:S(2)}, u32[]{:S(2)}) collective-permute-start(bf16[48,2048]{1,0:T(8,128)(2,1)S(1)} %pad_maximum_fusion.12), channel_id=1, source_target_pairs={{0,8},{4,12},{8,0},{12,4},{16,24},{20,28},{24,16},{28,20},{1,9},{5... | collective-permute-start | bytes 589832 | tf_op jit(solution)/shard_map/ppermute | solution.py:192
  16.1 1.6 %collective-permute-start.4 = (bf16[48,2048]{1,0:T(8,128)(2,1)S(1)}, bf16[48,2048]{1,0:T(8,128)(2,1)S(1)}, u32[]{:S(2)}, u32[]{:S(2)}) collective-permute-start(bf16[48,2048]{1,0:T(8,128)(2,1)S(1)} %pad_maximum_fusion.13), channel_id=1, source_target_pairs={{0,16},{4,20},{8,24},{12,28},{16,0},{20,4},{24,8},{28,12},{1,17},{... | collective-permute-start | bytes 589832 | tf_op jit(solution)/shard_map/ppermute | solution.py:192
  17.6 2.6 %collective-permute-done.1 = bf16[48,2048]{1,0:T(8,128)(2,1)S(1)} collective-permute-done((bf16[48,2048]{1,0:T(8,128)(2,1)S(1)}, bf16[48,2048]{1,0:T(8,128)(2,1)S(1)}, u32[]{:S(2)}, u32[]{:S(2)}) %collective-permute-start.1) | collective-permute-done | bytes 196640 | tf_op jit(solution)/shard_map/ppermute | solution.py:192
  20.2 1.6 %collective-permute-start.2 = (bf16[96,2048]{1,0:T(8,128)(2,1)S(1)}, bf16[96,2048]{1,0:T(8,128)(2,1)S(1)}, u32[]{:S(2)}, u32[]{:S(2)}) collective-permute-start(bf16[96,2048]{1,0:T(8,128)(2,1)S(1)} %pad_maximum_fusion.3), channel_id=1, source_target_pairs={{0,16},{4,20},{8,24},{12,28},{16,0},{20,4},{24,8},{28,12},{1,17},{... | collective-permute-start | bytes 1179656 | tf_op jit(solution)/shard_map/ppermute | solution.py:192
  24.8 4.3 %collective-permute-done.5 = bf16[48,2048]{1,0:T(8,128)(2,1)S(1)} collective-permute-done((bf16[48,2048]{1,0:T(8,128)(2,1)S(1)}, bf16[48,2048]{1,0:T(8,128)(2,1)S(1)}, u32[]{:S(2)}, u32[]{:S(2)}) %collective-permute-start.5) | collective-permute-done | bytes 196640 | tf_op jit(solution)/shard_map/ppermute | solution.py:195
  29.2 1.9 %collective-permute-start.6 = (bf16[48,2048]{1,0:T(8,128)(2,1)S(1)}, bf16[48,2048]{1,0:T(8,128)(2,1)S(1)}, u32[]{:S(2)}, u32[]{:S(2)}) collective-permute-start(bf16[48,2048]{1,0:T(8,128)(2,1)S(1)} %get-tuple-element.84), channel_id=1, source_target_pairs={{0,8},{4,12},{8,0},{12,4},{16,24},{20,28},{24,16},{28,20},{1,9},{5... | collective-permute-start | bytes 589832 | tf_op jit(solution)/shard_map/ppermute | solution.py:192
  31.1 1.5 %collective-permute-start.7 = (bf16[48,2048]{1,0:T(8,128)(2,1)S(1)}, bf16[48,2048]{1,0:T(8,128)(2,1)S(1)}, u32[]{:S(2)}, u32[]{:S(2)}) collective-permute-start(bf16[48,2048]{1,0:T(8,128)(2,1)S(1)} %get-tuple-element.88), channel_id=1, source_target_pairs={{0,16},{4,20},{8,24},{12,28},{16,0},{20,4},{24,8},{28,12},{1,17},{... | collective-permute-start | bytes 589832 | tf_op jit(solution)/shard_map/ppermute | solution.py:192
  33.4 2.3 %hidden.2 = (bf16[192,512]{1,0:T(8,128)(2,1)S(1)}, bf16[192,512]{1,0:T(8,128)(2,1)S(1)}, bf16[192,512]{1,0:T(8,128)(2,1)S(1)}, bf16[192,512]{1,0:T(8,128)(2,1)S(1)}) custom-call(bf16[192,2048]{1,0:T(8,128)(2,1)S(1)} %pad_maximum_fusion.in_ref, bf16[192,2048]{1,0:T(8,128)(2,1)S(1)} %get-tuple-element.116.cot_ref, bf16[2048,512]{1,0:T(8,128)(2,1)S(1)} %bitcast.28, ...), custom_call_target="tpu_custom_call" | custom-call | flops 1610612736 | bytes 8388608 | tf_op jit(solution)/shard_map/hidden/pallas_call | solution.py:39
  35.7 1.6 %collective-permute-done.7 = bf16[48,2048]{1,0:T(8,128)(2,1)S(1)} collective-permute-done((bf16[48,2048]{1,0:T(8,128)(2,1)S(1)}, bf16[48,2048]{1,0:T(8,128)(2,1)S(1)}, u32[]{:S(2)}, u32[]{:S(2)}) %collective-permute-start.7) | collective-permute-done | bytes 196640 | tf_op jit(solution)/shard_map/ppermute | solution.py:192
  37.5 1.9 %collective-permute-start.12 = (bf16[96,2048]{1,0:T(8,128)(2,1)S(1)}, bf16[96,2048]{1,0:T(8,128)(2,1)S(1)}, u32[]{:S(2)}, u32[]{:S(2)}) collective-permute-start(bf16[96,2048]{1,0:T(8,128)(2,1)S(1)} %pad_maximum_fusion.5), channel_id=1, source_target_pairs={{0,16},{4,20},{8,24},{12,28},{16,0},{20,4},{24,8},{28,12},{1,17},{... | collective-permute-start | bytes 1179656 | tf_op jit(solution)/shard_map/ppermute | solution.py:192
  39.4 2.2 %rows.2 = (f32[1,2048]{1,0:T(1,128)S(1)}, f32[96,2048]{1,0:T(8,128)S(1)}, bf16[96,2048]{1,0:T(8,128)(2,1)S(1)}, f32[96,2048]{1,0:T(8,128)S(1)}, bf16[96,2048]{1,0:T(8,128)(2,1)S(1)}) custom-call(bf16[192,2048]{1,0:T(8,128)(2,1)S(1)} %pad_maximum_fusion.in_ref, bf16[192,512]{1,0:T(8,128)(2,1)S(1)} %get-tuple-element.71.hid_a, ...), custom_call_target="tpu_custom_call" | custom-call | flops 1610612736 | bytes 8388608 | tf_op jit(solution)/shard_map/rows/pallas_call | solution.py:39
  41.8 2.0 %collective-permute-start.11 = (bf16[96,2048]{1,0:T(8,128)(2,1)S(1)}, bf16[96,2048]{1,0:T(8,128)(2,1)S(1)}, u32[]{:S(2)}, u32[]{:S(2)}) collective-permute-start(bf16[96,2048]{1,0:T(8,128)(2,1)S(1)} %get-tuple-element.77), channel_id=1, source_target_pairs={{0,8},{4,12},{8,0},{12,4},{16,24},{20,28},{24,16},{28,20},{1,9},{5... | collective-permute-start | bytes 1179656 | tf_op jit(solution)/shard_map/ppermute | solution.py:192
  43.8 4.5 %collective-permute-done.13 = bf16[96,2048]{1,0:T(8,128)(2,1)S(1)} collective-permute-done((bf16[96,2048]{1,0:T(8,128)(2,1)S(1)}, bf16[96,2048]{1,0:T(8,128)(2,1)S(1)}, u32[]{:S(2)}, u32[]{:S(2)}) %collective-permute-start.13) | collective-permute-done | bytes 393248 | tf_op jit(solution)/shard_map/ppermute | solution.py:192
  49.8 2.3 %hidden.3 = (bf16[192,512]{1,0:T(8,128)(2,1)S(1)}, bf16[192,512]{1,0:T(8,128)(2,1)S(1)}, bf16[192,512]{1,0:T(8,128)(2,1)S(1)}, bf16[192,512]{1,0:T(8,128)(2,1)S(1)}) custom-call(bf16[192,2048]{1,0:T(8,128)(2,1)S(1)} %get-tuple-element.128.in_ref, bf16[192,2048]{1,0:T(8,128)(2,1)S(1)} %pad_maximum_fusion.1.cot_ref, bf16[2048,512]{1,0:T(8,128)(2,1)S(1)} %bitcast.30, ...), custom_call_target="tpu_custom_call" | custom-call | flops 1610612736 | bytes 8388608 | tf_op jit(solution)/shard_map/hidden/pallas_call | solution.py:39
  52.2 2.2 %rows.3 = (f32[1,2048]{1,0:T(1,128)S(1)}, f32[96,2048]{1,0:T(8,128)S(1)}, bf16[96,2048]{1,0:T(8,128)(2,1)S(1)}, f32[96,2048]{1,0:T(8,128)S(1)}, bf16[96,2048]{1,0:T(8,128)(2,1)S(1)}) custom-call(bf16[192,2048]{1,0:T(8,128)(2,1)S(1)} %get-tuple-element.128.in_ref, bf16[192,512]{1,0:T(8,128)(2,1)S(1)} %get-tuple-element.92.hid_a, ...), custom_call_target="tpu_custom_call" | custom-call | flops 1610612736 | bytes 8388608 | tf_op jit(solution)/shard_map/rows/pallas_call | solution.py:39
  54.5 1.6 %collective-permute-start.20 = (bf16[96,2048]{1,0:T(8,128)(2,1)S(1)}, bf16[96,2048]{1,0:T(8,128)(2,1)S(1)}, u32[]{:S(2)}, u32[]{:S(2)}) collective-permute-start(bf16[96,2048]{1,0:T(8,128)(2,1)S(1)} %get-tuple-element.102), channel_id=1, source_target_pairs={{0,16},{4,20},{8,24},{12,28},{16,0},{20,4},{24,8},{28,12},{1,17},{... | collective-permute-start | bytes 1179656 | tf_op jit(solution)/shard_map/ppermute | solution.py:192
  58.6 2.0 %collective-permute-done.22.left_b = bf16[384,2048]{1,0:T(8,128)(2,1)S(1)} collective-permute-done((bf16[384,2048]{1,0:T(8,128)(2,1)S(1)}, bf16[384,2048]{1,0:T(8,128)(2,1)S(1)}, u32[]{:S(2)}, u32[]{:S(2)}) %collective-permute-start.22) | collective-permute-done | bytes 1572896 | tf_op jit(solution)/shard_map/ppermute | solution.py:192
  61.5 3.2 %grad_up.1 = bf16[2048,512]{1,0:T(8,128)(2,1)} custom-call(bf16[384,2048]{1,0:T(8,128)(2,1)S(1)} %get-tuple-element.127.left_a, bf16[384,2048]{1,0:T(8,128)(2,1)S(1)} %collective-permute-done.22.left_b, bf16[384,512]{1,0:T(8,128)(2,1)S(1)} %pad_maximum_fusion.9.right_a, bf16[384,512]{1,0:T(8,128)(2,1)S(1)} %collective-permute-done.23.right_b), custom_call_target="tpu_custom_call" | custom-call | flops 805306368 | bytes 8388608 | tf_op jit(solution)/shard_map/grad_up/pallas_call | solution.py:39
  64.6 1.4 %collective-permute-done.20 = bf16[96,2048]{1,0:T(8,128)(2,1)S(1)} collective-permute-done((bf16[96,2048]{1,0:T(8,128)(2,1)S(1)}, bf16[96,2048]{1,0:T(8,128)(2,1)S(1)}, u32[]{:S(2)}, u32[]{:S(2)}) %collective-permute-start.20) | collective-permute-done | bytes 393248 | tf_op jit(solution)/shard_map/ppermute | solution.py:192
  66.1 1.5 %collective-permute-start.16 = (bf16[48,2048]{1,0:T(8,128)(2,1)S(1)}, bf16[48,2048]{1,0:T(8,128)(2,1)S(1)}, u32[]{:S(2)}, u32[]{:S(2)}) collective-permute-start(bf16[48,2048]{1,0:T(8,128)(2,1)S(1)} %fusion.6), channel_id=1, source_target_pairs={{0,16},{4,20},{8,24},{12,28},{16,0},{20,4},{24,8},{28,12},{1,17},{... | collective-permute-start | bytes 589832 | tf_op jit(solution)/shard_map/ppermute | solution.py:192
  67.6 2.2 %collective-permute-done.21 = bf16[104,2048]{1,0:T(8,128)(2,1)S(1)} collective-permute-done((bf16[104,2048]{1,0:T(8,128)(2,1)S(1)}, bf16[104,2048]{1,0:T(8,128)(2,1)S(1)}, u32[]{:S(2)}, u32[]{:S(2)}) %collective-permute-start.21) | collective-permute-done | bytes 426016 | tf_op jit(solution)/shard_map/ppermute | solution.py:192
  72.1 3.4 %grad_down.1 = bf16[512,2048]{1,0:T(8,128)(2,1)} custom-call(bf16[384,512]{1,0:T(8,128)(2,1)S(1)} %pad_maximum_fusion.7.left_a, bf16[384,512]{1,0:T(8,128)(2,1)S(1)} %collective-permute-done.17.left_b, bf16[384,2048]{1,0:T(8,128)(2,1)S(1)} %constant_dynamic-update-slice_fusion.7.right_a, bf16[384,2048]{1,0:T(8,128)(2,1)S(1)} %collective-permute-done.18.right_b), custom_call_target="tpu_custom_call" | custom-call | flops 805306368 | bytes 8388608 | tf_op jit(solution)/shard_map/grad_down/pallas_call | solution.py:39
  75.6 2.4 %collective-permute-start.19 = (bf16[48,2048]{1,0:T(8,128)(2,1)S(1)}, bf16[48,2048]{1,0:T(8,128)(2,1)S(1)}, u32[]{:S(2)}, u32[]{:S(2)}) collective-permute-start(bf16[48,2048]{1,0:T(8,128)(2,1)S(1)} %pad_maximum_fusion.17), channel_id=1, source_target_pairs={{0,3},{1,0},{2,1},{3,2},{4,7},{5,4},{6,5},{7,6},{8,11},{9,8},{10,9... | collective-permute-start | bytes 589832 | tf_op jit(solution)/shard_map/ppermute | solution.py:195
  79.1 2.1 %collective-permute-start.26 = (bf16[48,2048]{1,0:T(8,128)(2,1)S(1)}, bf16[48,2048]{1,0:T(8,128)(2,1)S(1)}, u32[]{:S(2)}, u32[]{:S(2)}) collective-permute-start(bf16[48,2048]{1,0:T(8,128)(2,1)S(1)} %pad_maximum_fusion.18), channel_id=1, source_target_pairs={{0,2},{1,3},{2,0},{3,1},{4,6},{5,7},{6,4},{7,5},{8,10},{9,11},{10,... | collective-permute-start | bytes 589832 | tf_op jit(solution)/shard_map/ppermute | solution.py:195
  83.4 2.3 %collective-permute-start.27 = (bf16[48,2048]{1,0:T(8,128)(2,1)S(1)}, bf16[48,2048]{1,0:T(8,128)(2,1)S(1)}, u32[]{:S(2)}, u32[]{:S(2)}) collective-permute-start(bf16[48,2048]{1,0:T(8,128)(2,1)S(1)} %pad_maximum_fusion.19), channel_id=1, source_target_pairs={{0,1},{1,2},{2,3},{3,0},{4,5},{5,6},{6,7},{7,4},{8,9},{9,10},{10,1... | collective-permute-start | bytes 589832 | tf_op jit(solution)/shard_map/ppermute | solution.py:195
  85.7 9.2 %collective-permute-done.29 = f32[16,128]{1,0:T(8,128)S(1)} collective-permute-done((f32[16,128]{1,0:T(8,128)S(1)}, f32[16,128]{1,0:T(8,128)S(1)}, u32[]{:S(2)}, u32[]{:S(2)}) %collective-permute-start.29) | collective-permute-done | bytes 8224 | tf_op jit(solution)/shard_map/ppermute | solution.py:357
  95.5 2.2 %tokens.1 = (bf16[128,2048]{1,0:T(8,128)(2,1)}, bf16[128,2048]{1,0:T(8,128)(2,1)}) custom-call(s32[1,128]{1,0:T(1,128)S(1)} %copy-done.4, bf16[128,2048]{1,0:T(8,128)(2,1)S(1)} %copy-done.2, f32[1,2048]{1,0:T(1,128)S(1)} %bitcast.38, bf16[48,2048]{1,0:T(8,128)(2,1)S(1)} %pad_maximum_fusion.16.refs_0_, bf16[48,2048]{1,0:T(8,128)(2,1)S(1)} %collective-permute-done.19.refs_1_, ...), custom_call_target="tpu_custom_call" | custom-call | tf_op jit(solution)/shard_map/tokens/pallas_call | solution.py:39
  (117 shorter events, 16.8 us)
Async XLA Ops:
  3.5 10.2 %collective-permute-start = (bf16[48,2048]{1,0:T(8,128)(2,1)}, bf16[48,2048]{1,0:T(8,128)(2,1)S(1)}, u32[]{:S(2)}, u32[]{:S(2)}) collective-permute-start(bf16[48,2048]{1,0:T(8,128)(2,1)} %get-tuple-element.60), channel_id=1, source_target_pairs={{0,1},{1,2},{2,3},{3,0},{4,5},{5,6},{6,7},{7,4},{8,9},{9,10},{10,1... | collective-permute-start | bytes 589832 | tf_op jit(solution)/shard_map/ppermute | solution.py:195
  10.1 23.3 %collective-permute-start.9 = (bf16[2048,1024]{1,0:T(8,128)(2,1)S(1)}, bf16[2048,1024]{1,0:T(8,128)(2,1)S(1)}, u32[]{:S(2)}, u32[]{:S(2)}) collective-permute-start(bf16[2048,1024]{1,0:T(8,128)(2,1)S(1)} %pack.1), channel_id=1, source_target_pairs={{0,4},{4,0},{8,12},{12,8},{16,20},{20,16},{24,28},{28,24},{1,5},{5... | collective-permute-start | bytes 12582920 | tf_op jit(solution)/shard_map/ppermute | solution.py:192
  13.7 11.1 %collective-permute-start.3 = (bf16[48,2048]{1,0:T(8,128)(2,1)S(1)}, bf16[48,2048]{1,0:T(8,128)(2,1)S(1)}, u32[]{:S(2)}, u32[]{:S(2)}) collective-permute-start(bf16[48,2048]{1,0:T(8,128)(2,1)S(1)} %copy-done.7), channel_id=1, source_target_pairs={{0,2},{1,3},{2,0},{3,1},{4,6},{5,7},{6,4},{7,5},{8,10},{9,11},{10,... | collective-permute-start | bytes 589832 | tf_op jit(solution)/shard_map/ppermute | solution.py:195
  14.5 5.7 %collective-permute-start.1 = (bf16[48,2048]{1,0:T(8,128)(2,1)S(1)}, bf16[48,2048]{1,0:T(8,128)(2,1)S(1)}, u32[]{:S(2)}, u32[]{:S(2)}) collective-permute-start(bf16[48,2048]{1,0:T(8,128)(2,1)S(1)} %pad_maximum_fusion.12), channel_id=1, source_target_pairs={{0,8},{4,12},{8,0},{12,4},{16,24},{20,28},{24,16},{28,20},{1,9},{5... | collective-permute-start | bytes 589832 | tf_op jit(solution)/shard_map/ppermute | solution.py:192
  16.1 7.1 %collective-permute-start.4 = (bf16[48,2048]{1,0:T(8,128)(2,1)S(1)}, bf16[48,2048]{1,0:T(8,128)(2,1)S(1)}, u32[]{:S(2)}, u32[]{:S(2)}) collective-permute-start(bf16[48,2048]{1,0:T(8,128)(2,1)S(1)} %pad_maximum_fusion.13), channel_id=1, source_target_pairs={{0,16},{4,20},{8,24},{12,28},{16,0},{20,4},{24,8},{28,12},{1,17},{... | collective-permute-start | bytes 589832 | tf_op jit(solution)/shard_map/ppermute | solution.py:192
  20.2 13.0 %collective-permute-start.2 = (bf16[96,2048]{1,0:T(8,128)(2,1)S(1)}, bf16[96,2048]{1,0:T(8,128)(2,1)S(1)}, u32[]{:S(2)}, u32[]{:S(2)}) collective-permute-start(bf16[96,2048]{1,0:T(8,128)(2,1)S(1)} %pad_maximum_fusion.3), channel_id=1, source_target_pairs={{0,16},{4,20},{8,24},{12,28},{16,0},{20,4},{24,8},{28,12},{1,17},{... | collective-permute-start | bytes 1179656 | tf_op jit(solution)/shard_map/ppermute | solution.py:192
  23.2 9.9 %collective-permute-start.8 = (bf16[96,2048]{1,0:T(8,128)(2,1)S(1)}, bf16[96,2048]{1,0:T(8,128)(2,1)S(1)}, u32[]{:S(2)}, u32[]{:S(2)}) collective-permute-start(bf16[96,2048]{1,0:T(8,128)(2,1)S(1)} %pad_maximum_fusion.4), channel_id=1, source_target_pairs={{0,8},{4,12},{8,0},{12,4},{16,24},{20,28},{24,16},{28,20},{1,9},{5... | collective-permute-start | bytes 1179656 | tf_op jit(solution)/shard_map/ppermute | solution.py:192
  23.4 5.7 %collective-permute-start.5 = (bf16[48,2048]{1,0:T(8,128)(2,1)S(1)}, bf16[48,2048]{1,0:T(8,128)(2,1)S(1)}, u32[]{:S(2)}, u32[]{:S(2)}) collective-permute-start(bf16[48,2048]{1,0:T(8,128)(2,1)S(1)} %copy-done.6), channel_id=1, source_target_pairs={{0,3},{1,0},{2,1},{3,2},{4,7},{5,4},{6,5},{7,6},{8,11},{9,8},{10,9... | collective-permute-start | bytes 589832 | tf_op jit(solution)/shard_map/ppermute | solution.py:195
  29.2 6.5 %collective-permute-start.6 = (bf16[48,2048]{1,0:T(8,128)(2,1)S(1)}, bf16[48,2048]{1,0:T(8,128)(2,1)S(1)}, u32[]{:S(2)}, u32[]{:S(2)}) collective-permute-start(bf16[48,2048]{1,0:T(8,128)(2,1)S(1)} %get-tuple-element.84), channel_id=1, source_target_pairs={{0,8},{4,12},{8,0},{12,4},{16,24},{20,28},{24,16},{28,20},{1,9},{5... | collective-permute-start | bytes 589832 | tf_op jit(solution)/shard_map/ppermute | solution.py:192
  31.1 6.2 %collective-permute-start.7 = (bf16[48,2048]{1,0:T(8,128)(2,1)S(1)}, bf16[48,2048]{1,0:T(8,128)(2,1)S(1)}, u32[]{:S(2)}, u32[]{:S(2)}) collective-permute-start(bf16[48,2048]{1,0:T(8,128)(2,1)S(1)} %get-tuple-element.88), channel_id=1, source_target_pairs={{0,16},{4,20},{8,24},{12,28},{16,0},{20,4},{24,8},{28,12},{1,17},{... | collective-permute-start | bytes 589832 | tf_op jit(solution)/shard_map/ppermute | solution.py:192
  37.3 11.1 %collective-permute-start.13 = (bf16[96,2048]{1,0:T(8,128)(2,1)S(1)}, bf16[96,2048]{1,0:T(8,128)(2,1)S(1)}, u32[]{:S(2)}, u32[]{:S(2)}) collective-permute-start(bf16[96,2048]{1,0:T(8,128)(2,1)S(1)} %pad_maximum_fusion.6), channel_id=1, source_target_pairs={{0,8},{4,12},{8,0},{12,4},{16,24},{20,28},{24,16},{28,20},{1,9},{5... | collective-permute-start | bytes 1179656 | tf_op jit(solution)/shard_map/ppermute | solution.py:192
  37.5 11.9 %collective-permute-start.12 = (bf16[96,2048]{1,0:T(8,128)(2,1)S(1)}, bf16[96,2048]{1,0:T(8,128)(2,1)S(1)}, u32[]{:S(2)}, u32[]{:S(2)}) collective-permute-start(bf16[96,2048]{1,0:T(8,128)(2,1)S(1)} %pad_maximum_fusion.5), channel_id=1, source_target_pairs={{0,16},{4,20},{8,24},{12,28},{16,0},{20,4},{24,8},{28,12},{1,17},{... | collective-permute-start | bytes 1179656 | tf_op jit(solution)/shard_map/ppermute | solution.py:192
  41.6 15.0 %collective-permute-start.10 = (bf16[96,2048]{1,0:T(8,128)(2,1)S(1)}, bf16[96,2048]{1,0:T(8,128)(2,1)S(1)}, u32[]{:S(2)}, u32[]{:S(2)}) collective-permute-start(bf16[96,2048]{1,0:T(8,128)(2,1)S(1)} %get-tuple-element.76), channel_id=1, source_target_pairs={{0,16},{4,20},{8,24},{12,28},{16,0},{20,4},{24,8},{28,12},{1,17},{... | collective-permute-start | bytes 1179656 | tf_op jit(solution)/shard_map/ppermute | solution.py:192
  41.8 15.1 %collective-permute-start.11 = (bf16[96,2048]{1,0:T(8,128)(2,1)S(1)}, bf16[96,2048]{1,0:T(8,128)(2,1)S(1)}, u32[]{:S(2)}, u32[]{:S(2)}) collective-permute-start(bf16[96,2048]{1,0:T(8,128)(2,1)S(1)} %get-tuple-element.77), channel_id=1, source_target_pairs={{0,8},{4,12},{8,0},{12,4},{16,24},{20,28},{24,16},{28,20},{1,9},{5... | collective-permute-start | bytes 1179656 | tf_op jit(solution)/shard_map/ppermute | solution.py:192
  54.4 1.9 %collective-permute-start.14 = (f32[1,2048]{1,0:T(1,128)S(1)}, f32[1,2048]{1,0:T(1,128)S(1)}, u32[]{:S(2)}, u32[]{:S(2)}) collective-permute-start(f32[1,2048]{1,0:T(1,128)S(1)} %add.52), channel_id=1, source_target_pairs={{0,4},{4,0},{8,12},{12,8},{16,20},{20,16},{24,28},{28,24},{1,5},{5... | collective-permute-start | bytes 24584 | tf_op jit(solution)/shard_map/ppermute | solution.py:192
  54.5 11.6 %collective-permute-start.20 = (bf16[96,2048]{1,0:T(8,128)(2,1)S(1)}, bf16[96,2048]{1,0:T(8,128)(2,1)S(1)}, u32[]{:S(2)}, u32[]{:S(2)}) collective-permute-start(bf16[96,2048]{1,0:T(8,128)(2,1)S(1)} %get-tuple-element.102), channel_id=1, source_target_pairs={{0,16},{4,20},{8,24},{12,28},{16,0},{20,4},{24,8},{28,12},{1,17},{... | collective-permute-start | bytes 1179656 | tf_op jit(solution)/shard_map/ppermute | solution.py:192
  56.1 15.0 %collective-permute-start.17 = (bf16[384,512]{1,0:T(8,128)(2,1)S(1)}, bf16[384,512]{1,0:T(8,128)(2,1)S(1)}, u32[]{:S(2)}, u32[]{:S(2)}) collective-permute-start(bf16[384,512]{1,0:T(8,128)(2,1)S(1)} %pad_maximum_fusion.8), channel_id=1, source_target_pairs={{0,4},{4,0},{8,12},{12,8},{16,20},{20,16},{24,28},{28,24},{1,5},{5... | collective-permute-start | bytes 1179656 | tf_op jit(solution)/shard_map/ppermute | solution.py:192
  56.3 2.1 %collective-permute-start.23 = (bf16[384,512]{1,0:T(8,128)(2,1)S(1)}, bf16[384,512]{1,0:T(8,128)(2,1)S(1)}, u32[]{:S(2)}, u32[]{:S(2)}) collective-permute-start(bf16[384,512]{1,0:T(8,128)(2,1)S(1)} %pad_maximum_fusion.10), channel_id=1, source_target_pairs={{0,4},{4,0},{8,12},{12,8},{16,20},{20,16},{24,28},{28,24},{1,5},{5... | collective-permute-start | bytes 1179656 | tf_op jit(solution)/shard_map/ppermute | solution.py:192
  56.6 4.0 %collective-permute-start.22 = (bf16[384,2048]{1,0:T(8,128)(2,1)S(1)}, bf16[384,2048]{1,0:T(8,128)(2,1)S(1)}, u32[]{:S(2)}, u32[]{:S(2)}) collective-permute-start(bf16[384,2048]{1,0:T(8,128)(2,1)S(1)} %get-tuple-element.127.left_a), channel_id=1, source_target_pairs={{0,4},{4,0},{8,12},{12,8},{16,20},{20,16},{24,28},{28,24},{1,5},{5... | collective-permute-start | bytes 4718600 | tf_op jit(solution)/shard_map/ppermute | solution.py:192
  57.1 12.7 %collective-permute-start.21 = (bf16[104,2048]{1,0:T(8,128)(2,1)S(1)}, bf16[104,2048]{1,0:T(8,128)(2,1)S(1)}, u32[]{:S(2)}, u32[]{:S(2)}) collective-permute-start(bf16[104,2048]{1,0:T(8,128)(2,1)S(1)} %pad_maximum_fusion.2), channel_id=1, source_target_pairs={{0,8},{4,12},{8,0},{12,4},{16,24},{20,28},{24,16},{28,20},{1,9},{5... | collective-permute-start | bytes 1277960 | tf_op jit(solution)/shard_map/ppermute | solution.py:192
  58.4 13.7 %collective-permute-start.18 = (bf16[384,2048]{1,0:T(8,128)(2,1)S(1)}, bf16[384,2048]{1,0:T(8,128)(2,1)S(1)}, u32[]{:S(2)}, u32[]{:S(2)}) collective-permute-start(bf16[384,2048]{1,0:T(8,128)(2,1)S(1)} %constant_dynamic-update-slice_fusion.7.right_a), channel_id=1, source_target_pairs={{0,4},{4,0},{8,12},{12,8},{16,20},{20,16},{24,28},{28,24},{1,5},{5... | collective-permute-start | bytes 4718600 | tf_op jit(solution)/shard_map/ppermute | solution.py:192
  60.6 14.8 %collective-permute-start.15 = (bf16[48,2048]{1,0:T(8,128)(2,1)S(1)}, bf16[48,2048]{1,0:T(8,128)(2,1)S(1)}, u32[]{:S(2)}, u32[]{:S(2)}) collective-permute-start(bf16[48,2048]{1,0:T(8,128)(2,1)S(1)} %slice.227), channel_id=1, source_target_pairs={{0,8},{4,12},{8,0},{12,4},{16,24},{20,28},{24,16},{28,20},{1,9},{5... | collective-permute-start | bytes 589832 | tf_op jit(solution)/shard_map/ppermute | solution.py:192
  66.1 9.4 %collective-permute-start.16 = (bf16[48,2048]{1,0:T(8,128)(2,1)S(1)}, bf16[48,2048]{1,0:T(8,128)(2,1)S(1)}, u32[]{:S(2)}, u32[]{:S(2)}) collective-permute-start(bf16[48,2048]{1,0:T(8,128)(2,1)S(1)} %fusion.6), channel_id=1, source_target_pairs={{0,16},{4,20},{8,24},{12,28},{16,0},{20,4},{24,8},{28,12},{1,17},{... | collective-permute-start | bytes 589832 | tf_op jit(solution)/shard_map/ppermute | solution.py:192
  70.0 8.1 %collective-permute-start.24 = (bf16[48,2048]{1,0:T(8,128)(2,1)S(1)}, bf16[48,2048]{1,0:T(8,128)(2,1)S(1)}, u32[]{:S(2)}, u32[]{:S(2)}) collective-permute-start(bf16[48,2048]{1,0:T(8,128)(2,1)S(1)} %slice.226), channel_id=1, source_target_pairs={{0,8},{4,12},{8,0},{12,4},{16,24},{20,28},{24,16},{28,20},{1,9},{5... | collective-permute-start | bytes 589832 | tf_op jit(solution)/shard_map/ppermute | solution.py:192
  71.1 7.0 %collective-permute-start.25 = (bf16[56,2048]{1,0:T(8,128)(2,1)S(1)}, bf16[56,2048]{1,0:T(8,128)(2,1)S(1)}, u32[]{:S(2)}, u32[]{:S(2)}) collective-permute-start(bf16[56,2048]{1,0:T(8,128)(2,1)S(1)} %pad_maximum_fusion.11), channel_id=1, source_target_pairs={{0,16},{4,20},{8,24},{12,28},{16,0},{20,4},{24,8},{28,12},{1,17},{... | collective-permute-start | bytes 688136 | tf_op jit(solution)/shard_map/ppermute | solution.py:192
  75.6 19.9 %collective-permute-start.19 = (bf16[48,2048]{1,0:T(8,128)(2,1)S(1)}, bf16[48,2048]{1,0:T(8,128)(2,1)S(1)}, u32[]{:S(2)}, u32[]{:S(2)}) collective-permute-start(bf16[48,2048]{1,0:T(8,128)(2,1)S(1)} %pad_maximum_fusion.17), channel_id=1, source_target_pairs={{0,3},{1,0},{2,1},{3,2},{4,7},{5,4},{6,5},{7,6},{8,11},{9,8},{10,9... | collective-permute-start | bytes 589832 | tf_op jit(solution)/shard_map/ppermute | solution.py:195
  78.1 17.5 %copy-start.2 = (bf16[128,2048]{1,0:T(8,128)(2,1)S(1)}, bf16[128,2048]{1,0:T(8,128)(2,1)}, u32[]{:S(2)}) copy-start(bf16[128,2048]{1,0:T(8,128)(2,1)} %tok_ref.1) | copy-start | bytes 1572868
  78.1 17.5 %copy-start.4 = (s32[1,128]{1,0:T(1,128)S(1)}, s32[1,128]{1,0:T(1,128)}, u32[]{:S(2)}) copy-start(s32[1,128]{1,0:T(1,128)} %get-tuple-element.58.slot_ref) | copy-start | bytes 1540
  78.3 3.8 %collective-permute-start.28 = (f32[16,128]{1,0:T(8,128)S(1)}, f32[16,128]{1,0:T(8,128)S(1)}, u32[]{:S(2)}, u32[]{:S(2)}) collective-permute-start(f32[16,128]{1,0:T(8,128)S(1)} %bitcast.45), channel_id=1, source_target_pairs={{0,1},{1,0},{2,3},{3,2},{4,5},{5,4},{6,7},{7,6},{8,9},{9,8},{10,11... | collective-permute-start | bytes 24584 | tf_op jit(solution)/shard_map/ppermute | solution.py:357
  79.1 16.4 %collective-permute-start.26 = (bf16[48,2048]{1,0:T(8,128)(2,1)S(1)}, bf16[48,2048]{1,0:T(8,128)(2,1)S(1)}, u32[]{:S(2)}, u32[]{:S(2)}) collective-permute-start(bf16[48,2048]{1,0:T(8,128)(2,1)S(1)} %pad_maximum_fusion.18), channel_id=1, source_target_pairs={{0,2},{1,3},{2,0},{3,1},{4,6},{5,7},{6,4},{7,5},{8,10},{9,11},{10,... | collective-permute-start | bytes 589832 | tf_op jit(solution)/shard_map/ppermute | solution.py:195
  82.1 12.8 %collective-permute-start.29 = (f32[16,128]{1,0:T(8,128)S(1)}, f32[16,128]{1,0:T(8,128)S(1)}, u32[]{:S(2)}, u32[]{:S(2)}) collective-permute-start(f32[16,128]{1,0:T(8,128)S(1)} %add.66), channel_id=1, source_target_pairs={{0,2},{1,3},{2,0},{3,1},{4,6},{5,7},{6,4},{7,5},{8,10},{9,11},{10,... | collective-permute-start | bytes 24584 | tf_op jit(solution)/shard_map/ppermute | solution.py:357
  83.4 12.1 %collective-permute-start.27 = (bf16[48,2048]{1,0:T(8,128)(2,1)S(1)}, bf16[48,2048]{1,0:T(8,128)(2,1)S(1)}, u32[]{:S(2)}, u32[]{:S(2)}) collective-permute-start(bf16[48,2048]{1,0:T(8,128)(2,1)S(1)} %pad_maximum_fusion.19), channel_id=1, source_target_pairs={{0,1},{1,2},{2,3},{3,0},{4,5},{5,6},{6,7},{7,4},{8,9},{9,10},{10,1... | collective-permute-start | bytes 589832 | tf_op jit(solution)/shard_map/ppermute | solution.py:195
  (6 other events, 37.6 us)

commit v6 on v5

--- a/solution.py
+++ b/solution.py
@@ -79,7 +79,7 @@
     ahead = id_ref[...] - lax.axis_index("exp").astype(jnp.int32)
     ahead = jnp.where(ahead < 0, ahead + groups, ahead)
     slots = jnp.where(ranks < capacity, ahead * capacity + ranks, -1)
-    slot_ref[...] = slots
+    slot_ref[...] = jnp.where(slots < 0, -2 * groups * capacity, ahead * 2 * capacity + ranks)
     copies[1].wait()
     copies[2].wait()
     wide = tok_ref[...].astype(f32)
@@ -159,13 +159,17 @@
 def token_kernel(capacity, slot_ref, tok_ref, gain_ref, *refs):
     blocks, mixed_ref, grad_ref = refs[:-2], refs[-2], refs[-1]
     count = slot_ref.shape[1]
-    rows = lax.broadcasted_iota(jnp.int32, (2 * capacity, count), 0)
-    mixed, d_normed = 0.0, 0.0
-    for k, ref in enumerate(blocks):
-        places = block_places(slot_ref[...], k, capacity)
-        block = ref[...]
-        mixed += mm(jnp.where(rows == places, 1.0, 0.0).astype(bf16), block, TN)
-        d_normed += mm(jnp.where(rows == places + capacity, 1.0, 0.0).astype(bf16), block, TN)
+    wanted = jnp.concatenate([slot_ref[...], slot_ref[...] + capacity], axis=1)
+    if 2 * capacity % 16:
+        parts = [ref[...] for ref in blocks]
+    else:
+        parts = [jnp.concatenate([ref[...] for ref in blocks], axis=0)]
+    found, start = 0.0, 0
+    for part in parts:
+        rows = lax.broadcasted_iota(jnp.int32, (part.shape[0], 2 * count), 0) + start
+        found += mm(jnp.where(rows == wanted, 1.0, 0.0).astype(bf16), part, TN)
+        start += part.shape[0]
+    mixed, d_normed = found[:count], found[count:]
     mixed_ref[...] = mixed.astype(bf16)
     wide = tok_ref[...].astype(f32)
     scales = lax.rsqrt(jnp.mean(wide * wide, axis=1, keepdims=True) + 1e-06)
@@ -357,13 +361,14 @@
         total = total + lax.ppermute(total, "exp", [(i, i ^ step) for i in range(groups)])
         step *= 2
     total = total.reshape(1, width)
-    grad_gain = (total / gain_row).reshape(width)
     mixed, grad_tokens = call(
         "tokens",
         functools.partial(token_kernel, capacity),
         [shaped((count, width))] * 2,
         (slot_row, tokens, gain_row, *home),
     )
+    total = after(total, grad_tokens)
+    grad_gain = (total / gain_row).reshape(width)
     return (mixed, grad_tokens, grad_up[None], grad_down[None], grad_gain)
 
 

time: 98 us -> 97.3 us (level)
  waiting for transfers between devices: 34.9 us -> 36.5 us
  starting transfers between devices: 34.6 us -> 33.1 us
    ppermute x6, starting transfers between devices: 11.9 us -> 10.3 us  [shift(): lax.ppermute(x, 'exp', [(i, (i + k) % groups) for i in range(groups)])]
    ppermute x2, waiting for transfers between devices: 10.1 us -> 11.7 us  [local(): lax.ppermute(total, 'exp', [(i, i ^ step) for i in range(groups)])]
where the time goes in v6:
time: 97.3 us; the launch traced here: 97 us
  waiting for transfers between devices  36.5 us (38%)
  starting transfers between devices  33.1 us (34%)
  Pallas kernels  20.2 us (21%)
  local copies, waits for them, and re-layouts  4.31 us (4%)
  other arithmetic  1.79 us (2%)
  between operations  1.24 us (1%)
    ppermute x22, starting transfers between devices, swap(): return lax.ppermute(x, 'rep', [(i, i ^ bit) for i in range(copies)])  20.5 us
    pallas_call x9, Pallas kernels, call(): pl.pallas_call(kernel, name=name, out_shape=out_shape, in_specs=[pl.Block...  20.2 us
    ppermute x22, waiting for transfers between devices, swap(): return lax.ppermute(x, 'rep', [(i, i ^ bit) for i in range(copies)])  17.6 us
    ppermute x2, waiting for transfers between devices, local(): lax.ppermute(total, 'exp', [(i, i ^ step) for i in range(groups)])  11.7 us
    ppermute x6, starting transfers between devices, shift(): lax.ppermute(x, 'exp', [(i, (i + k) % groups) for i in range(groups)])  10.3 us
    ppermute x6, waiting for transfers between devices, shift(): lax.ppermute(x, 'exp', [(i, (i + k) % groups) for i in range(groups)])  7.26 us
    unnamed x29, local copies, waits for them, and re-layouts  4.04 us
    ppermute x2, starting transfers between devices, local(): lax.ppermute(total, 'exp', [(i, i ^ step) for i in range(groups)])  2.31 us
  transfers between devices with their start and end apart: 30, of which 14 were waited for; matrix products, arithmetic and copies ran while one was open for 2% of the time, Pallas kernels for 16%

profile of v6, /device:TPU:0, one launch (start us, length us, event | category | flops | bytes accessed | tf_op | source)
XLA Modules:
  0.0 97.0 jit_solution(11757419117966219607)
XLA Ops:
  0.6 2.8 %place.1 = (s32[1,128]{1,0:T(1,128)}, bf16[48,2048]{1,0:T(8,128)(2,1)}, bf16[48,2048]{1,0:T(8,128)(2,1)}, bf16[48,2048]{1,0:T(8,128)(2,1)}, bf16[48,2048]{1,0:T(8,128)(2,1)}) custom-call(bf16[128,2048]{1,0:T(8,128)(2,1)} %tok_ref.1, s32[1,128]{1,0:T(1,128)} %bitcast.50, f32[1,2048]{1,0:T(1,128)} %bitcast.37, bf16[128,2048]{1,0:T(8,128)(2,1)} %cot_in.1), custom_call_target="tpu_custom_call" | custom-call | tf_op jit(solution)/shard_map/place/pallas_call | solution.py:39
  3.5 3.1 %collective-permute-start = (bf16[48,2048]{1,0:T(8,128)(2,1)}, bf16[48,2048]{1,0:T(8,128)(2,1)S(1)}, u32[]{:S(2)}, u32[]{:S(2)}) collective-permute-start(bf16[48,2048]{1,0:T(8,128)(2,1)} %get-tuple-element.61), channel_id=1, source_target_pairs={{0,1},{1,2},{2,3},{3,0},{4,5},{5,6},{6,7},{7,4},{8,9},{9,10},{10,1... | collective-permute-start | bytes 589832 | tf_op jit(solution)/shard_map/ppermute | solution.py:199
  6.6 1.6 %copy-done = bf16[1,2048,512]{2,1,0:T(8,128)(2,1)S(1)} copy-done((bf16[1,2048,512]{2,1,0:T(8,128)(2,1)S(1)}, bf16[1,2048,512]{2,1,0:T(8,128)(2,1)}, u32[]{:S(2)}) %copy-start) | copy-done | bytes 2097176
  8.1 1.6 %copy-done.1 = bf16[1,512,2048]{2,1,0:T(8,128)(2,1)S(1)} copy-done((bf16[1,512,2048]{2,1,0:T(8,128)(2,1)S(1)}, bf16[1,512,2048]{2,1,0:T(8,128)(2,1)}, u32[]{:S(2)}) %copy-start.1) | copy-done | bytes 2097176
  10.7 3.0 %collective-permute-done = bf16[48,2048]{1,0:T(8,128)(2,1)S(1)} collective-permute-done((bf16[48,2048]{1,0:T(8,128)(2,1)}, bf16[48,2048]{1,0:T(8,128)(2,1)S(1)}, u32[]{:S(2)}, u32[]{:S(2)}) %collective-permute-start) | collective-permute-done | bytes 196640 | tf_op jit(solution)/shard_map/ppermute | solution.py:199
  14.5 1.6 %collective-permute-start.1 = (bf16[48,2048]{1,0:T(8,128)(2,1)S(1)}, bf16[48,2048]{1,0:T(8,128)(2,1)S(1)}, u32[]{:S(2)}, u32[]{:S(2)}) collective-permute-start(bf16[48,2048]{1,0:T(8,128)(2,1)S(1)} %pad_maximum_fusion.12), channel_id=1, source_target_pairs={{0,8},{4,12},{8,0},{12,4},{16,24},{20,28},{24,16},{28,20},{1,9},{5... | collective-permute-start | bytes 589832 | tf_op jit(solution)/shard_map/ppermute | solution.py:196
  16.1 1.6 %collective-permute-start.4 = (bf16[48,2048]{1,0:T(8,128)(2,1)S(1)}, bf16[48,2048]{1,0:T(8,128)(2,1)S(1)}, u32[]{:S(2)}, u32[]{:S(2)}) collective-permute-start(bf16[48,2048]{1,0:T(8,128)(2,1)S(1)} %pad_maximum_fusion.13), channel_id=1, source_target_pairs={{0,16},{4,20},{8,24},{12,28},{16,0},{20,4},{24,8},{28,12},{1,17},{... | collective-permute-start | bytes 589832 | tf_op jit(solution)/shard_map/ppermute | solution.py:196
  17.6 2.6 %collective-permute-done.1 = bf16[48,2048]{1,0:T(8,128)(2,1)S(1)} collective-permute-done((bf16[48,2048]{1,0:T(8,128)(2,1)S(1)}, bf16[48,2048]{1,0:T(8,128)(2,1)S(1)}, u32[]{:S(2)}, u32[]{:S(2)}) %collective-permute-start.1) | collective-permute-done | bytes 196640 | tf_op jit(solution)/shard_map/ppermute | solution.py:196
  20.2 1.6 %collective-permute-start.2 = (bf16[96,2048]{1,0:T(8,128)(2,1)S(1)}, bf16[96,2048]{1,0:T(8,128)(2,1)S(1)}, u32[]{:S(2)}, u32[]{:S(2)}) collective-permute-start(bf16[96,2048]{1,0:T(8,128)(2,1)S(1)} %pad_maximum_fusion.3), channel_id=1, source_target_pairs={{0,16},{4,20},{8,24},{12,28},{16,0},{20,4},{24,8},{28,12},{1,17},{... | collective-permute-start | bytes 1179656 | tf_op jit(solution)/shard_map/ppermute | solution.py:196
  24.8 4.3 %collective-permute-done.5 = bf16[48,2048]{1,0:T(8,128)(2,1)S(1)} collective-permute-done((bf16[48,2048]{1,0:T(8,128)(2,1)S(1)}, bf16[48,2048]{1,0:T(8,128)(2,1)S(1)}, u32[]{:S(2)}, u32[]{:S(2)}) %collective-permute-start.5) | collective-permute-done | bytes 196640 | tf_op jit(solution)/shard_map/ppermute | solution.py:199
  29.2 1.9 %collective-permute-start.6 = (bf16[48,2048]{1,0:T(8,128)(2,1)S(1)}, bf16[48,2048]{1,0:T(8,128)(2,1)S(1)}, u32[]{:S(2)}, u32[]{:S(2)}) collective-permute-start(bf16[48,2048]{1,0:T(8,128)(2,1)S(1)} %get-tuple-element.85), channel_id=1, source_target_pairs={{0,8},{4,12},{8,0},{12,4},{16,24},{20,28},{24,16},{28,20},{1,9},{5... | collective-permute-start | bytes 589832 | tf_op jit(solution)/shard_map/ppermute | solution.py:196
  31.1 1.5 %collective-permute-start.7 = (bf16[48,2048]{1,0:T(8,128)(2,1)S(1)}, bf16[48,2048]{1,0:T(8,128)(2,1)S(1)}, u32[]{:S(2)}, u32[]{:S(2)}) collective-permute-start(bf16[48,2048]{1,0:T(8,128)(2,1)S(1)} %get-tuple-element.89), channel_id=1, source_target_pairs={{0,16},{4,20},{8,24},{12,28},{16,0},{20,4},{24,8},{28,12},{1,17},{... | collective-permute-start | bytes 589832 | tf_op jit(solution)/shard_map/ppermute | solution.py:196
  33.4 2.3 %hidden.2 = (bf16[192,512]{1,0:T(8,128)(2,1)S(1)}, bf16[192,512]{1,0:T(8,128)(2,1)S(1)}, bf16[192,512]{1,0:T(8,128)(2,1)S(1)}, bf16[192,512]{1,0:T(8,128)(2,1)S(1)}) custom-call(bf16[192,2048]{1,0:T(8,128)(2,1)S(1)} %pad_maximum_fusion.in_ref, bf16[192,2048]{1,0:T(8,128)(2,1)S(1)} %get-tuple-element.118.cot_ref, bf16[2048,512]{1,0:T(8,128)(2,1)S(1)} %bitcast.28, ...), custom_call_target="tpu_custom_call" | custom-call | flops 1610612736 | bytes 8388608 | tf_op jit(solution)/shard_map/hidden/pallas_call | solution.py:39
  35.7 1.6 %collective-permute-done.7 = bf16[48,2048]{1,0:T(8,128)(2,1)S(1)} collective-permute-done((bf16[48,2048]{1,0:T(8,128)(2,1)S(1)}, bf16[48,2048]{1,0:T(8,128)(2,1)S(1)}, u32[]{:S(2)}, u32[]{:S(2)}) %collective-permute-start.7) | collective-permute-done | bytes 196640 | tf_op jit(solution)/shard_map/ppermute | solution.py:196
  37.5 1.9 %collective-permute-start.12 = (bf16[96,2048]{1,0:T(8,128)(2,1)S(1)}, bf16[96,2048]{1,0:T(8,128)(2,1)S(1)}, u32[]{:S(2)}, u32[]{:S(2)}) collective-permute-start(bf16[96,2048]{1,0:T(8,128)(2,1)S(1)} %pad_maximum_fusion.5), channel_id=1, source_target_pairs={{0,16},{4,20},{8,24},{12,28},{16,0},{20,4},{24,8},{28,12},{1,17},{... | collective-permute-start | bytes 1179656 | tf_op jit(solution)/shard_map/ppermute | solution.py:196
  39.4 2.2 %rows.2 = (f32[1,2048]{1,0:T(1,128)S(1)}, f32[96,2048]{1,0:T(8,128)S(1)}, bf16[96,2048]{1,0:T(8,128)(2,1)S(1)}, f32[96,2048]{1,0:T(8,128)S(1)}, bf16[96,2048]{1,0:T(8,128)(2,1)S(1)}) custom-call(bf16[192,2048]{1,0:T(8,128)(2,1)S(1)} %pad_maximum_fusion.in_ref, bf16[192,512]{1,0:T(8,128)(2,1)S(1)} %get-tuple-element.72.hid_a, ...), custom_call_target="tpu_custom_call" | custom-call | flops 1610612736 | bytes 8388608 | tf_op jit(solution)/shard_map/rows/pallas_call | solution.py:39
  41.8 2.0 %collective-permute-start.11 = (bf16[96,2048]{1,0:T(8,128)(2,1)S(1)}, bf16[96,2048]{1,0:T(8,128)(2,1)S(1)}, u32[]{:S(2)}, u32[]{:S(2)}) collective-permute-start(bf16[96,2048]{1,0:T(8,128)(2,1)S(1)} %get-tuple-element.78), channel_id=1, source_target_pairs={{0,8},{4,12},{8,0},{12,4},{16,24},{20,28},{24,16},{28,20},{1,9},{5... | collective-permute-start | bytes 1179656 | tf_op jit(solution)/shard_map/ppermute | solution.py:196
  43.8 4.5 %collective-permute-done.13 = bf16[96,2048]{1,0:T(8,128)(2,1)S(1)} collective-permute-done((bf16[96,2048]{1,0:T(8,128)(2,1)S(1)}, bf16[96,2048]{1,0:T(8,128)(2,1)S(1)}, u32[]{:S(2)}, u32[]{:S(2)}) %collective-permute-start.13) | collective-permute-done | bytes 393248 | tf_op jit(solution)/shard_map/ppermute | solution.py:196
  49.8 2.3 %hidden.3 = (bf16[192,512]{1,0:T(8,128)(2,1)S(1)}, bf16[192,512]{1,0:T(8,128)(2,1)S(1)}, bf16[192,512]{1,0:T(8,128)(2,1)S(1)}, bf16[192,512]{1,0:T(8,128)(2,1)S(1)}) custom-call(bf16[192,2048]{1,0:T(8,128)(2,1)S(1)} %get-tuple-element.130.in_ref, bf16[192,2048]{1,0:T(8,128)(2,1)S(1)} %pad_maximum_fusion.1.cot_ref, bf16[2048,512]{1,0:T(8,128)(2,1)S(1)} %bitcast.30, ...), custom_call_target="tpu_custom_call" | custom-call | flops 1610612736 | bytes 8388608 | tf_op jit(solution)/shard_map/hidden/pallas_call | solution.py:39
  52.2 2.2 %rows.3 = (f32[1,2048]{1,0:T(1,128)S(1)}, f32[96,2048]{1,0:T(8,128)S(1)}, bf16[96,2048]{1,0:T(8,128)(2,1)S(1)}, f32[96,2048]{1,0:T(8,128)S(1)}, bf16[96,2048]{1,0:T(8,128)(2,1)S(1)}) custom-call(bf16[192,2048]{1,0:T(8,128)(2,1)S(1)} %get-tuple-element.130.in_ref, bf16[192,512]{1,0:T(8,128)(2,1)S(1)} %get-tuple-element.93.hid_a, ...), custom_call_target="tpu_custom_call" | custom-call | flops 1610612736 | bytes 8388608 | tf_op jit(solution)/shard_map/rows/pallas_call | solution.py:39
  54.5 1.6 %collective-permute-start.20 = (bf16[96,2048]{1,0:T(8,128)(2,1)S(1)}, bf16[96,2048]{1,0:T(8,128)(2,1)S(1)}, u32[]{:S(2)}, u32[]{:S(2)}) collective-permute-start(bf16[96,2048]{1,0:T(8,128)(2,1)S(1)} %get-tuple-element.103), channel_id=1, source_target_pairs={{0,16},{4,20},{8,24},{12,28},{16,0},{20,4},{24,8},{28,12},{1,17},{... | collective-permute-start | bytes 1179656 | tf_op jit(solution)/shard_map/ppermute | solution.py:196
  58.6 2.0 %collective-permute-done.22.left_b = bf16[384,2048]{1,0:T(8,128)(2,1)S(1)} collective-permute-done((bf16[384,2048]{1,0:T(8,128)(2,1)S(1)}, bf16[384,2048]{1,0:T(8,128)(2,1)S(1)}, u32[]{:S(2)}, u32[]{:S(2)}) %collective-permute-start.22) | collective-permute-done | bytes 1572896 | tf_op jit(solution)/shard_map/ppermute | solution.py:196
  61.5 3.2 %grad_up.1 = bf16[2048,512]{1,0:T(8,128)(2,1)} custom-call(bf16[384,2048]{1,0:T(8,128)(2,1)S(1)} %get-tuple-element.129.left_a, bf16[384,2048]{1,0:T(8,128)(2,1)S(1)} %collective-permute-done.22.left_b, bf16[384,512]{1,0:T(8,128)(2,1)S(1)} %pad_maximum_fusion.9.right_a, bf16[384,512]{1,0:T(8,128)(2,1)S(1)} %collective-permute-done.23.right_b), custom_call_target="tpu_custom_call" | custom-call | flops 805306368 | bytes 8388608 | tf_op jit(solution)/shard_map/grad_up/pallas_call | solution.py:39
  64.6 1.4 %collective-permute-done.20 = bf16[96,2048]{1,0:T(8,128)(2,1)S(1)} collective-permute-done((bf16[96,2048]{1,0:T(8,128)(2,1)S(1)}, bf16[96,2048]{1,0:T(8,128)(2,1)S(1)}, u32[]{:S(2)}, u32[]{:S(2)}) %collective-permute-start.20) | collective-permute-done | bytes 393248 | tf_op jit(solution)/shard_map/ppermute | solution.py:196
  66.1 1.5 %collective-permute-start.16 = (bf16[48,2048]{1,0:T(8,128)(2,1)S(1)}, bf16[48,2048]{1,0:T(8,128)(2,1)S(1)}, u32[]{:S(2)}, u32[]{:S(2)}) collective-permute-start(bf16[48,2048]{1,0:T(8,128)(2,1)S(1)} %fusion.6), channel_id=1, source_target_pairs={{0,16},{4,20},{8,24},{12,28},{16,0},{20,4},{24,8},{28,12},{1,17},{... | collective-permute-start | bytes 589832 | tf_op jit(solution)/shard_map/ppermute | solution.py:196
  67.6 2.2 %collective-permute-done.21 = bf16[104,2048]{1,0:T(8,128)(2,1)S(1)} collective-permute-done((bf16[104,2048]{1,0:T(8,128)(2,1)S(1)}, bf16[104,2048]{1,0:T(8,128)(2,1)S(1)}, u32[]{:S(2)}, u32[]{:S(2)}) %collective-permute-start.21) | collective-permute-done | bytes 426016 | tf_op jit(solution)/shard_map/ppermute | solution.py:196
  72.1 3.4 %grad_down.1 = bf16[512,2048]{1,0:T(8,128)(2,1)} custom-call(bf16[384,512]{1,0:T(8,128)(2,1)S(1)} %pad_maximum_fusion.7.left_a, bf16[384,512]{1,0:T(8,128)(2,1)S(1)} %collective-permute-done.17.left_b, bf16[384,2048]{1,0:T(8,128)(2,1)S(1)} %constant_dynamic-update-slice_fusion.7.right_a, bf16[384,2048]{1,0:T(8,128)(2,1)S(1)} %collective-permute-done.18.right_b), custom_call_target="tpu_custom_call" | custom-call | flops 805306368 | bytes 8388608 | tf_op jit(solution)/shard_map/grad_down/pallas_call | solution.py:39
  75.6 2.4 %collective-permute-start.19 = (bf16[48,2048]{1,0:T(8,128)(2,1)S(1)}, bf16[48,2048]{1,0:T(8,128)(2,1)S(1)}, u32[]{:S(2)}, u32[]{:S(2)}) collective-permute-start(bf16[48,2048]{1,0:T(8,128)(2,1)S(1)} %pad_maximum_fusion.17), channel_id=1, source_target_pairs={{0,3},{1,0},{2,1},{3,2},{4,7},{5,4},{6,5},{7,6},{8,11},{9,8},{10,9... | collective-permute-start | bytes 589832 | tf_op jit(solution)/shard_map/ppermute | solution.py:199
  79.2 2.1 %collective-permute-start.26 = (bf16[48,2048]{1,0:T(8,128)(2,1)S(1)}, bf16[48,2048]{1,0:T(8,128)(2,1)S(1)}, u32[]{:S(2)}, u32[]{:S(2)}) collective-permute-start(bf16[48,2048]{1,0:T(8,128)(2,1)S(1)} %pad_maximum_fusion.18), channel_id=1, source_target_pairs={{0,2},{1,3},{2,0},{3,1},{4,6},{5,7},{6,4},{7,5},{8,10},{9,11},{10,... | collective-permute-start | bytes 589832 | tf_op jit(solution)/shard_map/ppermute | solution.py:199
  82.1 1.4 %collective-permute-start.29 = (f32[16,128]{1,0:T(8,128)S(1)}, f32[16,128]{1,0:T(8,128)S(1)}, u32[]{:S(2)}, u32[]{:S(2)}) collective-permute-start(f32[16,128]{1,0:T(8,128)S(1)} %add.66), channel_id=1, source_target_pairs={{0,2},{1,3},{2,0},{3,1},{4,6},{5,7},{6,4},{7,5},{8,10},{9,11},{10,... | collective-permute-start | bytes 24584 | tf_op jit(solution)/shard_map/ppermute | solution.py:361
  83.5 11.5 %collective-permute-done.29 = f32[16,128]{1,0:T(8,128)S(1)} collective-permute-done((f32[16,128]{1,0:T(8,128)S(1)}, f32[16,128]{1,0:T(8,128)S(1)}, u32[]{:S(2)}, u32[]{:S(2)}) %collective-permute-start.29) | collective-permute-done | bytes 8224 | tf_op jit(solution)/shard_map/ppermute | solution.py:361
  95.0 1.4 %tokens.1 = (bf16[128,2048]{1,0:T(8,128)(2,1)}, bf16[128,2048]{1,0:T(8,128)(2,1)}) custom-call(s32[1,128]{1,0:T(1,128)S(1)} %copy-done.4, bf16[128,2048]{1,0:T(8,128)(2,1)S(1)} %copy-done.2, f32[1,2048]{1,0:T(1,128)S(1)} %bitcast.38, bf16[48,2048]{1,0:T(8,128)(2,1)S(1)} %pad_maximum_fusion.16.refs_0_, bf16[48,2048]{1,0:T(8,128)(2,1)S(1)} %collective-permute-done.19.refs_1_, ...), custom_call_target="tpu_custom_call" | custom-call | tf_op jit(solution)/shard_map/tokens/pallas_call | solution.py:39
  (118 shorter events, 15.4 us)
Async XLA Ops:
  3.5 10.2 %collective-permute-start = (bf16[48,2048]{1,0:T(8,128)(2,1)}, bf16[48,2048]{1,0:T(8,128)(2,1)S(1)}, u32[]{:S(2)}, u32[]{:S(2)}) collective-permute-start(bf16[48,2048]{1,0:T(8,128)(2,1)} %get-tuple-element.61), channel_id=1, source_target_pairs={{0,1},{1,2},{2,3},{3,0},{4,5},{5,6},{6,7},{7,4},{8,9},{9,10},{10,1... | collective-permute-start | bytes 589832 | tf_op jit(solution)/shard_map/ppermute | solution.py:199
  10.1 23.3 %collective-permute-start.9 = (bf16[2048,1024]{1,0:T(8,128)(2,1)S(1)}, bf16[2048,1024]{1,0:T(8,128)(2,1)S(1)}, u32[]{:S(2)}, u32[]{:S(2)}) collective-permute-start(bf16[2048,1024]{1,0:T(8,128)(2,1)S(1)} %pack.1), channel_id=1, source_target_pairs={{0,4},{4,0},{8,12},{12,8},{16,20},{20,16},{24,28},{28,24},{1,5},{5... | collective-permute-start | bytes 12582920 | tf_op jit(solution)/shard_map/ppermute | solution.py:196
  13.7 11.1 %collective-permute-start.3 = (bf16[48,2048]{1,0:T(8,128)(2,1)S(1)}, bf16[48,2048]{1,0:T(8,128)(2,1)S(1)}, u32[]{:S(2)}, u32[]{:S(2)}) collective-permute-start(bf16[48,2048]{1,0:T(8,128)(2,1)S(1)} %copy-done.7), channel_id=1, source_target_pairs={{0,2},{1,3},{2,0},{3,1},{4,6},{5,7},{6,4},{7,5},{8,10},{9,11},{10,... | collective-permute-start | bytes 589832 | tf_op jit(solution)/shard_map/ppermute | solution.py:199
  14.5 5.7 %collective-permute-start.1 = (bf16[48,2048]{1,0:T(8,128)(2,1)S(1)}, bf16[48,2048]{1,0:T(8,128)(2,1)S(1)}, u32[]{:S(2)}, u32[]{:S(2)}) collective-permute-start(bf16[48,2048]{1,0:T(8,128)(2,1)S(1)} %pad_maximum_fusion.12), channel_id=1, source_target_pairs={{0,8},{4,12},{8,0},{12,4},{16,24},{20,28},{24,16},{28,20},{1,9},{5... | collective-permute-start | bytes 589832 | tf_op jit(solution)/shard_map/ppermute | solution.py:196
  16.1 7.1 %collective-permute-start.4 = (bf16[48,2048]{1,0:T(8,128)(2,1)S(1)}, bf16[48,2048]{1,0:T(8,128)(2,1)S(1)}, u32[]{:S(2)}, u32[]{:S(2)}) collective-permute-start(bf16[48,2048]{1,0:T(8,128)(2,1)S(1)} %pad_maximum_fusion.13), channel_id=1, source_target_pairs={{0,16},{4,20},{8,24},{12,28},{16,0},{20,4},{24,8},{28,12},{1,17},{... | collective-permute-start | bytes 589832 | tf_op jit(solution)/shard_map/ppermute | solution.py:196
  20.2 13.0 %collective-permute-start.2 = (bf16[96,2048]{1,0:T(8,128)(2,1)S(1)}, bf16[96,2048]{1,0:T(8,128)(2,1)S(1)}, u32[]{:S(2)}, u32[]{:S(2)}) collective-permute-start(bf16[96,2048]{1,0:T(8,128)(2,1)S(1)} %pad_maximum_fusion.3), channel_id=1, source_target_pairs={{0,16},{4,20},{8,24},{12,28},{16,0},{20,4},{24,8},{28,12},{1,17},{... | collective-permute-start | bytes 1179656 | tf_op jit(solution)/shard_map/ppermute | solution.py:196
  23.2 9.9 %collective-permute-start.8 = (bf16[96,2048]{1,0:T(8,128)(2,1)S(1)}, bf16[96,2048]{1,0:T(8,128)(2,1)S(1)}, u32[]{:S(2)}, u32[]{:S(2)}) collective-permute-start(bf16[96,2048]{1,0:T(8,128)(2,1)S(1)} %pad_maximum_fusion.4), channel_id=1, source_target_pairs={{0,8},{4,12},{8,0},{12,4},{16,24},{20,28},{24,16},{28,20},{1,9},{5... | collective-permute-start | bytes 1179656 | tf_op jit(solution)/shard_map/ppermute | solution.py:196
  23.4 5.7 %collective-permute-start.5 = (bf16[48,2048]{1,0:T(8,128)(2,1)S(1)}, bf16[48,2048]{1,0:T(8,128)(2,1)S(1)}, u32[]{:S(2)}, u32[]{:S(2)}) collective-permute-start(bf16[48,2048]{1,0:T(8,128)(2,1)S(1)} %copy-done.6), channel_id=1, source_target_pairs={{0,3},{1,0},{2,1},{3,2},{4,7},{5,4},{6,5},{7,6},{8,11},{9,8},{10,9... | collective-permute-start | bytes 589832 | tf_op jit(solution)/shard_map/ppermute | solution.py:199
  29.2 6.5 %collective-permute-start.6 = (bf16[48,2048]{1,0:T(8,128)(2,1)S(1)}, bf16[48,2048]{1,0:T(8,128)(2,1)S(1)}, u32[]{:S(2)}, u32[]{:S(2)}) collective-permute-start(bf16[48,2048]{1,0:T(8,128)(2,1)S(1)} %get-tuple-element.85), channel_id=1, source_target_pairs={{0,8},{4,12},{8,0},{12,4},{16,24},{20,28},{24,16},{28,20},{1,9},{5... | collective-permute-start | bytes 589832 | tf_op jit(solution)/shard_map/ppermute | solution.py:196
  31.1 6.2 %collective-permute-start.7 = (bf16[48,2048]{1,0:T(8,128)(2,1)S(1)}, bf16[48,2048]{1,0:T(8,128)(2,1)S(1)}, u32[]{:S(2)}, u32[]{:S(2)}) collective-permute-start(bf16[48,2048]{1,0:T(8,128)(2,1)S(1)} %get-tuple-element.89), channel_id=1, source_target_pairs={{0,16},{4,20},{8,24},{12,28},{16,0},{20,4},{24,8},{28,12},{1,17},{... | collective-permute-start | bytes 589832 | tf_op jit(solution)/shard_map/ppermute | solution.py:196
  37.3 11.1 %collective-permute-start.13 = (bf16[96,2048]{1,0:T(8,128)(2,1)S(1)}, bf16[96,2048]{1,0:T(8,128)(2,1)S(1)}, u32[]{:S(2)}, u32[]{:S(2)}) collective-permute-start(bf16[96,2048]{1,0:T(8,128)(2,1)S(1)} %pad_maximum_fusion.6), channel_id=1, source_target_pairs={{0,8},{4,12},{8,0},{12,4},{16,24},{20,28},{24,16},{28,20},{1,9},{5... | collective-permute-start | bytes 1179656 | tf_op jit(solution)/shard_map/ppermute | solution.py:196
  37.5 11.9 %collective-permute-start.12 = (bf16[96,2048]{1,0:T(8,128)(2,1)S(1)}, bf16[96,2048]{1,0:T(8,128)(2,1)S(1)}, u32[]{:S(2)}, u32[]{:S(2)}) collective-permute-start(bf16[96,2048]{1,0:T(8,128)(2,1)S(1)} %pad_maximum_fusion.5), channel_id=1, source_target_pairs={{0,16},{4,20},{8,24},{12,28},{16,0},{20,4},{24,8},{28,12},{1,17},{... | collective-permute-start | bytes 1179656 | tf_op jit(solution)/shard_map/ppermute | solution.py:196
  41.6 15.0 %collective-permute-start.10 = (bf16[96,2048]{1,0:T(8,128)(2,1)S(1)}, bf16[96,2048]{1,0:T(8,128)(2,1)S(1)}, u32[]{:S(2)}, u32[]{:S(2)}) collective-permute-start(bf16[96,2048]{1,0:T(8,128)(2,1)S(1)} %get-tuple-element.77), channel_id=1, source_target_pairs={{0,16},{4,20},{8,24},{12,28},{16,0},{20,4},{24,8},{28,12},{1,17},{... | collective-permute-start | bytes 1179656 | tf_op jit(solution)/shard_map/ppermute | solution.py:196
  41.8 15.1 %collective-permute-start.11 = (bf16[96,2048]{1,0:T(8,128)(2,1)S(1)}, bf16[96,2048]{1,0:T(8,128)(2,1)S(1)}, u32[]{:S(2)}, u32[]{:S(2)}) collective-permute-start(bf16[96,2048]{1,0:T(8,128)(2,1)S(1)} %get-tuple-element.78), channel_id=1, source_target_pairs={{0,8},{4,12},{8,0},{12,4},{16,24},{20,28},{24,16},{28,20},{1,9},{5... | collective-permute-start | bytes 1179656 | tf_op jit(solution)/shard_map/ppermute | solution.py:196
  54.4 1.9 %collective-permute-start.14 = (f32[1,2048]{1,0:T(1,128)S(1)}, f32[1,2048]{1,0:T(1,128)S(1)}, u32[]{:S(2)}, u32[]{:S(2)}) collective-permute-start(f32[1,2048]{1,0:T(1,128)S(1)} %add.52), channel_id=1, source_target_pairs={{0,4},{4,0},{8,12},{12,8},{16,20},{20,16},{24,28},{28,24},{1,5},{5... | collective-permute-start | bytes 24584 | tf_op jit(solution)/shard_map/ppermute | solution.py:196
  54.5 11.6 %collective-permute-start.20 = (bf16[96,2048]{1,0:T(8,128)(2,1)S(1)}, bf16[96,2048]{1,0:T(8,128)(2,1)S(1)}, u32[]{:S(2)}, u32[]{:S(2)}) collective-permute-start(bf16[96,2048]{1,0:T(8,128)(2,1)S(1)} %get-tuple-element.103), channel_id=1, source_target_pairs={{0,16},{4,20},{8,24},{12,28},{16,0},{20,4},{24,8},{28,12},{1,17},{... | collective-permute-start | bytes 1179656 | tf_op jit(solution)/shard_map/ppermute | solution.py:196
  56.1 15.0 %collective-permute-start.17 = (bf16[384,512]{1,0:T(8,128)(2,1)S(1)}, bf16[384,512]{1,0:T(8,128)(2,1)S(1)}, u32[]{:S(2)}, u32[]{:S(2)}) collective-permute-start(bf16[384,512]{1,0:T(8,128)(2,1)S(1)} %pad_maximum_fusion.8), channel_id=1, source_target_pairs={{0,4},{4,0},{8,12},{12,8},{16,20},{20,16},{24,28},{28,24},{1,5},{5... | collective-permute-start | bytes 1179656 | tf_op jit(solution)/shard_map/ppermute | solution.py:196
  56.3 2.1 %collective-permute-start.23 = (bf16[384,512]{1,0:T(8,128)(2,1)S(1)}, bf16[384,512]{1,0:T(8,128)(2,1)S(1)}, u32[]{:S(2)}, u32[]{:S(2)}) collective-permute-start(bf16[384,512]{1,0:T(8,128)(2,1)S(1)} %pad_maximum_fusion.10), channel_id=1, source_target_pairs={{0,4},{4,0},{8,12},{12,8},{16,20},{20,16},{24,28},{28,24},{1,5},{5... | collective-permute-start | bytes 1179656 | tf_op jit(solution)/shard_map/ppermute | solution.py:196
  56.6 4.0 %collective-permute-start.22 = (bf16[384,2048]{1,0:T(8,128)(2,1)S(1)}, bf16[384,2048]{1,0:T(8,128)(2,1)S(1)}, u32[]{:S(2)}, u32[]{:S(2)}) collective-permute-start(bf16[384,2048]{1,0:T(8,128)(2,1)S(1)} %get-tuple-element.129.left_a), channel_id=1, source_target_pairs={{0,4},{4,0},{8,12},{12,8},{16,20},{20,16},{24,28},{28,24},{1,5},{5... | collective-permute-start | bytes 4718600 | tf_op jit(solution)/shard_map/ppermute | solution.py:196
  57.1 12.7 %collective-permute-start.21 = (bf16[104,2048]{1,0:T(8,128)(2,1)S(1)}, bf16[104,2048]{1,0:T(8,128)(2,1)S(1)}, u32[]{:S(2)}, u32[]{:S(2)}) collective-permute-start(bf16[104,2048]{1,0:T(8,128)(2,1)S(1)} %pad_maximum_fusion.2), channel_id=1, source_target_pairs={{0,8},{4,12},{8,0},{12,4},{16,24},{20,28},{24,16},{28,20},{1,9},{5... | collective-permute-start | bytes 1277960 | tf_op jit(solution)/shard_map/ppermute | solution.py:196
  58.4 13.7 %collective-permute-start.18 = (bf16[384,2048]{1,0:T(8,128)(2,1)S(1)}, bf16[384,2048]{1,0:T(8,128)(2,1)S(1)}, u32[]{:S(2)}, u32[]{:S(2)}) collective-permute-start(bf16[384,2048]{1,0:T(8,128)(2,1)S(1)} %constant_dynamic-update-slice_fusion.7.right_a), channel_id=1, source_target_pairs={{0,4},{4,0},{8,12},{12,8},{16,20},{20,16},{24,28},{28,24},{1,5},{5... | collective-permute-start | bytes 4718600 | tf_op jit(solution)/shard_map/ppermute | solution.py:196
  60.6 14.8 %collective-permute-start.15 = (bf16[48,2048]{1,0:T(8,128)(2,1)S(1)}, bf16[48,2048]{1,0:T(8,128)(2,1)S(1)}, u32[]{:S(2)}, u32[]{:S(2)}) collective-permute-start(bf16[48,2048]{1,0:T(8,128)(2,1)S(1)} %slice.227), channel_id=1, source_target_pairs={{0,8},{4,12},{8,0},{12,4},{16,24},{20,28},{24,16},{28,20},{1,9},{5... | collective-permute-start | bytes 589832 | tf_op jit(solution)/shard_map/ppermute | solution.py:196
  66.1 9.4 %collective-permute-start.16 = (bf16[48,2048]{1,0:T(8,128)(2,1)S(1)}, bf16[48,2048]{1,0:T(8,128)(2,1)S(1)}, u32[]{:S(2)}, u32[]{:S(2)}) collective-permute-start(bf16[48,2048]{1,0:T(8,128)(2,1)S(1)} %fusion.6), channel_id=1, source_target_pairs={{0,16},{4,20},{8,24},{12,28},{16,0},{20,4},{24,8},{28,12},{1,17},{... | collective-permute-start | bytes 589832 | tf_op jit(solution)/shard_map/ppermute | solution.py:196
  70.0 8.0 %collective-permute-start.24 = (bf16[48,2048]{1,0:T(8,128)(2,1)S(1)}, bf16[48,2048]{1,0:T(8,128)(2,1)S(1)}, u32[]{:S(2)}, u32[]{:S(2)}) collective-permute-start(bf16[48,2048]{1,0:T(8,128)(2,1)S(1)} %slice.226), channel_id=1, source_target_pairs={{0,8},{4,12},{8,0},{12,4},{16,24},{20,28},{24,16},{28,20},{1,9},{5... | collective-permute-start | bytes 589832 | tf_op jit(solution)/shard_map/ppermute | solution.py:196
  71.1 6.9 %collective-permute-start.25 = (bf16[56,2048]{1,0:T(8,128)(2,1)S(1)}, bf16[56,2048]{1,0:T(8,128)(2,1)S(1)}, u32[]{:S(2)}, u32[]{:S(2)}) collective-permute-start(bf16[56,2048]{1,0:T(8,128)(2,1)S(1)} %pad_maximum_fusion.11), channel_id=1, source_target_pairs={{0,16},{4,20},{8,24},{12,28},{16,0},{20,4},{24,8},{28,12},{1,17},{... | collective-permute-start | bytes 688136 | tf_op jit(solution)/shard_map/ppermute | solution.py:196
  75.6 19.3 %collective-permute-start.19 = (bf16[48,2048]{1,0:T(8,128)(2,1)S(1)}, bf16[48,2048]{1,0:T(8,128)(2,1)S(1)}, u32[]{:S(2)}, u32[]{:S(2)}) collective-permute-start(bf16[48,2048]{1,0:T(8,128)(2,1)S(1)} %pad_maximum_fusion.17), channel_id=1, source_target_pairs={{0,3},{1,0},{2,1},{3,2},{4,7},{5,4},{6,5},{7,6},{8,11},{9,8},{10,9... | collective-permute-start | bytes 589832 | tf_op jit(solution)/shard_map/ppermute | solution.py:199
  78.1 16.9 %copy-start.2 = (bf16[128,2048]{1,0:T(8,128)(2,1)S(1)}, bf16[128,2048]{1,0:T(8,128)(2,1)}, u32[]{:S(2)}) copy-start(bf16[128,2048]{1,0:T(8,128)(2,1)} %tok_ref.1) | copy-start | bytes 1572868
  78.1 16.9 %copy-start.3 = (f32[2048]{0:T(1024)S(1)}, f32[2048]{0:T(1024)}, u32[]{:S(2)}) copy-start(f32[2048]{0:T(1024)} %param.8) | copy-start | bytes 24580
  78.2 3.8 %collective-permute-start.28 = (f32[16,128]{1,0:T(8,128)S(1)}, f32[16,128]{1,0:T(8,128)S(1)}, u32[]{:S(2)}, u32[]{:S(2)}) collective-permute-start(f32[16,128]{1,0:T(8,128)S(1)} %bitcast.47), channel_id=1, source_target_pairs={{0,1},{1,0},{2,3},{3,2},{4,5},{5,4},{6,7},{7,6},{8,9},{9,8},{10,11... | collective-permute-start | bytes 24584 | tf_op jit(solution)/shard_map/ppermute | solution.py:361
  79.2 15.8 %collective-permute-start.26 = (bf16[48,2048]{1,0:T(8,128)(2,1)S(1)}, bf16[48,2048]{1,0:T(8,128)(2,1)S(1)}, u32[]{:S(2)}, u32[]{:S(2)}) collective-permute-start(bf16[48,2048]{1,0:T(8,128)(2,1)S(1)} %pad_maximum_fusion.18), channel_id=1, source_target_pairs={{0,2},{1,3},{2,0},{3,1},{4,6},{5,7},{6,4},{7,5},{8,10},{9,11},{10,... | collective-permute-start | bytes 589832 | tf_op jit(solution)/shard_map/ppermute | solution.py:199
  81.3 13.6 %collective-permute-start.27 = (bf16[48,2048]{1,0:T(8,128)(2,1)S(1)}, bf16[48,2048]{1,0:T(8,128)(2,1)S(1)}, u32[]{:S(2)}, u32[]{:S(2)}) collective-permute-start(bf16[48,2048]{1,0:T(8,128)(2,1)S(1)} %pad_maximum_fusion.19), channel_id=1, source_target_pairs={{0,1},{1,2},{2,3},{3,0},{4,5},{5,6},{6,7},{7,4},{8,9},{9,10},{10,1... | collective-permute-start | bytes 589832 | tf_op jit(solution)/shard_map/ppermute | solution.py:199
  82.1 12.9 %collective-permute-start.29 = (f32[16,128]{1,0:T(8,128)S(1)}, f32[16,128]{1,0:T(8,128)S(1)}, u32[]{:S(2)}, u32[]{:S(2)}) collective-permute-start(f32[16,128]{1,0:T(8,128)S(1)} %add.66), channel_id=1, source_target_pairs={{0,2},{1,3},{2,0},{3,1},{4,6},{5,7},{6,4},{7,5},{8,10},{9,11},{10,... | collective-permute-start | bytes 24584 | tf_op jit(solution)/shard_map/ppermute | solution.py:361
  (6 other events, 37.7 us)

commit v7 on v6

--- a/solution.py
+++ b/solution.py
@@ -86,12 +86,15 @@
     scales = lax.rsqrt(jnp.mean(wide * wide, axis=1, keepdims=True) + 1e-06)
     both[:count] = (wide * scales * gain_ref[...]).astype(bf16)
     copies[3].wait()
-    rows = lax.broadcasted_iota(jnp.int32, (2 * capacity, 2 * count), 0)
-    for k in range(groups):
-        places = block_places(slots, k, capacity)
-        wanted = jnp.concatenate([places, places + capacity], axis=1)
-        placing = jnp.where(rows == wanted, 1.0, 0.0).astype(bf16)
-        sends[k][...] = mm(placing, both[...]).astype(bf16)
+    starts = jnp.where(slots < 0, -2 * groups * capacity, ahead * 2 * capacity + ranks)
+    wanted = jnp.concatenate([starts, starts + capacity], axis=1)
+    step = 2 * capacity
+    wide_step = step if step % 8 else groups * step
+    for first in range(0, groups * step, wide_step):
+        rows = lax.broadcasted_iota(jnp.int32, (wide_step, 2 * count), 0) + first
+        found = mm(jnp.where(rows == wanted, 1.0, 0.0).astype(bf16), both[...])
+        for at in range(0, wide_step, step):
+            sends[(first + at) // step][...] = found[at : at + step].astype(bf16)
 
 
 def pack_kernel(up_ref, down_ref, pack_ref):
@@ -320,7 +323,7 @@
     in_1, cot_1 = [ordered(held) for held in steps[-1]]
     acts_1 = hidden(in_1, cot_1)
     events = [ordered(held) for held in steps[0]]
-    arrived += [shift(after(blocks[k], events), k) for k in range(early + 1, groups)]
+    arrived += [shift(after(blocks[k], events[1]), k) for k in range(early + 1, groups)]
     steps = list(gather(start(1), {0: [ordered(held) for held in steps[0]], len(bits) - 1: (acts_1,)}))
     parts_1 = products(after(in_1, steps[-2]), acts_1)
     in_2, cot_2 = [ordered(held) for held in after(steps[-1], parts_1)]

time: 97.3 us -> 96.1 us (0.988)
    ppermute x2, starting transfers between devices: 2.31 us -> 0.55 us  [local(): lax.ppermute(total, 'exp', [(i, i ^ step) for i in range(groups)])]
    ppermute x6, waiting for transfers between devices: 7.26 us -> 6.11 us  [shift(): lax.ppermute(x, 'exp', [(i, (i + k) % groups) for i in range(groups)])]
  transfers between devices with their start and end apart: 30 -> 30, of which waited for: 14 -> 15; matrix products, arithmetic and copies ran while one was open for 2% -> 2% of each run, Pallas kernels for 16% -> 17%
where the time goes in v7:
time: 96.1 us; the launch traced here: 95.9 us
  waiting for transfers between devices  35.7 us (37%)
  starting transfers between devices  33 us (34%)
  Pallas kernels  19.8 us (21%)
  local copies, waits for them, and re-layouts  4.3 us (4%)
  other arithmetic  1.79 us (2%)
  between operations  1.22 us (1%)
    ppermute x22, starting transfers between devices, swap(): return lax.ppermute(x, 'rep', [(i, i ^ bit) for i in range(copies)])  21.3 us
    pallas_call x9, Pallas kernels, call(): pl.pallas_call(kernel, name=name, out_shape=out_shape, in_specs=[pl.Block...  19.8 us
    ppermute x22, waiting for transfers between devices, swap(): return lax.ppermute(x, 'rep', [(i, i ^ bit) for i in range(copies)])  17.5 us
    ppermute x2, waiting for transfers between devices, local(): lax.ppermute(total, 'exp', [(i, i ^ step) for i in range(groups)])  12.1 us
    ppermute x6, starting transfers between devices, shift(): lax.ppermute(x, 'exp', [(i, (i + k) % groups) for i in range(groups)])  11.2 us
    ppermute x6, waiting for transfers between devices, shift(): lax.ppermute(x, 'exp', [(i, (i + k) % groups) for i in range(groups)])  6.11 us
    unnamed x29, local copies, waits for them, and re-layouts  4.03 us
  transfers between devices with their start and end apart: 30, of which 15 were waited for; matrix products, arithmetic and copies ran while one was open for 2% of the time, Pallas kernels for 17%

profile of v7, /device:TPU:0, one launch (start us, length us, event | category | flops | bytes accessed | tf_op | source)
XLA Modules:
  0.0 95.9 jit_solution(3231269532242409194)
XLA Ops:
  0.6 2.5 %place.1 = (s32[1,128]{1,0:T(1,128)}, bf16[48,2048]{1,0:T(8,128)(2,1)}, bf16[48,2048]{1,0:T(8,128)(2,1)}, bf16[48,2048]{1,0:T(8,128)(2,1)}, bf16[48,2048]{1,0:T(8,128)(2,1)}) custom-call(bf16[128,2048]{1,0:T(8,128)(2,1)} %tok_ref.1, s32[1,128]{1,0:T(1,128)} %bitcast.50, f32[1,2048]{1,0:T(1,128)} %bitcast.37, bf16[128,2048]{1,0:T(8,128)(2,1)} %cot_in.1), custom_call_target="tpu_custom_call" | custom-call | tf_op jit(solution)/shard_map/place/pallas_call | solution.py:39
  3.2 3.1 %collective-permute-start = (bf16[48,2048]{1,0:T(8,128)(2,1)}, bf16[48,2048]{1,0:T(8,128)(2,1)S(1)}, u32[]{:S(2)}, u32[]{:S(2)}) collective-permute-start(bf16[48,2048]{1,0:T(8,128)(2,1)} %get-tuple-element.61), channel_id=1, source_target_pairs={{0,1},{1,2},{2,3},{3,0},{4,5},{5,6},{6,7},{7,4},{8,9},{9,10},{10,1... | collective-permute-start | bytes 589832 | tf_op jit(solution)/shard_map/ppermute | solution.py:202
  6.3 1.6 %copy-done = bf16[1,2048,512]{2,1,0:T(8,128)(2,1)S(1)} copy-done((bf16[1,2048,512]{2,1,0:T(8,128)(2,1)S(1)}, bf16[1,2048,512]{2,1,0:T(8,128)(2,1)}, u32[]{:S(2)}) %copy-start) | copy-done | bytes 2097176
  7.8 1.6 %copy-done.1 = bf16[1,512,2048]{2,1,0:T(8,128)(2,1)S(1)} copy-done((bf16[1,512,2048]{2,1,0:T(8,128)(2,1)S(1)}, bf16[1,512,2048]{2,1,0:T(8,128)(2,1)}, u32[]{:S(2)}) %copy-start.1) | copy-done | bytes 2097176
  10.4 3.0 %collective-permute-done = bf16[48,2048]{1,0:T(8,128)(2,1)S(1)} collective-permute-done((bf16[48,2048]{1,0:T(8,128)(2,1)}, bf16[48,2048]{1,0:T(8,128)(2,1)S(1)}, u32[]{:S(2)}, u32[]{:S(2)}) %collective-permute-start) | collective-permute-done | bytes 196640 | tf_op jit(solution)/shard_map/ppermute | solution.py:202
  14.2 1.6 %collective-permute-start.4 = (bf16[48,2048]{1,0:T(8,128)(2,1)S(1)}, bf16[48,2048]{1,0:T(8,128)(2,1)S(1)}, u32[]{:S(2)}, u32[]{:S(2)}) collective-permute-start(bf16[48,2048]{1,0:T(8,128)(2,1)S(1)} %pad_maximum_fusion.13), channel_id=1, source_target_pairs={{0,16},{4,20},{8,24},{12,28},{16,0},{20,4},{24,8},{28,12},{1,17},{... | collective-permute-start | bytes 589832 | tf_op jit(solution)/shard_map/ppermute | solution.py:199
  15.8 1.6 %collective-permute-start.1 = (bf16[48,2048]{1,0:T(8,128)(2,1)S(1)}, bf16[48,2048]{1,0:T(8,128)(2,1)S(1)}, u32[]{:S(2)}, u32[]{:S(2)}) collective-permute-start(bf16[48,2048]{1,0:T(8,128)(2,1)S(1)} %pad_maximum_fusion.12), channel_id=1, source_target_pairs={{0,8},{4,12},{8,0},{12,4},{16,24},{20,28},{24,16},{28,20},{1,9},{5... | collective-permute-start | bytes 589832 | tf_op jit(solution)/shard_map/ppermute | solution.py:199
  17.3 2.6 %collective-permute-done.4 = bf16[48,2048]{1,0:T(8,128)(2,1)S(1)} collective-permute-done((bf16[48,2048]{1,0:T(8,128)(2,1)S(1)}, bf16[48,2048]{1,0:T(8,128)(2,1)S(1)}, u32[]{:S(2)}, u32[]{:S(2)}) %collective-permute-start.4) | collective-permute-done | bytes 196640 | tf_op jit(solution)/shard_map/ppermute | solution.py:199
  19.9 1.6 %collective-permute-start.8 = (bf16[96,2048]{1,0:T(8,128)(2,1)S(1)}, bf16[96,2048]{1,0:T(8,128)(2,1)S(1)}, u32[]{:S(2)}, u32[]{:S(2)}) collective-permute-start(bf16[96,2048]{1,0:T(8,128)(2,1)S(1)} %pad_maximum_fusion.4), channel_id=1, source_target_pairs={{0,8},{4,12},{8,0},{12,4},{16,24},{20,28},{24,16},{28,20},{1,9},{5... | collective-permute-start | bytes 1179656 | tf_op jit(solution)/shard_map/ppermute | solution.py:199
  23.0 1.5 %collective-permute-start.2 = (bf16[96,2048]{1,0:T(8,128)(2,1)S(1)}, bf16[96,2048]{1,0:T(8,128)(2,1)S(1)}, u32[]{:S(2)}, u32[]{:S(2)}) collective-permute-start(bf16[96,2048]{1,0:T(8,128)(2,1)S(1)} %pad_maximum_fusion.3), channel_id=1, source_target_pairs={{0,16},{4,20},{8,24},{12,28},{16,0},{20,4},{24,8},{28,12},{1,17},{... | collective-permute-start | bytes 1179656 | tf_op jit(solution)/shard_map/ppermute | solution.py:199
  24.5 3.1 %collective-permute-done.5 = bf16[48,2048]{1,0:T(8,128)(2,1)S(1)} collective-permute-done((bf16[48,2048]{1,0:T(8,128)(2,1)S(1)}, bf16[48,2048]{1,0:T(8,128)(2,1)S(1)}, u32[]{:S(2)}, u32[]{:S(2)}) %collective-permute-start.5) | collective-permute-done | bytes 196640 | tf_op jit(solution)/shard_map/ppermute | solution.py:202
  27.7 1.6 %collective-permute-start.6 = (bf16[48,2048]{1,0:T(8,128)(2,1)S(1)}, bf16[48,2048]{1,0:T(8,128)(2,1)S(1)}, u32[]{:S(2)}, u32[]{:S(2)}) collective-permute-start(bf16[48,2048]{1,0:T(8,128)(2,1)S(1)} %get-tuple-element.85), channel_id=1, source_target_pairs={{0,8},{4,12},{8,0},{12,4},{16,24},{20,28},{24,16},{28,20},{1,9},{5... | collective-permute-start | bytes 589832 | tf_op jit(solution)/shard_map/ppermute | solution.py:199
  29.3 1.5 %collective-permute-start.7 = (bf16[48,2048]{1,0:T(8,128)(2,1)S(1)}, bf16[48,2048]{1,0:T(8,128)(2,1)S(1)}, u32[]{:S(2)}, u32[]{:S(2)}) collective-permute-start(bf16[48,2048]{1,0:T(8,128)(2,1)S(1)} %get-tuple-element.89), channel_id=1, source_target_pairs={{0,16},{4,20},{8,24},{12,28},{16,0},{20,4},{24,8},{28,12},{1,17},{... | collective-permute-start | bytes 589832 | tf_op jit(solution)/shard_map/ppermute | solution.py:199
  31.0 2.3 %hidden.2 = (bf16[192,512]{1,0:T(8,128)(2,1)S(1)}, bf16[192,512]{1,0:T(8,128)(2,1)S(1)}, bf16[192,512]{1,0:T(8,128)(2,1)S(1)}, bf16[192,512]{1,0:T(8,128)(2,1)S(1)}) custom-call(bf16[192,2048]{1,0:T(8,128)(2,1)S(1)} %pad_maximum_fusion.in_ref, bf16[192,2048]{1,0:T(8,128)(2,1)S(1)} %get-tuple-element.118.cot_ref, bf16[2048,512]{1,0:T(8,128)(2,1)S(1)} %bitcast.28, ...), custom_call_target="tpu_custom_call" | custom-call | flops 1610612736 | bytes 8388608 | tf_op jit(solution)/shard_map/hidden/pallas_call | solution.py:39
  37.4 2.2 %rows.2 = (f32[1,2048]{1,0:T(1,128)S(1)}, f32[96,2048]{1,0:T(8,128)S(1)}, bf16[96,2048]{1,0:T(8,128)(2,1)S(1)}, f32[96,2048]{1,0:T(8,128)S(1)}, bf16[96,2048]{1,0:T(8,128)(2,1)S(1)}) custom-call(bf16[192,2048]{1,0:T(8,128)(2,1)S(1)} %pad_maximum_fusion.in_ref, bf16[192,512]{1,0:T(8,128)(2,1)S(1)} %get-tuple-element.72.hid_a, ...), custom_call_target="tpu_custom_call" | custom-call | flops 1610612736 | bytes 8388608 | tf_op jit(solution)/shard_map/rows/pallas_call | solution.py:39
  41.7 5.6 %collective-permute-done.13 = bf16[96,2048]{1,0:T(8,128)(2,1)S(1)} collective-permute-done((bf16[96,2048]{1,0:T(8,128)(2,1)S(1)}, bf16[96,2048]{1,0:T(8,128)(2,1)S(1)}, u32[]{:S(2)}, u32[]{:S(2)}) %collective-permute-start.13) | collective-permute-done | bytes 393248 | tf_op jit(solution)/shard_map/ppermute | solution.py:199
  47.3 1.4 %collective-permute-done.12 = bf16[96,2048]{1,0:T(8,128)(2,1)S(1)} collective-permute-done((bf16[96,2048]{1,0:T(8,128)(2,1)S(1)}, bf16[96,2048]{1,0:T(8,128)(2,1)S(1)}, u32[]{:S(2)}, u32[]{:S(2)}) %collective-permute-start.12) | collective-permute-done | bytes 393248 | tf_op jit(solution)/shard_map/ppermute | solution.py:199
  49.1 2.3 %hidden.3 = (bf16[192,512]{1,0:T(8,128)(2,1)S(1)}, bf16[192,512]{1,0:T(8,128)(2,1)S(1)}, bf16[192,512]{1,0:T(8,128)(2,1)S(1)}, bf16[192,512]{1,0:T(8,128)(2,1)S(1)}) custom-call(bf16[192,2048]{1,0:T(8,128)(2,1)S(1)} %get-tuple-element.130.in_ref, bf16[192,2048]{1,0:T(8,128)(2,1)S(1)} %pad_maximum_fusion.1.cot_ref, bf16[2048,512]{1,0:T(8,128)(2,1)S(1)} %bitcast.30, ...), custom_call_target="tpu_custom_call" | custom-call | flops 1610612736 | bytes 8388608 | tf_op jit(solution)/shard_map/hidden/pallas_call | solution.py:39
  51.5 2.2 %rows.3 = (f32[1,2048]{1,0:T(1,128)S(1)}, f32[96,2048]{1,0:T(8,128)S(1)}, bf16[96,2048]{1,0:T(8,128)(2,1)S(1)}, f32[96,2048]{1,0:T(8,128)S(1)}, bf16[96,2048]{1,0:T(8,128)(2,1)S(1)}) custom-call(bf16[192,2048]{1,0:T(8,128)(2,1)S(1)} %get-tuple-element.130.in_ref, bf16[192,512]{1,0:T(8,128)(2,1)S(1)} %get-tuple-element.93.hid_a, ...), custom_call_target="tpu_custom_call" | custom-call | flops 1610612736 | bytes 8388608 | tf_op jit(solution)/shard_map/rows/pallas_call | solution.py:39
  55.9 1.4 %collective-permute-start.21 = (bf16[104,2048]{1,0:T(8,128)(2,1)S(1)}, bf16[104,2048]{1,0:T(8,128)(2,1)S(1)}, u32[]{:S(2)}, u32[]{:S(2)}) collective-permute-start(bf16[104,2048]{1,0:T(8,128)(2,1)S(1)} %pad_maximum_fusion.2), channel_id=1, source_target_pairs={{0,8},{4,12},{8,0},{12,4},{16,24},{20,28},{24,16},{28,20},{1,9},{5... | collective-permute-start | bytes 1277960 | tf_op jit(solution)/shard_map/ppermute | solution.py:199
  57.5 1.7 %collective-permute-done.22.left_b = bf16[384,2048]{1,0:T(8,128)(2,1)S(1)} collective-permute-done((bf16[384,2048]{1,0:T(8,128)(2,1)S(1)}, bf16[384,2048]{1,0:T(8,128)(2,1)S(1)}, u32[]{:S(2)}, u32[]{:S(2)}) %collective-permute-start.22) | collective-permute-done | bytes 1572896 | tf_op jit(solution)/shard_map/ppermute | solution.py:199
  59.2 1.5 %collective-permute-start.15 = (bf16[48,2048]{1,0:T(8,128)(2,1)S(1)}, bf16[48,2048]{1,0:T(8,128)(2,1)S(1)}, u32[]{:S(2)}, u32[]{:S(2)}) collective-permute-start(bf16[48,2048]{1,0:T(8,128)(2,1)S(1)} %slice.227), channel_id=1, source_target_pairs={{0,8},{4,12},{8,0},{12,4},{16,24},{20,28},{24,16},{28,20},{1,9},{5... | collective-permute-start | bytes 589832 | tf_op jit(solution)/shard_map/ppermute | solution.py:199
  60.7 3.1 %grad_up.1 = bf16[2048,512]{1,0:T(8,128)(2,1)} custom-call(bf16[384,2048]{1,0:T(8,128)(2,1)S(1)} %get-tuple-element.129.left_a, bf16[384,2048]{1,0:T(8,128)(2,1)S(1)} %collective-permute-done.22.left_b, bf16[384,512]{1,0:T(8,128)(2,1)S(1)} %pad_maximum_fusion.9.right_a, bf16[384,512]{1,0:T(8,128)(2,1)S(1)} %collective-permute-done.23.right_b), custom_call_target="tpu_custom_call" | custom-call | flops 805306368 | bytes 8388608 | tf_op jit(solution)/shard_map/grad_up/pallas_call | solution.py:39
  63.9 1.6 %collective-permute-done.20 = bf16[96,2048]{1,0:T(8,128)(2,1)S(1)} collective-permute-done((bf16[96,2048]{1,0:T(8,128)(2,1)S(1)}, bf16[96,2048]{1,0:T(8,128)(2,1)S(1)}, u32[]{:S(2)}, u32[]{:S(2)}) %collective-permute-start.20) | collective-permute-done | bytes 393248 | tf_op jit(solution)/shard_map/ppermute | solution.py:199
  66.2 2.4 %collective-permute-done.21 = bf16[104,2048]{1,0:T(8,128)(2,1)S(1)} collective-permute-done((bf16[104,2048]{1,0:T(8,128)(2,1)S(1)}, bf16[104,2048]{1,0:T(8,128)(2,1)S(1)}, u32[]{:S(2)}, u32[]{:S(2)}) %collective-permute-start.21) | collective-permute-done | bytes 426016 | tf_op jit(solution)/shard_map/ppermute | solution.py:199
  68.8 1.4 %collective-permute-start.24 = (bf16[48,2048]{1,0:T(8,128)(2,1)S(1)}, bf16[48,2048]{1,0:T(8,128)(2,1)S(1)}, u32[]{:S(2)}, u32[]{:S(2)}) collective-permute-start(bf16[48,2048]{1,0:T(8,128)(2,1)S(1)} %slice.226), channel_id=1, source_target_pairs={{0,8},{4,12},{8,0},{12,4},{16,24},{20,28},{24,16},{28,20},{1,9},{5... | collective-permute-start | bytes 589832 | tf_op jit(solution)/shard_map/ppermute | solution.py:199
  71.3 3.4 %grad_down.1 = bf16[512,2048]{1,0:T(8,128)(2,1)} custom-call(bf16[384,512]{1,0:T(8,128)(2,1)S(1)} %pad_maximum_fusion.7.left_a, bf16[384,512]{1,0:T(8,128)(2,1)S(1)} %collective-permute-done.17.left_b, bf16[384,2048]{1,0:T(8,128)(2,1)S(1)} %constant_dynamic-update-slice_fusion.7.right_a, bf16[384,2048]{1,0:T(8,128)(2,1)S(1)} %collective-permute-done.18.right_b), custom_call_target="tpu_custom_call" | custom-call | flops 805306368 | bytes 8388608 | tf_op jit(solution)/shard_map/grad_down/pallas_call | solution.py:39
  74.8 3.2 %collective-permute-start.19 = (bf16[48,2048]{1,0:T(8,128)(2,1)S(1)}, bf16[48,2048]{1,0:T(8,128)(2,1)S(1)}, u32[]{:S(2)}, u32[]{:S(2)}) collective-permute-start(bf16[48,2048]{1,0:T(8,128)(2,1)S(1)} %pad_maximum_fusion.17), channel_id=1, source_target_pairs={{0,3},{1,0},{2,1},{3,2},{4,7},{5,4},{6,5},{7,6},{8,11},{9,8},{10,9... | collective-permute-start | bytes 589832 | tf_op jit(solution)/shard_map/ppermute | solution.py:202
  78.6 2.0 %collective-permute-start.26 = (bf16[48,2048]{1,0:T(8,128)(2,1)S(1)}, bf16[48,2048]{1,0:T(8,128)(2,1)S(1)}, u32[]{:S(2)}, u32[]{:S(2)}) collective-permute-start(bf16[48,2048]{1,0:T(8,128)(2,1)S(1)} %pad_maximum_fusion.18), channel_id=1, source_target_pairs={{0,2},{1,3},{2,0},{3,1},{4,6},{5,7},{6,4},{7,5},{8,10},{9,11},{10,... | collective-permute-start | bytes 589832 | tf_op jit(solution)/shard_map/ppermute | solution.py:202
  81.4 1.8 %collective-permute-done.28 = f32[16,128]{1,0:T(8,128)S(1)} collective-permute-done((f32[16,128]{1,0:T(8,128)S(1)}, f32[16,128]{1,0:T(8,128)S(1)}, u32[]{:S(2)}, u32[]{:S(2)}) %collective-permute-start.28) | collective-permute-done | bytes 8224 | tf_op jit(solution)/shard_map/ppermute | solution.py:364
  83.5 10.3 %collective-permute-done.29 = f32[16,128]{1,0:T(8,128)S(1)} collective-permute-done((f32[16,128]{1,0:T(8,128)S(1)}, f32[16,128]{1,0:T(8,128)S(1)}, u32[]{:S(2)}, u32[]{:S(2)}) %collective-permute-start.29) | collective-permute-done | bytes 8224 | tf_op jit(solution)/shard_map/ppermute | solution.py:364
  93.8 1.4 %tokens.1 = (bf16[128,2048]{1,0:T(8,128)(2,1)}, bf16[128,2048]{1,0:T(8,128)(2,1)}) custom-call(s32[1,128]{1,0:T(1,128)S(1)} %copy-done.4, bf16[128,2048]{1,0:T(8,128)(2,1)S(1)} %copy-done.2, f32[1,2048]{1,0:T(1,128)S(1)} %bitcast.38, bf16[48,2048]{1,0:T(8,128)(2,1)S(1)} %pad_maximum_fusion.16.refs_0_, bf16[48,2048]{1,0:T(8,128)(2,1)S(1)} %collective-permute-done.19.refs_1_, ...), custom_call_target="tpu_custom_call" | custom-call | tf_op jit(solution)/shard_map/tokens/pallas_call | solution.py:39
  (118 shorter events, 16.5 us)
Async XLA Ops:
  3.2 10.2 %collective-permute-start = (bf16[48,2048]{1,0:T(8,128)(2,1)}, bf16[48,2048]{1,0:T(8,128)(2,1)S(1)}, u32[]{:S(2)}, u32[]{:S(2)}) collective-permute-start(bf16[48,2048]{1,0:T(8,128)(2,1)} %get-tuple-element.61), channel_id=1, source_target_pairs={{0,1},{1,2},{2,3},{3,0},{4,5},{5,6},{6,7},{7,4},{8,9},{9,10},{10,1... | collective-permute-start | bytes 589832 | tf_op jit(solution)/shard_map/ppermute | solution.py:202
  9.8 21.2 %collective-permute-start.9 = (bf16[2048,1024]{1,0:T(8,128)(2,1)S(1)}, bf16[2048,1024]{1,0:T(8,128)(2,1)S(1)}, u32[]{:S(2)}, u32[]{:S(2)}) collective-permute-start(bf16[2048,1024]{1,0:T(8,128)(2,1)S(1)} %pack.1), channel_id=1, source_target_pairs={{0,4},{4,0},{8,12},{12,8},{16,20},{20,16},{24,28},{28,24},{1,5},{5... | collective-permute-start | bytes 12582920 | tf_op jit(solution)/shard_map/ppermute | solution.py:199
  13.4 11.1 %collective-permute-start.3 = (bf16[48,2048]{1,0:T(8,128)(2,1)S(1)}, bf16[48,2048]{1,0:T(8,128)(2,1)S(1)}, u32[]{:S(2)}, u32[]{:S(2)}) collective-permute-start(bf16[48,2048]{1,0:T(8,128)(2,1)S(1)} %copy-done.7), channel_id=1, source_target_pairs={{0,2},{1,3},{2,0},{3,1},{4,6},{5,7},{6,4},{7,5},{8,10},{9,11},{10,... | collective-permute-start | bytes 589832 | tf_op jit(solution)/shard_map/ppermute | solution.py:202
  14.2 5.7 %collective-permute-start.4 = (bf16[48,2048]{1,0:T(8,128)(2,1)S(1)}, bf16[48,2048]{1,0:T(8,128)(2,1)S(1)}, u32[]{:S(2)}, u32[]{:S(2)}) collective-permute-start(bf16[48,2048]{1,0:T(8,128)(2,1)S(1)} %pad_maximum_fusion.13), channel_id=1, source_target_pairs={{0,16},{4,20},{8,24},{12,28},{16,0},{20,4},{24,8},{28,12},{1,17},{... | collective-permute-start | bytes 589832 | tf_op jit(solution)/shard_map/ppermute | solution.py:199
  15.8 7.2 %collective-permute-start.1 = (bf16[48,2048]{1,0:T(8,128)(2,1)S(1)}, bf16[48,2048]{1,0:T(8,128)(2,1)S(1)}, u32[]{:S(2)}, u32[]{:S(2)}) collective-permute-start(bf16[48,2048]{1,0:T(8,128)(2,1)S(1)} %pad_maximum_fusion.12), channel_id=1, source_target_pairs={{0,8},{4,12},{8,0},{12,4},{16,24},{20,28},{24,16},{28,20},{1,9},{5... | collective-permute-start | bytes 589832 | tf_op jit(solution)/shard_map/ppermute | solution.py:199
  19.9 10.8 %collective-permute-start.8 = (bf16[96,2048]{1,0:T(8,128)(2,1)S(1)}, bf16[96,2048]{1,0:T(8,128)(2,1)S(1)}, u32[]{:S(2)}, u32[]{:S(2)}) collective-permute-start(bf16[96,2048]{1,0:T(8,128)(2,1)S(1)} %pad_maximum_fusion.4), channel_id=1, source_target_pairs={{0,8},{4,12},{8,0},{12,4},{16,24},{20,28},{24,16},{28,20},{1,9},{5... | collective-permute-start | bytes 1179656 | tf_op jit(solution)/shard_map/ppermute | solution.py:199
  21.5 6.1 %collective-permute-start.5 = (bf16[48,2048]{1,0:T(8,128)(2,1)S(1)}, bf16[48,2048]{1,0:T(8,128)(2,1)S(1)}, u32[]{:S(2)}, u32[]{:S(2)}) collective-permute-start(bf16[48,2048]{1,0:T(8,128)(2,1)S(1)} %copy-done.6), channel_id=1, source_target_pairs={{0,3},{1,0},{2,1},{3,2},{4,7},{5,4},{6,5},{7,6},{8,11},{9,8},{10,9... | collective-permute-start | bytes 589832 | tf_op jit(solution)/shard_map/ppermute | solution.py:202
  23.0 8.0 %collective-permute-start.2 = (bf16[96,2048]{1,0:T(8,128)(2,1)S(1)}, bf16[96,2048]{1,0:T(8,128)(2,1)S(1)}, u32[]{:S(2)}, u32[]{:S(2)}) collective-permute-start(bf16[96,2048]{1,0:T(8,128)(2,1)S(1)} %pad_maximum_fusion.3), channel_id=1, source_target_pairs={{0,16},{4,20},{8,24},{12,28},{16,0},{20,4},{24,8},{28,12},{1,17},{... | collective-permute-start | bytes 1179656 | tf_op jit(solution)/shard_map/ppermute | solution.py:199
  27.7 6.5 %collective-permute-start.6 = (bf16[48,2048]{1,0:T(8,128)(2,1)S(1)}, bf16[48,2048]{1,0:T(8,128)(2,1)S(1)}, u32[]{:S(2)}, u32[]{:S(2)}) collective-permute-start(bf16[48,2048]{1,0:T(8,128)(2,1)S(1)} %get-tuple-element.85), channel_id=1, source_target_pairs={{0,8},{4,12},{8,0},{12,4},{16,24},{20,28},{24,16},{28,20},{1,9},{5... | collective-permute-start | bytes 589832 | tf_op jit(solution)/shard_map/ppermute | solution.py:199
  29.3 5.9 %collective-permute-start.7 = (bf16[48,2048]{1,0:T(8,128)(2,1)S(1)}, bf16[48,2048]{1,0:T(8,128)(2,1)S(1)}, u32[]{:S(2)}, u32[]{:S(2)}) collective-permute-start(bf16[48,2048]{1,0:T(8,128)(2,1)S(1)} %get-tuple-element.89), channel_id=1, source_target_pairs={{0,16},{4,20},{8,24},{12,28},{16,0},{20,4},{24,8},{28,12},{1,17},{... | collective-permute-start | bytes 589832 | tf_op jit(solution)/shard_map/ppermute | solution.py:199
  35.2 12.1 %collective-permute-start.13 = (bf16[96,2048]{1,0:T(8,128)(2,1)S(1)}, bf16[96,2048]{1,0:T(8,128)(2,1)S(1)}, u32[]{:S(2)}, u32[]{:S(2)}) collective-permute-start(bf16[96,2048]{1,0:T(8,128)(2,1)S(1)} %pad_maximum_fusion.6), channel_id=1, source_target_pairs={{0,8},{4,12},{8,0},{12,4},{16,24},{20,28},{24,16},{28,20},{1,9},{5... | collective-permute-start | bytes 1179656 | tf_op jit(solution)/shard_map/ppermute | solution.py:199
  36.7 12.1 %collective-permute-start.12 = (bf16[96,2048]{1,0:T(8,128)(2,1)S(1)}, bf16[96,2048]{1,0:T(8,128)(2,1)S(1)}, u32[]{:S(2)}, u32[]{:S(2)}) collective-permute-start(bf16[96,2048]{1,0:T(8,128)(2,1)S(1)} %pad_maximum_fusion.5), channel_id=1, source_target_pairs={{0,16},{4,20},{8,24},{12,28},{16,0},{20,4},{24,8},{28,12},{1,17},{... | collective-permute-start | bytes 1179656 | tf_op jit(solution)/shard_map/ppermute | solution.py:199
  39.7 15.5 %collective-permute-start.10 = (bf16[96,2048]{1,0:T(8,128)(2,1)S(1)}, bf16[96,2048]{1,0:T(8,128)(2,1)S(1)}, u32[]{:S(2)}, u32[]{:S(2)}) collective-permute-start(bf16[96,2048]{1,0:T(8,128)(2,1)S(1)} %get-tuple-element.77), channel_id=1, source_target_pairs={{0,16},{4,20},{8,24},{12,28},{16,0},{20,4},{24,8},{28,12},{1,17},{... | collective-permute-start | bytes 1179656 | tf_op jit(solution)/shard_map/ppermute | solution.py:199
  41.1 14.6 %collective-permute-start.11 = (bf16[96,2048]{1,0:T(8,128)(2,1)S(1)}, bf16[96,2048]{1,0:T(8,128)(2,1)S(1)}, u32[]{:S(2)}, u32[]{:S(2)}) collective-permute-start(bf16[96,2048]{1,0:T(8,128)(2,1)S(1)} %get-tuple-element.78), channel_id=1, source_target_pairs={{0,8},{4,12},{8,0},{12,4},{16,24},{20,28},{24,16},{28,20},{1,9},{5... | collective-permute-start | bytes 1179656 | tf_op jit(solution)/shard_map/ppermute | solution.py:199
  53.8 1.2 %collective-permute-start.14 = (f32[1,2048]{1,0:T(1,128)S(1)}, f32[1,2048]{1,0:T(1,128)S(1)}, u32[]{:S(2)}, u32[]{:S(2)}) collective-permute-start(f32[1,2048]{1,0:T(1,128)S(1)} %add.52), channel_id=1, source_target_pairs={{0,4},{4,0},{8,12},{12,8},{16,20},{20,16},{24,28},{28,24},{1,5},{5... | collective-permute-start | bytes 24584 | tf_op jit(solution)/shard_map/ppermute | solution.py:199
  53.9 11.6 %collective-permute-start.20 = (bf16[96,2048]{1,0:T(8,128)(2,1)S(1)}, bf16[96,2048]{1,0:T(8,128)(2,1)S(1)}, u32[]{:S(2)}, u32[]{:S(2)}) collective-permute-start(bf16[96,2048]{1,0:T(8,128)(2,1)S(1)} %get-tuple-element.103), channel_id=1, source_target_pairs={{0,16},{4,20},{8,24},{12,28},{16,0},{20,4},{24,8},{28,12},{1,17},{... | collective-permute-start | bytes 1179656 | tf_op jit(solution)/shard_map/ppermute | solution.py:199
  54.7 15.7 %collective-permute-start.17 = (bf16[384,512]{1,0:T(8,128)(2,1)S(1)}, bf16[384,512]{1,0:T(8,128)(2,1)S(1)}, u32[]{:S(2)}, u32[]{:S(2)}) collective-permute-start(bf16[384,512]{1,0:T(8,128)(2,1)S(1)} %pad_maximum_fusion.8), channel_id=1, source_target_pairs={{0,4},{4,0},{8,12},{12,8},{16,20},{20,16},{24,28},{28,24},{1,5},{5... | collective-permute-start | bytes 1179656 | tf_op jit(solution)/shard_map/ppermute | solution.py:199
  55.0 2.4 %collective-permute-start.23 = (bf16[384,512]{1,0:T(8,128)(2,1)S(1)}, bf16[384,512]{1,0:T(8,128)(2,1)S(1)}, u32[]{:S(2)}, u32[]{:S(2)}) collective-permute-start(bf16[384,512]{1,0:T(8,128)(2,1)S(1)} %pad_maximum_fusion.10), channel_id=1, source_target_pairs={{0,4},{4,0},{8,12},{12,8},{16,20},{20,16},{24,28},{28,24},{1,5},{5... | collective-permute-start | bytes 1179656 | tf_op jit(solution)/shard_map/ppermute | solution.py:199
  55.2 4.0 %collective-permute-start.22 = (bf16[384,2048]{1,0:T(8,128)(2,1)S(1)}, bf16[384,2048]{1,0:T(8,128)(2,1)S(1)}, u32[]{:S(2)}, u32[]{:S(2)}) collective-permute-start(bf16[384,2048]{1,0:T(8,128)(2,1)S(1)} %get-tuple-element.129.left_a), channel_id=1, source_target_pairs={{0,4},{4,0},{8,12},{12,8},{16,20},{20,16},{24,28},{28,24},{1,5},{5... | collective-permute-start | bytes 4718600 | tf_op jit(solution)/shard_map/ppermute | solution.py:199
  55.9 12.7 %collective-permute-start.21 = (bf16[104,2048]{1,0:T(8,128)(2,1)S(1)}, bf16[104,2048]{1,0:T(8,128)(2,1)S(1)}, u32[]{:S(2)}, u32[]{:S(2)}) collective-permute-start(bf16[104,2048]{1,0:T(8,128)(2,1)S(1)} %pad_maximum_fusion.2), channel_id=1, source_target_pairs={{0,8},{4,12},{8,0},{12,4},{16,24},{20,28},{24,16},{28,20},{1,9},{5... | collective-permute-start | bytes 1277960 | tf_op jit(solution)/shard_map/ppermute | solution.py:199
  57.4 13.9 %collective-permute-start.18 = (bf16[384,2048]{1,0:T(8,128)(2,1)S(1)}, bf16[384,2048]{1,0:T(8,128)(2,1)S(1)}, u32[]{:S(2)}, u32[]{:S(2)}) collective-permute-start(bf16[384,2048]{1,0:T(8,128)(2,1)S(1)} %constant_dynamic-update-slice_fusion.7.right_a), channel_id=1, source_target_pairs={{0,4},{4,0},{8,12},{12,8},{16,20},{20,16},{24,28},{28,24},{1,5},{5... | collective-permute-start | bytes 4718600 | tf_op jit(solution)/shard_map/ppermute | solution.py:199
  59.2 15.4 %collective-permute-start.15 = (bf16[48,2048]{1,0:T(8,128)(2,1)S(1)}, bf16[48,2048]{1,0:T(8,128)(2,1)S(1)}, u32[]{:S(2)}, u32[]{:S(2)}) collective-permute-start(bf16[48,2048]{1,0:T(8,128)(2,1)S(1)} %slice.227), channel_id=1, source_target_pairs={{0,8},{4,12},{8,0},{12,4},{16,24},{20,28},{24,16},{28,20},{1,9},{5... | collective-permute-start | bytes 589832 | tf_op jit(solution)/shard_map/ppermute | solution.py:199
  65.5 9.2 %collective-permute-start.16 = (bf16[48,2048]{1,0:T(8,128)(2,1)S(1)}, bf16[48,2048]{1,0:T(8,128)(2,1)S(1)}, u32[]{:S(2)}, u32[]{:S(2)}) collective-permute-start(bf16[48,2048]{1,0:T(8,128)(2,1)S(1)} %fusion.6), channel_id=1, source_target_pairs={{0,16},{4,20},{8,24},{12,28},{16,0},{20,4},{24,8},{28,12},{1,17},{... | collective-permute-start | bytes 589832 | tf_op jit(solution)/shard_map/ppermute | solution.py:199
  68.8 9.3 %collective-permute-start.24 = (bf16[48,2048]{1,0:T(8,128)(2,1)S(1)}, bf16[48,2048]{1,0:T(8,128)(2,1)S(1)}, u32[]{:S(2)}, u32[]{:S(2)}) collective-permute-start(bf16[48,2048]{1,0:T(8,128)(2,1)S(1)} %slice.226), channel_id=1, source_target_pairs={{0,8},{4,12},{8,0},{12,4},{16,24},{20,28},{24,16},{28,20},{1,9},{5... | collective-permute-start | bytes 589832 | tf_op jit(solution)/shard_map/ppermute | solution.py:199
  70.4 7.7 %collective-permute-start.25 = (bf16[56,2048]{1,0:T(8,128)(2,1)S(1)}, bf16[56,2048]{1,0:T(8,128)(2,1)S(1)}, u32[]{:S(2)}, u32[]{:S(2)}) collective-permute-start(bf16[56,2048]{1,0:T(8,128)(2,1)S(1)} %pad_maximum_fusion.11), channel_id=1, source_target_pairs={{0,16},{4,20},{8,24},{12,28},{16,0},{20,4},{24,8},{28,12},{1,17},{... | collective-permute-start | bytes 688136 | tf_op jit(solution)/shard_map/ppermute | solution.py:199
  74.8 18.9 %collective-permute-start.19 = (bf16[48,2048]{1,0:T(8,128)(2,1)S(1)}, bf16[48,2048]{1,0:T(8,128)(2,1)S(1)}, u32[]{:S(2)}, u32[]{:S(2)}) collective-permute-start(bf16[48,2048]{1,0:T(8,128)(2,1)S(1)} %pad_maximum_fusion.17), channel_id=1, source_target_pairs={{0,3},{1,0},{2,1},{3,2},{4,7},{5,4},{6,5},{7,6},{8,11},{9,8},{10,9... | collective-permute-start | bytes 589832 | tf_op jit(solution)/shard_map/ppermute | solution.py:202
  78.1 15.7 %copy-start.2 = (bf16[128,2048]{1,0:T(8,128)(2,1)S(1)}, bf16[128,2048]{1,0:T(8,128)(2,1)}, u32[]{:S(2)}) copy-start(bf16[128,2048]{1,0:T(8,128)(2,1)} %tok_ref.1) | copy-start | bytes 1572868
  78.1 15.7 %copy-start.3 = (f32[2048]{0:T(1024)S(1)}, f32[2048]{0:T(1024)}, u32[]{:S(2)}) copy-start(f32[2048]{0:T(1024)} %param.8) | copy-start | bytes 24580
  78.2 5.0 %collective-permute-start.28 = (f32[16,128]{1,0:T(8,128)S(1)}, f32[16,128]{1,0:T(8,128)S(1)}, u32[]{:S(2)}, u32[]{:S(2)}) collective-permute-start(f32[16,128]{1,0:T(8,128)S(1)} %bitcast.47), channel_id=1, source_target_pairs={{0,1},{1,0},{2,3},{3,2},{4,5},{5,4},{6,7},{7,6},{8,9},{9,8},{10,11... | collective-permute-start | bytes 24584 | tf_op jit(solution)/shard_map/ppermute | solution.py:364
  78.6 15.2 %collective-permute-start.26 = (bf16[48,2048]{1,0:T(8,128)(2,1)S(1)}, bf16[48,2048]{1,0:T(8,128)(2,1)S(1)}, u32[]{:S(2)}, u32[]{:S(2)}) collective-permute-start(bf16[48,2048]{1,0:T(8,128)(2,1)S(1)} %pad_maximum_fusion.18), channel_id=1, source_target_pairs={{0,2},{1,3},{2,0},{3,1},{4,6},{5,7},{6,4},{7,5},{8,10},{9,11},{10,... | collective-permute-start | bytes 589832 | tf_op jit(solution)/shard_map/ppermute | solution.py:202
  80.6 13.2 %collective-permute-start.27 = (bf16[48,2048]{1,0:T(8,128)(2,1)S(1)}, bf16[48,2048]{1,0:T(8,128)(2,1)S(1)}, u32[]{:S(2)}, u32[]{:S(2)}) collective-permute-start(bf16[48,2048]{1,0:T(8,128)(2,1)S(1)} %pad_maximum_fusion.19), channel_id=1, source_target_pairs={{0,1},{1,2},{2,3},{3,0},{4,5},{5,6},{6,7},{7,4},{8,9},{9,10},{10,1... | collective-permute-start | bytes 589832 | tf_op jit(solution)/shard_map/ppermute | solution.py:202
  83.3 10.5 %collective-permute-start.29 = (f32[16,128]{1,0:T(8,128)S(1)}, f32[16,128]{1,0:T(8,128)S(1)}, u32[]{:S(2)}, u32[]{:S(2)}) collective-permute-start(f32[16,128]{1,0:T(8,128)S(1)} %add.66), channel_id=1, source_target_pairs={{0,2},{1,3},{2,0},{3,1},{4,6},{5,7},{6,4},{7,5},{8,10},{9,11},{10,... | collective-permute-start | bytes 24584 | tf_op jit(solution)/shard_map/ppermute | solution.py:364
  (6 other events, 35.5 us)

commit v8 on v7

--- a/solution.py
+++ b/solution.py
@@ -150,10 +150,10 @@
                 keep_back[to, at] = part
 
 
-def grad_kernel(left_a, left_b, right_a, right_b, out_ref, left, right):
+def grad_kernel(starts, left_a, left_b, right_a, right_b, out_ref, left, right):
     rows = left_a.shape[0]
-    left[:rows], left[rows:] = left_a[...], left_b[...]
-    right[:rows], right[rows:] = right_a[...], right_b[...]
+    left[:rows], left[rows:] = left_a[...], left_b[pl.ds(starts[0], rows)]
+    right[:rows], right[rows:] = right_a[...], right_b[pl.ds(starts[1], rows)]
     for i in range(out_ref.shape[0] // 256):
         at = pl.ds(i * 256, 256)
         out_ref[at, :] = mm(left[:, at], right[...], TN).astype(bf16)
@@ -333,20 +333,21 @@
     hid_a, hid_b, pre_a, pre_b = [join(a, b) for a, b in zip(acts_1, acts_2)]
     wide_rows = pltpu.VMEM((4 * rows, width), bf16)
     unit_rows = pltpu.VMEM((4 * rows, units), bf16)
+    units_got = swap(join(hid_b, pre_b), 1)
     grad_down = call(
         "grad_down",
-        grad_kernel,
+        functools.partial(grad_kernel, (0, 0)),
         shaped((units, width)),
-        (hid_a, swap(hid_b, 1), cot_all, swap(cot_all, 1)),
+        (hid_a, units_got, cot_all, swap(cot_all, 1)),
         work // 4,
         8 << 20,
         [unit_rows, wide_rows],
     )
     grad_up = call(
         "grad_up",
-        grad_kernel,
+        functools.partial(grad_kernel, (0, 2 * rows)),
         shaped((width, units)),
-        (in_all, swap(in_all, 1), pre_a, swap(pre_b, 1)),
+        (in_all, swap(in_all, 1), pre_a, units_got),
         work // 4,
         8 << 20,
         [wide_rows, unit_rows],

time: 96.1 us -> 96 us (level)
    ppermute x22 -> x21, waiting for transfers between devices: 17.5 us -> 17.4 us  [swap(): return lax.ppermute(x, 'rep', [(i, i ^ bit) for i in range(copies)])]
    ppermute x22 -> x21, starting transfers between devices: 21.3 us -> 21.4 us  [swap(): return lax.ppermute(x, 'rep', [(i, i ^ bit) for i in range(copies)])]
  transfers between devices with their start and end apart: 30 -> 29, of which waited for: 15 -> 15; matrix products, arithmetic and copies ran while one was open for 2% -> 2% of each run, Pallas kernels for 17% -> 17%
where the time goes in v8:
time: 96 us; the launch traced here: 95.8 us
  waiting for transfers between devices  36.1 us (38%)
  starting transfers between devices  32.6 us (34%)
  Pallas kernels  19.9 us (21%)
  local copies, waits for them, and re-layouts  4.3 us (4%)
  other arithmetic  1.77 us (2%)
  between operations  1.2 us (1%)
    ppermute x21, starting transfers between devices, swap(): return lax.ppermute(x, 'rep', [(i, i ^ bit) for i in range(copies)])  21.4 us
    pallas_call x9, Pallas kernels, call(): pl.pallas_call(kernel, name=name, out_shape=out_shape, in_specs=[pl.Block...  19.9 us
    ppermute x21, waiting for transfers between devices, swap(): return lax.ppermute(x, 'rep', [(i, i ^ bit) for i in range(copies)])  17.4 us
    ppermute x2, waiting for transfers between devices, local(): lax.ppermute(total, 'exp', [(i, i ^ step) for i in range(groups)])  12.6 us
    ppermute x6, starting transfers between devices, shift(): lax.ppermute(x, 'exp', [(i, (i + k) % groups) for i in range(groups)])  10.9 us
    ppermute x6, waiting for transfers between devices, shift(): lax.ppermute(x, 'exp', [(i, (i + k) % groups) for i in range(groups)])  6.11 us
    unnamed x29, local copies, waits for them, and re-layouts  4.03 us
  transfers between devices with their start and end apart: 29, of which 15 were waited for; matrix products, arithmetic and copies ran while one was open for 2% of the time, Pallas kernels for 17%

profile of v8, /device:TPU:0, one launch (start us, length us, event | category | flops | bytes accessed | tf_op | source)
XLA Modules:
  0.0 95.8 jit_solution(16011199991015633173)
XLA Ops:
  0.6 2.5 %place.1 = (s32[1,128]{1,0:T(1,128)}, bf16[48,2048]{1,0:T(8,128)(2,1)}, bf16[48,2048]{1,0:T(8,128)(2,1)}, bf16[48,2048]{1,0:T(8,128)(2,1)}, bf16[48,2048]{1,0:T(8,128)(2,1)}) custom-call(bf16[128,2048]{1,0:T(8,128)(2,1)} %tok_ref.1, s32[1,128]{1,0:T(1,128)} %bitcast.50, f32[1,2048]{1,0:T(1,128)} %bitcast.37, bf16[128,2048]{1,0:T(8,128)(2,1)} %cot_in.1), custom_call_target="tpu_custom_call" | custom-call | tf_op jit(solution)/shard_map/place/pallas_call | solution.py:39
  3.2 3.1 %collective-permute-start = (bf16[48,2048]{1,0:T(8,128)(2,1)}, bf16[48,2048]{1,0:T(8,128)(2,1)S(1)}, u32[]{:S(2)}, u32[]{:S(2)}) collective-permute-start(bf16[48,2048]{1,0:T(8,128)(2,1)} %get-tuple-element.61), channel_id=1, source_target_pairs={{0,1},{1,2},{2,3},{3,0},{4,5},{5,6},{6,7},{7,4},{8,9},{9,10},{10,1... | collective-permute-start | bytes 589832 | tf_op jit(solution)/shard_map/ppermute | solution.py:202
  6.3 1.6 %copy-done = bf16[1,2048,512]{2,1,0:T(8,128)(2,1)S(1)} copy-done((bf16[1,2048,512]{2,1,0:T(8,128)(2,1)S(1)}, bf16[1,2048,512]{2,1,0:T(8,128)(2,1)}, u32[]{:S(2)}) %copy-start) | copy-done | bytes 2097176
  7.8 1.6 %copy-done.1 = bf16[1,512,2048]{2,1,0:T(8,128)(2,1)S(1)} copy-done((bf16[1,512,2048]{2,1,0:T(8,128)(2,1)S(1)}, bf16[1,512,2048]{2,1,0:T(8,128)(2,1)}, u32[]{:S(2)}) %copy-start.1) | copy-done | bytes 2097176
  10.4 3.0 %collective-permute-done = bf16[48,2048]{1,0:T(8,128)(2,1)S(1)} collective-permute-done((bf16[48,2048]{1,0:T(8,128)(2,1)}, bf16[48,2048]{1,0:T(8,128)(2,1)S(1)}, u32[]{:S(2)}, u32[]{:S(2)}) %collective-permute-start) | collective-permute-done | bytes 196640 | tf_op jit(solution)/shard_map/ppermute | solution.py:202
  14.2 1.6 %collective-permute-start.4 = (bf16[48,2048]{1,0:T(8,128)(2,1)S(1)}, bf16[48,2048]{1,0:T(8,128)(2,1)S(1)}, u32[]{:S(2)}, u32[]{:S(2)}) collective-permute-start(bf16[48,2048]{1,0:T(8,128)(2,1)S(1)} %pad_maximum_fusion.12), channel_id=1, source_target_pairs={{0,16},{4,20},{8,24},{12,28},{16,0},{20,4},{24,8},{28,12},{1,17},{... | collective-permute-start | bytes 589832 | tf_op jit(solution)/shard_map/ppermute | solution.py:199
  15.8 1.6 %collective-permute-start.1 = (bf16[48,2048]{1,0:T(8,128)(2,1)S(1)}, bf16[48,2048]{1,0:T(8,128)(2,1)S(1)}, u32[]{:S(2)}, u32[]{:S(2)}) collective-permute-start(bf16[48,2048]{1,0:T(8,128)(2,1)S(1)} %pad_maximum_fusion.11), channel_id=1, source_target_pairs={{0,8},{4,12},{8,0},{12,4},{16,24},{20,28},{24,16},{28,20},{1,9},{5... | collective-permute-start | bytes 589832 | tf_op jit(solution)/shard_map/ppermute | solution.py:199
  17.3 2.6 %collective-permute-done.4 = bf16[48,2048]{1,0:T(8,128)(2,1)S(1)} collective-permute-done((bf16[48,2048]{1,0:T(8,128)(2,1)S(1)}, bf16[48,2048]{1,0:T(8,128)(2,1)S(1)}, u32[]{:S(2)}, u32[]{:S(2)}) %collective-permute-start.4) | collective-permute-done | bytes 196640 | tf_op jit(solution)/shard_map/ppermute | solution.py:199
  19.9 1.6 %collective-permute-start.8 = (bf16[96,2048]{1,0:T(8,128)(2,1)S(1)}, bf16[96,2048]{1,0:T(8,128)(2,1)S(1)}, u32[]{:S(2)}, u32[]{:S(2)}) collective-permute-start(bf16[96,2048]{1,0:T(8,128)(2,1)S(1)} %pad_maximum_fusion.5), channel_id=1, source_target_pairs={{0,8},{4,12},{8,0},{12,4},{16,24},{20,28},{24,16},{28,20},{1,9},{5... | collective-permute-start | bytes 1179656 | tf_op jit(solution)/shard_map/ppermute | solution.py:199
  23.0 1.5 %collective-permute-start.2 = (bf16[96,2048]{1,0:T(8,128)(2,1)S(1)}, bf16[96,2048]{1,0:T(8,128)(2,1)S(1)}, u32[]{:S(2)}, u32[]{:S(2)}) collective-permute-start(bf16[96,2048]{1,0:T(8,128)(2,1)S(1)} %pad_maximum_fusion.4), channel_id=1, source_target_pairs={{0,16},{4,20},{8,24},{12,28},{16,0},{20,4},{24,8},{28,12},{1,17},{... | collective-permute-start | bytes 1179656 | tf_op jit(solution)/shard_map/ppermute | solution.py:199
  24.5 3.1 %collective-permute-done.5 = bf16[48,2048]{1,0:T(8,128)(2,1)S(1)} collective-permute-done((bf16[48,2048]{1,0:T(8,128)(2,1)S(1)}, bf16[48,2048]{1,0:T(8,128)(2,1)S(1)}, u32[]{:S(2)}, u32[]{:S(2)}) %collective-permute-start.5) | collective-permute-done | bytes 196640 | tf_op jit(solution)/shard_map/ppermute | solution.py:202
  27.7 1.6 %collective-permute-start.6 = (bf16[48,2048]{1,0:T(8,128)(2,1)S(1)}, bf16[48,2048]{1,0:T(8,128)(2,1)S(1)}, u32[]{:S(2)}, u32[]{:S(2)}) collective-permute-start(bf16[48,2048]{1,0:T(8,128)(2,1)S(1)} %get-tuple-element.85), channel_id=1, source_target_pairs={{0,8},{4,12},{8,0},{12,4},{16,24},{20,28},{24,16},{28,20},{1,9},{5... | collective-permute-start | bytes 589832 | tf_op jit(solution)/shard_map/ppermute | solution.py:199
  29.3 1.5 %collective-permute-start.7 = (bf16[48,2048]{1,0:T(8,128)(2,1)S(1)}, bf16[48,2048]{1,0:T(8,128)(2,1)S(1)}, u32[]{:S(2)}, u32[]{:S(2)}) collective-permute-start(bf16[48,2048]{1,0:T(8,128)(2,1)S(1)} %get-tuple-element.89), channel_id=1, source_target_pairs={{0,16},{4,20},{8,24},{12,28},{16,0},{20,4},{24,8},{28,12},{1,17},{... | collective-permute-start | bytes 589832 | tf_op jit(solution)/shard_map/ppermute | solution.py:199
  31.0 2.3 %hidden.2 = (bf16[192,512]{1,0:T(8,128)(2,1)S(1)}, bf16[192,512]{1,0:T(8,128)(2,1)S(1)}, bf16[192,512]{1,0:T(8,128)(2,1)S(1)}, bf16[192,512]{1,0:T(8,128)(2,1)S(1)}) custom-call(bf16[192,2048]{1,0:T(8,128)(2,1)S(1)} %pad_maximum_fusion.in_ref, bf16[192,2048]{1,0:T(8,128)(2,1)S(1)} %get-tuple-element.118.cot_ref, bf16[2048,512]{1,0:T(8,128)(2,1)S(1)} %bitcast.28, ...), custom_call_target="tpu_custom_call" | custom-call | flops 1610612736 | bytes 8388608 | tf_op jit(solution)/shard_map/hidden/pallas_call | solution.py:39
  35.2 1.4 %collective-permute-start.13 = (bf16[96,2048]{1,0:T(8,128)(2,1)S(1)}, bf16[96,2048]{1,0:T(8,128)(2,1)S(1)}, u32[]{:S(2)}, u32[]{:S(2)}) collective-permute-start(bf16[96,2048]{1,0:T(8,128)(2,1)S(1)} %pad_maximum_fusion.7), channel_id=1, source_target_pairs={{0,8},{4,12},{8,0},{12,4},{16,24},{20,28},{24,16},{28,20},{1,9},{5... | collective-permute-start | bytes 1179656 | tf_op jit(solution)/shard_map/ppermute | solution.py:199
  37.4 2.2 %rows.2 = (f32[1,2048]{1,0:T(1,128)S(1)}, f32[96,2048]{1,0:T(8,128)S(1)}, bf16[96,2048]{1,0:T(8,128)(2,1)S(1)}, f32[96,2048]{1,0:T(8,128)S(1)}, bf16[96,2048]{1,0:T(8,128)(2,1)S(1)}) custom-call(bf16[192,2048]{1,0:T(8,128)(2,1)S(1)} %pad_maximum_fusion.in_ref, bf16[192,512]{1,0:T(8,128)(2,1)S(1)} %get-tuple-element.72.hid_a, ...), custom_call_target="tpu_custom_call" | custom-call | flops 1610612736 | bytes 8388608 | tf_op jit(solution)/shard_map/rows/pallas_call | solution.py:39
  39.7 1.4 %collective-permute-start.10 = (bf16[96,2048]{1,0:T(8,128)(2,1)S(1)}, bf16[96,2048]{1,0:T(8,128)(2,1)S(1)}, u32[]{:S(2)}, u32[]{:S(2)}) collective-permute-start(bf16[96,2048]{1,0:T(8,128)(2,1)S(1)} %get-tuple-element.77), channel_id=1, source_target_pairs={{0,16},{4,20},{8,24},{12,28},{16,0},{20,4},{24,8},{28,12},{1,17},{... | collective-permute-start | bytes 1179656 | tf_op jit(solution)/shard_map/ppermute | solution.py:199
  41.7 5.6 %collective-permute-done.13 = bf16[96,2048]{1,0:T(8,128)(2,1)S(1)} collective-permute-done((bf16[96,2048]{1,0:T(8,128)(2,1)S(1)}, bf16[96,2048]{1,0:T(8,128)(2,1)S(1)}, u32[]{:S(2)}, u32[]{:S(2)}) %collective-permute-start.13) | collective-permute-done | bytes 393248 | tf_op jit(solution)/shard_map/ppermute | solution.py:199
  47.3 1.4 %collective-permute-done.12 = bf16[96,2048]{1,0:T(8,128)(2,1)S(1)} collective-permute-done((bf16[96,2048]{1,0:T(8,128)(2,1)S(1)}, bf16[96,2048]{1,0:T(8,128)(2,1)S(1)}, u32[]{:S(2)}, u32[]{:S(2)}) %collective-permute-start.12) | collective-permute-done | bytes 393248 | tf_op jit(solution)/shard_map/ppermute | solution.py:199
  49.1 2.3 %hidden.3 = (bf16[192,512]{1,0:T(8,128)(2,1)S(1)}, bf16[192,512]{1,0:T(8,128)(2,1)S(1)}, bf16[192,512]{1,0:T(8,128)(2,1)S(1)}, bf16[192,512]{1,0:T(8,128)(2,1)S(1)}) custom-call(bf16[192,2048]{1,0:T(8,128)(2,1)S(1)} %get-tuple-element.130.in_ref, bf16[192,2048]{1,0:T(8,128)(2,1)S(1)} %pad_maximum_fusion.1.cot_ref, bf16[2048,512]{1,0:T(8,128)(2,1)S(1)} %bitcast.30, ...), custom_call_target="tpu_custom_call" | custom-call | flops 1610612736 | bytes 8388608 | tf_op jit(solution)/shard_map/hidden/pallas_call | solution.py:39
  51.5 2.2 %rows.3 = (f32[1,2048]{1,0:T(1,128)S(1)}, f32[96,2048]{1,0:T(8,128)S(1)}, bf16[96,2048]{1,0:T(8,128)(2,1)S(1)}, f32[96,2048]{1,0:T(8,128)S(1)}, bf16[96,2048]{1,0:T(8,128)(2,1)S(1)}) custom-call(bf16[192,2048]{1,0:T(8,128)(2,1)S(1)} %get-tuple-element.130.in_ref, bf16[192,512]{1,0:T(8,128)(2,1)S(1)} %get-tuple-element.93.hid_a, ...), custom_call_target="tpu_custom_call" | custom-call | flops 1610612736 | bytes 8388608 | tf_op jit(solution)/shard_map/rows/pallas_call | solution.py:39
  55.8 1.4 %collective-permute-start.21 = (bf16[104,2048]{1,0:T(8,128)(2,1)S(1)}, bf16[104,2048]{1,0:T(8,128)(2,1)S(1)}, u32[]{:S(2)}, u32[]{:S(2)}) collective-permute-start(bf16[104,2048]{1,0:T(8,128)(2,1)S(1)} %pad_maximum_fusion.3), channel_id=1, source_target_pairs={{0,8},{4,12},{8,0},{12,4},{16,24},{20,28},{24,16},{28,20},{1,9},{5... | collective-permute-start | bytes 1277960 | tf_op jit(solution)/shard_map/ppermute | solution.py:199
  60.5 3.2 %grad_up.1 = bf16[2048,512]{1,0:T(8,128)(2,1)} custom-call(bf16[384,2048]{1,0:T(8,128)(2,1)S(1)} %get-tuple-element.129.left_a, bf16[384,2048]{1,0:T(8,128)(2,1)S(1)} %collective-permute-done.22.left_b, bf16[384,512]{1,0:T(8,128)(2,1)S(1)} %pad_maximum_fusion.9.right_a, bf16[768,512]{1,0:T(8,128)(2,1)S(1)} %collective-permute-done.17.left_b.right_b), custom_call_target="tpu_custom_call" | custom-call | flops 805306368 | bytes 8388608 | tf_op jit(solution)/shard_map/grad_up/pallas_call | solution.py:39
  63.7 2.2 %collective-permute-done.20 = bf16[96,2048]{1,0:T(8,128)(2,1)S(1)} collective-permute-done((bf16[96,2048]{1,0:T(8,128)(2,1)S(1)}, bf16[96,2048]{1,0:T(8,128)(2,1)S(1)}, u32[]{:S(2)}, u32[]{:S(2)}) %collective-permute-start.20) | collective-permute-done | bytes 393248 | tf_op jit(solution)/shard_map/ppermute | solution.py:199
  65.9 2.7 %collective-permute-done.21 = bf16[104,2048]{1,0:T(8,128)(2,1)S(1)} collective-permute-done((bf16[104,2048]{1,0:T(8,128)(2,1)S(1)}, bf16[104,2048]{1,0:T(8,128)(2,1)S(1)}, u32[]{:S(2)}, u32[]{:S(2)}) %collective-permute-start.21) | collective-permute-done | bytes 426016 | tf_op jit(solution)/shard_map/ppermute | solution.py:199
  68.7 1.4 %collective-permute-start.23 = (bf16[48,2048]{1,0:T(8,128)(2,1)S(1)}, bf16[48,2048]{1,0:T(8,128)(2,1)S(1)}, u32[]{:S(2)}, u32[]{:S(2)}) collective-permute-start(bf16[48,2048]{1,0:T(8,128)(2,1)S(1)} %slice.226), channel_id=1, source_target_pairs={{0,8},{4,12},{8,0},{12,4},{16,24},{20,28},{24,16},{28,20},{1,9},{5... | collective-permute-start | bytes 589832 | tf_op jit(solution)/shard_map/ppermute | solution.py:199
  71.2 3.4 %grad_down.1 = bf16[512,2048]{1,0:T(8,128)(2,1)} custom-call(bf16[384,512]{1,0:T(8,128)(2,1)S(1)} %pad_maximum_fusion.8.left_a, bf16[768,512]{1,0:T(8,128)(2,1)S(1)} %collective-permute-done.17.left_b.right_b, bf16[384,2048]{1,0:T(8,128)(2,1)S(1)} %constant_dynamic-update-slice_fusion.7.right_a, bf16[384,2048]{1,0:T(8,128)(2,1)S(1)} %collective-permute-done.18.right_b), custom_call_target="tpu_custom_call" | custom-call | flops 805306368 | bytes 8388608 | tf_op jit(solution)/shard_map/grad_down/pallas_call | solution.py:39
  74.8 3.2 %collective-permute-start.19 = (bf16[48,2048]{1,0:T(8,128)(2,1)S(1)}, bf16[48,2048]{1,0:T(8,128)(2,1)S(1)}, u32[]{:S(2)}, u32[]{:S(2)}) collective-permute-start(bf16[48,2048]{1,0:T(8,128)(2,1)S(1)} %pad_maximum_fusion.16), channel_id=1, source_target_pairs={{0,3},{1,0},{2,1},{3,2},{4,7},{5,4},{6,5},{7,6},{8,11},{9,8},{10,9... | collective-permute-start | bytes 589832 | tf_op jit(solution)/shard_map/ppermute | solution.py:202
  78.3 2.2 %collective-permute-start.25 = (bf16[48,2048]{1,0:T(8,128)(2,1)S(1)}, bf16[48,2048]{1,0:T(8,128)(2,1)S(1)}, u32[]{:S(2)}, u32[]{:S(2)}) collective-permute-start(bf16[48,2048]{1,0:T(8,128)(2,1)S(1)} %pad_maximum_fusion.17), channel_id=1, source_target_pairs={{0,2},{1,3},{2,0},{3,1},{4,6},{5,7},{6,4},{7,5},{8,10},{9,11},{10,... | collective-permute-start | bytes 589832 | tf_op jit(solution)/shard_map/ppermute | solution.py:202
  80.8 2.4 %collective-permute-done.27 = f32[16,128]{1,0:T(8,128)S(1)} collective-permute-done((f32[16,128]{1,0:T(8,128)S(1)}, f32[16,128]{1,0:T(8,128)S(1)}, u32[]{:S(2)}, u32[]{:S(2)}) %collective-permute-start.27) | collective-permute-done | bytes 8224 | tf_op jit(solution)/shard_map/ppermute | solution.py:365
  83.4 10.3 %collective-permute-done.28 = f32[16,128]{1,0:T(8,128)S(1)} collective-permute-done((f32[16,128]{1,0:T(8,128)S(1)}, f32[16,128]{1,0:T(8,128)S(1)}, u32[]{:S(2)}, u32[]{:S(2)}) %collective-permute-start.28) | collective-permute-done | bytes 8224 | tf_op jit(solution)/shard_map/ppermute | solution.py:365
  93.8 1.4 %tokens.1 = (bf16[128,2048]{1,0:T(8,128)(2,1)}, bf16[128,2048]{1,0:T(8,128)(2,1)}) custom-call(s32[1,128]{1,0:T(1,128)S(1)} %copy-done.4, bf16[128,2048]{1,0:T(8,128)(2,1)S(1)} %copy-done.2, f32[1,2048]{1,0:T(1,128)S(1)} %bitcast.38, bf16[48,2048]{1,0:T(8,128)(2,1)S(1)} %pad_maximum_fusion.15.refs_0_, bf16[48,2048]{1,0:T(8,128)(2,1)S(1)} %collective-permute-done.19.refs_1_, ...), custom_call_target="tpu_custom_call" | custom-call | tf_op jit(solution)/shard_map/tokens/pallas_call | solution.py:39
  (115 shorter events, 15.3 us)
Async XLA Ops:
  3.2 10.2 %collective-permute-start = (bf16[48,2048]{1,0:T(8,128)(2,1)}, bf16[48,2048]{1,0:T(8,128)(2,1)S(1)}, u32[]{:S(2)}, u32[]{:S(2)}) collective-permute-start(bf16[48,2048]{1,0:T(8,128)(2,1)} %get-tuple-element.61), channel_id=1, source_target_pairs={{0,1},{1,2},{2,3},{3,0},{4,5},{5,6},{6,7},{7,4},{8,9},{9,10},{10,1... | collective-permute-start | bytes 589832 | tf_op jit(solution)/shard_map/ppermute | solution.py:202
  9.8 21.2 %collective-permute-start.9 = (bf16[2048,1024]{1,0:T(8,128)(2,1)S(1)}, bf16[2048,1024]{1,0:T(8,128)(2,1)S(1)}, u32[]{:S(2)}, u32[]{:S(2)}) collective-permute-start(bf16[2048,1024]{1,0:T(8,128)(2,1)S(1)} %pack.1), channel_id=1, source_target_pairs={{0,4},{4,0},{8,12},{12,8},{16,20},{20,16},{24,28},{28,24},{1,5},{5... | collective-permute-start | bytes 12582920 | tf_op jit(solution)/shard_map/ppermute | solution.py:199
  13.4 11.1 %collective-permute-start.3 = (bf16[48,2048]{1,0:T(8,128)(2,1)S(1)}, bf16[48,2048]{1,0:T(8,128)(2,1)S(1)}, u32[]{:S(2)}, u32[]{:S(2)}) collective-permute-start(bf16[48,2048]{1,0:T(8,128)(2,1)S(1)} %copy-done.7), channel_id=1, source_target_pairs={{0,2},{1,3},{2,0},{3,1},{4,6},{5,7},{6,4},{7,5},{8,10},{9,11},{10,... | collective-permute-start | bytes 589832 | tf_op jit(solution)/shard_map/ppermute | solution.py:202
  14.2 5.7 %collective-permute-start.4 = (bf16[48,2048]{1,0:T(8,128)(2,1)S(1)}, bf16[48,2048]{1,0:T(8,128)(2,1)S(1)}, u32[]{:S(2)}, u32[]{:S(2)}) collective-permute-start(bf16[48,2048]{1,0:T(8,128)(2,1)S(1)} %pad_maximum_fusion.12), channel_id=1, source_target_pairs={{0,16},{4,20},{8,24},{12,28},{16,0},{20,4},{24,8},{28,12},{1,17},{... | collective-permute-start | bytes 589832 | tf_op jit(solution)/shard_map/ppermute | solution.py:199
  15.8 7.2 %collective-permute-start.1 = (bf16[48,2048]{1,0:T(8,128)(2,1)S(1)}, bf16[48,2048]{1,0:T(8,128)(2,1)S(1)}, u32[]{:S(2)}, u32[]{:S(2)}) collective-permute-start(bf16[48,2048]{1,0:T(8,128)(2,1)S(1)} %pad_maximum_fusion.11), channel_id=1, source_target_pairs={{0,8},{4,12},{8,0},{12,4},{16,24},{20,28},{24,16},{28,20},{1,9},{5... | collective-permute-start | bytes 589832 | tf_op jit(solution)/shard_map/ppermute | solution.py:199
  19.9 10.8 %collective-permute-start.8 = (bf16[96,2048]{1,0:T(8,128)(2,1)S(1)}, bf16[96,2048]{1,0:T(8,128)(2,1)S(1)}, u32[]{:S(2)}, u32[]{:S(2)}) collective-permute-start(bf16[96,2048]{1,0:T(8,128)(2,1)S(1)} %pad_maximum_fusion.5), channel_id=1, source_target_pairs={{0,8},{4,12},{8,0},{12,4},{16,24},{20,28},{24,16},{28,20},{1,9},{5... | collective-permute-start | bytes 1179656 | tf_op jit(solution)/shard_map/ppermute | solution.py:199
  21.5 6.1 %collective-permute-start.5 = (bf16[48,2048]{1,0:T(8,128)(2,1)S(1)}, bf16[48,2048]{1,0:T(8,128)(2,1)S(1)}, u32[]{:S(2)}, u32[]{:S(2)}) collective-permute-start(bf16[48,2048]{1,0:T(8,128)(2,1)S(1)} %copy-done.6), channel_id=1, source_target_pairs={{0,3},{1,0},{2,1},{3,2},{4,7},{5,4},{6,5},{7,6},{8,11},{9,8},{10,9... | collective-permute-start | bytes 589832 | tf_op jit(solution)/shard_map/ppermute | solution.py:202
  23.0 8.0 %collective-permute-start.2 = (bf16[96,2048]{1,0:T(8,128)(2,1)S(1)}, bf16[96,2048]{1,0:T(8,128)(2,1)S(1)}, u32[]{:S(2)}, u32[]{:S(2)}) collective-permute-start(bf16[96,2048]{1,0:T(8,128)(2,1)S(1)} %pad_maximum_fusion.4), channel_id=1, source_target_pairs={{0,16},{4,20},{8,24},{12,28},{16,0},{20,4},{24,8},{28,12},{1,17},{... | collective-permute-start | bytes 1179656 | tf_op jit(solution)/shard_map/ppermute | solution.py:199
  27.7 6.5 %collective-permute-start.6 = (bf16[48,2048]{1,0:T(8,128)(2,1)S(1)}, bf16[48,2048]{1,0:T(8,128)(2,1)S(1)}, u32[]{:S(2)}, u32[]{:S(2)}) collective-permute-start(bf16[48,2048]{1,0:T(8,128)(2,1)S(1)} %get-tuple-element.85), channel_id=1, source_target_pairs={{0,8},{4,12},{8,0},{12,4},{16,24},{20,28},{24,16},{28,20},{1,9},{5... | collective-permute-start | bytes 589832 | tf_op jit(solution)/shard_map/ppermute | solution.py:199
  29.3 5.9 %collective-permute-start.7 = (bf16[48,2048]{1,0:T(8,128)(2,1)S(1)}, bf16[48,2048]{1,0:T(8,128)(2,1)S(1)}, u32[]{:S(2)}, u32[]{:S(2)}) collective-permute-start(bf16[48,2048]{1,0:T(8,128)(2,1)S(1)} %get-tuple-element.89), channel_id=1, source_target_pairs={{0,16},{4,20},{8,24},{12,28},{16,0},{20,4},{24,8},{28,12},{1,17},{... | collective-permute-start | bytes 589832 | tf_op jit(solution)/shard_map/ppermute | solution.py:199
  35.2 12.1 %collective-permute-start.13 = (bf16[96,2048]{1,0:T(8,128)(2,1)S(1)}, bf16[96,2048]{1,0:T(8,128)(2,1)S(1)}, u32[]{:S(2)}, u32[]{:S(2)}) collective-permute-start(bf16[96,2048]{1,0:T(8,128)(2,1)S(1)} %pad_maximum_fusion.7), channel_id=1, source_target_pairs={{0,8},{4,12},{8,0},{12,4},{16,24},{20,28},{24,16},{28,20},{1,9},{5... | collective-permute-start | bytes 1179656 | tf_op jit(solution)/shard_map/ppermute | solution.py:199
  36.7 12.1 %collective-permute-start.12 = (bf16[96,2048]{1,0:T(8,128)(2,1)S(1)}, bf16[96,2048]{1,0:T(8,128)(2,1)S(1)}, u32[]{:S(2)}, u32[]{:S(2)}) collective-permute-start(bf16[96,2048]{1,0:T(8,128)(2,1)S(1)} %pad_maximum_fusion.6), channel_id=1, source_target_pairs={{0,16},{4,20},{8,24},{12,28},{16,0},{20,4},{24,8},{28,12},{1,17},{... | collective-permute-start | bytes 1179656 | tf_op jit(solution)/shard_map/ppermute | solution.py:199
  39.7 15.5 %collective-permute-start.10 = (bf16[96,2048]{1,0:T(8,128)(2,1)S(1)}, bf16[96,2048]{1,0:T(8,128)(2,1)S(1)}, u32[]{:S(2)}, u32[]{:S(2)}) collective-permute-start(bf16[96,2048]{1,0:T(8,128)(2,1)S(1)} %get-tuple-element.77), channel_id=1, source_target_pairs={{0,16},{4,20},{8,24},{12,28},{16,0},{20,4},{24,8},{28,12},{1,17},{... | collective-permute-start | bytes 1179656 | tf_op jit(solution)/shard_map/ppermute | solution.py:199
  41.1 14.6 %collective-permute-start.11 = (bf16[96,2048]{1,0:T(8,128)(2,1)S(1)}, bf16[96,2048]{1,0:T(8,128)(2,1)S(1)}, u32[]{:S(2)}, u32[]{:S(2)}) collective-permute-start(bf16[96,2048]{1,0:T(8,128)(2,1)S(1)} %get-tuple-element.78), channel_id=1, source_target_pairs={{0,8},{4,12},{8,0},{12,4},{16,24},{20,28},{24,16},{28,20},{1,9},{5... | collective-permute-start | bytes 1179656 | tf_op jit(solution)/shard_map/ppermute | solution.py:199
  53.8 1.2 %collective-permute-start.14 = (f32[1,2048]{1,0:T(1,128)S(1)}, f32[1,2048]{1,0:T(1,128)S(1)}, u32[]{:S(2)}, u32[]{:S(2)}) collective-permute-start(f32[1,2048]{1,0:T(1,128)S(1)} %add.52), channel_id=1, source_target_pairs={{0,4},{4,0},{8,12},{12,8},{16,20},{20,16},{24,28},{28,24},{1,5},{5... | collective-permute-start | bytes 24584 | tf_op jit(solution)/shard_map/ppermute | solution.py:199
  53.9 12.0 %collective-permute-start.20 = (bf16[96,2048]{1,0:T(8,128)(2,1)S(1)}, bf16[96,2048]{1,0:T(8,128)(2,1)S(1)}, u32[]{:S(2)}, u32[]{:S(2)}) collective-permute-start(bf16[96,2048]{1,0:T(8,128)(2,1)S(1)} %get-tuple-element.103), channel_id=1, source_target_pairs={{0,16},{4,20},{8,24},{12,28},{16,0},{20,4},{24,8},{28,12},{1,17},{... | collective-permute-start | bytes 1179656 | tf_op jit(solution)/shard_map/ppermute | solution.py:199
  54.7 2.7 %collective-permute-start.17 = (bf16[768,512]{1,0:T(8,128)(2,1)S(1)}, bf16[768,512]{1,0:T(8,128)(2,1)S(1)}, u32[]{:S(2)}, u32[]{:S(2)}) collective-permute-start(bf16[768,512]{1,0:T(8,128)(2,1)S(1)} %pad_maximum_fusion.2), channel_id=1, source_target_pairs={{0,4},{4,0},{8,12},{12,8},{16,20},{20,16},{24,28},{28,24},{1,5},{5... | collective-permute-start | bytes 2359304 | tf_op jit(solution)/shard_map/ppermute | solution.py:199
  55.0 4.2 %collective-permute-start.22 = (bf16[384,2048]{1,0:T(8,128)(2,1)S(1)}, bf16[384,2048]{1,0:T(8,128)(2,1)S(1)}, u32[]{:S(2)}, u32[]{:S(2)}) collective-permute-start(bf16[384,2048]{1,0:T(8,128)(2,1)S(1)} %get-tuple-element.129.left_a), channel_id=1, source_target_pairs={{0,4},{4,0},{8,12},{12,8},{16,20},{20,16},{24,28},{28,24},{1,5},{5... | collective-permute-start | bytes 4718600 | tf_op jit(solution)/shard_map/ppermute | solution.py:199
  55.2 16.0 %collective-permute-start.18 = (bf16[384,2048]{1,0:T(8,128)(2,1)S(1)}, bf16[384,2048]{1,0:T(8,128)(2,1)S(1)}, u32[]{:S(2)}, u32[]{:S(2)}) collective-permute-start(bf16[384,2048]{1,0:T(8,128)(2,1)S(1)} %constant_dynamic-update-slice_fusion.7.right_a), channel_id=1, source_target_pairs={{0,4},{4,0},{8,12},{12,8},{16,20},{20,16},{24,28},{28,24},{1,5},{5... | collective-permute-start | bytes 4718600 | tf_op jit(solution)/shard_map/ppermute | solution.py:199
  55.8 12.7 %collective-permute-start.21 = (bf16[104,2048]{1,0:T(8,128)(2,1)S(1)}, bf16[104,2048]{1,0:T(8,128)(2,1)S(1)}, u32[]{:S(2)}, u32[]{:S(2)}) collective-permute-start(bf16[104,2048]{1,0:T(8,128)(2,1)S(1)} %pad_maximum_fusion.3), channel_id=1, source_target_pairs={{0,8},{4,12},{8,0},{12,4},{16,24},{20,28},{24,16},{28,20},{1,9},{5... | collective-permute-start | bytes 1277960 | tf_op jit(solution)/shard_map/ppermute | solution.py:199
  57.4 17.2 %collective-permute-start.15 = (bf16[48,2048]{1,0:T(8,128)(2,1)S(1)}, bf16[48,2048]{1,0:T(8,128)(2,1)S(1)}, u32[]{:S(2)}, u32[]{:S(2)}) collective-permute-start(bf16[48,2048]{1,0:T(8,128)(2,1)S(1)} %slice.227), channel_id=1, source_target_pairs={{0,8},{4,12},{8,0},{12,4},{16,24},{20,28},{24,16},{28,20},{1,9},{5... | collective-permute-start | bytes 589832 | tf_op jit(solution)/shard_map/ppermute | solution.py:199
  59.2 15.4 %collective-permute-start.16 = (bf16[48,2048]{1,0:T(8,128)(2,1)S(1)}, bf16[48,2048]{1,0:T(8,128)(2,1)S(1)}, u32[]{:S(2)}, u32[]{:S(2)}) collective-permute-start(bf16[48,2048]{1,0:T(8,128)(2,1)S(1)} %fusion.6), channel_id=1, source_target_pairs={{0,16},{4,20},{8,24},{12,28},{16,0},{20,4},{24,8},{28,12},{1,17},{... | collective-permute-start | bytes 589832 | tf_op jit(solution)/shard_map/ppermute | solution.py:199
  68.7 9.3 %collective-permute-start.23 = (bf16[48,2048]{1,0:T(8,128)(2,1)S(1)}, bf16[48,2048]{1,0:T(8,128)(2,1)S(1)}, u32[]{:S(2)}, u32[]{:S(2)}) collective-permute-start(bf16[48,2048]{1,0:T(8,128)(2,1)S(1)} %slice.226), channel_id=1, source_target_pairs={{0,8},{4,12},{8,0},{12,4},{16,24},{20,28},{24,16},{28,20},{1,9},{5... | collective-permute-start | bytes 589832 | tf_op jit(solution)/shard_map/ppermute | solution.py:199
  70.3 7.7 %collective-permute-start.24 = (bf16[56,2048]{1,0:T(8,128)(2,1)S(1)}, bf16[56,2048]{1,0:T(8,128)(2,1)S(1)}, u32[]{:S(2)}, u32[]{:S(2)}) collective-permute-start(bf16[56,2048]{1,0:T(8,128)(2,1)S(1)} %pad_maximum_fusion.10), channel_id=1, source_target_pairs={{0,16},{4,20},{8,24},{12,28},{16,0},{20,4},{24,8},{28,12},{1,17},{... | collective-permute-start | bytes 688136 | tf_op jit(solution)/shard_map/ppermute | solution.py:199
  74.8 19.0 %collective-permute-start.19 = (bf16[48,2048]{1,0:T(8,128)(2,1)S(1)}, bf16[48,2048]{1,0:T(8,128)(2,1)S(1)}, u32[]{:S(2)}, u32[]{:S(2)}) collective-permute-start(bf16[48,2048]{1,0:T(8,128)(2,1)S(1)} %pad_maximum_fusion.16), channel_id=1, source_target_pairs={{0,3},{1,0},{2,1},{3,2},{4,7},{5,4},{6,5},{7,6},{8,11},{9,8},{10,9... | collective-permute-start | bytes 589832 | tf_op jit(solution)/shard_map/ppermute | solution.py:202
  78.0 15.7 %copy-start.2 = (bf16[128,2048]{1,0:T(8,128)(2,1)S(1)}, bf16[128,2048]{1,0:T(8,128)(2,1)}, u32[]{:S(2)}) copy-start(bf16[128,2048]{1,0:T(8,128)(2,1)} %tok_ref.1) | copy-start | bytes 1572868
  78.0 15.7 %copy-start.3 = (f32[2048]{0:T(1024)S(1)}, f32[2048]{0:T(1024)}, u32[]{:S(2)}) copy-start(f32[2048]{0:T(1024)} %param.8) | copy-start | bytes 24580
  78.1 15.7 %copy-start.4 = (s32[1,128]{1,0:T(1,128)S(1)}, s32[1,128]{1,0:T(1,128)}, u32[]{:S(2)}) copy-start(s32[1,128]{1,0:T(1,128)} %get-tuple-element.59.slot_ref) | copy-start | bytes 1540
  78.2 5.0 %collective-permute-start.27 = (f32[16,128]{1,0:T(8,128)S(1)}, f32[16,128]{1,0:T(8,128)S(1)}, u32[]{:S(2)}, u32[]{:S(2)}) collective-permute-start(f32[16,128]{1,0:T(8,128)S(1)} %bitcast.47), channel_id=1, source_target_pairs={{0,1},{1,0},{2,3},{3,2},{4,5},{5,4},{6,7},{7,6},{8,9},{9,8},{10,11... | collective-permute-start | bytes 24584 | tf_op jit(solution)/shard_map/ppermute | solution.py:365
  78.3 15.4 %collective-permute-start.25 = (bf16[48,2048]{1,0:T(8,128)(2,1)S(1)}, bf16[48,2048]{1,0:T(8,128)(2,1)S(1)}, u32[]{:S(2)}, u32[]{:S(2)}) collective-permute-start(bf16[48,2048]{1,0:T(8,128)(2,1)S(1)} %pad_maximum_fusion.17), channel_id=1, source_target_pairs={{0,2},{1,3},{2,0},{3,1},{4,6},{5,7},{6,4},{7,5},{8,10},{9,11},{10,... | collective-permute-start | bytes 589832 | tf_op jit(solution)/shard_map/ppermute | solution.py:202
  80.5 13.2 %collective-permute-start.26 = (bf16[48,2048]{1,0:T(8,128)(2,1)S(1)}, bf16[48,2048]{1,0:T(8,128)(2,1)S(1)}, u32[]{:S(2)}, u32[]{:S(2)}) collective-permute-start(bf16[48,2048]{1,0:T(8,128)(2,1)S(1)} %pad_maximum_fusion.18), channel_id=1, source_target_pairs={{0,1},{1,2},{2,3},{3,0},{4,5},{5,6},{6,7},{7,4},{8,9},{9,10},{10,1... | collective-permute-start | bytes 589832 | tf_op jit(solution)/shard_map/ppermute | solution.py:202
  83.2 10.5 %collective-permute-start.28 = (f32[16,128]{1,0:T(8,128)S(1)}, f32[16,128]{1,0:T(8,128)S(1)}, u32[]{:S(2)}, u32[]{:S(2)}) collective-permute-start(f32[16,128]{1,0:T(8,128)S(1)} %add.66), channel_id=1, source_target_pairs={{0,2},{1,3},{2,0},{3,1},{4,6},{5,7},{6,4},{7,5},{8,10},{9,11},{10,... | collective-permute-start | bytes 24584 | tf_op jit(solution)/shard_map/ppermute | solution.py:365
  (5 other events, 19.8 us)
